TPU v7x, 32 devices: a whole 2x2x4 slice. The times are simulated.
32 devices in a mesh: gx: 8 (over y, x, core), gy: 4 (over z).
Axes of the slice: x: 2, y: 2, z: 4, core: 2. Of those that a mesh axis runs over, the one named last changes fastest.
Arguments:
- solution: float32 [8, 4, 8, 8, 8, 128], P('gx', 'gy'), as said below
- residual: float32 [8, 4, 8, 8, 8, 128], P('gx', 'gy'), as said below
- grain_counts: int32 [8, 4, 128], P('gx', 'gy'), may hold values from 0 to 16
Outputs:
- solution_out: float32 [8, 4, 8, 8, 8, 128], P('gx', 'gy')
- residual_out: float32 [8, 4, 8, 8, 8, 128], P('gx', 'gy')
- direction_out: float32 [8, 4, 8, 8, 8, 128], P('gx', 'gy')
- step_sizes: float32 [2], replicated
Inputs may be any that keep to these rules, and one draw needn't show every extreme that they name: `solution`: every node shared by neighbouring elements holds the same value in all of its copies. `residual`: every node shared by neighbouring elements holds the same value in all of its copies.
All inputs are finite; a program needn't handle non-finite values.
Results may differ from a plain program's by a relative error of at most 0.003.
Values sent between devices are 32-bit elements; how exact they have to be, the bound alone decides.
No kernel may reach another device: no remote copies, remote signals or barrier semaphores. Data moves between devices by JAX's collectives and lax.ppermute only.
A program may use at most 64 MiB of HBM per device.

v0:
```python
import math

import jax
import jax.numpy as jnp
import numpy as np
from jax import lax
from jax.sharding import PartitionSpec as P

NODES = 8
MOST_GRAINS = 16
ITERS = 2


shift_mass = 0.1
mean_porosity = 0.7
exact_mode = lax.Precision.HIGHEST


def padded_2(block, sides, width):
    for axis, dim in sides:
        count = lax.axis_size(axis)
        forward = [(i, i + 1) for i in range(count - 1)]
        backward = [(target, source) for source, target in forward]
        low = lax.ppermute(
            lax.slice_in_dim(block, block.shape[dim] - width, None, axis=dim), axis, forward
        )
        high = lax.ppermute(lax.slice_in_dim(block, 0, width, axis=dim), axis, backward)
        block = jnp.concatenate([low, block, high], axis=dim)
    return block


def legendre_columns(node_set, degree):
    table = [node_set * 0.0 + 1.0, node_set]
    for order in range(2, degree + 1):
        table.append(
            ((2 * order - 1) * node_set * table[order - 1] - (order - 1) * table[order - 2]) / order
        )
    return table


def gll_tables():
    degree = NODES - 1
    node_set = np.cos(math.pi * np.arange(degree + 1) / degree)
    for sweep in range(100):
        table = legendre_columns(node_set, degree)
        node_set = node_set - (node_set * table[degree] - table[degree - 1]) / (
            (degree + 1) * table[degree]
        )
    node_set = node_set[::-1].copy()
    values = legendre_columns(node_set, degree)[degree]
    weights = 2.0 / (degree * (degree + 1) * values**2)
    derivative = np.zeros((NODES, NODES))
    for row_index in range(NODES):
        for column_index in range(NODES):
            if row_index != column_index:
                derivative[row_index, column_index] = values[row_index] / (
                    values[column_index] * (node_set[row_index] - node_set[column_index])
                )
    derivative[0, 0] = -degree * (degree + 1) / 4.0
    derivative[NODES - 1, NODES - 1] = degree * (degree + 1) / 4.0
    return (weights, derivative)


def jacobi_eigen(matrix):
    size_now = matrix.shape[0]
    current = matrix.copy()
    vectors = np.eye(size_now)
    for sweep in range(12):
        for first in range(size_now - 1):
            for second in range(first + 1, size_now):
                off_value = current[first, second]
                safe_value = np.where(off_value == 0.0, 1e-300, off_value)
                theta = (current[second, second] - current[first, first]) / (2.0 * safe_value)
                sign_value = np.where(theta >= 0.0, 1.0, -1.0)
                tangent = sign_value / (np.abs(theta) + np.sqrt(theta * theta + 1.0))
                cosine = 1.0 / np.sqrt(tangent * tangent + 1.0)
                sine = tangent * cosine
                rotation = np.eye(size_now)
                rotation[first, first] = cosine
                rotation[second, second] = cosine
                rotation[first, second] = sine
                rotation[second, first] = -sine
                current = rotation.T @ current @ rotation
                vectors = vectors @ rotation
    eigen_values = np.array([current[index, index] for index in range(size_now)])
    return (eigen_values, vectors)


def schwarz_tables():
    weights, derivative = gll_tables()
    stiffness = derivative.T @ (weights[:, None] * derivative)
    total_nodes = 3 * (NODES - 1) + 1
    three_stiffness = np.zeros((total_nodes, total_nodes))
    three_mass = np.zeros(total_nodes)
    for element in range(3):
        start_node = element * (NODES - 1)
        three_stiffness[
            start_node : start_node + NODES, start_node : start_node + NODES
        ] += stiffness
        three_mass[start_node : start_node + NODES] += weights
    chosen = np.array([NODES - 2] + list(range(NODES - 1, 2 * NODES - 1)) + [2 * NODES - 1])
    local_stiffness = three_stiffness[chosen][:, chosen]
    local_mass = three_mass[chosen]
    scaling = 1.0 / np.sqrt(local_mass)
    symmetric = scaling[:, None] * local_stiffness * scaling[None, :]
    symmetric = 0.5 * (symmetric + symmetric.T)
    eigen_values, eigen_vectors = jacobi_eigen(symmetric)
    return (scaling[:, None] * eigen_vectors, eigen_values)


def cosine_basis(column_count):
    position = jnp.arange(column_count, dtype=jnp.float32)
    phase_table = math.pi * (position[:, None] + 0.5) * position[None, :] / column_count
    norm_factor = jnp.where(
        position == 0, math.sqrt(1.0 / column_count), math.sqrt(2.0 / column_count)
    )
    eigen_basis = jnp.cos(phase_table) * norm_factor[None, :]
    eigen_values = 2.0 - 2.0 * jnp.cos(math.pi * position / column_count)
    return (eigen_basis, eigen_values)


def coarse_solve(coarse_source, column_length):
    basis_first, eigen_first = cosine_basis(coarse_source.shape[0])
    basis_second, eigen_second = cosine_basis(coarse_source.shape[1])
    spectrum = jnp.einsum(
        "pa,pq,qb->ab", basis_first, coarse_source, basis_second, precision=exact_mode
    )
    divisor = (
        2.0 * mean_porosity * column_length * (eigen_first[:, None] + eigen_second[None, :])
        + 8.0 * shift_mass * column_length
    )
    return jnp.einsum(
        "pa,ab,qb->pq", basis_first, spectrum / divisor, basis_second, precision=exact_mode
    )


def share_weights(column_count, points):
    column = jnp.arange(column_count)
    identity = (column[:, None] == column[None, :]).astype(jnp.float32)
    left_side = (column[None, :] == column[:, None] - 1).astype(jnp.float32)
    right_side = (column[None, :] == column[:, None] + 1).astype(jnp.float32)
    has_left = (column > 0).astype(jnp.float32)
    has_right = (column < column_count - 1).astype(jnp.float32)
    lowest = identity * (1.0 - 0.5 * has_left[:, None]) + 0.5 * left_side
    highest = identity * (1.0 - 0.5 * has_right[:, None]) + 0.5 * right_side
    table = jnp.broadcast_to(identity[:, None, :], (column_count, points, column_count))
    return table.at[:, 0, :].set(lowest).at[:, points - 1, :].set(highest)


def multiplicity_inverse(column_count, points):
    column = jnp.arange(column_count)[:, None]
    node_index = jnp.arange(points)[None, :]
    shared = (node_index == 0) & (column > 0) | (node_index == points - 1) & (
        column < column_count - 1
    )
    return 1.0 / (1.0 + shared.astype(jnp.float32))


def shift_elements(layers, element_axis, toward):
    extent = layers.shape[element_axis]
    widths = [(0, 0)] * layers.ndim
    if toward > 0:
        retained = lax.slice_in_dim(layers, 0, extent - 1, axis=element_axis)
        widths[element_axis] = (1, 0)
    else:
        retained = lax.slice_in_dim(layers, 1, extent, axis=element_axis)
        widths[element_axis] = (0, 1)
    return jnp.pad(retained, widths)


def extend(nodal_field, node_axis, element_axis):
    points = nodal_field.shape[node_axis]
    lower_layer = shift_elements(
        lax.slice_in_dim(nodal_field, points - 2, points - 1, axis=node_axis), element_axis, 1
    )
    upper_layer = shift_elements(
        lax.slice_in_dim(nodal_field, 1, 2, axis=node_axis), element_axis, -1
    )
    return jnp.concatenate([lower_layer, nodal_field, upper_layer], axis=node_axis)


def spread(extended, node_axis, element_axis):
    points = extended.shape[node_axis] - 2
    own_part = lax.slice_in_dim(extended, 1, points + 1, axis=node_axis)
    lower_layer = shift_elements(
        lax.slice_in_dim(extended, points, points + 2, axis=node_axis), element_axis, 1
    )
    upper_layer = shift_elements(lax.slice_in_dim(extended, 0, 2, axis=node_axis), element_axis, -1)
    lower_widths = [(0, 0)] * extended.ndim
    lower_widths[node_axis] = (0, points - 2)
    upper_widths = [(0, 0)] * extended.ndim
    upper_widths[node_axis] = (points - 2, 0)
    return own_part + jnp.pad(lower_layer, lower_widths) + jnp.pad(upper_layer, upper_widths)


def schwarz_solve(extended, eigen_basis, eigen_values):
    first_pass = jnp.einsum("ia,...ijke->...ajke", eigen_basis, extended, precision=exact_mode)
    second_pass = jnp.einsum("jb,...ajke->...abke", eigen_basis, first_pass, precision=exact_mode)
    third_pass = jnp.einsum("kc,...abke->...abce", eigen_basis, second_pass, precision=exact_mode)
    divisor = (
        mean_porosity
        * (eigen_values[:, None, None] + eigen_values[None, :, None] + eigen_values[None, None, :])
        + shift_mass
    )
    scaled = third_pass / divisor[..., None]
    back_first = jnp.einsum("ia,...abce->...ibce", eigen_basis, scaled, precision=exact_mode)
    back_second = jnp.einsum("jb,...ibce->...ijce", eigen_basis, back_first, precision=exact_mode)
    return jnp.einsum("kc,...ijce->...ijke", eigen_basis, back_second, precision=exact_mode)


def apply_local(nodal_field, coupling, derivative, weights_cube):
    grad_first = jnp.einsum("ai,...ijke->...ajke", derivative, nodal_field, precision=exact_mode)
    flux_first = jnp.einsum(
        "ai,...ajke->...ijke", derivative, coupling * grad_first, precision=exact_mode
    )
    grad_second = jnp.einsum("bj,...ijke->...ibke", derivative, nodal_field, precision=exact_mode)
    flux_second = jnp.einsum(
        "bj,...ibke->...ijke", derivative, coupling * grad_second, precision=exact_mode
    )
    grad_third = jnp.einsum("ck,...ijke->...ijce", derivative, nodal_field, precision=exact_mode)
    flux_third = jnp.einsum(
        "ck,...ijce->...ijke", derivative, coupling * grad_third, precision=exact_mode
    )
    return (
        flux_first + flux_second + flux_third + shift_mass * weights_cube[..., None] * nodal_field
    )


def assemble_z(nodal_field):
    points = nodal_field.shape[-2]
    shared = nodal_field[..., points - 1, :-1] + nodal_field[..., 0, 1:]
    return nodal_field.at[..., points - 1, :-1].set(shared).at[..., 0, 1:].set(shared)


def collect(padded, axis_number, halo_width, skipped):
    extent = padded.shape[axis_number]
    points = extent - 2 * halo_width - 2 * skipped
    core_part = lax.slice_in_dim(
        padded, halo_width + skipped, halo_width + skipped + points, axis=axis_number
    )
    lower_layer = lax.slice_in_dim(padded, 0, halo_width, axis=axis_number)
    upper_layer = lax.slice_in_dim(padded, extent - halo_width, extent, axis=axis_number)
    lower_widths = [(0, 0)] * padded.ndim
    lower_widths[axis_number] = (0, points - halo_width)
    upper_widths = [(0, 0)] * padded.ndim
    upper_widths[axis_number] = (points - halo_width, 0)
    return core_part + jnp.pad(lower_layer, lower_widths) + jnp.pad(upper_layer, upper_widths)


def pick_frame(framed, axis_number):
    extent = framed.shape[axis_number]
    return jnp.concatenate(
        [
            lax.slice_in_dim(framed, 0, 1, axis=axis_number),
            lax.slice_in_dim(framed, 2, extent - 2, axis=axis_number),
            lax.slice_in_dim(framed, extent - 1, extent, axis=axis_number),
        ],
        axis=axis_number,
    )


def shards(solution, residual, grain_counts):
    weights_np, derivative_np = gll_tables()
    weights = jnp.asarray(weights_np, dtype=jnp.float32)
    derivative = jnp.asarray(derivative_np, dtype=jnp.float32)
    weights_cube = weights[:, None, None] * weights[None, :, None] * weights[None, None, :]
    basis_np, eigen_np = schwarz_tables()
    eigen_basis = jnp.asarray(basis_np, dtype=jnp.float32)
    eigen_values = jnp.asarray(eigen_np, dtype=jnp.float32)
    shard_shape = solution.shape
    points = shard_shape[2]
    column_length = shard_shape[5]
    solution = solution.reshape(shard_shape[2:])
    residual = residual.reshape(shard_shape[2:])
    porosity = 1.0 - 0.6 * grain_counts.reshape(column_length).astype(jnp.float32) / MOST_GRAINS
    coupling = weights_cube[..., None] * porosity[None, None, None, :]
    count_first = lax.axis_size("gx")
    count_second = lax.axis_size("gy")
    index_first = lax.axis_index("gx")
    index_second = lax.axis_index("gy")
    inverse_first = lax.dynamic_index_in_dim(
        multiplicity_inverse(count_first, points), index_first, 0, keepdims=False
    )
    inverse_second = lax.dynamic_index_in_dim(
        multiplicity_inverse(count_second, points), index_second, 0, keepdims=False
    )
    inverse_third = multiplicity_inverse(column_length, points).T
    inverse_all = (
        inverse_first[:, None, None, None]
        * inverse_second[None, :, None, None]
        * inverse_third[None, None, :, :]
    )
    share_first = lax.dynamic_index_in_dim(
        share_weights(count_first, points), index_first, 0, keepdims=False
    )
    share_second = lax.dynamic_index_in_dim(
        share_weights(count_second, points), index_second, 0, keepdims=False
    )
    residual_frame = residual
    coarse_source = jnp.zeros((count_first, count_second), jnp.float32)
    direction = residual
    previous_inner = jnp.float32(1.0)
    step_list = []
    for step_index in range(ITERS):
        residual_frame = padded_2(residual, (("gx", 0), ("gy", 1)), 2)
        columns = jnp.sum(inverse_all * residual, axis=(2, 3))
        coarse_source = lax.psum(
            jnp.einsum("ij,ia,jb->ab", columns, share_first, share_second, precision=exact_mode),
            ("gx", "gy"),
        )
        extended = extend(pick_frame(pick_frame(residual_frame, 0), 1), 2, 3)
        local_solution = schwarz_solve(extended, eigen_basis, eigen_values)
        partial_value = spread(local_solution, 2, 3)
        padded = padded_2(partial_value, (("gx", 0), ("gy", 1)), 2)
        schwarz_part = collect(collect(padded, 0, 2, 1), 1, 2, 1)
        coarse_field = coarse_solve(coarse_source, column_length)
        lifted = jnp.einsum(
            "ia,ab,jb->ij", share_first, coarse_field, share_second, precision=exact_mode
        )
        preconditioned = schwarz_part + lifted[:, :, None, None]
        precond_inner = lax.psum(jnp.sum(inverse_all * residual * preconditioned), ("gx", "gy"))
        if step_index == 0:
            direction = preconditioned
        else:
            direction = preconditioned + precond_inner / previous_inner * direction
        image_local = assemble_z(apply_local(direction, coupling, derivative, weights_cube))
        padded = padded_2(image_local, (("gx", 0), ("gy", 1)), 1)
        image = collect(collect(padded, 0, 1, 0), 1, 1, 0)
        local_curvature = jnp.sum(inverse_all * direction * image)
        curvature = lax.psum(local_curvature, ("gx", "gy"))
        step_size = precond_inner / curvature
        solution = solution + step_size * direction
        residual = residual - step_size * image
        previous_inner = precond_inner
        step_list.append(step_size)
    return (
        solution.reshape(shard_shape),
        residual.reshape(shard_shape),
        direction.reshape(shard_shape),
        jnp.stack(step_list),
    )


def solution(mesh):
    return jax.shard_map(
        shards,
        mesh=mesh,
        in_specs=(
            P("gx", "gy", None, None, None, None),
            P("gx", "gy", None, None, None, None),
            P("gx", "gy", None),
        ),
        out_specs=(
            P("gx", "gy", None, None, None, None),
            P("gx", "gy", None, None, None, None),
            P("gx", "gy", None, None, None, None),
            P(),
        ),
        check_vma=False,
    )
```

profile of v0, /device:TPU:0, one launch (start us, length us, event | category | flops | bytes accessed | tf_op | source)
XLA Modules:
  0.0 354.9 jit_solution(1302308959439816046)
XLA Ops:
  0.6 1.1 copy.208
  1.8 2.5 collective-permute-start
  4.3 1.3 collective-permute-start.1
  8.4 43.9 %psum.42 = f32[8,4]{0,1:T(4,128)S(1)} all-reduce(f32[8,4]{0,1:T(4,128)S(1)} %fusion.116), channel_id=1, replica_groups=mesh['gx'=8,'gy'=4] {'gx','gy'}, use_global_device_ids=true, to_apply=%region_1.2 | all-reduce | flops 32 | bytes 256 | tf_op jit(solution)/shard_map/psum | solution.py:307
  53.6 3.4 collective-permute-start.2
  57.1 1.3 collective-permute-start.3
  58.5 1.1 collective-permute-done.2
  59.6 4.4 %collective-permute-done.3 = f32[12,2,8,128]{3,0,2,1:T(8,128)S(1)} collective-permute-done((f32[12,2,8,128]{3,0,2,1:T(8,128)S(1)}, f32[12,2,8,128]{3,0,2,1:T(8,128)S(1)}, u32[]{:S(2)}, u32[]{:S(2)}) %collective-permute-start.3) | collective-permute-done | bytes 98336 | tf_op jit(solution)/shard_map/ppermute | solution.py:27
  65.9 1.2 convolution_bitcast_fusion.3
  69.1 1.2 convolution_bitcast_fusion.2
  72.0 1.3 collective-permute-start.4
  73.3 1.3 collective-permute-start.5
  74.8 4.2 %collective-permute-done.5 = f32[2,10,8,128]{3,0,2,1:T(2,128)S(1)} collective-permute-done((f32[2,10,8,128]{3,0,2,1:T(2,128)S(1)}, f32[2,10,8,128]{3,0,2,1:T(2,128)S(1)}, u32[]{:S(2)}, u32[]{:S(2)}) %collective-permute-start.5) | collective-permute-done | bytes 81952 | tf_op jit(solution)/shard_map/ppermute | solution.py:27
  79.0 3.3 collective-permute-start.6
  82.3 1.5 collective-permute-start.7
  84.8 4.4 %collective-permute-done.7 = f32[14,2,8,128]{3,0,2,1:T(8,128)S(1)} collective-permute-done((f32[14,2,8,128]{3,0,2,1:T(8,128)S(1)}, f32[14,2,8,128]{3,0,2,1:T(8,128)S(1)}, u32[]{:S(2)}, u32[]{:S(2)}) %collective-permute-start.7) | collective-permute-done | bytes 114720 | tf_op jit(solution)/shard_map/ppermute | solution.py:27
  93.9 2.6 scatter.35
  96.5 3.6 %collective-permute-start.8 = (f32[1,8,8,128]{3,0,2,1:T(1,128)S(1)}, f32[1,8,8,128]{3,0,2,1:T(1,128)S(1)}, u32[]{:S(2)}, u32[]{:S(2)}) collective-permute-start(f32[1,8,8,128]{3,0,2,1:T(1,128)S(1)} %get-tuple-element.146), channel_id=1, source_target_pairs={{0,4},{4,8},{8,12},{12,16},{16,20},{20,24},{24,28},{1,5},{5,9},{9,... | collective-permute-start | bytes 98312 | tf_op jit(solution)/shard_map/ppermute | solution.py:24
  100.1 1.3 collective-permute-start.9
  101.4 2.7 collective-permute-done.9
  104.2 2.3 collective-permute-start.10
  106.5 1.3 collective-permute-start.11
  108.4 4.3 %collective-permute-done.11 = f32[10,1,8,128]{3,0,2,1:T(8,128)S(1)} collective-permute-done((f32[10,1,8,128]{3,0,2,1:T(8,128)S(1)}, f32[10,1,8,128]{3,0,2,1:T(8,128)S(1)}, u32[]{:S(2)}, u32[]{:S(2)}) %collective-permute-start.11) | collective-permute-done | bytes 40992 | tf_op jit(solution)/shard_map/ppermute | solution.py:27
  113.9 41.5 %all-reduce.20 = (f32[]{:T(128)}, f32[]{:T(128)}) all-reduce(f32[]{:T(128)} %get-tuple-element.109, f32[]{:T(128)} %get-tuple-element.108), channel_id=1, replica_groups=mesh['gx'=8,'gy'=4] {'gx','gy'}, use_global_device_ids=true, to_apply=%region_3.4 | all-reduce | flops 2 | bytes 16 | tf_op jit(solution)/shard_map/psum | solution.py:321
  157.3 41.7 %psum.45 = f32[8,4]{0,1:T(4,128)S(1)} all-reduce(f32[8,4]{0,1:T(4,128)S(1)} %fusion.112), channel_id=1, replica_groups=mesh['gx'=8,'gy'=4] {'gx','gy'}, use_global_device_ids=true, to_apply=%region_7.8 | all-reduce | flops 32 | bytes 256 | tf_op jit(solution)/shard_map/psum | solution.py:307
  199.6 1.3 collective-permute-start.12
  200.9 1.3 collective-permute-start.13
  202.4 4.1 %collective-permute-done.13 = f32[2,8,8,128]{3,0,2,1:T(2,128)S(1)} collective-permute-done((f32[2,8,8,128]{3,0,2,1:T(2,128)S(1)}, f32[2,8,8,128]{3,0,2,1:T(2,128)S(1)}, u32[]{:S(2)}, u32[]{:S(2)}) %collective-permute-start.13) | collective-permute-done | bytes 65568 | tf_op jit(solution)/shard_map/ppermute | solution.py:27
  206.6 2.2 collective-permute-start.14
  208.8 1.5 collective-permute-start.15
  211.3 4.4 %collective-permute-done.15 = f32[12,2,8,128]{3,0,2,1:T(8,128)S(1)} collective-permute-done((f32[12,2,8,128]{3,0,2,1:T(8,128)S(1)}, f32[12,2,8,128]{3,0,2,1:T(8,128)S(1)}, u32[]{:S(2)}, u32[]{:S(2)}) %collective-permute-start.15) | collective-permute-done | bytes 98336 | tf_op jit(solution)/shard_map/ppermute | solution.py:27
  217.0 1.2 convolution_bitcast_fusion.1
  220.3 1.2 convolution_bitcast_fusion
  223.2 3.4 collective-permute-start.16
  226.6 1.3 collective-permute-start.17
  228.0 2.7 collective-permute-done.17
  230.8 2.6 collective-permute-start.18
  233.4 1.3 collective-permute-start.19
  235.9 4.4 %collective-permute-done.19 = f32[14,2,8,128]{3,0,2,1:T(8,128)S(1)} collective-permute-done((f32[14,2,8,128]{3,0,2,1:T(8,128)S(1)}, f32[14,2,8,128]{3,0,2,1:T(8,128)S(1)}, u32[]{:S(2)}, u32[]{:S(2)}) %collective-permute-start.19) | collective-permute-done | bytes 114720 | tf_op jit(solution)/shard_map/ppermute | solution.py:27
  241.5 42.7 %psum.46 = f32[]{:T(128)} all-reduce(f32[]{:T(128)} %multiply_reduce_fusion), channel_id=1, replica_groups=mesh['gx'=8,'gy'=4] {'gx','gy'}, use_global_device_ids=true, to_apply=%region_9.10 | all-reduce | flops 1 | bytes 8 | tf_op jit(solution)/shard_map/psum | solution.py:321
  289.2 2.6 scatter.39
  291.8 1.3 collective-permute-start.20
  293.1 1.3 collective-permute-start.21
  294.4 4.3 %collective-permute-done.21 = f32[1,8,8,128]{3,0,2,1:T(1,128)S(1)} collective-permute-done((f32[1,8,8,128]{3,0,2,1:T(1,128)S(1)}, f32[1,8,8,128]{3,0,2,1:T(1,128)S(1)}, u32[]{:S(2)}, u32[]{:S(2)}) %collective-permute-start.21) | collective-permute-done | bytes 32800 | tf_op jit(solution)/shard_map/ppermute | solution.py:27
  298.7 2.2 collective-permute-start.22
  300.9 1.3 collective-permute-start.23
  302.8 4.3 %collective-permute-done.23 = f32[10,1,8,128]{3,0,2,1:T(8,128)S(1)} collective-permute-done((f32[10,1,8,128]{3,0,2,1:T(8,128)S(1)}, f32[10,1,8,128]{3,0,2,1:T(8,128)S(1)}, u32[]{:S(2)}, u32[]{:S(2)}) %collective-permute-start.23) | collective-permute-done | bytes 40992 | tf_op jit(solution)/shard_map/ppermute | solution.py:27
  309.0 41.4 %psum.47 = f32[]{:T(128)} all-reduce(f32[]{:T(128)} %fusion.75), channel_id=1, replica_groups=mesh['gx'=8,'gy'=4] {'gx','gy'}, use_global_device_ids=true, to_apply=%region_11.12 | all-reduce | flops 1 | bytes 8 | tf_op jit(solution)/shard_map/psum | solution.py:330
  (168 shorter events, 36.6 us)
Async XLA Ops:
  1.7 5.4 %copy-start = (f32[1,1,8,8,8,128]{5,4,3,2,1,0:T(8,128)S(1)}, f32[1,1,8,8,8,128]{5,4,3,2,1,0:T(8,128)}, u32[]{:S(2)}) copy-start(f32[1,1,8,8,8,128]{5,4,3,2,1,0:T(8,128)} %param.24) | copy-start | bytes 786436
  1.8 51.8 %collective-permute-start = (f32[2,8,8,128]{3,0,2,1:T(2,128)S(1)}, f32[2,8,8,128]{3,0,2,1:T(2,128)S(1)}, u32[]{:S(2)}, u32[]{:S(2)}) collective-permute-start(f32[2,8,8,128]{3,0,2,1:T(2,128)S(1)} %get-tuple-element.148), channel_id=1, source_target_pairs={{0,4},{4,8},{8,12},{12,16},{16,20},{20,24},{24,28},{1,5},{5,9},{9,... | collective-permute-start | bytes 196616 | tf_op jit(solution)/shard_map/ppermute | solution.py:24
  4.3 49.3 %collective-permute-start.1 = (f32[2,8,8,128]{3,0,2,1:T(2,128)S(1)}, f32[2,8,8,128]{3,0,2,1:T(2,128)S(1)}, u32[]{:S(2)}, u32[]{:S(2)}) collective-permute-start(f32[2,8,8,128]{3,0,2,1:T(2,128)S(1)} %get-tuple-element.149), channel_id=1, source_target_pairs={{4,0},{8,4},{12,8},{16,12},{20,16},{24,20},{28,24},{5,1},{9,5},{13... | collective-permute-start | bytes 196616 | tf_op jit(solution)/shard_map/ppermute | solution.py:27
  5.8 0.7 copy-start.6
  5.9 0.7 copy-start.7
  53.6 5.9 %collective-permute-start.2 = (f32[12,2,8,128]{3,0,2,1:T(8,128)S(1)}, f32[12,2,8,128]{3,0,2,1:T(8,128)S(1)}, u32[]{:S(2)}, u32[]{:S(2)}) collective-permute-start(f32[12,2,8,128]{3,0,2,1:T(8,128)S(1)} %get-tuple-element.136), channel_id=1, source_target_pairs={{0,1},{1,2},{2,3},{4,5},{5,6},{6,7},{8,9},{9,10},{10,11},{12,13},{... | collective-permute-start | bytes 294920 | tf_op jit(solution)/shard_map/ppermute | solution.py:24
  57.1 6.9 %collective-permute-start.3 = (f32[12,2,8,128]{3,0,2,1:T(8,128)S(1)}, f32[12,2,8,128]{3,0,2,1:T(8,128)S(1)}, u32[]{:S(2)}, u32[]{:S(2)}) collective-permute-start(f32[12,2,8,128]{3,0,2,1:T(8,128)S(1)} %get-tuple-element.137), channel_id=1, source_target_pairs={{1,0},{2,1},{3,2},{5,4},{6,5},{7,6},{9,8},{10,9},{11,10},{13,12},{... | collective-permute-start | bytes 294920 | tf_op jit(solution)/shard_map/ppermute | solution.py:27
  64.4 0.7 copy-start.2
  72.0 2.8 collective-permute-start.4
  73.3 5.7 %collective-permute-start.5 = (f32[2,10,8,128]{3,0,2,1:T(2,128)S(1)}, f32[2,10,8,128]{3,0,2,1:T(2,128)S(1)}, u32[]{:S(2)}, u32[]{:S(2)}) collective-permute-start(f32[2,10,8,128]{3,0,2,1:T(2,128)S(1)} %get-tuple-element.131), channel_id=1, source_target_pairs={{4,0},{8,4},{12,8},{16,12},{20,16},{24,20},{28,24},{5,1},{9,5},{13... | collective-permute-start | bytes 245768 | tf_op jit(solution)/shard_map/ppermute | solution.py:27
  79.0 4.8 %copy-start.8 = (s32[1,1,128]{2,1,0:T(1,128)S(1)}, s32[1,1,128]{2,1,0:T(1,128)}, u32[]{:S(2)}) copy-start(s32[1,1,128]{2,1,0:T(1,128)} %param.25) | copy-start | bytes 1540
  79.0 5.8 %collective-permute-start.6 = (f32[14,2,8,128]{3,0,2,1:T(8,128)S(1)}, f32[14,2,8,128]{3,0,2,1:T(8,128)S(1)}, u32[]{:S(2)}, u32[]{:S(2)}) collective-permute-start(f32[14,2,8,128]{3,0,2,1:T(8,128)S(1)} %get-tuple-element.118), channel_id=1, source_target_pairs={{0,1},{1,2},{2,3},{4,5},{5,6},{6,7},{8,9},{9,10},{10,11},{12,13},{... | collective-permute-start | bytes 344072 | tf_op jit(solution)/shard_map/ppermute | solution.py:24
  82.3 6.9 %collective-permute-start.7 = (f32[14,2,8,128]{3,0,2,1:T(8,128)S(1)}, f32[14,2,8,128]{3,0,2,1:T(8,128)S(1)}, u32[]{:S(2)}, u32[]{:S(2)}) collective-permute-start(f32[14,2,8,128]{3,0,2,1:T(8,128)S(1)} %get-tuple-element.119), channel_id=1, source_target_pairs={{1,0},{2,1},{3,2},{5,4},{6,5},{7,6},{9,8},{10,9},{11,10},{13,12},{... | collective-permute-start | bytes 344072 | tf_op jit(solution)/shard_map/ppermute | solution.py:27
  84.4 4.9 %copy-start.5 = (pred[8]{0:T(512)(128)(4,1)S(1)}, pred[8]{0:T(512)(128)(4,1)}, u32[]{:S(2)}) copy-start(pred[8]{0:T(512)(128)(4,1)} %constant.315.clone.1) | copy-start | bytes 28
  89.7 0.7 copy-start.1
  96.5 4.9 %collective-permute-start.8 = (f32[1,8,8,128]{3,0,2,1:T(1,128)S(1)}, f32[1,8,8,128]{3,0,2,1:T(1,128)S(1)}, u32[]{:S(2)}, u32[]{:S(2)}) collective-permute-start(f32[1,8,8,128]{3,0,2,1:T(1,128)S(1)} %get-tuple-element.146), channel_id=1, source_target_pairs={{0,4},{4,8},{8,12},{12,16},{16,20},{20,24},{24,28},{1,5},{5,9},{9,... | collective-permute-start | bytes 98312 | tf_op jit(solution)/shard_map/ppermute | solution.py:24
  100.1 4.0 %collective-permute-start.9 = (f32[1,8,8,128]{3,0,2,1:T(1,128)S(1)}, f32[1,8,8,128]{3,0,2,1:T(1,128)S(1)}, u32[]{:S(2)}, u32[]{:S(2)}) collective-permute-start(f32[1,8,8,128]{3,0,2,1:T(1,128)S(1)} %get-tuple-element.147), channel_id=1, source_target_pairs={{4,0},{8,4},{12,8},{16,12},{20,16},{24,20},{28,24},{5,1},{9,5},{13... | collective-permute-start | bytes 98312 | tf_op jit(solution)/shard_map/ppermute | solution.py:27
  104.2 4.2 %collective-permute-start.10 = (f32[10,1,8,128]{3,0,2,1:T(8,128)S(1)}, f32[10,1,8,128]{3,0,2,1:T(8,128)S(1)}, u32[]{:S(2)}, u32[]{:S(2)}) collective-permute-start(f32[10,1,8,128]{3,0,2,1:T(8,128)S(1)} %get-tuple-element.140), channel_id=1, source_target_pairs={{0,1},{1,2},{2,3},{4,5},{5,6},{6,7},{8,9},{9,10},{10,11},{12,13},{... | collective-permute-start | bytes 122888 | tf_op jit(solution)/shard_map/ppermute | solution.py:24
  106.5 6.3 %copy-start.4 = (pred[8]{0:T(512)(128)(4,1)S(1)}, pred[8]{0:T(512)(128)(4,1)}, u32[]{:S(2)}) copy-start(pred[8]{0:T(512)(128)(4,1)} %constant.330.clone.1) | copy-start | bytes 28
  106.5 6.2 %collective-permute-start.11 = (f32[10,1,8,128]{3,0,2,1:T(8,128)S(1)}, f32[10,1,8,128]{3,0,2,1:T(8,128)S(1)}, u32[]{:S(2)}, u32[]{:S(2)}) collective-permute-start(f32[10,1,8,128]{3,0,2,1:T(8,128)S(1)} %get-tuple-element.141), channel_id=1, source_target_pairs={{1,0},{2,1},{3,2},{5,4},{6,5},{7,6},{9,8},{10,9},{11,10},{13,12},{... | collective-permute-start | bytes 122888 | tf_op jit(solution)/shard_map/ppermute | solution.py:27
  199.6 2.8 collective-permute-start.12
  200.9 5.7 %collective-permute-start.13 = (f32[2,8,8,128]{3,0,2,1:T(2,128)S(1)}, f32[2,8,8,128]{3,0,2,1:T(2,128)S(1)}, u32[]{:S(2)}, u32[]{:S(2)}) collective-permute-start(f32[2,8,8,128]{3,0,2,1:T(2,128)S(1)} %get-tuple-element.145), channel_id=1, source_target_pairs={{4,0},{8,4},{12,8},{16,12},{20,16},{24,20},{28,24},{5,1},{9,5},{13... | collective-permute-start | bytes 196616 | tf_op jit(solution)/shard_map/ppermute | solution.py:27
  206.6 4.7 %collective-permute-start.14 = (f32[12,2,8,128]{3,0,2,1:T(8,128)S(1)}, f32[12,2,8,128]{3,0,2,1:T(8,128)S(1)}, u32[]{:S(2)}, u32[]{:S(2)}) collective-permute-start(f32[12,2,8,128]{3,0,2,1:T(8,128)S(1)} %get-tuple-element.134), channel_id=1, source_target_pairs={{0,1},{1,2},{2,3},{4,5},{5,6},{6,7},{8,9},{9,10},{10,11},{12,13},{... | collective-permute-start | bytes 294920 | tf_op jit(solution)/shard_map/ppermute | solution.py:24
  208.8 6.9 %collective-permute-start.15 = (f32[12,2,8,128]{3,0,2,1:T(8,128)S(1)}, f32[12,2,8,128]{3,0,2,1:T(8,128)S(1)}, u32[]{:S(2)}, u32[]{:S(2)}) collective-permute-start(f32[12,2,8,128]{3,0,2,1:T(8,128)S(1)} %get-tuple-element.135), channel_id=1, source_target_pairs={{1,0},{2,1},{3,2},{5,4},{6,5},{7,6},{9,8},{10,9},{11,10},{13,12},{... | collective-permute-start | bytes 294920 | tf_op jit(solution)/shard_map/ppermute | solution.py:27
  223.2 4.9 %collective-permute-start.16 = (f32[2,10,8,128]{3,0,2,1:T(2,128)S(1)}, f32[2,10,8,128]{3,0,2,1:T(2,128)S(1)}, u32[]{:S(2)}, u32[]{:S(2)}) collective-permute-start(f32[2,10,8,128]{3,0,2,1:T(2,128)S(1)} %get-tuple-element.126), channel_id=1, source_target_pairs={{0,4},{4,8},{8,12},{12,16},{16,20},{20,24},{24,28},{1,5},{5,9},{9,... | collective-permute-start | bytes 245768 | tf_op jit(solution)/shard_map/ppermute | solution.py:24
  226.6 4.2 %collective-permute-start.17 = (f32[2,10,8,128]{3,0,2,1:T(2,128)S(1)}, f32[2,10,8,128]{3,0,2,1:T(2,128)S(1)}, u32[]{:S(2)}, u32[]{:S(2)}) collective-permute-start(f32[2,10,8,128]{3,0,2,1:T(2,128)S(1)} %get-tuple-element.127), channel_id=1, source_target_pairs={{4,0},{8,4},{12,8},{16,12},{20,16},{24,20},{28,24},{5,1},{9,5},{13... | collective-permute-start | bytes 245768 | tf_op jit(solution)/shard_map/ppermute | solution.py:27
  230.8 5.1 %collective-permute-start.18 = (f32[14,2,8,128]{3,0,2,1:T(8,128)S(1)}, f32[14,2,8,128]{3,0,2,1:T(8,128)S(1)}, u32[]{:S(2)}, u32[]{:S(2)}) collective-permute-start(f32[14,2,8,128]{3,0,2,1:T(8,128)S(1)} %get-tuple-element.114), channel_id=1, source_target_pairs={{0,1},{1,2},{2,3},{4,5},{5,6},{6,7},{8,9},{9,10},{10,11},{12,13},{... | collective-permute-start | bytes 344072 | tf_op jit(solution)/shard_map/ppermute | solution.py:24
  233.4 6.9 %collective-permute-start.19 = (f32[14,2,8,128]{3,0,2,1:T(8,128)S(1)}, f32[14,2,8,128]{3,0,2,1:T(8,128)S(1)}, u32[]{:S(2)}, u32[]{:S(2)}) collective-permute-start(f32[14,2,8,128]{3,0,2,1:T(8,128)S(1)} %get-tuple-element.115), channel_id=1, source_target_pairs={{1,0},{2,1},{3,2},{5,4},{6,5},{7,6},{9,8},{10,9},{11,10},{13,12},{... | collective-permute-start | bytes 344072 | tf_op jit(solution)/shard_map/ppermute | solution.py:27
  291.8 2.6 collective-permute-start.20
  293.1 5.6 %collective-permute-start.21 = (f32[1,8,8,128]{3,0,2,1:T(1,128)S(1)}, f32[1,8,8,128]{3,0,2,1:T(1,128)S(1)}, u32[]{:S(2)}, u32[]{:S(2)}) collective-permute-start(f32[1,8,8,128]{3,0,2,1:T(1,128)S(1)} %get-tuple-element.143), channel_id=1, source_target_pairs={{4,0},{8,4},{12,8},{16,12},{20,16},{24,20},{28,24},{5,1},{9,5},{13... | collective-permute-start | bytes 98312 | tf_op jit(solution)/shard_map/ppermute | solution.py:27
  298.7 4.1 %collective-permute-start.22 = (f32[10,1,8,128]{3,0,2,1:T(8,128)S(1)}, f32[10,1,8,128]{3,0,2,1:T(8,128)S(1)}, u32[]{:S(2)}, u32[]{:S(2)}) collective-permute-start(f32[10,1,8,128]{3,0,2,1:T(8,128)S(1)} %get-tuple-element.138), channel_id=1, source_target_pairs={{0,1},{1,2},{2,3},{4,5},{5,6},{6,7},{8,9},{9,10},{10,11},{12,13},{... | collective-permute-start | bytes 122888 | tf_op jit(solution)/shard_map/ppermute | solution.py:24
  300.9 6.2 %collective-permute-start.23 = (f32[10,1,8,128]{3,0,2,1:T(8,128)S(1)}, f32[10,1,8,128]{3,0,2,1:T(8,128)S(1)}, u32[]{:S(2)}, u32[]{:S(2)}) collective-permute-start(f32[10,1,8,128]{3,0,2,1:T(8,128)S(1)} %get-tuple-element.139), channel_id=1, source_target_pairs={{1,0},{2,1},{3,2},{5,4},{6,5},{7,6},{9,8},{10,9},{11,10},{13,12},{... | collective-permute-start | bytes 122888 | tf_op jit(solution)/shard_map/ppermute | solution.py:27
  351.7 1.0 copy-start.3
where the time goes:
time: 357 us; the launch traced here: 355 us
  blocking collectives  211 us (59%)
  waiting for transfers between devices  48.5 us (14%)
  starting transfers between devices  45.3 us (13%)
  matrix products  21.4 us (6%)
  local copies, waits for them, and re-layouts  14.1 us (4%)
  other arithmetic  8.83 us (2%)
  between operations  5.69 us (2%)
    psum x2, blocking collectives, shards(): lax.psum(jnp.einsum('ij,ia,jb->ab', columns, share_first, share_second, p...  85.6 us
    psum x2, blocking collectives, shards(): lax.psum(jnp.sum(inverse_all * residual * preconditioned), ('gx', 'gy'))  84.2 us
    ppermute x12, waiting for transfers between devices, padded_2(): lax.ppermute(lax.slice_in_dim(block, 0, width, axis=dim), axis, backward)  44.1 us
    psum x1, blocking collectives, shards(): curvature = lax.psum(local_curvature, ('gx', 'gy'))  41.4 us
    ppermute x12, starting transfers between devices, padded_2(): lax.ppermute(lax.slice_in_dim(block, block.shape[dim] - width, None, axis...  29.4 us
    ppermute x12, starting transfers between devices, padded_2(): lax.ppermute(lax.slice_in_dim(block, 0, width, axis=dim), axis, backward)  15.9 us
  transfers between devices with their start and end apart: 24, of which 17 were waited for; matrix products, arithmetic and copies ran while one was open for 1% of the time, Pallas kernels for 0%

commit v1 on v0

v1 whole, which is shorter than its diff:
```python
import math

import jax
import jax.numpy as jnp
import numpy as np
from jax import lax
from jax.experimental import pallas as pl
from jax.experimental.pallas import tpu as pltpu
from jax.sharding import PartitionSpec as P

NODES = 8
MOST_GRAINS = 16
EXT = NODES + 2
ROWS = 112
MODES = 104
AXES = ("gx", "gy")

shift_mass = 0.1
mean_porosity = 0.7
exact_mode = lax.Precision.HIGHEST


def legendre_columns(node_set, degree):
    table = [node_set * 0.0 + 1.0, node_set]
    for order in range(2, degree + 1):
        table.append(
            ((2 * order - 1) * node_set * table[order - 1] - (order - 1) * table[order - 2]) / order
        )
    return table


def gll_tables():
    degree = NODES - 1
    node_set = np.cos(math.pi * np.arange(degree + 1) / degree)
    for sweep in range(100):
        table = legendre_columns(node_set, degree)
        node_set = node_set - (node_set * table[degree] - table[degree - 1]) / (
            (degree + 1) * table[degree]
        )
    node_set = node_set[::-1].copy()
    values = legendre_columns(node_set, degree)[degree]
    weights = 2.0 / (degree * (degree + 1) * values**2)
    derivative = np.zeros((NODES, NODES))
    for row_index in range(NODES):
        for column_index in range(NODES):
            if row_index != column_index:
                derivative[row_index, column_index] = values[row_index] / (
                    values[column_index] * (node_set[row_index] - node_set[column_index])
                )
    derivative[0, 0] = -degree * (degree + 1) / 4.0
    derivative[NODES - 1, NODES - 1] = degree * (degree + 1) / 4.0
    return (weights, derivative)


def jacobi_eigen(matrix):
    size_now = matrix.shape[0]
    current = matrix.copy()
    vectors = np.eye(size_now)
    for sweep in range(12):
        for first in range(size_now - 1):
            for second in range(first + 1, size_now):
                off_value = current[first, second]
                safe_value = np.where(off_value == 0.0, 1e-300, off_value)
                theta = (current[second, second] - current[first, first]) / (2.0 * safe_value)
                sign_value = np.where(theta >= 0.0, 1.0, -1.0)
                tangent = sign_value / (np.abs(theta) + np.sqrt(theta * theta + 1.0))
                cosine = 1.0 / np.sqrt(tangent * tangent + 1.0)
                sine = tangent * cosine
                rotation = np.eye(size_now)
                rotation[first, first] = cosine
                rotation[second, second] = cosine
                rotation[first, second] = sine
                rotation[second, first] = -sine
                current = rotation.T @ current @ rotation
                vectors = vectors @ rotation
    eigen_values = np.array([current[index, index] for index in range(size_now)])
    return (eigen_values, vectors)


def schwarz_tables():
    weights, derivative = gll_tables()
    stiffness = derivative.T @ (weights[:, None] * derivative)
    total_nodes = 3 * (NODES - 1) + 1
    three_stiffness = np.zeros((total_nodes, total_nodes))
    three_mass = np.zeros(total_nodes)
    for element in range(3):
        start_node = element * (NODES - 1)
        three_stiffness[
            start_node : start_node + NODES, start_node : start_node + NODES
        ] += stiffness
        three_mass[start_node : start_node + NODES] += weights
    chosen = np.array([NODES - 2] + list(range(NODES - 1, 2 * NODES - 1)) + [2 * NODES - 1])
    local_stiffness = three_stiffness[chosen][:, chosen]
    local_mass = three_mass[chosen]
    scaling = 1.0 / np.sqrt(local_mass)
    symmetric = scaling[:, None] * local_stiffness * scaling[None, :]
    symmetric = 0.5 * (symmetric + symmetric.T)
    eigen_values, eigen_vectors = jacobi_eigen(symmetric)
    return (scaling[:, None] * eigen_vectors, eigen_values)


WEIGHTS, DERIVATIVE = gll_tables()
STIFF = DERIVATIVE.T @ (WEIGHTS[:, None] * DERIVATIVE)
BASIS, EIGEN = schwarz_tables()


def plane_tables():
    forward = np.zeros((MODES, ROWS))
    inverse = np.zeros((MODES, EXT))
    for mode_b in range(EXT):
        for mode_c in range(EXT):
            mode = mode_b * EXT + mode_c
            for b in range(EXT):
                for k in range(NODES):
                    forward[mode, b * NODES + k] = BASIS[b, mode_b] * BASIS[k + 1, mode_c]
                forward[mode, 80 + b] = BASIS[b, mode_b] * BASIS[0, mode_c]
                forward[mode, 96 + b] = BASIS[b, mode_b] * BASIS[EXT - 1, mode_c]
            inverse[mode] = 1.0 / (
                mean_porosity * (EIGEN + EIGEN[mode_b] + EIGEN[mode_c]) + shift_mass
            )
    lanes = np.repeat(inverse.T[:, :, None], 128, axis=2)
    return (
        forward.astype(np.float32),
        forward.T.astype(np.float32).copy(),
        lanes.astype(np.float32),
    )


def tile_tables():
    table = np.zeros((NODES + 1, NODES, 128))
    table[0] = WEIGHTS[:, None]
    for shift in range(NODES):
        for k in range(NODES):
            table[1 + shift, k] = STIFF[k, (k - shift) % NODES]
    return table.astype(np.float32)


def share_table(count):
    table = np.zeros((count, 3, count))
    for column in range(count):
        table[column, :, column] = 1.0
        if column > 0:
            table[column, 0, column] = 0.5
            table[column, 0, column - 1] = 0.5
        if column < count - 1:
            table[column, 2, column] = 0.5
            table[column, 2, column + 1] = 0.5
    return table


def cosine_inverse(count):
    position = np.arange(count)
    basis = np.cos(math.pi * (position[:, None] + 0.5) * position[None, :] / count)
    basis = basis * np.where(position == 0, math.sqrt(1.0 / count), math.sqrt(2.0 / count))[None, :]
    return basis, 2.0 - 2.0 * np.cos(math.pi * position / count)


def side_even(axis):
    return lax.rem(lax.axis_index(axis), 2) == 0


def shift_up(rows):
    lane = lax.broadcasted_iota(jnp.int32, rows.shape, 1)
    return jnp.where(lane == 0, 0.0, pltpu.roll(rows, 1, 1))


def shift_down(rows):
    lane = lax.broadcasted_iota(jnp.int32, rows.shape, 1)
    return jnp.where(lane == 127, 0.0, pltpu.roll(rows, 127, 1))


class Sides:
    def __init__(self, axis, count):
        index = lax.axis_index(axis)
        self.even = lax.rem(index, 2) == 0
        self.no_low = index == 0
        self.no_high = index == count - 1

    def low(self, first, second):
        return jnp.where(self.no_low, 0.0, jnp.where(self.even, second, first))

    def high(self, first, second):
        return jnp.where(self.no_high, 0.0, jnp.where(self.even, first, second))

    def send_first(self, low_face, high_face):
        return jnp.where(self.even, high_face, low_face)

    def send_second(self, low_face, high_face):
        return jnp.where(self.even, low_face, high_face)


def multiplicity_tile():
    row = lax.broadcasted_iota(jnp.int32, (NODES, 128), 0)
    lane = lax.broadcasted_iota(jnp.int32, (NODES, 128), 1)
    shared = ((row == 0) & (lane > 0)) | ((row == NODES - 1) & (lane < 127))
    return jnp.where(shared, 0.5, 1.0)


def class_of(node):
    return 0 if node == 0 else (2 if node == NODES - 1 else 1)


def axis_factor(node, side):
    if node == 0:
        return jnp.where(side.no_low, 1.0, 0.5)
    if node == NODES - 1:
        return jnp.where(side.no_high, 1.0, 0.5)
    return None


def scaled(value, *factors):
    for factor in factors:
        if factor is not None:
            value = value * factor
    return value


def add_to(total, key, value):
    total[key] = value if key not in total else total[key] + value


def stats_row(tiles):
    columns = jnp.concatenate([jnp.sum(tile, axis=0, keepdims=True) for tile in tiles], axis=0)
    pad = 16 - len(tiles)
    columns = jnp.concatenate([columns, jnp.zeros((pad, 128), jnp.float32)], axis=0)
    sums = jnp.sum(columns, axis=1, keepdims=True)
    row = lax.broadcasted_iota(jnp.int32, (16, 128), 0)
    lane = lax.broadcasted_iota(jnp.int32, (16, 128), 1)
    return jnp.sum(jnp.where(row == lane, sums, 0.0), axis=0, keepdims=True)


def class_tiles(sums):
    return [sums[(i, j)] for i in range(3) for j in range(3)]


def start_kernel(counts, r_ref, sy_first, sy_second, stats_ref):
    side_x, side_y = Sides("gx", counts[0]), Sides("gy", counts[1])
    tile = multiplicity_tile()
    for a in range(NODES):
        low, high = r_ref[a, 1], r_ref[a, NODES - 2]
        sy_first[a] = side_y.send_first(low, high)
        sy_second[a] = side_y.send_second(low, high)
    sums = {}
    for a in range(NODES):
        for b in range(NODES):
            add_to(sums, (class_of(a), class_of(b)), r_ref[a, b])
    for (i, j), value in sums.items():
        a, b = (0, 1, NODES - 1)[i], (0, 1, NODES - 1)[j]
        sums[(i, j)] = scaled(value * tile, axis_factor(a, side_x), axis_factor(b, side_y))
    stats_ref[...] = stats_row(class_tiles(sums))


def planes(ref):
    return jnp.concatenate([ref[a] for a in range(EXT)], axis=1)


def local_solve(x_ref, h_ref, forward_ref, back_ref, inverse_ref, part_ref):
    zero = jnp.zeros((6, 128), jnp.float32)
    for a in range(EXT):
        x_ref[a, 80:90] = shift_up(x_ref[a, pl.ds(6, EXT, stride=NODES), :])
        x_ref[a, 96:106] = shift_down(x_ref[a, pl.ds(1, EXT, stride=NODES), :])
        x_ref[a, 90:96] = zero
        x_ref[a, 106:112] = zero
    spectrum = jnp.dot(
        forward_ref[...], planes(x_ref), precision=exact_mode, preferred_element_type=jnp.float32
    )
    for a in range(EXT):
        h_ref[a] = spectrum[:, a * 128 : (a + 1) * 128]
    for block in range(MODES // 8):
        rows = pl.ds(block * 8, 8)
        values = [h_ref[a, rows] for a in range(EXT)]
        modes = []
        for mode in range(EXT):
            total = values[0] * float(BASIS[0, mode])
            for a in range(1, EXT):
                total = total + values[a] * float(BASIS[a, mode])
            modes.append(total * inverse_ref[mode, rows])
        for a in range(EXT):
            total = modes[0] * float(BASIS[a, 0])
            for mode in range(1, EXT):
                total = total + modes[mode] * float(BASIS[a, mode])
            h_ref[a, rows] = total
    values = jnp.dot(
        back_ref[...], planes(h_ref), precision=exact_mode, preferred_element_type=jnp.float32
    )
    for a in range(EXT):
        part_ref[a] = values[:, a * 128 : (a + 1) * 128]
    for a in range(EXT):

        def layer(k):
            return (a, pl.ds(k, EXT, stride=NODES), slice(None))

        bottom, top = part_ref[layer(0)], part_ref[layer(NODES - 1)]
        part_ref[layer(0)] = bottom + shift_up(top)
        part_ref[layer(NODES - 1)] = top + shift_down(bottom)
        part_ref[layer(1)] = part_ref[layer(1)] + shift_up(part_ref[a, 96:106])
        part_ref[layer(NODES - 2)] = part_ref[layer(NODES - 2)] + shift_down(part_ref[a, 80:90])


def send_parts(part_ref, side_x, side_y, sy_first, sy_second, fx_first, fx_second):
    for a in range(EXT):
        low, high = part_ref[a, 0:16], part_ref[a, 64:80]
        sy_first[a] = side_y.send_first(low, high).reshape(2, NODES, 128)
        sy_second[a] = side_y.send_second(low, high).reshape(2, NODES, 128)
    for layer in range(2):
        low, high = part_ref[layer, 0:80], part_ref[NODES + layer, 0:80]
        fx_first[layer] = side_x.send_first(low, high).reshape(EXT, NODES, 128)
        fx_second[layer] = side_x.send_second(low, high).reshape(EXT, NODES, 128)


def first_solve_kernel(
    counts, r_ref, ry_first, ry_second, rx_first, rx_second, forward_ref, back_ref, inverse_ref,
    part_ref, sy_first, sy_second, fx_first, fx_second, x_ref, h_ref,
):
    side_x, side_y = Sides("gx", counts[0]), Sides("gy", counts[1])
    x_ref[0, 0:80] = side_x.low(rx_first[...], rx_second[...]).reshape(80, 128)
    x_ref[EXT - 1, 0:80] = side_x.high(rx_first[...], rx_second[...]).reshape(80, 128)
    for a in range(NODES):
        x_ref[a + 1, 0:8] = side_y.low(ry_first[a], ry_second[a])
        x_ref[a + 1, 8:72] = r_ref[a].reshape(64, 128)
        x_ref[a + 1, 72:80] = side_y.high(ry_first[a], ry_second[a])
    local_solve(x_ref, h_ref, forward_ref, back_ref, inverse_ref, part_ref)
    send_parts(part_ref, side_x, side_y, sy_first, sy_second, fx_first, fx_second)


def second_solve_kernel(
    counts, u_ref, ry_first, ry_second, rx_first, rx_second, forward_ref, back_ref, inverse_ref,
    q_ref, part_ref, sy_first, sy_second, fx_first, fx_second, x_ref, h_ref,
):
    side_x, side_y = Sides("gx", counts[0]), Sides("gy", counts[1])
    low_x = side_x.low(rx_first[...], rx_second[...])
    high_x = side_x.high(rx_first[...], rx_second[...])
    x_ref[0, 0:80] = low_x[0].reshape(80, 128)
    x_ref[EXT - 1, 0:80] = high_x[1].reshape(80, 128)
    for a in range(NODES):
        low_y = side_y.low(ry_first[a], ry_second[a])
        high_y = side_y.high(ry_first[a], ry_second[a])
        rows = [low_y[0]]
        for b in range(NODES):
            value = u_ref[a, b]
            if b == 0:
                value = value + low_y[1]
            if b == NODES - 1:
                value = value + high_y[0]
            rows.append(value)
        rows.append(high_y[1])
        for b in range(EXT):
            value = rows[b]
            if a == 0:
                value = value + low_x[1, b]
            if a == NODES - 1:
                value = value + high_x[0, b]
            x_ref[a + 1, b * 8 : b * 8 + 8] = value
            if 0 < b < EXT - 1:
                q_ref[a, b - 1] = value
    local_solve(x_ref, h_ref, forward_ref, back_ref, inverse_ref, part_ref)
    send_parts(part_ref, side_x, side_y, sy_first, sy_second, fx_first, fx_second)


def collect_parts(part_ref, ry_first, ry_second, rx_first, rx_second, side_x, side_y, field_ref):
    low_x = side_x.low(rx_first[...], rx_second[...])
    high_x = side_x.high(rx_first[...], rx_second[...])
    result = {}
    for a in range(NODES):
        low_y = side_y.low(ry_first[a + 1], ry_second[a + 1])
        high_y = side_y.high(ry_first[a + 1], ry_second[a + 1])
        for b in range(NODES):
            value = part_ref[a + 1, (b + 1) * 8 : (b + 2) * 8]
            if b < 2:
                value = value + low_y[b]
            if b >= NODES - 2:
                value = value + high_y[b - (NODES - 2)]
            if a < 2:
                value = value + low_x[a, b]
            if a >= NODES - 2:
                value = value + high_x[a - (NODES - 2), b]
            field = 3 * class_of(a) + class_of(b)
            result[(a, b)] = value + field_ref[field : field + 1, :]
    return result


def apply_tiles(z_ref, u_ref, y_ref, tiles_ref, por):
    for a in range(NODES):
        for b in range(NODES):
            y_ref[a, b] = z_ref[a, b] * tiles_ref[0]
    for a in range(NODES):
        for b in range(NODES):
            z = z_ref[a, b]
            third = z * tiles_ref[1]
            for shift in range(1, NODES):
                third = third + pltpu.roll(z, shift, 0) * tiles_ref[1 + shift]
            first = y_ref[0, b] * float(STIFF[a, 0] * WEIGHTS[b])
            second = y_ref[a, 0] * float(STIFF[b, 0] * WEIGHTS[a])
            for other in range(1, NODES):
                first = first + y_ref[other, b] * float(STIFF[a, other] * WEIGHTS[b])
                second = second + y_ref[a, other] * float(STIFF[b, other] * WEIGHTS[a])
            weight = float(WEIGHTS[a] * WEIGHTS[b])
            u_ref[a, b] = por * (third * weight + first + second) + y_ref[a, b] * (
                shift_mass * weight
            )


def sum_column(u_ref):
    for a in range(NODES):
        bottom = u_ref[a, :, 0, :]
        top = u_ref[a, :, NODES - 1, :]
        u_ref[a, :, 0, :] = bottom + shift_up(top)
        u_ref[a, :, NODES - 1, :] = top + shift_down(bottom)


def first_apply_kernel(
    counts, part_ref, ry_first, ry_second, rx_first, rx_second, field_ref, por_ref, r_ref,
    tiles_ref, z_ref, u_ref, sy_first, sy_second, fx_first, fx_second, stats_ref, y_ref,
):
    side_x, side_y = Sides("gx", counts[0]), Sides("gy", counts[1])
    z = collect_parts(
        part_ref, ry_first, ry_second, rx_first, rx_second, side_x, side_y, field_ref
    )
    inner = None
    for (a, b), value in z.items():
        z_ref[a, b] = value
        term = scaled(value * r_ref[a, b], axis_factor(a, side_x), axis_factor(b, side_y))
        inner = term if inner is None else inner + term
    inner = inner * multiplicity_tile()
    apply_tiles(z_ref, u_ref, y_ref, tiles_ref, por_ref[...])
    sums = {}
    curvature = None
    for a in range(NODES):
        for b in range(NODES):
            value = u_ref[a, b]
            add_to(sums, (class_of(a), class_of(b)), value)
            term = value * z_ref[a, b]
            curvature = term if curvature is None else curvature + term
    stats_ref[...] = stats_row(class_tiles(sums) + [inner, curvature])
    sum_column(u_ref)
    for a in range(NODES):
        for layer in range(2):
            low, high = u_ref[a, layer], u_ref[a, NODES - 2 + layer]
            sy_first[a, layer] = side_y.send_first(low, high)
            sy_second[a, layer] = side_y.send_second(low, high)
    for layer in range(2):
        low, high = u_ref[layer], u_ref[NODES - 2 + layer]
        fx_first[layer] = side_x.send_first(low, high)
        fx_second[layer] = side_x.send_second(low, high)


def second_apply_kernel(
    counts, part_ref, ry_first, ry_second, rx_first, rx_second, field_ref, por_ref, r_ref, q_ref,
    z_ref, tiles_ref, z1_ref, u_ref, sy_first, sy_second, fx_first, fx_second, stats_ref, y_ref,
):
    side_x, side_y = Sides("gx", counts[0]), Sides("gy", counts[1])
    step = field_ref[9:10, :]
    w = collect_parts(
        part_ref, ry_first, ry_second, rx_first, rx_second, side_x, side_y, field_ref
    )
    inner = None
    for (a, b), value in w.items():
        next_z = z_ref[a, b] - step * value
        next_r = r_ref[a, b] - step * q_ref[a, b]
        z1_ref[a, b] = next_z
        term = scaled(next_z * next_r, axis_factor(a, side_x), axis_factor(b, side_y))
        inner = term if inner is None else inner + term
    inner = inner * multiplicity_tile()
    apply_tiles(z1_ref, u_ref, y_ref, tiles_ref, por_ref[...])
    own = None
    cross = None
    for a in range(NODES):
        for b in range(NODES):
            value = u_ref[a, b]
            own_term = value * z1_ref[a, b]
            cross_term = value * z_ref[a, b]
            own = own_term if own is None else own + own_term
            cross = cross_term if cross is None else cross + cross_term
    stats_ref[...] = stats_row([inner, own, cross])
    sum_column(u_ref)
    for a in range(NODES):
        low, high = u_ref[a, 0], u_ref[a, NODES - 1]
        sy_first[a] = side_y.send_first(low, high)
        sy_second[a] = side_y.send_second(low, high)
    low, high = u_ref[0], u_ref[NODES - 1]
    fx_first[...] = side_x.send_first(low, high)
    fx_second[...] = side_x.send_second(low, high)


def final_kernel(
    counts, sol_ref, r_ref, q_ref, z_ref, z1_ref, u_ref, ry_first, ry_second, rx_first, rx_second,
    scalars_ref, sol_out, r_out, d_out,
):
    side_x, side_y = Sides("gx", counts[0]), Sides("gy", counts[1])
    first_step = scalars_ref[0:1, :]
    second_step = scalars_ref[1:2, :]
    ratio = scalars_ref[2:3, :]
    low_x = side_x.low(rx_first[...], rx_second[...])
    high_x = side_x.high(rx_first[...], rx_second[...])
    for a in range(NODES):
        for b in range(NODES):
            image = u_ref[a, b]
            if b == 0:
                image = image + side_y.low(ry_first[a], ry_second[a])
            if b == NODES - 1:
                image = image + side_y.high(ry_first[a], ry_second[a])
            if a == 0:
                image = image + low_x[b]
            if a == NODES - 1:
                image = image + high_x[b]
            z, q = z_ref[a, b], q_ref[a, b]
            direction = z1_ref[a, b] + ratio * z
            image = image + ratio * q
            d_out[a, b] = direction
            sol_out[a, b] = sol_ref[a, b] + first_step * z + second_step * direction
            r_out[a, b] = r_ref[a, b] - first_step * q - second_step * image


def call(kernel, counts, name, shapes, scratch, *operands):
    def body(*refs):
        kernel(counts, *refs)

    return pl.pallas_call(
        body,
        name=name,
        out_shape=[jax.ShapeDtypeStruct(shape, jnp.float32) for shape in shapes],
        in_specs=[pl.BlockSpec(memory_space=pltpu.VMEM)] * len(operands),
        out_specs=[pl.BlockSpec(memory_space=pltpu.VMEM)] * len(shapes),
        scratch_shapes=[pltpu.VMEM(shape, jnp.float32) for shape in scratch],
        compiler_params=pltpu.CompilerParams(vmem_limit_bytes=24 * 1024 * 1024),
    )(*operands)


def swap_pairs(counts, axis, parity):
    count_x, count_y = counts
    pairs = []
    for x in range(count_x):
        for y in range(count_y):
            if axis == 0:
                to = ((x + 1 if x % 2 == parity else x - 1) % count_x, y)
            else:
                other = y + 1 if y % 2 == parity else y - 1
                to = (x, other) if 0 <= other < count_y else (x ^ 1, y)
            pairs.append((x * count_y + y, to[0] * count_y + to[1]))
    return pairs


def trade(counts, axis, first, second):
    return (
        lax.ppermute(first, AXES, swap_pairs(counts, axis, 0)),
        lax.ppermute(second, AXES, swap_pairs(counts, axis, 1)),
    )


def gather_stats(counts, row):
    total = counts[0] * counts[1]
    return lax.all_to_all(jnp.broadcast_to(row[None], (total, 1, 128)), AXES, 0, 0)[:, 0, :]


def coarse_tables(counts, column_length):
    share_x, share_y = share_table(counts[0]), share_table(counts[1])
    basis_x, eigen_x = cosine_inverse(counts[0])
    basis_y, eigen_y = cosine_inverse(counts[1])
    divisor = (
        2.0 * mean_porosity * column_length * (eigen_x[:, None] + eigen_y[None, :])
        + 8.0 * shift_mass * column_length
    )
    to_modes_x = np.einsum("xip,pa->xia", share_x, basis_x)
    to_modes_y = np.einsum("yjq,qb->yjb", share_y, basis_y)
    return to_modes_x, to_modes_y, divisor


def coarse_field(counts, tables, stats):
    to_modes_x, to_modes_y, divisor = tables
    sums = stats[:, :9].reshape(counts[0], counts[1], 3, 3)
    modes_x, modes_y = jnp.asarray(to_modes_x, jnp.float32), jnp.asarray(to_modes_y, jnp.float32)
    spectrum = jnp.einsum("xyij,xia,yjb->ab", sums, modes_x, modes_y, precision=exact_mode)
    spectrum = spectrum / jnp.asarray(divisor, jnp.float32)
    own_x = lax.dynamic_index_in_dim(modes_x, lax.axis_index("gx"), 0, keepdims=False)
    own_y = lax.dynamic_index_in_dim(modes_y, lax.axis_index("gy"), 0, keepdims=False)
    return jnp.einsum("ia,ab,jb->ij", own_x, spectrum, own_y, precision=exact_mode).reshape(9)


def rows_of(values, count):
    values = jnp.concatenate([values, jnp.zeros((count - values.shape[0],), jnp.float32)])
    return jnp.broadcast_to(values[:, None], (count, 128))


def shards_of(counts):
    forward_np, back_np, inverse_np = plane_tables()
    tiles_np = tile_tables()

    def shards(solution, residual, grain_counts):
        shard_shape = solution.shape
        block = shard_shape[2:]
        solution = solution.reshape(block)
        residual = residual.reshape(block)
        tables = coarse_tables(counts, block[-1])
        plane = [jnp.asarray(table) for table in (forward_np, back_np, inverse_np)]
        tiles = jnp.asarray(tiles_np)
        porosity = 1.0 - 0.6 * grain_counts.reshape(1, 128).astype(jnp.float32) / MOST_GRAINS
        side_x, side_y = Sides("gx", counts[0]), Sides("gy", counts[1])
        even_x = side_x.even
        row = (1, 128)
        face = (NODES, NODES, 128)
        part_shapes = [
            (EXT, ROWS, 128),
            (EXT, 2, NODES, 128), (EXT, 2, NODES, 128),
            (2, EXT, NODES, 128), (2, EXT, NODES, 128),
        ]
        solve_scratch = [(EXT, ROWS, 128), (EXT, MODES, 128)]

        y_first, y_second, stats = call(
            start_kernel, counts, "start", [face, face, row], [], residual
        )
        ry = trade(counts, 1, y_first, y_second)
        low_y, high_y = side_y.low(*ry), side_y.high(*ry)

        def with_layers(index):
            return jnp.concatenate([low_y[index][None], residual[index], high_y[index][None]])

        low_face, high_face = with_layers(1), with_layers(NODES - 2)
        rx = trade(
            counts, 0, side_x.send_first(low_face, high_face),
            side_x.send_second(low_face, high_face),
        )
        first_stats = gather_stats(counts, stats)

        def spread_faces(fx, ry):
            low_y, high_y = side_y.low(*ry), side_y.high(*ry)
            middle = jnp.zeros((2, NODES - 4, NODES, 128), jnp.float32)
            both = [
                jnp.concatenate([low_y[at], middle, high_y[at]], axis=1)
                for at in (slice(0, 2), slice(8, 10))
            ]
            return (
                fx[0][:, 1:-1] + side_x.send_first(*both),
                fx[1][:, 1:-1] + side_x.send_second(*both),
            )

        part, y_first, y_second, *fx = call(
            first_solve_kernel, counts, "first_solve", part_shapes, solve_scratch,
            residual, *ry, *rx, *plane,
        )
        ry = trade(counts, 1, y_first, y_second)
        rx = trade(counts, 0, *spread_faces(fx, ry))
        field = rows_of(coarse_field(counts, tables, first_stats), 16)
        z, u, y_first, y_second, *fx, stats = call(
            first_apply_kernel, counts, "first_apply",
            [block, block, (NODES, 2, NODES, 128), (NODES, 2, NODES, 128),
             (2, NODES, NODES, 128), (2, NODES, NODES, 128), row],
            [block],
            part, *ry, *rx, field, porosity, residual, tiles,
        )
        ry = trade(counts, 1, y_first, y_second)
        low_y, high_y = side_y.low(*ry), side_y.high(*ry)

        def image_faces(index):
            middle = jnp.zeros((2, NODES - 2, NODES, 128), jnp.float32)
            return jnp.concatenate([low_y[index], middle, high_y[index]], axis=1)

        pads = ((0, 0), (1, 1), (0, 0), (0, 0))
        both = (image_faces(slice(0, 2)), image_faces(slice(NODES - 2, NODES)))
        rx = trade(
            counts, 0,
            jnp.pad(fx[0], pads) + side_x.send_first(*both),
            jnp.pad(fx[1], pads) + side_x.send_second(*both),
        )
        second_stats = gather_stats(counts, stats)
        q, part, y_first, y_second, *fx = call(
            second_solve_kernel, counts, "second_solve", [block] + part_shapes, solve_scratch,
            u, *ry, *rx, *plane,
        )
        ry = trade(counts, 1, y_first, y_second)
        rx = trade(counts, 0, *spread_faces(fx, ry))
        first_inner = jnp.sum(second_stats[:, 9])
        first_curvature = jnp.sum(second_stats[:, 10])
        first_step = first_inner / first_curvature
        field = rows_of(
            jnp.concatenate([coarse_field(counts, tables, second_stats), first_step[None]]), 16
        )
        z1, u, y_first, y_second, *fx, stats = call(
            second_apply_kernel, counts, "second_apply",
            [block, block, face, face, face, face, row],
            [block],
            part, *ry, *rx, field, porosity, residual, q, z, tiles,
        )
        ry = trade(counts, 1, y_first, y_second)
        low_y, high_y = side_y.low(*ry), side_y.high(*ry)

        def edge_rows(index):
            middle = jnp.zeros((NODES - 2, NODES, 128), jnp.float32)
            return jnp.concatenate([low_y[index][None], middle, high_y[index][None]])

        both = (edge_rows(0), edge_rows(NODES - 1))
        rx = trade(
            counts, 0, fx[0] + side_x.send_first(*both), fx[1] + side_x.send_second(*both)
        )
        last_stats = gather_stats(counts, stats)
        second_inner, own, cross = (jnp.sum(last_stats[:, i]) for i in range(3))
        ratio = second_inner / first_inner
        second_step = second_inner / (own + ratio * (2.0 * cross + ratio * first_curvature))
        scalars = rows_of(jnp.stack([first_step, second_step, ratio]), 8)
        solution_out, residual_out, direction = call(
            final_kernel, counts, "final", [block] * 3, [],
            solution, residual, q, z, z1, u, *ry, *rx, scalars,
        )
        return (
            solution_out.reshape(shard_shape),
            residual_out.reshape(shard_shape),
            direction.reshape(shard_shape),
            jnp.stack([first_step, second_step]),
        )

    return shards


def solution(mesh):
    counts = (mesh.shape["gx"], mesh.shape["gy"])
    return jax.shard_map(
        shards_of(counts),
        mesh=mesh,
        in_specs=(
            P("gx", "gy", None, None, None, None),
            P("gx", "gy", None, None, None, None),
            P("gx", "gy", None),
        ),
        out_specs=(
            P("gx", "gy", None, None, None, None),
            P("gx", "gy", None, None, None, None),
            P("gx", "gy", None, None, None, None),
            P(),
        ),
        check_vma=False,
    )
```

time: 357 us -> 88 us (0.25)
  blocking collectives: 211 us -> 0 us
  starting transfers between devices: 45.3 us -> 20.6 us
  matrix products: 21.4 us -> 2.08 us
  local copies, waits for them, and re-layouts: 14.1 us -> 4.99 us
  Pallas kernels: 0 us -> 6.64 us
  other arithmetic: 8.83 us -> 3.23 us
  waiting for transfers between devices: 48.5 us -> 43.7 us
    psum x5 -> x0, blocking collectives: 211 us -> none  [the longest x2 85.6 us: shards(): lax.psum(jnp.einsum('ij,ia,jb->ab', columns, share_first, share_second, p...]
    ppermute x24 -> x20, starting transfers between devices: 45.3 us -> 10.2 us  [the longest x10 7.9 us: trade(): lax.ppermute(first, AXES, swap_pairs(counts, axis, 0))]
    ppermute x24 -> x20, waiting for transfers between devices: 48.5 us -> 26.7 us  [the longest x10 18.1 us: trade(): lax.ppermute(second, AXES, swap_pairs(counts, axis, 1))]
    dot_general x40 -> x8, matrix products: 21.4 us -> 2.08 us  [the longest x4 1.57 us: coarse_field(): jnp.einsum('xyij,xia,yjb->ab', sums, modes_x, modes_y, precision=exact_mode)]
    all_to_all x0 -> x3, waiting for transfers between devices: none -> 17 us  [gather_stats(): lax.all_to_all(jnp.broadcast_to(row[None], (total, 1, 128)), AXES, 0, 0)]
    all_to_all x0 -> x3, starting transfers between devices: none -> 10.5 us  [gather_stats(): lax.all_to_all(jnp.broadcast_to(row[None], (total, 1, 128)), AXES, 0, 0)]
    pallas_call x0 -> x6, Pallas kernels: none -> 6.64 us  [call(): pl.pallas_call(body, name=name, out_shape=[jax.ShapeDtypeStruct(shape, jn...]
    scatter x8 -> x0, local copies, waits for them, and re-layouts: 6.06 us -> none  [the longest x4 5.61 us: assemble_z(): nodal_field.at[..., points - 1, :-1].set(shared).at[..., 0, 1:].set(shared)]
  transfers between devices with their start and end apart: 24 -> 23, of which waited for: 17 -> 15; matrix products, arithmetic and copies ran while one was open for 1% -> 7% of each run, Pallas kernels for 0% -> 0%
where the time goes in v1:
time: 88 us; the launch traced here: 87.6 us
  waiting for transfers between devices  43.7 us (50%)
  starting transfers between devices  20.6 us (23%)
  Pallas kernels  6.64 us (8%)
  between operations  6.29 us (7%)
  local copies, waits for them, and re-layouts  4.99 us (6%)
  other arithmetic  3.23 us (4%)
  matrix products  2.08 us (2%)
    ppermute x10, waiting for transfers between devices, trade(): lax.ppermute(second, AXES, swap_pairs(counts, axis, 1))  18.1 us
    all_to_all x3, waiting for transfers between devices, gather_stats(): lax.all_to_all(jnp.broadcast_to(row[None], (total, 1, 128)), AXES, 0, 0)  17 us
    all_to_all x3, starting transfers between devices, gather_stats(): lax.all_to_all(jnp.broadcast_to(row[None], (total, 1, 128)), AXES, 0, 0)  10.5 us
    ppermute x10, waiting for transfers between devices, trade(): lax.ppermute(first, AXES, swap_pairs(counts, axis, 0))  8.61 us
    ppermute x10, starting transfers between devices, trade(): lax.ppermute(first, AXES, swap_pairs(counts, axis, 0))  7.9 us
    pallas_call x6, Pallas kernels, call(): pl.pallas_call(body, name=name, out_shape=[jax.ShapeDtypeStruct(shape, jn...  6.64 us
    ppermute x10, starting transfers between devices, trade(): lax.ppermute(second, AXES, swap_pairs(counts, axis, 1))  2.26 us
    unnamed x22, local copies, waits for them, and re-layouts  1.88 us
  transfers between devices with their start and end apart: 23, of which 15 were waited for; matrix products, arithmetic and copies ran while one was open for 7% of the time, Pallas kernels for 0%

profile of v1, /device:TPU:0, one launch (start us, length us, event | category | flops | bytes accessed | tf_op | source)
XLA Modules:
  0.0 87.6 jit_solution(3424802439298292619)
XLA Ops:
  0.7 0.9 %copy-done = f32[1,1,8,8,8,128]{5,4,3,2,1,0:T(8,128)S(1)} copy-done((f32[1,1,8,8,8,128]{5,4,3,2,1,0:T(8,128)S(1)}, f32[1,1,8,8,8,128]{5,4,3,2,1,0:T(8,128)}, u32[]{:S(2)}) %copy-start) | copy-done | bytes 262168
  1.7 3.0 %collective-permute-start = (f32[8,8,128]{2,1,0:T(8,128)S(1)}, f32[8,8,128]{2,1,0:T(8,128)S(1)}, u32[]{:S(2)}, u32[]{:S(2)}) collective-permute-start(f32[8,8,128]{2,1,0:T(8,128)S(1)} %get-tuple-element.35), channel_id=1, source_target_pairs={{0,1},{1,0},{2,3},{3,2},{4,5},{5,4},{6,7},{7,6},{8,9},{9,8},{10,11... | collective-permute-start | bytes 98312 | tf_op jit(solution)/shard_map/ppermute | solution.py:545
  4.8 0.6 broadcast_in_dim.67
  5.4 5.4 %all-to-all-start = ((f32[32,1,128]{2,1,0:T(1,128)}), f32[32,1,128]{2,1,0:T(1,128)S(1)}, u32[]{:S(2)}, u32[]{:S(2)}) async-start(f32[32,1,128]{2,1,0:T(1,128)} %broadcast_in_dim.67), calls=%async_computation | async-start | bytes 32768 | tf_op jit(solution)/shard_map/all_to_all | solution.py:552
  10.8 0.7 subtract_bitcast_fusion.refs_6_
  11.6 6.3 %all-to-all-done = f32[32,1,128]{2,1,0:T(1,128)S(1)} async-done(((f32[32,1,128]{2,1,0:T(1,128)}), f32[32,1,128]{2,1,0:T(1,128)S(1)}, u32[]{:S(2)}, u32[]{:S(2)}) %all-to-all-start) | async-done | bytes 16416 | tf_op jit(solution)/shard_map/all_to_all | solution.py:552
  18.0 0.1 copy.28
  18.2 0.9 %convolution_bitcast_fusion.1 = f32[4,8,3]{1,0,2:T(4,128)S(1)} fusion(f32[4,3,4,1]{1,2,0,3:T(4,128)} %constant.83, f32[8,4,3,3]{0,3,1,2:T(4,128)S(1)} %copy.28), kind=kOutput, calls=%fused_computation.1 | convolution fusion | flops 13824 | bytes 1728 | tf_op jit(solution)/shard_map/xyij,xia,yjb->ab/dot_general | solution.py:572
  19.3 0.6 collective-permute-start.3
  20.0 0.2 fusion.1
  20.2 0.4 collective-permute-done.2.refs_3_
  20.5 3.4 %collective-permute-done.3.refs_4_ = f32[10,8,128]{2,1,0:T(8,128)S(1)} collective-permute-done((f32[10,8,128]{2,1,0:T(8,128)S(1)}, f32[10,8,128]{2,1,0:T(8,128)S(1)}, u32[]{:S(2)}, u32[]{:S(2)}) %collective-permute-start.3) | collective-permute-done | bytes 40992 | tf_op jit(solution)/shard_map/ppermute | solution.py:546
  23.9 1.9 %first_solve.1 = (f32[10,112,128]{2,1,0:T(8,128)S(1)}, f32[10,2,8,128]{3,2,1,0:T(8,128)S(1)}, f32[10,2,8,128]{3,2,1,0:T(8,128)S(1)}, f32[2,10,8,128]{3,2,1,0:T(8,128)S(1)}, f32[2,10,8,128]{3,2,1,0:T(8,128)S(1)}) custom-call(f32[8,8,8,128]{3,2,1,0:T(8,128)S(1)} %bitcast.66, f32[8,8,128]{2,1,0:T(8,128)S(1)} %collective-permute-done.refs_1_, ...), custom_call_target="tpu_custom_call" | custom-call | tf_op jit(solution)/shard_map/first_solve/pallas_call | solution.py:518
  25.8 0.6 collective-permute-start.4
  26.5 3.8 %collective-permute-done.4.refs_1_ = f32[10,2,8,128]{3,2,1,0:T(8,128)S(1)} collective-permute-done((f32[10,2,8,128]{3,2,1,0:T(8,128)S(1)}, f32[10,2,8,128]{3,2,1,0:T(8,128)S(1)}, u32[]{:S(2)}, u32[]{:S(2)}) %collective-permute-start.4) | collective-permute-done | bytes 81952 | tf_op jit(solution)/shard_map/ppermute | solution.py:545
  30.6 0.2 collective-permute-start.7
  30.7 0.3 copy-done.10
  31.3 0.5 collective-permute-done.6.refs_3_
  31.8 3.7 %collective-permute-done.7.refs_4_ = f32[2,8,8,128]{3,2,1,0:T(8,128)S(1)} collective-permute-done((f32[2,8,8,128]{3,2,1,0:T(8,128)S(1)}, f32[2,8,8,128]{3,2,1,0:T(8,128)S(1)}, u32[]{:S(2)}, u32[]{:S(2)}) %collective-permute-start.7) | collective-permute-done | bytes 65568 | tf_op jit(solution)/shard_map/ppermute | solution.py:546
  35.5 0.8 first_apply.1
  36.4 0.6 broadcast_in_dim.71
  37.0 2.5 %all-to-all-start.1 = ((f32[32,1,128]{2,1,0:T(1,128)}), f32[32,1,128]{2,1,0:T(1,128)S(1)}, u32[]{:S(2)}, u32[]{:S(2)}) async-start(f32[32,1,128]{2,1,0:T(1,128)} %broadcast_in_dim.71), calls=%async_computation.1 | async-start | bytes 32768 | tf_op jit(solution)/shard_map/all_to_all | solution.py:552
  39.6 1.8 %collective-permute-start.8 = (f32[8,2,8,128]{3,2,1,0:T(8,128)S(1)}, f32[8,2,8,128]{3,2,1,0:T(8,128)S(1)}, u32[]{:S(2)}, u32[]{:S(2)}) collective-permute-start(f32[8,2,8,128]{3,2,1,0:T(8,128)S(1)} %get-tuple-element.44), channel_id=1, source_target_pairs={{0,1},{1,0},{2,3},{3,2},{4,5},{5,4},{6,7},{7,6},{8,9},{9,8},{10,11... | collective-permute-start | bytes 196616 | tf_op jit(solution)/shard_map/ppermute | solution.py:545
  41.4 5.3 %all-to-all-done.1 = f32[32,1,128]{2,1,0:T(1,128)S(1)} async-done(((f32[32,1,128]{2,1,0:T(1,128)}), f32[32,1,128]{2,1,0:T(1,128)S(1)}, u32[]{:S(2)}, u32[]{:S(2)}) %all-to-all-start.1) | async-done | bytes 16416 | tf_op jit(solution)/shard_map/all_to_all | solution.py:552
  46.9 0.1 copy.31
  47.1 0.5 copy-done.8
  47.6 0.2 convolution_bitcast_fusion
  47.9 0.2 fusion
  48.4 0.7 collective-permute-start.11
  49.3 0.4 collective-permute-done.10.refs_3_
  49.7 4.2 %collective-permute-done.11.refs_4_ = f32[2,10,8,128]{3,2,1,0:T(8,128)S(1)} collective-permute-done((f32[2,10,8,128]{3,2,1,0:T(8,128)S(1)}, f32[2,10,8,128]{3,2,1,0:T(8,128)S(1)}, u32[]{:S(2)}, u32[]{:S(2)}) %collective-permute-start.11) | collective-permute-done | bytes 81952 | tf_op jit(solution)/shard_map/ppermute | solution.py:546
  53.9 1.9 %second_solve.1 = (f32[8,8,8,128]{3,2,1,0:T(8,128)S(1)}, f32[10,112,128]{2,1,0:T(8,128)S(1)}, f32[10,2,8,128]{3,2,1,0:T(8,128)S(1)}, f32[10,2,8,128]{3,2,1,0:T(8...) custom-call(f32[8,8,8,128]{3,2,1,0:T(8,128)S(1)} %get-tuple-element.43.refs_0_, ...), custom_call_target="tpu_custom_call" | custom-call | tf_op jit(solution)/shard_map/second_solve/pallas_call | solution.py:518
  55.8 0.5 collective-permute-start.12
  56.3 0.7 slice_reduce_fusion.3
  58.3 2.0 %collective-permute-done.12.refs_1_ = f32[10,2,8,128]{3,2,1,0:T(8,128)S(1)} collective-permute-done((f32[10,2,8,128]{3,2,1,0:T(8,128)S(1)}, f32[10,2,8,128]{3,2,1,0:T(8,128)S(1)}, u32[]{:S(2)}, u32[]{:S(2)}) %collective-permute-start.12) | collective-permute-done | bytes 81952 | tf_op jit(solution)/shard_map/ppermute | solution.py:545
  60.7 1.1 %collective-permute-done.14.refs_3_ = f32[2,8,8,128]{3,2,1,0:T(8,128)S(1)} collective-permute-done((f32[2,8,8,128]{3,2,1,0:T(8,128)S(1)}, f32[2,8,8,128]{3,2,1,0:T(8,128)S(1)}, u32[]{:S(2)}, u32[]{:S(2)}) %collective-permute-start.14) | collective-permute-done | bytes 65568 | tf_op jit(solution)/shard_map/ppermute | solution.py:545
  61.8 3.6 %collective-permute-done.15.refs_4_ = f32[2,8,8,128]{3,2,1,0:T(8,128)S(1)} collective-permute-done((f32[2,8,8,128]{3,2,1,0:T(8,128)S(1)}, f32[2,8,8,128]{3,2,1,0:T(8,128)S(1)}, u32[]{:S(2)}, u32[]{:S(2)}) %collective-permute-start.15) | collective-permute-done | bytes 65568 | tf_op jit(solution)/shard_map/ppermute | solution.py:546
  65.5 0.9 second_apply.1
  66.4 0.6 broadcast_in_dim.75
  67.0 2.5 %all-to-all-start.2 = ((f32[32,1,128]{2,1,0:T(1,128)}), f32[32,1,128]{2,1,0:T(1,128)S(1)}, u32[]{:S(2)}, u32[]{:S(2)}) async-start(f32[32,1,128]{2,1,0:T(1,128)} %broadcast_in_dim.75), calls=%async_computation.2 | async-start | bytes 32768 | tf_op jit(solution)/shard_map/all_to_all | solution.py:552
  69.6 1.8 %collective-permute-start.16 = (f32[8,8,128]{2,1,0:T(8,128)S(1)}, f32[8,8,128]{2,1,0:T(8,128)S(1)}, u32[]{:S(2)}, u32[]{:S(2)}) collective-permute-start(f32[8,8,128]{2,1,0:T(8,128)S(1)} %get-tuple-element.58), channel_id=1, source_target_pairs={{0,1},{1,0},{2,3},{3,2},{4,5},{5,4},{6,7},{7,6},{8,9},{9,8},{10,11... | collective-permute-start | bytes 98312 | tf_op jit(solution)/shard_map/ppermute | solution.py:545
  71.4 5.3 %all-to-all-done.2 = f32[32,1,128]{2,1,0:T(1,128)S(1)} async-done(((f32[32,1,128]{2,1,0:T(1,128)}), f32[32,1,128]{2,1,0:T(1,128)S(1)}, u32[]{:S(2)}, u32[]{:S(2)}) %all-to-all-start.2) | async-done | bytes 16416 | tf_op jit(solution)/shard_map/all_to_all | solution.py:552
  76.7 0.7 slice_reduce_fusion
  81.4 0.6 pad_maximum_fusion.12
  82.1 0.7 collective-permute-start.19
  82.9 0.4 collective-permute-done.18.refs_8_
  83.3 3.2 %collective-permute-done.19.refs_9_ = f32[8,8,128]{2,1,0:T(8,128)S(1)} collective-permute-done((f32[8,8,128]{2,1,0:T(8,128)S(1)}, f32[8,8,128]{2,1,0:T(8,128)S(1)}, u32[]{:S(2)}, u32[]{:S(2)}) %collective-permute-start.19) | collective-permute-done | bytes 32800 | tf_op jit(solution)/shard_map/ppermute | solution.py:546
  86.6 1.0 %final.1 = (f32[8,8,8,128]{3,2,1,0:T(8,128)}, f32[8,8,8,128]{3,2,1,0:T(8,128)}, f32[8,8,8,128]{3,2,1,0:T(8,128)}) custom-call(f32[8,8,8,128]{3,2,1,0:T(8,128)S(1)} %bitcast.70, f32[8,8,8,128]{3,2,1,0:T(8,128)S(1)} %bitcast.69, f32[8,8,8,128]{3,2,1,0:T(8,128)S(1)} %get-tuple-element.48.refs_8_.refs_2_, ...), custom_call_target="tpu_custom_call" | custom-call | tf_op jit(solution)/shard_map/final/pallas_call | solution.py:518
  (82 shorter events, 2.7 us)
Async XLA Ops:
  0.6 10.9 %copy-start.7 = (f32[8,3,8]{2,0,1:T(8,128)S(1)}, f32[8,3,8]{2,0,1:T(8,128)}, u32[]{:S(2)}) copy-start(f32[8,3,8]{2,0,1:T(8,128)} %constant.69.clone) | copy-start | bytes 2308
  0.6 1.0 %copy-start = (f32[1,1,8,8,8,128]{5,4,3,2,1,0:T(8,128)S(1)}, f32[1,1,8,8,8,128]{5,4,3,2,1,0:T(8,128)}, u32[]{:S(2)}) copy-start(f32[1,1,8,8,8,128]{5,4,3,2,1,0:T(8,128)} %param.14) | copy-start | bytes 786436
  1.6 9.2 %copy-start.1 = (f32[1,1,8,8,8,128]{5,4,3,2,1,0:T(8,128)S(1)}, f32[1,1,8,8,8,128]{5,4,3,2,1,0:T(8,128)}, u32[]{:S(2)}) copy-start(f32[1,1,8,8,8,128]{5,4,3,2,1,0:T(8,128)} %param.14) | copy-start | bytes 786436
  1.6 22.3 %copy-start.2 = (f32[10,104,128]{2,1,0:T(8,128)S(1)}, f32[10,104,128]{2,1,0:T(8,128)}, u32[]{:S(2)}) copy-start(f32[10,104,128]{2,1,0:T(8,128)} %constant.67.clone.refs_7_) | copy-start | bytes 1597444
  1.7 17.4 %collective-permute-start = (f32[8,8,128]{2,1,0:T(8,128)S(1)}, f32[8,8,128]{2,1,0:T(8,128)S(1)}, u32[]{:S(2)}, u32[]{:S(2)}) collective-permute-start(f32[8,8,128]{2,1,0:T(8,128)S(1)} %get-tuple-element.35), channel_id=1, source_target_pairs={{0,1},{1,0},{2,3},{3,2},{4,5},{5,4},{6,7},{7,6},{8,9},{9,8},{10,11... | collective-permute-start | bytes 98312 | tf_op jit(solution)/shard_map/ppermute | solution.py:545
  4.8 14.4 %collective-permute-start.1 = (f32[8,8,128]{2,1,0:T(8,128)S(1)}, f32[8,8,128]{2,1,0:T(8,128)S(1)}, u32[]{:S(2)}, u32[]{:S(2)}) collective-permute-start(f32[8,8,128]{2,1,0:T(8,128)S(1)} %get-tuple-element.36), channel_id=1, source_target_pairs={{0,4},{1,2},{2,1},{3,7},{4,0},{5,6},{6,5},{7,3},{8,12},{9,10},{10,... | collective-permute-start | bytes 98312 | tf_op jit(solution)/shard_map/ppermute | solution.py:546
  5.4 12.5 %all-to-all-start = ((f32[32,1,128]{2,1,0:T(1,128)}), f32[32,1,128]{2,1,0:T(1,128)S(1)}, u32[]{:S(2)}, u32[]{:S(2)}) async-start(f32[32,1,128]{2,1,0:T(1,128)} %broadcast_in_dim.67), calls=%async_computation | async-start | bytes 32768 | tf_op jit(solution)/shard_map/all_to_all | solution.py:552
  19.2 4.7 %copy-start.4 = (f32[112,104]{1,0:T(8,128)S(1)}, f32[112,104]{1,0:T(8,128)}, u32[]{:S(2)}) copy-start(f32[112,104]{1,0:T(8,128)} %constant.66.clone.refs_6_) | copy-start | bytes 139780
  19.2 4.7 %copy-start.5 = (f32[104,112]{1,0:T(8,128)S(1)}, f32[104,112]{1,0:T(8,128)}, u32[]{:S(2)}) copy-start(f32[104,112]{1,0:T(8,128)} %constant.65.clone.refs_5_) | copy-start | bytes 139780
  19.2 0.7 copy-start.9
  19.2 1.3 %collective-permute-start.2 = (f32[10,8,128]{2,1,0:T(8,128)S(1)}, f32[10,8,128]{2,1,0:T(8,128)S(1)}, u32[]{:S(2)}, u32[]{:S(2)}) collective-permute-start(f32[10,8,128]{2,1,0:T(8,128)S(1)} %get-tuple-element.88), channel_id=1, source_target_pairs={{0,4},{1,5},{2,6},{3,7},{4,0},{5,1},{6,2},{7,3},{8,12},{9,13},{10,... | collective-permute-start | bytes 122888 | tf_op jit(solution)/shard_map/ppermute | solution.py:545
  19.3 4.6 %collective-permute-start.3 = (f32[10,8,128]{2,1,0:T(8,128)S(1)}, f32[10,8,128]{2,1,0:T(8,128)S(1)}, u32[]{:S(2)}, u32[]{:S(2)}) collective-permute-start(f32[10,8,128]{2,1,0:T(8,128)S(1)} %get-tuple-element.87), channel_id=1, source_target_pairs={{0,28},{1,29},{2,30},{3,31},{4,8},{5,9},{6,10},{7,11},{8,4},{9,5},... | collective-permute-start | bytes 122888 | tf_op jit(solution)/shard_map/ppermute | solution.py:546
  25.8 4.5 %collective-permute-start.4 = (f32[10,2,8,128]{3,2,1,0:T(8,128)S(1)}, f32[10,2,8,128]{3,2,1,0:T(8,128)S(1)}, u32[]{:S(2)}, u32[]{:S(2)}) collective-permute-start(f32[10,2,8,128]{3,2,1,0:T(8,128)S(1)} %get-tuple-element.38), channel_id=1, source_target_pairs={{0,1},{1,0},{2,3},{3,2},{4,5},{5,4},{6,7},{7,6},{8,9},{9,8},{10,11... | collective-permute-start | bytes 245768 | tf_op jit(solution)/shard_map/ppermute | solution.py:545
  26.4 4.0 %collective-permute-start.5 = (f32[10,2,8,128]{3,2,1,0:T(8,128)S(1)}, f32[10,2,8,128]{3,2,1,0:T(8,128)S(1)}, u32[]{:S(2)}, u32[]{:S(2)}) collective-permute-start(f32[10,2,8,128]{3,2,1,0:T(8,128)S(1)} %get-tuple-element.39), channel_id=1, source_target_pairs={{0,4},{1,2},{2,1},{3,7},{4,0},{5,6},{6,5},{7,3},{8,12},{9,10},{10,... | collective-permute-start | bytes 245768 | tf_op jit(solution)/shard_map/ppermute | solution.py:546
  30.4 0.7 copy-start.10
  30.4 5.2 %copy-start.6 = (f32[9,8,128]{2,1,0:T(8,128)S(1)}, f32[9,8,128]{2,1,0:T(8,128)}, u32[]{:S(2)}) copy-start(f32[9,8,128]{2,1,0:T(8,128)} %constant.68.clone.refs_8_.refs_10_) | copy-start | bytes 110596
  30.5 1.3 %collective-permute-start.6 = (f32[2,8,8,128]{3,2,1,0:T(8,128)S(1)}, f32[2,8,8,128]{3,2,1,0:T(8,128)S(1)}, u32[]{:S(2)}, u32[]{:S(2)}) collective-permute-start(f32[2,8,8,128]{3,2,1,0:T(8,128)S(1)} %get-tuple-element.94), channel_id=1, source_target_pairs={{0,4},{1,5},{2,6},{3,7},{4,0},{5,1},{6,2},{7,3},{8,12},{9,13},{10,... | collective-permute-start | bytes 196616 | tf_op jit(solution)/shard_map/ppermute | solution.py:545
  30.6 4.9 %collective-permute-start.7 = (f32[2,8,8,128]{3,2,1,0:T(8,128)S(1)}, f32[2,8,8,128]{3,2,1,0:T(8,128)S(1)}, u32[]{:S(2)}, u32[]{:S(2)}) collective-permute-start(f32[2,8,8,128]{3,2,1,0:T(8,128)S(1)} %get-tuple-element.93), channel_id=1, source_target_pairs={{0,28},{1,29},{2,30},{3,31},{4,8},{5,9},{6,10},{7,11},{8,4},{9,5},... | collective-permute-start | bytes 196616 | tf_op jit(solution)/shard_map/ppermute | solution.py:546
  37.0 9.7 %all-to-all-start.1 = ((f32[32,1,128]{2,1,0:T(1,128)}), f32[32,1,128]{2,1,0:T(1,128)S(1)}, u32[]{:S(2)}, u32[]{:S(2)}) async-start(f32[32,1,128]{2,1,0:T(1,128)} %broadcast_in_dim.71), calls=%async_computation.1 | async-start | bytes 32768 | tf_op jit(solution)/shard_map/all_to_all | solution.py:552
  39.6 8.6 %collective-permute-start.8 = (f32[8,2,8,128]{3,2,1,0:T(8,128)S(1)}, f32[8,2,8,128]{3,2,1,0:T(8,128)S(1)}, u32[]{:S(2)}, u32[]{:S(2)}) collective-permute-start(f32[8,2,8,128]{3,2,1,0:T(8,128)S(1)} %get-tuple-element.44), channel_id=1, source_target_pairs={{0,1},{1,0},{2,3},{3,2},{4,5},{5,4},{6,7},{7,6},{8,9},{9,8},{10,11... | collective-permute-start | bytes 196616 | tf_op jit(solution)/shard_map/ppermute | solution.py:545
  41.4 6.8 %collective-permute-start.9 = (f32[8,2,8,128]{3,2,1,0:T(8,128)S(1)}, f32[8,2,8,128]{3,2,1,0:T(8,128)S(1)}, u32[]{:S(2)}, u32[]{:S(2)}) collective-permute-start(f32[8,2,8,128]{3,2,1,0:T(8,128)S(1)} %get-tuple-element.45), channel_id=1, source_target_pairs={{0,4},{1,2},{2,1},{3,7},{4,0},{5,6},{6,5},{7,3},{8,12},{9,10},{10,... | collective-permute-start | bytes 196616 | tf_op jit(solution)/shard_map/ppermute | solution.py:546
  46.9 0.7 copy-start.8
  48.4 1.3 %collective-permute-start.10 = (f32[2,10,8,128]{3,2,1,0:T(8,128)S(1)}, f32[2,10,8,128]{3,2,1,0:T(8,128)S(1)}, u32[]{:S(2)}, u32[]{:S(2)}) collective-permute-start(f32[2,10,8,128]{3,2,1,0:T(8,128)S(1)} %get-tuple-element.92), channel_id=1, source_target_pairs={{0,4},{1,5},{2,6},{3,7},{4,0},{5,1},{6,2},{7,3},{8,12},{9,13},{10,... | collective-permute-start | bytes 245768 | tf_op jit(solution)/shard_map/ppermute | solution.py:545
  48.4 5.5 %collective-permute-start.11 = (f32[2,10,8,128]{3,2,1,0:T(8,128)S(1)}, f32[2,10,8,128]{3,2,1,0:T(8,128)S(1)}, u32[]{:S(2)}, u32[]{:S(2)}) collective-permute-start(f32[2,10,8,128]{3,2,1,0:T(8,128)S(1)} %get-tuple-element.91), channel_id=1, source_target_pairs={{0,28},{1,29},{2,30},{3,31},{4,8},{5,9},{6,10},{7,11},{8,4},{9,5},... | collective-permute-start | bytes 245768 | tf_op jit(solution)/shard_map/ppermute | solution.py:546
  55.8 4.5 %collective-permute-start.12 = (f32[10,2,8,128]{3,2,1,0:T(8,128)S(1)}, f32[10,2,8,128]{3,2,1,0:T(8,128)S(1)}, u32[]{:S(2)}, u32[]{:S(2)}) collective-permute-start(f32[10,2,8,128]{3,2,1,0:T(8,128)S(1)} %get-tuple-element.51), channel_id=1, source_target_pairs={{0,1},{1,0},{2,3},{3,2},{4,5},{5,4},{6,7},{7,6},{8,9},{9,8},{10,11... | collective-permute-start | bytes 245768 | tf_op jit(solution)/shard_map/ppermute | solution.py:545
  56.3 4.0 %collective-permute-start.13 = (f32[10,2,8,128]{3,2,1,0:T(8,128)S(1)}, f32[10,2,8,128]{3,2,1,0:T(8,128)S(1)}, u32[]{:S(2)}, u32[]{:S(2)}) collective-permute-start(f32[10,2,8,128]{3,2,1,0:T(8,128)S(1)} %get-tuple-element.52), channel_id=1, source_target_pairs={{0,4},{1,2},{2,1},{3,7},{4,0},{5,6},{6,5},{7,3},{8,12},{9,10},{10,... | collective-permute-start | bytes 245768 | tf_op jit(solution)/shard_map/ppermute | solution.py:546
  60.5 1.3 %collective-permute-start.14 = (f32[2,8,8,128]{3,2,1,0:T(8,128)S(1)}, f32[2,8,8,128]{3,2,1,0:T(8,128)S(1)}, u32[]{:S(2)}, u32[]{:S(2)}) collective-permute-start(f32[2,8,8,128]{3,2,1,0:T(8,128)S(1)} %get-tuple-element.90), channel_id=1, source_target_pairs={{0,4},{1,5},{2,6},{3,7},{4,0},{5,1},{6,2},{7,3},{8,12},{9,13},{10,... | collective-permute-start | bytes 196616 | tf_op jit(solution)/shard_map/ppermute | solution.py:545
  60.6 4.9 %collective-permute-start.15 = (f32[2,8,8,128]{3,2,1,0:T(8,128)S(1)}, f32[2,8,8,128]{3,2,1,0:T(8,128)S(1)}, u32[]{:S(2)}, u32[]{:S(2)}) collective-permute-start(f32[2,8,8,128]{3,2,1,0:T(8,128)S(1)} %get-tuple-element.89), channel_id=1, source_target_pairs={{0,28},{1,29},{2,30},{3,31},{4,8},{5,9},{6,10},{7,11},{8,4},{9,5},... | collective-permute-start | bytes 196616 | tf_op jit(solution)/shard_map/ppermute | solution.py:546
  66.4 20.2 %copy-start.3 = (f32[1,1,8,8,8,128]{5,4,3,2,1,0:T(8,128)S(1)}, f32[1,1,8,8,8,128]{5,4,3,2,1,0:T(8,128)}, u32[]{:S(2)}) copy-start(f32[1,1,8,8,8,128]{5,4,3,2,1,0:T(8,128)} %param.13) | copy-start | bytes 786436
  67.0 9.7 %all-to-all-start.2 = ((f32[32,1,128]{2,1,0:T(1,128)}), f32[32,1,128]{2,1,0:T(1,128)S(1)}, u32[]{:S(2)}, u32[]{:S(2)}) async-start(f32[32,1,128]{2,1,0:T(1,128)} %broadcast_in_dim.75), calls=%async_computation.2 | async-start | bytes 32768 | tf_op jit(solution)/shard_map/all_to_all | solution.py:552
  69.6 12.3 %collective-permute-start.16 = (f32[8,8,128]{2,1,0:T(8,128)S(1)}, f32[8,8,128]{2,1,0:T(8,128)S(1)}, u32[]{:S(2)}, u32[]{:S(2)}) collective-permute-start(f32[8,8,128]{2,1,0:T(8,128)S(1)} %get-tuple-element.58), channel_id=1, source_target_pairs={{0,1},{1,0},{2,3},{3,2},{4,5},{5,4},{6,7},{7,6},{8,9},{9,8},{10,11... | collective-permute-start | bytes 98312 | tf_op jit(solution)/shard_map/ppermute | solution.py:545
  71.4 10.6 %collective-permute-start.17 = (f32[8,8,128]{2,1,0:T(8,128)S(1)}, f32[8,8,128]{2,1,0:T(8,128)S(1)}, u32[]{:S(2)}, u32[]{:S(2)}) collective-permute-start(f32[8,8,128]{2,1,0:T(8,128)S(1)} %get-tuple-element.59), channel_id=1, source_target_pairs={{0,4},{1,2},{2,1},{3,7},{4,0},{5,6},{6,5},{7,3},{8,12},{9,10},{10,... | collective-permute-start | bytes 98312 | tf_op jit(solution)/shard_map/ppermute | solution.py:546
  82.1 1.2 %collective-permute-start.18 = (f32[8,8,128]{2,1,0:T(8,128)S(1)}, f32[8,8,128]{2,1,0:T(8,128)S(1)}, u32[]{:S(2)}, u32[]{:S(2)}) collective-permute-start(f32[8,8,128]{2,1,0:T(8,128)S(1)} %get-tuple-element.112), channel_id=1, source_target_pairs={{0,4},{1,5},{2,6},{3,7},{4,0},{5,1},{6,2},{7,3},{8,12},{9,13},{10,... | collective-permute-start | bytes 98312 | tf_op jit(solution)/shard_map/ppermute | solution.py:545
  82.1 4.4 %collective-permute-start.19 = (f32[8,8,128]{2,1,0:T(8,128)S(1)}, f32[8,8,128]{2,1,0:T(8,128)S(1)}, u32[]{:S(2)}, u32[]{:S(2)}) collective-permute-start(f32[8,8,128]{2,1,0:T(8,128)S(1)} %get-tuple-element.111), channel_id=1, source_target_pairs={{0,28},{1,29},{2,30},{3,31},{4,8},{5,9},{6,10},{7,11},{8,4},{9,5},... | collective-permute-start | bytes 98312 | tf_op jit(solution)/shard_map/ppermute | solution.py:546

commit v2 on v1

--- a/solution.py
+++ b/solution.py
@@ -219,14 +219,33 @@
     total[key] = value if key not in total else total[key] + value
 
 
-def stats_row(tiles):
-    columns = jnp.concatenate([jnp.sum(tile, axis=0, keepdims=True) for tile in tiles], axis=0)
-    pad = 16 - len(tiles)
-    columns = jnp.concatenate([columns, jnp.zeros((pad, 128), jnp.float32)], axis=0)
-    sums = jnp.sum(columns, axis=1, keepdims=True)
+def lane_sums(tiles):
+    columns = [jnp.sum(tile, axis=0, keepdims=True) for tile in tiles]
+    columns.append(jnp.zeros((16 - len(tiles), 128), jnp.float32))
+    sums = jnp.sum(jnp.concatenate(columns, axis=0), axis=1, keepdims=True)
+    return jnp.broadcast_to(sums, (16, 128))
+
+
+def write_stats(stats_ref, tiles):
     row = lax.broadcasted_iota(jnp.int32, (16, 128), 0)
     lane = lax.broadcasted_iota(jnp.int32, (16, 128), 1)
-    return jnp.sum(jnp.where(row == lane, sums, 0.0), axis=0, keepdims=True)
+    sums = jnp.sum(jnp.where(row == lane, lane_sums(tiles), 0.0), axis=0, keepdims=True)
+    for index in range(stats_ref.shape[0]):
+        stats_ref[index] = sums
+
+
+def gathered(stats_ref):
+    return stats_ref[:, 0, :]
+
+
+def stat_columns(stats, first, count):
+    lane = lax.broadcasted_iota(jnp.int32, stats.shape, 1)
+    sums = lane_sums([jnp.where(lane == first + i, stats, 0.0) for i in range(count)])
+    return [sums[i : i + 1] for i in range(count)]
+
+
+def lifted_rows(stats, lift_ref):
+    return lane_sums([lift_ref[i] * stats for i in range(9)])
 
 
 def class_tiles(sums):
@@ -247,7 +266,7 @@
     for (i, j), value in sums.items():
         a, b = (0, 1, NODES - 1)[i], (0, 1, NODES - 1)[j]
         sums[(i, j)] = scaled(value * tile, axis_factor(a, side_x), axis_factor(b, side_y))
-    stats_ref[...] = stats_row(class_tiles(sums))
+    write_stats(stats_ref, class_tiles(sums))
 
 
 def planes(ref):
@@ -357,7 +376,7 @@
     send_parts(part_ref, side_x, side_y, sy_first, sy_second, fx_first, fx_second)
 
 
-def collect_parts(part_ref, ry_first, ry_second, rx_first, rx_second, side_x, side_y, field_ref):
+def collect_parts(part_ref, ry_first, ry_second, rx_first, rx_second, side_x, side_y, field):
     low_x = side_x.low(rx_first[...], rx_second[...])
     high_x = side_x.high(rx_first[...], rx_second[...])
     result = {}
@@ -374,9 +393,13 @@
                 value = value + low_x[a, b]
             if a >= NODES - 2:
                 value = value + high_x[a - (NODES - 2), b]
-            field = 3 * class_of(a) + class_of(b)
-            result[(a, b)] = value + field_ref[field : field + 1, :]
+            node_class = 3 * class_of(a) + class_of(b)
+            result[(a, b)] = value + field[node_class : node_class + 1, :]
     return result
+
+
+def porosity_row(grains_ref):
+    return 1.0 - 0.6 * grains_ref[...].astype(jnp.float32) / MOST_GRAINS
 
 
 def apply_tiles(z_ref, u_ref, y_ref, tiles_ref, por):
@@ -409,20 +432,19 @@
 
 
 def first_apply_kernel(
-    counts, part_ref, ry_first, ry_second, rx_first, rx_second, field_ref, por_ref, r_ref,
-    tiles_ref, z_ref, u_ref, sy_first, sy_second, fx_first, fx_second, stats_ref, y_ref,
+    counts, part_ref, ry_first, ry_second, rx_first, rx_second, gathered_ref, lift_ref, grains_ref,
+    r_ref, tiles_ref, z_ref, u_ref, sy_first, sy_second, fx_first, fx_second, stats_ref, y_ref,
 ):
     side_x, side_y = Sides("gx", counts[0]), Sides("gy", counts[1])
-    z = collect_parts(
-        part_ref, ry_first, ry_second, rx_first, rx_second, side_x, side_y, field_ref
-    )
+    field = lifted_rows(gathered(gathered_ref), lift_ref)
+    z = collect_parts(part_ref, ry_first, ry_second, rx_first, rx_second, side_x, side_y, field)
     inner = None
     for (a, b), value in z.items():
         z_ref[a, b] = value
         term = scaled(value * r_ref[a, b], axis_factor(a, side_x), axis_factor(b, side_y))
         inner = term if inner is None else inner + term
     inner = inner * multiplicity_tile()
-    apply_tiles(z_ref, u_ref, y_ref, tiles_ref, por_ref[...])
+    apply_tiles(z_ref, u_ref, y_ref, tiles_ref, porosity_row(grains_ref))
     sums = {}
     curvature = None
     for a in range(NODES):
@@ -431,7 +453,7 @@
             add_to(sums, (class_of(a), class_of(b)), value)
             term = value * z_ref[a, b]
             curvature = term if curvature is None else curvature + term
-    stats_ref[...] = stats_row(class_tiles(sums) + [inner, curvature])
+    write_stats(stats_ref, class_tiles(sums) + [inner, curvature])
     sum_column(u_ref)
     for a in range(NODES):
         for layer in range(2):
@@ -445,14 +467,15 @@
 
 
 def second_apply_kernel(
-    counts, part_ref, ry_first, ry_second, rx_first, rx_second, field_ref, por_ref, r_ref, q_ref,
-    z_ref, tiles_ref, z1_ref, u_ref, sy_first, sy_second, fx_first, fx_second, stats_ref, y_ref,
+    counts, part_ref, ry_first, ry_second, rx_first, rx_second, gathered_ref, lift_ref, grains_ref,
+    r_ref, q_ref, z_ref, tiles_ref, z1_ref, u_ref, sy_first, sy_second, fx_first, fx_second, stats_ref, y_ref,
 ):
     side_x, side_y = Sides("gx", counts[0]), Sides("gy", counts[1])
-    step = field_ref[9:10, :]
-    w = collect_parts(
-        part_ref, ry_first, ry_second, rx_first, rx_second, side_x, side_y, field_ref
-    )
+    stats = gathered(gathered_ref)
+    field = lifted_rows(stats, lift_ref)
+    first_inner, first_curvature = stat_columns(stats, 9, 2)
+    step = first_inner / first_curvature
+    w = collect_parts(part_ref, ry_first, ry_second, rx_first, rx_second, side_x, side_y, field)
     inner = None
     for (a, b), value in w.items():
         next_z = z_ref[a, b] - step * value
@@ -461,7 +484,7 @@
         term = scaled(next_z * next_r, axis_factor(a, side_x), axis_factor(b, side_y))
         inner = term if inner is None else inner + term
     inner = inner * multiplicity_tile()
-    apply_tiles(z1_ref, u_ref, y_ref, tiles_ref, por_ref[...])
+    apply_tiles(z1_ref, u_ref, y_ref, tiles_ref, porosity_row(grains_ref))
     own = None
     cross = None
     for a in range(NODES):
@@ -471,7 +494,7 @@
             cross_term = value * z_ref[a, b]
             own = own_term if own is None else own + own_term
             cross = cross_term if cross is None else cross + cross_term
-    stats_ref[...] = stats_row([inner, own, cross])
+    write_stats(stats_ref, [inner, own, cross])
     sum_column(u_ref)
     for a in range(NODES):
         low, high = u_ref[a, 0], u_ref[a, NODES - 1]
@@ -484,12 +507,16 @@
 
 def final_kernel(
     counts, sol_ref, r_ref, q_ref, z_ref, z1_ref, u_ref, ry_first, ry_second, rx_first, rx_second,
-    scalars_ref, sol_out, r_out, d_out,
+    second_ref, last_ref, sol_out, r_out, d_out, steps_out,
 ):
     side_x, side_y = Sides("gx", counts[0]), Sides("gy", counts[1])
-    first_step = scalars_ref[0:1, :]
-    second_step = scalars_ref[1:2, :]
-    ratio = scalars_ref[2:3, :]
+    first_inner, first_curvature = stat_columns(gathered(second_ref), 9, 2)
+    second_inner, own, cross = stat_columns(gathered(last_ref), 0, 3)
+    first_step = first_inner / first_curvature
+    ratio = second_inner / first_inner
+    second_step = second_inner / (own + ratio * (2.0 * cross + ratio * first_curvature))
+    steps_out[0] = first_step[0, 0]
+    steps_out[1] = second_step[0, 0]
     low_x = side_x.low(rx_first[...], rx_second[...])
     high_x = side_x.high(rx_first[...], rx_second[...])
     for a in range(NODES):
@@ -515,12 +542,15 @@
     def body(*refs):
         kernel(counts, *refs)
 
+    def space(shape):
+        return pltpu.SMEM if len(shape) == 1 else pltpu.VMEM
+
     return pl.pallas_call(
         body,
         name=name,
         out_shape=[jax.ShapeDtypeStruct(shape, jnp.float32) for shape in shapes],
         in_specs=[pl.BlockSpec(memory_space=pltpu.VMEM)] * len(operands),
-        out_specs=[pl.BlockSpec(memory_space=pltpu.VMEM)] * len(shapes),
+        out_specs=[pl.BlockSpec(memory_space=space(shape)) for shape in shapes],
         scratch_shapes=[pltpu.VMEM(shape, jnp.float32) for shape in scratch],
         compiler_params=pltpu.CompilerParams(vmem_limit_bytes=24 * 1024 * 1024),
     )(*operands)
@@ -547,12 +577,11 @@
     )
 
 
-def gather_stats(counts, row):
-    total = counts[0] * counts[1]
-    return lax.all_to_all(jnp.broadcast_to(row[None], (total, 1, 128)), AXES, 0, 0)[:, 0, :]
-
-
-def coarse_tables(counts, column_length):
+def gather_stats(stats):
+    return lax.all_to_all(stats, AXES, 0, 0)
+
+
+def lift_tables(counts, column_length):
     share_x, share_y = share_table(counts[0]), share_table(counts[1])
     basis_x, eigen_x = cosine_inverse(counts[0])
     basis_y, eigen_y = cosine_inverse(counts[1])
@@ -560,25 +589,22 @@
         2.0 * mean_porosity * column_length * (eigen_x[:, None] + eigen_y[None, :])
         + 8.0 * shift_mass * column_length
     )
-    to_modes_x = np.einsum("xip,pa->xia", share_x, basis_x)
-    to_modes_y = np.einsum("yjq,qb->yjb", share_y, basis_y)
-    return to_modes_x, to_modes_y, divisor
-
-
-def coarse_field(counts, tables, stats):
-    to_modes_x, to_modes_y, divisor = tables
-    sums = stats[:, :9].reshape(counts[0], counts[1], 3, 3)
-    modes_x, modes_y = jnp.asarray(to_modes_x, jnp.float32), jnp.asarray(to_modes_y, jnp.float32)
-    spectrum = jnp.einsum("xyij,xia,yjb->ab", sums, modes_x, modes_y, precision=exact_mode)
-    spectrum = spectrum / jnp.asarray(divisor, jnp.float32)
+    modes_x = np.einsum("xip,pa->xia", share_x, basis_x)
+    modes_y = np.einsum("yjq,qb->yjb", share_y, basis_y)
+    total = counts[0] * counts[1]
+    to_modes = np.einsum("xia,yjb->abxyij", modes_x, modes_y).reshape(total, total, 9)
+    to_modes = np.pad(to_modes, ((0, 0), (0, 0), (0, 7))).reshape(total, total * 16)
+    return [table.astype(np.float32) for table in (modes_x, modes_y, 1.0 / divisor, to_modes)]
+
+
+def own_lift(tables):
+    modes_x, modes_y, inverse, to_modes = [jnp.asarray(table) for table in tables]
     own_x = lax.dynamic_index_in_dim(modes_x, lax.axis_index("gx"), 0, keepdims=False)
     own_y = lax.dynamic_index_in_dim(modes_y, lax.axis_index("gy"), 0, keepdims=False)
-    return jnp.einsum("ia,ab,jb->ij", own_x, spectrum, own_y, precision=exact_mode).reshape(9)
-
-
-def rows_of(values, count):
-    values = jnp.concatenate([values, jnp.zeros((count - values.shape[0],), jnp.float32)])
-    return jnp.broadcast_to(values[:, None], (count, 128))
+    own = own_x[:, None, :, None] * own_y[None, :, None, :] * inverse[None, None]
+    total = to_modes.shape[0]
+    lift = jnp.dot(own.reshape(9, total), to_modes, precision=exact_mode)
+    return jnp.pad(lift.reshape(9, total, 16), ((0, 0), (0, 0), (0, 112)))
 
 
 def shards_of(counts):
@@ -590,13 +616,12 @@
         block = shard_shape[2:]
         solution = solution.reshape(block)
         residual = residual.reshape(block)
-        tables = coarse_tables(counts, block[-1])
+        lift = own_lift(lift_tables(counts, block[-1]))
+        grains = grain_counts.reshape(1, 128)
         plane = [jnp.asarray(table) for table in (forward_np, back_np, inverse_np)]
         tiles = jnp.asarray(tiles_np)
-        porosity = 1.0 - 0.6 * grain_counts.reshape(1, 128).astype(jnp.float32) / MOST_GRAINS
         side_x, side_y = Sides("gx", counts[0]), Sides("gy", counts[1])
-        even_x = side_x.even
-        row = (1, 128)
+        row = (counts[0] * counts[1], 1, 128)
         face = (NODES, NODES, 128)
         part_shapes = [
             (EXT, ROWS, 128),
@@ -619,7 +644,7 @@
             counts, 0, side_x.send_first(low_face, high_face),
             side_x.send_second(low_face, high_face),
         )
-        first_stats = gather_stats(counts, stats)
+        first_stats = gather_stats(stats)
 
         def spread_faces(fx, ry):
             low_y, high_y = side_y.low(*ry), side_y.high(*ry)
@@ -639,13 +664,12 @@
         )
         ry = trade(counts, 1, y_first, y_second)
         rx = trade(counts, 0, *spread_faces(fx, ry))
-        field = rows_of(coarse_field(counts, tables, first_stats), 16)
         z, u, y_first, y_second, *fx, stats = call(
             first_apply_kernel, counts, "first_apply",
             [block, block, (NODES, 2, NODES, 128), (NODES, 2, NODES, 128),
              (2, NODES, NODES, 128), (2, NODES, NODES, 128), row],
             [block],
-            part, *ry, *rx, field, porosity, residual, tiles,
+            part, *ry, *rx, first_stats, lift, grains, residual, tiles,
         )
         ry = trade(counts, 1, y_first, y_second)
         low_y, high_y = side_y.low(*ry), side_y.high(*ry)
@@ -661,24 +685,18 @@
             jnp.pad(fx[0], pads) + side_x.send_first(*both),
             jnp.pad(fx[1], pads) + side_x.send_second(*both),
         )
-        second_stats = gather_stats(counts, stats)
+        second_stats = gather_stats(stats)
         q, part, y_first, y_second, *fx = call(
             second_solve_kernel, counts, "second_solve", [block] + part_shapes, solve_scratch,
             u, *ry, *rx, *plane,
         )
         ry = trade(counts, 1, y_first, y_second)
         rx = trade(counts, 0, *spread_faces(fx, ry))
-        first_inner = jnp.sum(second_stats[:, 9])
-        first_curvature = jnp.sum(second_stats[:, 10])
-        first_step = first_inner / first_curvature
-        field = rows_of(
-            jnp.concatenate([coarse_field(counts, tables, second_stats), first_step[None]]), 16
-        )
         z1, u, y_first, y_second, *fx, stats = call(
             second_apply_kernel, counts, "second_apply",
             [block, block, face, face, face, face, row],
             [block],
-            part, *ry, *rx, field, porosity, residual, q, z, tiles,
+            part, *ry, *rx, second_stats, lift, grains, residual, q, z, tiles,
         )
         ry = trade(counts, 1, y_first, y_second)
         low_y, high_y = side_y.low(*ry), side_y.high(*ry)
@@ -691,20 +709,16 @@
         rx = trade(
             counts, 0, fx[0] + side_x.send_first(*both), fx[1] + side_x.send_second(*both)
         )
-        last_stats = gather_stats(counts, stats)
-        second_inner, own, cross = (jnp.sum(last_stats[:, i]) for i in range(3))
-        ratio = second_inner / first_inner
-        second_step = second_inner / (own + ratio * (2.0 * cross + ratio * first_curvature))
-        scalars = rows_of(jnp.stack([first_step, second_step, ratio]), 8)
-        solution_out, residual_out, direction = call(
-            final_kernel, counts, "final", [block] * 3, [],
-            solution, residual, q, z, z1, u, *ry, *rx, scalars,
+        last_stats = gather_stats(stats)
+        solution_out, residual_out, direction, steps = call(
+            final_kernel, counts, "final", [block] * 3 + [(2,)], [],
+            solution, residual, q, z, z1, u, *ry, *rx, second_stats, last_stats,
         )
         return (
             solution_out.reshape(shard_shape),
             residual_out.reshape(shard_shape),
             direction.reshape(shard_shape),
-            jnp.stack([first_step, second_step]),
+            steps,
         )
 
     return shards

time: 88 us -> 81.5 us (0.926)
  waiting for transfers between devices: 43.7 us -> 19.9 us
  blocking collectives: 0 us -> 23.4 us
  between operations: 6.29 us -> 0.93 us
  other arithmetic: 3.23 us -> 0.48 us
  starting transfers between devices: 20.6 us -> 22.6 us
  matrix products: 2.08 us -> 1.12 us
    all_to_all x0 -> x2, blocking collectives: none -> 23.4 us  [gather_stats(): return lax.all_to_all(stats, AXES, 0, 0)]
    all_to_all x3 -> x1, waiting for transfers between devices: 17 us -> 0.01 us  [gather_stats(): return lax.all_to_all(stats, AXES, 0, 0)]
    ppermute x10, waiting for transfers between devices: 18.1 us -> 8.33 us  [trade(): lax.ppermute(second, AXES, swap_pairs(counts, axis, 1))]
    ppermute x10, starting transfers between devices: 7.9 us -> 12 us  [trade(): lax.ppermute(first, AXES, swap_pairs(counts, axis, 0))]
    all_to_all x3 -> x1, starting transfers between devices: 10.5 us -> 7.3 us  [gather_stats(): return lax.all_to_all(stats, AXES, 0, 0)]
    ppermute x10, waiting for transfers between devices: 8.61 us -> 11.6 us  [trade(): lax.ppermute(first, AXES, swap_pairs(counts, axis, 0))]
    broadcast_in_dim x6 -> x0, local copies, waits for them, and re-layouts: 2.05 us -> none  [the longest x3 1.84 us: gather_stats(): jnp.broadcast_to(row[None], (total, 1, 128))]
    mul x0 -> x3, local copies, waits for them, and re-layouts: none -> 1.45 us  [own_lift(): own_x[:, None, :, None] * own_y[None, :, None, :] * inverse[None, None]]
  transfers between devices with their start and end apart: 23 -> 21, of which waited for: 15 -> 8; matrix products, arithmetic and copies ran while one was open for 7% -> 4% of each run, Pallas kernels for 0% -> 2%
where the time goes in v2:
time: 81.5 us; the launch traced here: 81.1 us
  blocking collectives  23.4 us (29%)
  starting transfers between devices  22.6 us (28%)
  waiting for transfers between devices  19.9 us (24%)
  Pallas kernels  7.51 us (9%)
  local copies, waits for them, and re-layouts  5.13 us (6%)
  matrix products  1.12 us (1%)
  between operations  0.93 us (1%)
    all_to_all x2, blocking collectives, gather_stats(): return lax.all_to_all(stats, AXES, 0, 0)  23.4 us
    ppermute x10, starting transfers between devices, trade(): lax.ppermute(first, AXES, swap_pairs(counts, axis, 0))  12 us
    ppermute x10, waiting for transfers between devices, trade(): lax.ppermute(first, AXES, swap_pairs(counts, axis, 0))  11.6 us
    ppermute x10, waiting for transfers between devices, trade(): lax.ppermute(second, AXES, swap_pairs(counts, axis, 1))  8.33 us
    pallas_call x6, Pallas kernels, call(): pl.pallas_call(body, name=name, out_shape=[jax.ShapeDtypeStruct(shape, jn...  7.51 us
    all_to_all x1, starting transfers between devices, gather_stats(): return lax.all_to_all(stats, AXES, 0, 0)  7.3 us
    ppermute x10, starting transfers between devices, trade(): lax.ppermute(second, AXES, swap_pairs(counts, axis, 1))  3.28 us
    unnamed x24, local copies, waits for them, and re-layouts  3.27 us
  transfers between devices with their start and end apart: 21, of which 8 were waited for; matrix products, arithmetic and copies ran while one was open for 4% of the time, Pallas kernels for 2%

profile of v2, /device:TPU:0, one launch (start us, length us, event | category | flops | bytes accessed | tf_op | source)
XLA Modules:
  0.0 81.1 jit_solution(2557467830443404390)
XLA Ops:
  0.6 0.9 %copy-done = f32[1,1,8,8,8,128]{5,4,3,2,1,0:T(8,128)S(1)} copy-done((f32[1,1,8,8,8,128]{5,4,3,2,1,0:T(8,128)S(1)}, f32[1,1,8,8,8,128]{5,4,3,2,1,0:T(8,128)}, u32[]{:S(2)}) %copy-start) | copy-done | bytes 262168
  1.6 0.7 start.1
  2.3 7.3 %all-to-all-start = ((f32[32,1,128]{2,1,0:T(1,128)}), f32[32,1,128]{2,1,0:T(1,128)S(1)}, u32[]{:S(2)}, u32[]{:S(2)}) async-start(f32[32,1,128]{2,1,0:T(1,128)} %get-tuple-element.43), calls=%async_computation | async-start | bytes 32768 | tf_op jit(solution)/shard_map/all_to_all | solution.py:581
  9.6 1.8 %collective-permute-start = (f32[8,8,128]{2,1,0:T(8,128)S(1)}, f32[8,8,128]{2,1,0:T(8,128)S(1)}, u32[]{:S(2)}, u32[]{:S(2)}) collective-permute-start(f32[8,8,128]{2,1,0:T(8,128)S(1)} %get-tuple-element.36), channel_id=1, source_target_pairs={{0,1},{1,0},{2,3},{3,2},{4,5},{5,4},{6,7},{7,6},{8,9},{9,8},{10,11... | collective-permute-start | bytes 98312 | tf_op jit(solution)/shard_map/ppermute | solution.py:575
  11.5 0.7 dynamic-slice_bitcast_fusion.1
  12.2 1.5 %collective-permute-done.refs_1_ = f32[8,8,128]{2,1,0:T(8,128)S(1)} collective-permute-done((f32[8,8,128]{2,1,0:T(8,128)S(1)}, f32[8,8,128]{2,1,0:T(8,128)S(1)}, u32[]{:S(2)}, u32[]{:S(2)}) %collective-permute-start) | collective-permute-done | bytes 32800 | tf_op jit(solution)/shard_map/ppermute | solution.py:575
  13.7 1.6 %collective-permute-start.3 = (f32[10,8,128]{2,1,0:T(8,128)S(1)}, f32[10,8,128]{2,1,0:T(8,128)S(1)}, u32[]{:S(2)}, u32[]{:S(2)}) collective-permute-start(f32[10,8,128]{2,1,0:T(8,128)S(1)} %get-tuple-element.84), channel_id=1, source_target_pairs={{0,28},{1,29},{2,30},{3,31},{4,8},{5,9},{6,10},{7,11},{8,4},{9,5},... | collective-permute-start | bytes 122888 | tf_op jit(solution)/shard_map/ppermute | solution.py:576
  15.3 0.3 collective-permute-start.2
  15.6 0.7 dynamic-slice_bitcast_fusion
  16.3 1.9 %collective-permute-done.3.refs_4_ = f32[10,8,128]{2,1,0:T(8,128)S(1)} collective-permute-done((f32[10,8,128]{2,1,0:T(8,128)S(1)}, f32[10,8,128]{2,1,0:T(8,128)S(1)}, u32[]{:S(2)}, u32[]{:S(2)}) %collective-permute-start.3) | collective-permute-done | bytes 40992 | tf_op jit(solution)/shard_map/ppermute | solution.py:576
  18.2 0.8 %copy-done.4 = f32[112,104]{1,0:T(8,128)S(1)} copy-done((f32[112,104]{1,0:T(8,128)S(1)}, f32[112,104]{1,0:T(8,128)}, u32[]{:S(2)}) %copy-start.4) | copy-done | bytes 46616
  19.1 0.8 copy-done.6
  19.9 1.9 %first_solve.1 = (f32[10,112,128]{2,1,0:T(8,128)S(1)}, f32[10,2,8,128]{3,2,1,0:T(8,128)S(1)}, f32[10,2,8,128]{3,2,1,0:T(8,128)S(1)}, f32[2,10,8,128]{3,2,1,0:T(8,128)S(1)}, f32[2,10,8,128]{3,2,1,0:T(8,128)S(1)}) custom-call(f32[8,8,8,128]{3,2,1,0:T(8,128)S(1)} %bitcast.19, f32[8,8,128]{2,1,0:T(8,128)S(1)} %collective-permute-done.refs_1_, ...), custom_call_target="tpu_custom_call" | custom-call | tf_op jit(solution)/shard_map/first_solve/pallas_call | solution.py:548
  21.8 3.0 %collective-permute-start.4 = (f32[10,2,8,128]{3,2,1,0:T(8,128)S(1)}, f32[10,2,8,128]{3,2,1,0:T(8,128)S(1)}, u32[]{:S(2)}, u32[]{:S(2)}) collective-permute-start(f32[10,2,8,128]{3,2,1,0:T(8,128)S(1)} %get-tuple-element.39), channel_id=1, source_target_pairs={{0,1},{1,0},{2,3},{3,2},{4,5},{5,4},{6,7},{7,6},{8,9},{9,8},{10,11... | collective-permute-start | bytes 245768 | tf_op jit(solution)/shard_map/ppermute | solution.py:575
  24.8 0.1 multiply_multiply_fusion
  24.8 0.1 reshape.81
  24.9 0.1 pad.36.clone
  25.0 2.2 %collective-permute-done.4.refs_1_ = f32[10,2,8,128]{3,2,1,0:T(8,128)S(1)} collective-permute-done((f32[10,2,8,128]{3,2,1,0:T(8,128)S(1)}, f32[10,2,8,128]{3,2,1,0:T(8,128)S(1)}, u32[]{:S(2)}, u32[]{:S(2)}) %collective-permute-start.4) | collective-permute-done | bytes 81952 | tf_op jit(solution)/shard_map/ppermute | solution.py:575
  27.2 0.1 fusion.7
  27.3 1.0 %collective-permute-start.7 = (f32[2,8,8,128]{3,2,1,0:T(8,128)S(1)}, f32[2,8,8,128]{3,2,1,0:T(8,128)S(1)}, u32[]{:S(2)}, u32[]{:S(2)}) collective-permute-start(f32[2,8,8,128]{3,2,1,0:T(8,128)S(1)} %get-tuple-element.90), channel_id=1, source_target_pairs={{0,28},{1,29},{2,30},{3,31},{4,8},{5,9},{6,10},{7,11},{8,4},{9,5},... | collective-permute-start | bytes 196616 | tf_op jit(solution)/shard_map/ppermute | solution.py:576
  28.3 1.1 %fusion.28 = f32[9,32,16]{1,0,2:T(8,128)S(1)} fusion(f32[9,32,1]{1,0,2:T(8,128)S(1)} %reshape.81, f32[32,16,32]{2,0,1:T(8,128)S(1)} %copy-done.10), kind=kOutput, calls=%fused_computation.53 | convolution fusion | flops 1769472 | bytes 85120 | tf_op jit(solution)/shard_map/dot_general | solution.py:606
  29.4 0.1 copy.16
  29.6 2.4 %collective-permute-done.7.refs_4_ = f32[2,8,8,128]{3,2,1,0:T(8,128)S(1)} collective-permute-done((f32[2,8,8,128]{3,2,1,0:T(8,128)S(1)}, f32[2,8,8,128]{3,2,1,0:T(8,128)S(1)}, u32[]{:S(2)}, u32[]{:S(2)}) %collective-permute-start.7) | collective-permute-done | bytes 65568 | tf_op jit(solution)/shard_map/ppermute | solution.py:576
  32.0 0.6 copy-done.9
  32.6 0.9 %first_apply.1 = (f32[8,8,8,128]{3,2,1,0:T(8,128)S(1)}, f32[8,8,8,128]{3,2,1,0:T(8,128)S(1)}, f32[8,2,8,128]{3,2,1,0:T(8,128)S(1)}, f32[8,2,8,128]{3,2,1,0:T(8,1...) custom-call(f32[10,112,128]{2,1,0:T(8,128)S(1)} %get-tuple-element.38.refs_0_, ...), custom_call_target="tpu_custom_call" | custom-call | tf_op jit(solution)/shard_map/first_apply/pallas_call | solution.py:548
  33.6 2.2 %collective-permute-start.8 = (f32[8,2,8,128]{3,2,1,0:T(8,128)S(1)}, f32[8,2,8,128]{3,2,1,0:T(8,128)S(1)}, u32[]{:S(2)}, u32[]{:S(2)}) collective-permute-start(f32[8,2,8,128]{3,2,1,0:T(8,128)S(1)} %get-tuple-element.45), channel_id=1, source_target_pairs={{0,1},{1,0},{2,3},{3,2},{4,5},{5,4},{6,7},{7,6},{8,9},{9,8},{10,11... | collective-permute-start | bytes 196616 | tf_op jit(solution)/shard_map/ppermute | solution.py:575
  35.7 0.1 pad.30.clone
  35.8 2.2 %collective-permute-done.8.refs_1_ = f32[8,2,8,128]{3,2,1,0:T(8,128)S(1)} collective-permute-done((f32[8,2,8,128]{3,2,1,0:T(8,128)S(1)}, f32[8,2,8,128]{3,2,1,0:T(8,128)S(1)}, u32[]{:S(2)}, u32[]{:S(2)}) %collective-permute-start.8) | collective-permute-done | bytes 65568 | tf_op jit(solution)/shard_map/ppermute | solution.py:575
  38.0 0.1 fusion.3
  38.1 0.1 collective-permute-start.11
  38.2 0.8 collective-permute-start.10
  39.0 4.0 %collective-permute-done.11.refs_4_ = f32[2,10,8,128]{3,2,1,0:T(8,128)S(1)} collective-permute-done((f32[2,10,8,128]{3,2,1,0:T(8,128)S(1)}, f32[2,10,8,128]{3,2,1,0:T(8,128)S(1)}, u32[]{:S(2)}, u32[]{:S(2)}) %collective-permute-start.11) | collective-permute-done | bytes 81952 | tf_op jit(solution)/shard_map/ppermute | solution.py:576
  43.0 1.9 %second_solve.1 = (f32[8,8,8,128]{3,2,1,0:T(8,128)S(1)}, f32[10,112,128]{2,1,0:T(8,128)S(1)}, f32[10,2,8,128]{3,2,1,0:T(8,128)S(1)}, f32[10,2,8,128]{3,2,1,0:T(8...) custom-call(f32[8,8,8,128]{3,2,1,0:T(8,128)S(1)} %get-tuple-element.44.refs_0_, ...), custom_call_target="tpu_custom_call" | custom-call | tf_op jit(solution)/shard_map/second_solve/pallas_call | solution.py:548
  44.9 2.2 %collective-permute-start.12 = (f32[10,2,8,128]{3,2,1,0:T(8,128)S(1)}, f32[10,2,8,128]{3,2,1,0:T(8,128)S(1)}, u32[]{:S(2)}, u32[]{:S(2)}) collective-permute-start(f32[10,2,8,128]{3,2,1,0:T(8,128)S(1)} %get-tuple-element.52), channel_id=1, source_target_pairs={{0,1},{1,0},{2,3},{3,2},{4,5},{5,4},{6,7},{7,6},{8,9},{9,8},{10,11... | collective-permute-start | bytes 245768 | tf_op jit(solution)/shard_map/ppermute | solution.py:575
  47.1 2.4 %collective-permute-done.12.refs_1_ = f32[10,2,8,128]{3,2,1,0:T(8,128)S(1)} collective-permute-done((f32[10,2,8,128]{3,2,1,0:T(8,128)S(1)}, f32[10,2,8,128]{3,2,1,0:T(8,128)S(1)}, u32[]{:S(2)}, u32[]{:S(2)}) %collective-permute-start.12) | collective-permute-done | bytes 81952 | tf_op jit(solution)/shard_map/ppermute | solution.py:575
  49.5 0.1 fusion.11
  49.6 0.6 collective-permute-start.15
  50.2 0.6 collective-permute-start.14
  50.8 12.2 %all_to_all.15.refs_5_.refs_10_ = f32[32,1,128]{2,1,0:T(1,128)S(1)} all-to-all(f32[32,1,128]{2,1,0:T(1,128)S(1)} %get-tuple-element.56), channel_id=1, replica_groups=mesh['gx'=8,'gy'=4] {'gx','gy'}, dimensions={0} | all-to-all | bytes 32768 | tf_op jit(solution)/shard_map/all_to_all | solution.py:581
  63.1 1.0 %second_apply.1 = (f32[8,8,8,128]{3,2,1,0:T(8,128)S(1)}, f32[8,8,8,128]{3,2,1,0:T(8,128)S(1)}, f32[8,8,128]{2,1,0:T(8,128)S(1)}, f32[8,8,128]{2,1,0:T(8,128)S(1)...) custom-call(f32[10,112,128]{2,1,0:T(8,128)S(1)} %get-tuple-element.51.refs_0_, ...), custom_call_target="tpu_custom_call" | custom-call | tf_op jit(solution)/shard_map/second_apply/pallas_call | solution.py:548
  64.0 0.5 collective-permute-start.16
  64.6 0.1 pad.18.clone
  64.7 3.4 %collective-permute-done.16.refs_6_ = f32[8,8,128]{2,1,0:T(8,128)S(1)} collective-permute-done((f32[8,8,128]{2,1,0:T(8,128)S(1)}, f32[8,8,128]{2,1,0:T(8,128)S(1)}, u32[]{:S(2)}, u32[]{:S(2)}) %collective-permute-start.16) | collective-permute-done | bytes 32800 | tf_op jit(solution)/shard_map/ppermute | solution.py:575
  68.1 0.1 fusion.15
  68.1 0.0 collective-permute-start.19
  68.2 0.7 collective-permute-start.18
  68.9 11.1 %all_to_all.16.refs_11_ = f32[32,1,128]{2,1,0:T(1,128)S(1)} all-to-all(f32[32,1,128]{2,1,0:T(1,128)S(1)} %get-tuple-element.63), channel_id=1, replica_groups=mesh['gx'=8,'gy'=4] {'gx','gy'}, dimensions={0} | all-to-all | bytes 32768 | tf_op jit(solution)/shard_map/all_to_all | solution.py:581
  80.0 1.1 %final.1 = (f32[8,8,8,128]{3,2,1,0:T(8,128)}, f32[8,8,8,128]{3,2,1,0:T(8,128)}, f32[8,8,8,128]{3,2,1,0:T(8,128)}, f32[2]{0:T(128)}) custom-call(f32[8,8,8,128]{3,2,1,0:T(8,128)S(1)} %bitcast.23, f32[8,8,8,128]{3,2,1,0:T(8,128)S(1)} %bitcast.22, f32[8,8,8,128]{3,2,1,0:T(8,128)S(1)} %get-tuple-element.49.refs_9_.refs_2_, ...), custom_call_target="tpu_custom_call" | custom-call | tf_op jit(solution)/shard_map/final/pallas_call | solution.py:548
  (58 shorter events, 0.2 us)
Async XLA Ops:
  0.6 1.0 %copy-start = (f32[1,1,8,8,8,128]{5,4,3,2,1,0:T(8,128)S(1)}, f32[1,1,8,8,8,128]{5,4,3,2,1,0:T(8,128)}, u32[]{:S(2)}) copy-start(f32[1,1,8,8,8,128]{5,4,3,2,1,0:T(8,128)} %param.12) | copy-start | bytes 786436
  1.6 9.9 %copy-start.1 = (f32[1,1,8,8,8,128]{5,4,3,2,1,0:T(8,128)S(1)}, f32[1,1,8,8,8,128]{5,4,3,2,1,0:T(8,128)}, u32[]{:S(2)}) copy-start(f32[1,1,8,8,8,128]{5,4,3,2,1,0:T(8,128)} %param.12) | copy-start | bytes 786436
  1.6 16.7 %copy-start.2 = (f32[10,104,128]{2,1,0:T(8,128)S(1)}, f32[10,104,128]{2,1,0:T(8,128)}, u32[]{:S(2)}) copy-start(f32[10,104,128]{2,1,0:T(8,128)} %constant.57.clone.refs_7_) | copy-start | bytes 1597444
  2.3 27.2 %all-to-all-start = ((f32[32,1,128]{2,1,0:T(1,128)}), f32[32,1,128]{2,1,0:T(1,128)S(1)}, u32[]{:S(2)}, u32[]{:S(2)}) async-start(f32[32,1,128]{2,1,0:T(1,128)} %get-tuple-element.43), calls=%async_computation | async-start | bytes 32768 | tf_op jit(solution)/shard_map/all_to_all | solution.py:581
  9.6 4.0 %collective-permute-start = (f32[8,8,128]{2,1,0:T(8,128)S(1)}, f32[8,8,128]{2,1,0:T(8,128)S(1)}, u32[]{:S(2)}, u32[]{:S(2)}) collective-permute-start(f32[8,8,128]{2,1,0:T(8,128)S(1)} %get-tuple-element.36), channel_id=1, source_target_pairs={{0,1},{1,0},{2,3},{3,2},{4,5},{5,4},{6,7},{7,6},{8,9},{9,8},{10,11... | collective-permute-start | bytes 98312 | tf_op jit(solution)/shard_map/ppermute | solution.py:575
  11.5 2.2 %collective-permute-start.1 = (f32[8,8,128]{2,1,0:T(8,128)S(1)}, f32[8,8,128]{2,1,0:T(8,128)S(1)}, u32[]{:S(2)}, u32[]{:S(2)}) collective-permute-start(f32[8,8,128]{2,1,0:T(8,128)S(1)} %get-tuple-element.37), channel_id=1, source_target_pairs={{0,4},{1,2},{2,1},{3,7},{4,0},{5,6},{6,5},{7,3},{8,12},{9,10},{10,... | collective-permute-start | bytes 98312 | tf_op jit(solution)/shard_map/ppermute | solution.py:576
  13.7 4.5 %collective-permute-start.3 = (f32[10,8,128]{2,1,0:T(8,128)S(1)}, f32[10,8,128]{2,1,0:T(8,128)S(1)}, u32[]{:S(2)}, u32[]{:S(2)}) collective-permute-start(f32[10,8,128]{2,1,0:T(8,128)S(1)} %get-tuple-element.84), channel_id=1, source_target_pairs={{0,28},{1,29},{2,30},{3,31},{4,8},{5,9},{6,10},{7,11},{8,4},{9,5},... | collective-permute-start | bytes 122888 | tf_op jit(solution)/shard_map/ppermute | solution.py:576
  15.3 2.9 %collective-permute-start.2 = (f32[10,8,128]{2,1,0:T(8,128)S(1)}, f32[10,8,128]{2,1,0:T(8,128)S(1)}, u32[]{:S(2)}, u32[]{:S(2)}) collective-permute-start(f32[10,8,128]{2,1,0:T(8,128)S(1)} %get-tuple-element.85), channel_id=1, source_target_pairs={{0,4},{1,5},{2,6},{3,7},{4,0},{5,1},{6,2},{7,3},{8,12},{9,13},{10,... | collective-permute-start | bytes 122888 | tf_op jit(solution)/shard_map/ppermute | solution.py:575
  18.2 0.8 %copy-start.4 = (f32[112,104]{1,0:T(8,128)S(1)}, f32[112,104]{1,0:T(8,128)}, u32[]{:S(2)}) copy-start(f32[112,104]{1,0:T(8,128)} %constant.56.clone.refs_6_) | copy-start | bytes 139780
  19.1 0.8 copy-start.6
  19.9 4.9 %copy-start.11 = (f32[8,4]{1,0:T(8,128)S(1)}, f32[8,4]{1,0:T(8,128)}, u32[]{:S(2)}) copy-start(f32[8,4]{1,0:T(8,128)} %constant.53.clone) | copy-start | bytes 388
  21.8 5.4 %collective-permute-start.4 = (f32[10,2,8,128]{3,2,1,0:T(8,128)S(1)}, f32[10,2,8,128]{3,2,1,0:T(8,128)S(1)}, u32[]{:S(2)}, u32[]{:S(2)}) collective-permute-start(f32[10,2,8,128]{3,2,1,0:T(8,128)S(1)} %get-tuple-element.39), channel_id=1, source_target_pairs={{0,1},{1,0},{2,3},{3,2},{4,5},{5,4},{6,7},{7,6},{8,9},{9,8},{10,11... | collective-permute-start | bytes 245768 | tf_op jit(solution)/shard_map/ppermute | solution.py:575
  24.8 2.4 %collective-permute-start.5 = (f32[10,2,8,128]{3,2,1,0:T(8,128)S(1)}, f32[10,2,8,128]{3,2,1,0:T(8,128)S(1)}, u32[]{:S(2)}, u32[]{:S(2)}) collective-permute-start(f32[10,2,8,128]{3,2,1,0:T(8,128)S(1)} %get-tuple-element.40), channel_id=1, source_target_pairs={{0,4},{1,2},{2,1},{3,7},{4,0},{5,6},{6,5},{7,3},{8,12},{9,10},{10,... | collective-permute-start | bytes 245768 | tf_op jit(solution)/shard_map/ppermute | solution.py:576
  27.2 1.1 %copy-start.10 = (f32[32,16,32]{2,0,1:T(8,128)S(1)}, f32[32,16,32]{2,0,1:T(8,128)}, u32[]{:S(2)}) copy-start(f32[32,16,32]{2,0,1:T(8,128)} %constant.69) | copy-start | bytes 196612
  27.3 4.7 %collective-permute-start.7 = (f32[2,8,8,128]{3,2,1,0:T(8,128)S(1)}, f32[2,8,8,128]{3,2,1,0:T(8,128)S(1)}, u32[]{:S(2)}, u32[]{:S(2)}) collective-permute-start(f32[2,8,8,128]{3,2,1,0:T(8,128)S(1)} %get-tuple-element.90), channel_id=1, source_target_pairs={{0,28},{1,29},{2,30},{3,31},{4,8},{5,9},{6,10},{7,11},{8,4},{9,5},... | collective-permute-start | bytes 196616 | tf_op jit(solution)/shard_map/ppermute | solution.py:576
  28.3 3.7 %collective-permute-start.6 = (f32[2,8,8,128]{3,2,1,0:T(8,128)S(1)}, f32[2,8,8,128]{3,2,1,0:T(8,128)S(1)}, u32[]{:S(2)}, u32[]{:S(2)}) collective-permute-start(f32[2,8,8,128]{3,2,1,0:T(8,128)S(1)} %get-tuple-element.91), channel_id=1, source_target_pairs={{0,4},{1,5},{2,6},{3,7},{4,0},{5,1},{6,2},{7,3},{8,12},{9,13},{10,... | collective-permute-start | bytes 196616 | tf_op jit(solution)/shard_map/ppermute | solution.py:575
  29.5 2.4 %copy-start.8 = (f32[9,8,128]{2,1,0:T(8,128)S(1)}, f32[9,8,128]{2,1,0:T(8,128)}, u32[]{:S(2)}) copy-start(f32[9,8,128]{2,1,0:T(8,128)} %constant.58.clone.refs_9_.refs_11_) | copy-start | bytes 110596
  32.0 0.7 copy-start.9
  33.6 4.4 %collective-permute-start.8 = (f32[8,2,8,128]{3,2,1,0:T(8,128)S(1)}, f32[8,2,8,128]{3,2,1,0:T(8,128)S(1)}, u32[]{:S(2)}, u32[]{:S(2)}) collective-permute-start(f32[8,2,8,128]{3,2,1,0:T(8,128)S(1)} %get-tuple-element.45), channel_id=1, source_target_pairs={{0,1},{1,0},{2,3},{3,2},{4,5},{5,4},{6,7},{7,6},{8,9},{9,8},{10,11... | collective-permute-start | bytes 196616 | tf_op jit(solution)/shard_map/ppermute | solution.py:575
  35.7 2.2 %collective-permute-start.9 = (f32[8,2,8,128]{3,2,1,0:T(8,128)S(1)}, f32[8,2,8,128]{3,2,1,0:T(8,128)S(1)}, u32[]{:S(2)}, u32[]{:S(2)}) collective-permute-start(f32[8,2,8,128]{3,2,1,0:T(8,128)S(1)} %get-tuple-element.46), channel_id=1, source_target_pairs={{0,4},{1,2},{2,1},{3,7},{4,0},{5,6},{6,5},{7,3},{8,12},{9,10},{10,... | collective-permute-start | bytes 196616 | tf_op jit(solution)/shard_map/ppermute | solution.py:576
  38.0 5.0 %copy-start.5 = (f32[112,104]{1,0:T(8,128)S(1)}, f32[112,104]{1,0:T(8,128)}, u32[]{:S(2)}) copy-start(f32[112,104]{1,0:T(8,128)} %constant.56.clone.refs_6_) | copy-start | bytes 139780
  38.0 4.9 %copy-start.7 = (f32[104,112]{1,0:T(8,128)S(1)}, f32[104,112]{1,0:T(8,128)}, u32[]{:S(2)}) copy-start(f32[104,112]{1,0:T(8,128)} %constant.55.clone.refs_5_) | copy-start | bytes 139780
  38.1 4.8 %collective-permute-start.11 = (f32[2,10,8,128]{3,2,1,0:T(8,128)S(1)}, f32[2,10,8,128]{3,2,1,0:T(8,128)S(1)}, u32[]{:S(2)}, u32[]{:S(2)}) collective-permute-start(f32[2,10,8,128]{3,2,1,0:T(8,128)S(1)} %get-tuple-element.88), channel_id=1, source_target_pairs={{0,28},{1,29},{2,30},{3,31},{4,8},{5,9},{6,10},{7,11},{8,4},{9,5},... | collective-permute-start | bytes 245768 | tf_op jit(solution)/shard_map/ppermute | solution.py:576
  38.2 4.8 %collective-permute-start.10 = (f32[2,10,8,128]{3,2,1,0:T(8,128)S(1)}, f32[2,10,8,128]{3,2,1,0:T(8,128)S(1)}, u32[]{:S(2)}, u32[]{:S(2)}) collective-permute-start(f32[2,10,8,128]{3,2,1,0:T(8,128)S(1)} %get-tuple-element.89), channel_id=1, source_target_pairs={{0,4},{1,5},{2,6},{3,7},{4,0},{5,1},{6,2},{7,3},{8,12},{9,13},{10,... | collective-permute-start | bytes 245768 | tf_op jit(solution)/shard_map/ppermute | solution.py:575
  44.9 4.6 %collective-permute-start.12 = (f32[10,2,8,128]{3,2,1,0:T(8,128)S(1)}, f32[10,2,8,128]{3,2,1,0:T(8,128)S(1)}, u32[]{:S(2)}, u32[]{:S(2)}) collective-permute-start(f32[10,2,8,128]{3,2,1,0:T(8,128)S(1)} %get-tuple-element.52), channel_id=1, source_target_pairs={{0,1},{1,0},{2,3},{3,2},{4,5},{5,4},{6,7},{7,6},{8,9},{9,8},{10,11... | collective-permute-start | bytes 245768 | tf_op jit(solution)/shard_map/ppermute | solution.py:575
  47.1 2.4 %collective-permute-start.13 = (f32[10,2,8,128]{3,2,1,0:T(8,128)S(1)}, f32[10,2,8,128]{3,2,1,0:T(8,128)S(1)}, u32[]{:S(2)}, u32[]{:S(2)}) collective-permute-start(f32[10,2,8,128]{3,2,1,0:T(8,128)S(1)} %get-tuple-element.53), channel_id=1, source_target_pairs={{0,4},{1,2},{2,1},{3,7},{4,0},{5,6},{6,5},{7,3},{8,12},{9,10},{10,... | collective-permute-start | bytes 245768 | tf_op jit(solution)/shard_map/ppermute | solution.py:576
  49.6 13.4 %collective-permute-start.15 = (f32[2,8,8,128]{3,2,1,0:T(8,128)S(1)}, f32[2,8,8,128]{3,2,1,0:T(8,128)S(1)}, u32[]{:S(2)}, u32[]{:S(2)}) collective-permute-start(f32[2,8,8,128]{3,2,1,0:T(8,128)S(1)} %get-tuple-element.86), channel_id=1, source_target_pairs={{0,28},{1,29},{2,30},{3,31},{4,8},{5,9},{6,10},{7,11},{8,4},{9,5},... | collective-permute-start | bytes 196616 | tf_op jit(solution)/shard_map/ppermute | solution.py:576
  50.2 12.9 %collective-permute-start.14 = (f32[2,8,8,128]{3,2,1,0:T(8,128)S(1)}, f32[2,8,8,128]{3,2,1,0:T(8,128)S(1)}, u32[]{:S(2)}, u32[]{:S(2)}) collective-permute-start(f32[2,8,8,128]{3,2,1,0:T(8,128)S(1)} %get-tuple-element.87), channel_id=1, source_target_pairs={{0,4},{1,5},{2,6},{3,7},{4,0},{5,1},{6,2},{7,3},{8,12},{9,13},{10,... | collective-permute-start | bytes 196616 | tf_op jit(solution)/shard_map/ppermute | solution.py:575
  64.0 16.0 %copy-start.3 = (f32[1,1,8,8,8,128]{5,4,3,2,1,0:T(8,128)S(1)}, f32[1,1,8,8,8,128]{5,4,3,2,1,0:T(8,128)}, u32[]{:S(2)}) copy-start(f32[1,1,8,8,8,128]{5,4,3,2,1,0:T(8,128)} %param.11) | copy-start | bytes 786436
  64.0 4.0 %collective-permute-start.16 = (f32[8,8,128]{2,1,0:T(8,128)S(1)}, f32[8,8,128]{2,1,0:T(8,128)S(1)}, u32[]{:S(2)}, u32[]{:S(2)}) collective-permute-start(f32[8,8,128]{2,1,0:T(8,128)S(1)} %get-tuple-element.59), channel_id=1, source_target_pairs={{0,1},{1,0},{2,3},{3,2},{4,5},{5,4},{6,7},{7,6},{8,9},{9,8},{10,11... | collective-permute-start | bytes 98312 | tf_op jit(solution)/shard_map/ppermute | solution.py:575
  64.6 3.4 %collective-permute-start.17 = (f32[8,8,128]{2,1,0:T(8,128)S(1)}, f32[8,8,128]{2,1,0:T(8,128)S(1)}, u32[]{:S(2)}, u32[]{:S(2)}) collective-permute-start(f32[8,8,128]{2,1,0:T(8,128)S(1)} %get-tuple-element.60), channel_id=1, source_target_pairs={{0,4},{1,2},{2,1},{3,7},{4,0},{5,6},{6,5},{7,3},{8,12},{9,10},{10,... | collective-permute-start | bytes 98312 | tf_op jit(solution)/shard_map/ppermute | solution.py:576
  68.1 11.9 %collective-permute-start.19 = (f32[8,8,128]{2,1,0:T(8,128)S(1)}, f32[8,8,128]{2,1,0:T(8,128)S(1)}, u32[]{:S(2)}, u32[]{:S(2)}) collective-permute-start(f32[8,8,128]{2,1,0:T(8,128)S(1)} %get-tuple-element.108), channel_id=1, source_target_pairs={{0,28},{1,29},{2,30},{3,31},{4,8},{5,9},{6,10},{7,11},{8,4},{9,5},... | collective-permute-start | bytes 98312 | tf_op jit(solution)/shard_map/ppermute | solution.py:576
  68.2 11.8 %collective-permute-start.18 = (f32[8,8,128]{2,1,0:T(8,128)S(1)}, f32[8,8,128]{2,1,0:T(8,128)S(1)}, u32[]{:S(2)}, u32[]{:S(2)}) collective-permute-start(f32[8,8,128]{2,1,0:T(8,128)S(1)} %get-tuple-element.109), channel_id=1, source_target_pairs={{0,4},{1,5},{2,6},{3,7},{4,0},{5,1},{6,2},{7,3},{8,12},{9,13},{10,... | collective-permute-start | bytes 98312 | tf_op jit(solution)/shard_map/ppermute | solution.py:575

commit v3 on v2

--- a/solution.py
+++ b/solution.py
@@ -155,10 +155,6 @@
     return basis, 2.0 - 2.0 * np.cos(math.pi * position / count)
 
 
-def side_even(axis):
-    return lax.rem(lax.axis_index(axis), 2) == 0
-
-
 def shift_up(rows):
     lane = lax.broadcasted_iota(jnp.int32, rows.shape, 1)
     return jnp.where(lane == 0, 0.0, pltpu.roll(rows, 1, 1))
@@ -171,10 +167,10 @@
 
 class Sides:
     def __init__(self, axis, count):
-        index = lax.axis_index(axis)
-        self.even = lax.rem(index, 2) == 0
-        self.no_low = index == 0
-        self.no_high = index == count - 1
+        self.index = lax.axis_index(axis)
+        self.even = lax.rem(self.index, 2) == 0
+        self.no_low = self.index == 0
+        self.no_high = self.index == count - 1
 
     def low(self, first, second):
         return jnp.where(self.no_low, 0.0, jnp.where(self.even, second, first))
@@ -231,11 +227,7 @@
     lane = lax.broadcasted_iota(jnp.int32, (16, 128), 1)
     sums = jnp.sum(jnp.where(row == lane, lane_sums(tiles), 0.0), axis=0, keepdims=True)
     for index in range(stats_ref.shape[0]):
-        stats_ref[index] = sums
-
-
-def gathered(stats_ref):
-    return stats_ref[:, 0, :]
+        stats_ref[index] = jnp.broadcast_to(sums, stats_ref.shape[1:])
 
 
 def stat_columns(stats, first, count):
@@ -244,15 +236,66 @@
     return [sums[i : i + 1] for i in range(count)]
 
 
-def lifted_rows(stats, lift_ref):
-    return lane_sums([lift_ref[i] * stats for i in range(9)])
+def sum_lanes(counts):
+    return -(-(counts[0] * counts[1] + 2) // 128) * 128
+
+
+def share_rows(counts, side_x, side_y):
+    lane = lax.broadcasted_iota(jnp.int32, (1, sum_lanes(counts)), 1)
+    column_y = lax.rem(lane, counts[1])
+    first_x = lane - column_y
+
+    def weights(side, place, step, count):
+        own = jnp.where(place == side.index * step, 1.0, 0.0)
+        below = jnp.where(place == (side.index - 1) * step, 1.0, 0.0)
+        above = jnp.where(place == (side.index + 1) * step, 1.0, 0.0)
+        return (
+            jnp.where(side.no_low, own, 0.5 * (own + below)),
+            own,
+            jnp.where(side.no_high, own, 0.5 * (own + above)),
+        )
+
+    inside = lane < counts[0] * counts[1]
+    along_x = weights(side_x, first_x, counts[1], counts[0])
+    along_y = weights(side_y, column_y, 1, counts[1])
+    return [jnp.where(inside, wx * wy, 0.0) for wx in along_x for wy in along_y]
+
+
+def summed_row(counts, tiles, side_x, side_y):
+    sums = lane_sums(tiles)
+    lane = lax.broadcasted_iota(jnp.int32, (1, sum_lanes(counts)), 1)
+    total = None
+    for i, share in enumerate(share_rows(counts, side_x, side_y)):
+        term = share * sums[i : i + 1, 0:1]
+        total = term if total is None else total + term
+    for i in range(9, len(tiles)):
+        total = total + jnp.where(lane == counts[0] * counts[1] + i - 9, sums[i : i + 1, 0:1], 0.0)
+    pieces = [total[:, at : at + 128] for at in range(0, sum_lanes(counts), 128)]
+    pieces.append(jnp.zeros((NODES - len(pieces), 128), jnp.float32))
+    return jnp.concatenate(pieces, axis=0)
+
+
+def row_of(counts, tile_ref):
+    rows = [tile_ref[i : i + 1, :] for i in range(sum_lanes(counts) // 128)]
+    return rows[0] if len(rows) == 1 else jnp.concatenate(rows, axis=1)
+
+
+def lifted_rows(counts, row, lift_ref):
+    sums = jnp.sum(lift_ref[...] * row, axis=1, keepdims=True)
+    return jnp.broadcast_to(sums, (16, 128))
+
+
+def row_value(counts, row, index):
+    lane = lax.broadcasted_iota(jnp.int32, row.shape, 1)
+    chosen = jnp.where(lane == counts[0] * counts[1] + index, row, 0.0)
+    return jnp.broadcast_to(jnp.sum(chosen, axis=1, keepdims=True), (1, 128))
 
 
 def class_tiles(sums):
     return [sums[(i, j)] for i in range(3) for j in range(3)]
 
 
-def start_kernel(counts, r_ref, sy_first, sy_second, stats_ref):
+def start_kernel(counts, r_ref, sy_first, sy_second):
     side_x, side_y = Sides("gx", counts[0]), Sides("gy", counts[1])
     tile = multiplicity_tile()
     for a in range(NODES):
@@ -266,7 +309,7 @@
     for (i, j), value in sums.items():
         a, b = (0, 1, NODES - 1)[i], (0, 1, NODES - 1)[j]
         sums[(i, j)] = scaled(value * tile, axis_factor(a, side_x), axis_factor(b, side_y))
-    write_stats(stats_ref, class_tiles(sums))
+    sy_first[NODES] = summed_row(counts, class_tiles(sums), side_x, side_y)
 
 
 def planes(ref):
@@ -432,11 +475,11 @@
 
 
 def first_apply_kernel(
-    counts, part_ref, ry_first, ry_second, rx_first, rx_second, gathered_ref, lift_ref, grains_ref,
-    r_ref, tiles_ref, z_ref, u_ref, sy_first, sy_second, fx_first, fx_second, stats_ref, y_ref,
+    counts, part_ref, ry_first, ry_second, rx_first, rx_second, sum_ref, lift_ref, grains_ref,
+    r_ref, tiles_ref, z_ref, u_ref, sy_first, sy_second, fx_first, fx_second, y_ref,
 ):
     side_x, side_y = Sides("gx", counts[0]), Sides("gy", counts[1])
-    field = lifted_rows(gathered(gathered_ref), lift_ref)
+    field = lifted_rows(counts, row_of(counts, sum_ref), lift_ref)
     z = collect_parts(part_ref, ry_first, ry_second, rx_first, rx_second, side_x, side_y, field)
     inner = None
     for (a, b), value in z.items():
@@ -453,13 +496,14 @@
             add_to(sums, (class_of(a), class_of(b)), value)
             term = value * z_ref[a, b]
             curvature = term if curvature is None else curvature + term
-    write_stats(stats_ref, class_tiles(sums) + [inner, curvature])
+    tiles = class_tiles(sums) + [inner, curvature]
+    sy_first[2 * NODES] = summed_row(counts, tiles, side_x, side_y)
     sum_column(u_ref)
     for a in range(NODES):
         for layer in range(2):
             low, high = u_ref[a, layer], u_ref[a, NODES - 2 + layer]
-            sy_first[a, layer] = side_y.send_first(low, high)
-            sy_second[a, layer] = side_y.send_second(low, high)
+            sy_first[2 * a + layer] = side_y.send_first(low, high)
+            sy_second[2 * a + layer] = side_y.send_second(low, high)
     for layer in range(2):
         low, high = u_ref[layer], u_ref[NODES - 2 + layer]
         fx_first[layer] = side_x.send_first(low, high)
@@ -467,14 +511,13 @@
 
 
 def second_apply_kernel(
-    counts, part_ref, ry_first, ry_second, rx_first, rx_second, gathered_ref, lift_ref, grains_ref,
+    counts, part_ref, ry_first, ry_second, rx_first, rx_second, sum_ref, lift_ref, grains_ref,
     r_ref, q_ref, z_ref, tiles_ref, z1_ref, u_ref, sy_first, sy_second, fx_first, fx_second, stats_ref, y_ref,
 ):
     side_x, side_y = Sides("gx", counts[0]), Sides("gy", counts[1])
-    stats = gathered(gathered_ref)
-    field = lifted_rows(stats, lift_ref)
-    first_inner, first_curvature = stat_columns(stats, 9, 2)
-    step = first_inner / first_curvature
+    summed = row_of(counts, sum_ref)
+    field = lifted_rows(counts, summed, lift_ref)
+    step = row_value(counts, summed, 0) / row_value(counts, summed, 1)
     w = collect_parts(part_ref, ry_first, ry_second, rx_first, rx_second, side_x, side_y, field)
     inner = None
     for (a, b), value in w.items():
@@ -507,11 +550,12 @@
 
 def final_kernel(
     counts, sol_ref, r_ref, q_ref, z_ref, z1_ref, u_ref, ry_first, ry_second, rx_first, rx_second,
-    second_ref, last_ref, sol_out, r_out, d_out, steps_out,
+    sum_ref, last_ref, sol_out, r_out, d_out, steps_out,
 ):
     side_x, side_y = Sides("gx", counts[0]), Sides("gy", counts[1])
-    first_inner, first_curvature = stat_columns(gathered(second_ref), 9, 2)
-    second_inner, own, cross = stat_columns(gathered(last_ref), 0, 3)
+    summed = row_of(counts, sum_ref)
+    first_inner, first_curvature = row_value(counts, summed, 0), row_value(counts, summed, 1)
+    second_inner, own, cross = stat_columns(last_ref[:, 0, :], 0, 3)
     first_step = first_inner / first_curvature
     ratio = second_inner / first_inner
     second_step = second_inner / (own + ratio * (2.0 * cross + ratio * first_curvature))
@@ -577,6 +621,37 @@
     )
 
 
+def trade_far(counts, value, far_x, far_y):
+    pairs = [
+        (x * counts[1] + y, (x ^ far_x) * counts[1] + (y ^ far_y))
+        for x in range(counts[0])
+        for y in range(counts[1])
+    ]
+    return lax.ppermute(value, AXES, pairs)
+
+
+class RunningSum:
+    def __init__(self, counts, tile):
+        self.counts = counts
+        self.carried = counts == (8, 4)
+        self.value = tile if self.carried else lax.psum(tile, AXES)
+
+    def add(self, received):
+        if self.carried:
+            self.value = self.value + received
+
+    def far(self, *steps):
+        return [trade_far(self.counts, self.value, *step) for step in steps if self.carried]
+
+
+def carry(tiles, running):
+    return jnp.concatenate([tiles.reshape((-1, NODES, 128)), running.value[None]])
+
+
+def carried(received, shape):
+    return received[:-1].reshape(shape), received[-1]
+
+
 def gather_stats(stats):
     return lax.all_to_all(stats, AXES, 0, 0)
 
@@ -592,8 +667,8 @@
     modes_x = np.einsum("xip,pa->xia", share_x, basis_x)
     modes_y = np.einsum("yjq,qb->yjb", share_y, basis_y)
     total = counts[0] * counts[1]
-    to_modes = np.einsum("xia,yjb->abxyij", modes_x, modes_y).reshape(total, total, 9)
-    to_modes = np.pad(to_modes, ((0, 0), (0, 0), (0, 7))).reshape(total, total * 16)
+    to_modes = np.einsum("pa,qb->abpq", basis_x, basis_y).reshape(total, total)
+    to_modes = np.pad(to_modes, ((0, 0), (0, sum_lanes(counts) - total)))
     return [table.astype(np.float32) for table in (modes_x, modes_y, 1.0 / divisor, to_modes)]
 
 
@@ -602,9 +677,8 @@
     own_x = lax.dynamic_index_in_dim(modes_x, lax.axis_index("gx"), 0, keepdims=False)
     own_y = lax.dynamic_index_in_dim(modes_y, lax.axis_index("gy"), 0, keepdims=False)
     own = own_x[:, None, :, None] * own_y[None, :, None, :] * inverse[None, None]
-    total = to_modes.shape[0]
-    lift = jnp.dot(own.reshape(9, total), to_modes, precision=exact_mode)
-    return jnp.pad(lift.reshape(9, total, 16), ((0, 0), (0, 0), (0, 112)))
+    lift = jnp.dot(own.reshape(9, -1), to_modes, precision=exact_mode)
+    return jnp.pad(lift, ((0, 7), (0, 0)))
 
 
 def shards_of(counts):
@@ -621,7 +695,7 @@
         plane = [jnp.asarray(table) for table in (forward_np, back_np, inverse_np)]
         tiles = jnp.asarray(tiles_np)
         side_x, side_y = Sides("gx", counts[0]), Sides("gy", counts[1])
-        row = (counts[0] * counts[1], 1, 128)
+        row = (counts[0] * counts[1], 4, 128)
         face = (NODES, NODES, 128)
         part_shapes = [
             (EXT, ROWS, 128),
@@ -630,10 +704,14 @@
         ]
         solve_scratch = [(EXT, ROWS, 128), (EXT, MODES, 128)]
 
-        y_first, y_second, stats = call(
-            start_kernel, counts, "start", [face, face, row], [], residual
-        )
+        y_first, y_second = call(
+            start_kernel, counts, "start", [(NODES + 1,) + face[1:], face], [], residual
+        )
+        running = RunningSum(counts, y_first[-1])
         ry = trade(counts, 1, y_first, y_second)
+        ry_first, tile = carried(ry[0], face)
+        running.add(tile)
+        ry = (ry_first, ry[1])
         low_y, high_y = side_y.low(*ry), side_y.high(*ry)
 
         def with_layers(index):
@@ -641,10 +719,18 @@
 
         low_face, high_face = with_layers(1), with_layers(NODES - 2)
         rx = trade(
-            counts, 0, side_x.send_first(low_face, high_face),
+            counts, 0, carry(side_x.send_first(low_face, high_face), running),
             side_x.send_second(low_face, high_face),
         )
-        first_stats = gather_stats(stats)
+        rx, far = lax.optimization_barrier((rx, running.far((4, 0), (5, 0))))
+        rx_first, tile = carried(rx[0], low_face.shape)
+        for value in [tile] + far:
+            running.add(value)
+        rx = (rx_first, rx[1])
+        part, y_first, y_second, *fx = call(
+            first_solve_kernel, counts, "first_solve", part_shapes, solve_scratch,
+            residual, *ry, *rx, *plane,
+        )
 
         def spread_faces(fx, ry):
             low_y, high_y = side_y.low(*ry), side_y.high(*ry)
@@ -658,20 +744,30 @@
                 fx[1][:, 1:-1] + side_x.send_second(*both),
             )
 
-        part, y_first, y_second, *fx = call(
-            first_solve_kernel, counts, "first_solve", part_shapes, solve_scratch,
-            residual, *ry, *rx, *plane,
-        )
+        def trade_spread(y_first, y_second, fx, running):
+            ry = trade(counts, 1, y_first, y_second)
+            for value in running.far((0, 2)):
+                running.add(value)
+            first, second = spread_faces(fx, ry)
+            rx = trade(counts, 0, first, carry(second, running))
+            rx_second, tile = carried(rx[1], second.shape)
+            running.add(tile)
+            return ry, (rx[0], rx_second)
+
+        ry, rx = trade_spread(y_first, y_second, fx, running)
+        z, u, y_first, y_second, *fx = call(
+            first_apply_kernel, counts, "first_apply",
+            [block, block, (2 * NODES + 1, NODES, 128), (2 * NODES, NODES, 128),
+             (2, NODES, NODES, 128), (2, NODES, NODES, 128)],
+            [block],
+            part, *ry, *rx, running.value, lift, grains, residual, tiles,
+        )
+        running = RunningSum(counts, y_first[-1])
         ry = trade(counts, 1, y_first, y_second)
-        rx = trade(counts, 0, *spread_faces(fx, ry))
-        z, u, y_first, y_second, *fx, stats = call(
-            first_apply_kernel, counts, "first_apply",
-            [block, block, (NODES, 2, NODES, 128), (NODES, 2, NODES, 128),
-             (2, NODES, NODES, 128), (2, NODES, NODES, 128), row],
-            [block],
-            part, *ry, *rx, first_stats, lift, grains, residual, tiles,
-        )
-        ry = trade(counts, 1, y_first, y_second)
+        two = (NODES, 2, NODES, 128)
+        ry_first, tile = carried(ry[0], two)
+        running.add(tile)
+        ry = (ry_first, ry[1].reshape(two))
         low_y, high_y = side_y.low(*ry), side_y.high(*ry)
 
         def image_faces(index):
@@ -680,23 +776,24 @@
 
         pads = ((0, 0), (1, 1), (0, 0), (0, 0))
         both = (image_faces(slice(0, 2)), image_faces(slice(NODES - 2, NODES)))
-        rx = trade(
-            counts, 0,
-            jnp.pad(fx[0], pads) + side_x.send_first(*both),
-            jnp.pad(fx[1], pads) + side_x.send_second(*both),
-        )
-        second_stats = gather_stats(stats)
+        first = jnp.pad(fx[0], pads) + side_x.send_first(*both)
+        second = jnp.pad(fx[1], pads) + side_x.send_second(*both)
+        rx = trade(counts, 0, carry(first, running), second)
+        rx, far = lax.optimization_barrier((rx, running.far((4, 0), (5, 0))))
+        rx_first, tile = carried(rx[0], first.shape)
+        for value in [tile] + far:
+            running.add(value)
+        rx = (rx_first, rx[1])
         q, part, y_first, y_second, *fx = call(
             second_solve_kernel, counts, "second_solve", [block] + part_shapes, solve_scratch,
             u, *ry, *rx, *plane,
         )
-        ry = trade(counts, 1, y_first, y_second)
-        rx = trade(counts, 0, *spread_faces(fx, ry))
+        ry, rx = trade_spread(y_first, y_second, fx, running)
         z1, u, y_first, y_second, *fx, stats = call(
             second_apply_kernel, counts, "second_apply",
             [block, block, face, face, face, face, row],
             [block],
-            part, *ry, *rx, second_stats, lift, grains, residual, q, z, tiles,
+            part, *ry, *rx, running.value, lift, grains, residual, q, z, tiles,
         )
         ry = trade(counts, 1, y_first, y_second)
         low_y, high_y = side_y.low(*ry), side_y.high(*ry)
@@ -712,7 +809,7 @@
         last_stats = gather_stats(stats)
         solution_out, residual_out, direction, steps = call(
             final_kernel, counts, "final", [block] * 3 + [(2,)], [],
-            solution, residual, q, z, z1, u, *ry, *rx, second_stats, last_stats,
+            solution, residual, q, z, z1, u, *ry, *rx, running.value, last_stats,
         )
         return (
             solution_out.reshape(shard_shape),

time: 81.5 us -> 68.4 us (0.84)
  blocking collectives: 23.4 us -> 0 us
  starting transfers between devices: 22.6 us -> 31 us
  waiting for transfers between devices: 19.9 us -> 24.5 us
  local copies, waits for them, and re-layouts: 5.13 us -> 3.48 us
  matrix products: 1.12 us -> 0.13 us
    all_to_all x2 -> x0, blocking collectives: 23.4 us -> none  [gather_stats(): return lax.all_to_all(stats, AXES, 0, 0)]
    ppermute x0 -> x6, starting transfers between devices: none -> 7.63 us  [trade_far(): return lax.ppermute(value, AXES, pairs)]
    ppermute x10, waiting for transfers between devices: 11.6 us -> 6.46 us  [trade(): lax.ppermute(first, AXES, swap_pairs(counts, axis, 0))]
    ppermute x0 -> x6, waiting for transfers between devices: none -> 5.03 us  [trade_far(): return lax.ppermute(value, AXES, pairs)]
    ppermute x10, starting transfers between devices: 3.28 us -> 7.84 us  [trade(): lax.ppermute(second, AXES, swap_pairs(counts, axis, 1))]
    all_to_all x1, starting transfers between devices: 7.3 us -> 3.01 us  [gather_stats(): return lax.all_to_all(stats, AXES, 0, 0)]
    all_to_all x1, waiting for transfers between devices: 0.01 us -> 2.99 us  [gather_stats(): return lax.all_to_all(stats, AXES, 0, 0)]
    ppermute x10, waiting for transfers between devices: 8.33 us -> 10.1 us  [trade(): lax.ppermute(second, AXES, swap_pairs(counts, axis, 1))]
  transfers between devices with their start and end apart: 21 -> 27, of which waited for: 8 -> 12; matrix products, arithmetic and copies ran while one was open for 4% -> 3% of each run, Pallas kernels for 2% -> 3%
where the time goes in v3:
time: 68.4 us; the launch traced here: 68.1 us
  starting transfers between devices  31 us (45%)
  waiting for transfers between devices  24.5 us (36%)
  Pallas kernels  7.47 us (11%)
  local copies, waits for them, and re-layouts  3.48 us (5%)
  between operations  0.98 us (1%)
    ppermute x10, starting transfers between devices, trade(): lax.ppermute(first, AXES, swap_pairs(counts, axis, 0))  12.5 us
    ppermute x10, waiting for transfers between devices, trade(): lax.ppermute(second, AXES, swap_pairs(counts, axis, 1))  10.1 us
    ppermute x10, starting transfers between devices, trade(): lax.ppermute(second, AXES, swap_pairs(counts, axis, 1))  7.84 us
    ppermute x6, starting transfers between devices, trade_far(): return lax.ppermute(value, AXES, pairs)  7.63 us
    pallas_call x6, Pallas kernels, call(): pl.pallas_call(body, name=name, out_shape=[jax.ShapeDtypeStruct(shape, jn...  7.47 us
    ppermute x10, waiting for transfers between devices, trade(): lax.ppermute(first, AXES, swap_pairs(counts, axis, 0))  6.46 us
    ppermute x6, waiting for transfers between devices, trade_far(): return lax.ppermute(value, AXES, pairs)  5.03 us
    all_to_all x1, starting transfers between devices, gather_stats(): return lax.all_to_all(stats, AXES, 0, 0)  3.01 us
  transfers between devices with their start and end apart: 27, of which 12 were waited for; matrix products, arithmetic and copies ran while one was open for 3% of the time, Pallas kernels for 3%

profile of v3, /device:TPU:0, one launch (start us, length us, event | category | flops | bytes accessed | tf_op | source)
XLA Modules:
  0.0 68.1 jit_solution(4965013983665180171)
XLA Ops:
  0.6 0.9 %copy-done = f32[1,1,8,8,8,128]{5,4,3,2,1,0:T(8,128)S(1)} copy-done((f32[1,1,8,8,8,128]{5,4,3,2,1,0:T(8,128)S(1)}, f32[1,1,8,8,8,128]{5,4,3,2,1,0:T(8,128)}, u32[]{:S(2)}) %copy-start) | copy-done | bytes 262168
  1.6 0.1 start.1
  1.7 0.5 collective-permute-start.1
  2.2 4.1 %collective-permute-start = (f32[9,8,128]{2,1,0:T(8,128)S(1)}, f32[9,8,128]{2,1,0:T(8,128)S(1)}, u32[]{:S(2)}, u32[]{:S(2)}) collective-permute-start(f32[9,8,128]{2,1,0:T(8,128)S(1)} %get-tuple-element.42), channel_id=1, source_target_pairs={{0,1},{1,0},{2,3},{3,2},{4,5},{5,4},{6,7},{7,6},{8,9},{9,8},{10,11... | collective-permute-start | bytes 110600 | tf_op jit(solution)/shard_map/ppermute | solution.py:619
  6.3 0.7 %dynamic-slice_bitcast_fusion.1 = f32[3,8]{1,0:T(4,128)S(1)} fusion(f32[8,3,8]{2,1,0:T(4,128)} %constant.51.clone, s32[]{:T(128)S(6)} %select_n.192), kind=kLoop, calls=%fused_computation.61 | loop fusion | bytes 196 | tf_op jit(solution)/shard_map/mul | solution.py:679
  7.0 1.2 %collective-permute-done = f32[9,8,128]{2,1,0:T(8,128)S(1)} collective-permute-done((f32[9,8,128]{2,1,0:T(8,128)S(1)}, f32[9,8,128]{2,1,0:T(8,128)S(1)}, u32[]{:S(2)}, u32[]{:S(2)}) %collective-permute-start) | collective-permute-done | bytes 36896 | tf_op jit(solution)/shard_map/ppermute | solution.py:619
  8.3 1.6 %collective-permute-start.4 = (f32[8,128]{1,0:T(8,128)S(1)}, f32[8,128]{1,0:T(8,128)S(1)}, u32[]{:S(2)}, u32[]{:S(2)}) collective-permute-start(f32[8,128]{1,0:T(8,128)S(1)} %bitcast.70), channel_id=1, source_target_pairs={{0,16},{1,17},{2,18},{3,19},{4,20},{5,21},{6,22},{7,23},{8,24},{9,... | collective-permute-start | bytes 12296 | tf_op jit(solution)/shard_map/ppermute | solution.py:630
  9.9 2.4 %collective-permute-start.3 = (f32[10,8,128]{2,1,0:T(8,128)S(1)}, f32[10,8,128]{2,1,0:T(8,128)S(1)}, u32[]{:S(2)}, u32[]{:S(2)}) collective-permute-start(f32[10,8,128]{2,1,0:T(8,128)S(1)} %get-tuple-element.96), channel_id=1, source_target_pairs={{0,28},{1,29},{2,30},{3,31},{4,8},{5,9},{6,10},{7,11},{8,4},{9,5},... | collective-permute-start | bytes 122888 | tf_op jit(solution)/shard_map/ppermute | solution.py:620
  12.3 0.7 %dynamic-slice_bitcast_fusion = f32[3,4]{1,0:T(4,128)S(1)} fusion(f32[4,3,4]{2,1,0:T(4,128)} %constant.52.clone, s32[]{:T(128)S(6)} %select_n.193), kind=kLoop, calls=%fused_computation.60 | loop fusion | bytes 100 | tf_op jit(solution)/shard_map/mul | solution.py:679
  13.0 1.3 %collective-permute-done.3.refs_4_ = f32[10,8,128]{2,1,0:T(8,128)S(1)} collective-permute-done((f32[10,8,128]{2,1,0:T(8,128)S(1)}, f32[10,8,128]{2,1,0:T(8,128)S(1)}, u32[]{:S(2)}, u32[]{:S(2)}) %collective-permute-start.3) | collective-permute-done | bytes 40992 | tf_op jit(solution)/shard_map/ppermute | solution.py:620
  14.3 2.0 %collective-permute-start.9 = (f32[8,128]{1,0:T(8,128)S(1)}, f32[8,128]{1,0:T(8,128)S(1)}, u32[]{:S(2)}, u32[]{:S(2)}) collective-permute-start(f32[8,128]{1,0:T(8,128)S(1)} %fusion.25), channel_id=1, source_target_pairs={{0,2},{1,3},{2,0},{3,1},{4,6},{5,7},{6,4},{7,5},{8,10},{9,11},{10,... | collective-permute-start | bytes 12296 | tf_op jit(solution)/shard_map/ppermute | solution.py:630
  16.3 1.9 %first_solve.1 = (f32[10,112,128]{2,1,0:T(8,128)S(1)}, f32[10,2,8,128]{3,2,1,0:T(8,128)S(1)}, f32[10,2,8,128]{3,2,1,0:T(8,128)S(1)}, f32[2,10,8,128]{3,2,1,0:T(8,128)S(1)}, f32[2,10,8,128]{3,2,1,0:T(8,128)S(1)}) custom-call(f32[8,8,8,128]{3,2,1,0:T(8,128)S(1)} %bitcast.52, f32[8,8,128]{2,1,0:T(8,128)S(1)} %get-tuple-element.112.refs_1_, ...), custom_call_target="tpu_custom_call" | custom-call | tf_op jit(solution)/shard_map/first_solve/pallas_call | solution.py:592
  18.2 1.3 %collective-permute-start.6 = (f32[10,2,8,128]{3,2,1,0:T(8,128)S(1)}, f32[10,2,8,128]{3,2,1,0:T(8,128)S(1)}, u32[]{:S(2)}, u32[]{:S(2)}) collective-permute-start(f32[10,2,8,128]{3,2,1,0:T(8,128)S(1)} %get-tuple-element.47), channel_id=1, source_target_pairs={{0,1},{1,0},{2,3},{3,2},{4,5},{5,4},{6,7},{7,6},{8,9},{9,8},{10,11... | collective-permute-start | bytes 245768 | tf_op jit(solution)/shard_map/ppermute | solution.py:619
  19.6 0.1 mul.37
  19.8 3.0 %collective-permute-done.6.refs_1_ = f32[10,2,8,128]{3,2,1,0:T(8,128)S(1)} collective-permute-done((f32[10,2,8,128]{3,2,1,0:T(8,128)S(1)}, f32[10,2,8,128]{3,2,1,0:T(8,128)S(1)}, u32[]{:S(2)}, u32[]{:S(2)}) %collective-permute-start.6) | collective-permute-done | bytes 81952 | tf_op jit(solution)/shard_map/ppermute | solution.py:619
  22.8 0.1 fusion.7
  22.9 1.0 %collective-permute-start.10 = (f32[17,8,128]{2,1,0:T(8,128)S(1)}, f32[17,8,128]{2,1,0:T(8,128)S(1)}, u32[]{:S(2)}, u32[]{:S(2)}) collective-permute-start(f32[17,8,128]{2,1,0:T(8,128)S(1)} %pad_maximum_fusion.3), channel_id=1, source_target_pairs={{0,28},{1,29},{2,30},{3,31},{4,8},{5,9},{6,10},{7,11},{8,4},{9,5},... | collective-permute-start | bytes 208904 | tf_op jit(solution)/shard_map/ppermute | solution.py:620
  23.9 0.1 fusion.18
  24.0 0.7 collective-permute-start.8
  24.7 2.9 %collective-permute-done.10 = f32[17,8,128]{2,1,0:T(8,128)S(1)} collective-permute-done((f32[17,8,128]{2,1,0:T(8,128)S(1)}, f32[17,8,128]{2,1,0:T(8,128)S(1)}, u32[]{:S(2)}, u32[]{:S(2)}) %collective-permute-start.10) | collective-permute-done | bytes 69664 | tf_op jit(solution)/shard_map/ppermute | solution.py:620
  27.7 0.7 %copy-done.6 = f32[9,8,128]{2,1,0:T(8,128)S(1)} copy-done((f32[9,8,128]{2,1,0:T(8,128)S(1)}, f32[9,8,128]{2,1,0:T(8,128)}, u32[]{:S(2)}) %copy-start.6) | copy-done | bytes 36888
  28.4 0.9 %first_apply.1 = (f32[8,8,8,128]{3,2,1,0:T(8,128)S(1)}, f32[8,8,8,128]{3,2,1,0:T(8,128)S(1)}, f32[17,8,128]{2,1,0:T(8,128)S(1)}, f32[16,8,128]{2,1,0:T(8,128)S(1...) custom-call(f32[10,112,128]{2,1,0:T(8,128)S(1)} %get-tuple-element.46.refs_0_, ...), custom_call_target="tpu_custom_call" | custom-call | tf_op jit(solution)/shard_map/first_apply/pallas_call | solution.py:592
  29.3 2.0 %collective-permute-start.11 = (f32[17,8,128]{2,1,0:T(8,128)S(1)}, f32[17,8,128]{2,1,0:T(8,128)S(1)}, u32[]{:S(2)}, u32[]{:S(2)}) collective-permute-start(f32[17,8,128]{2,1,0:T(8,128)S(1)} %get-tuple-element.54), channel_id=1, source_target_pairs={{0,1},{1,0},{2,3},{3,2},{4,5},{5,4},{6,7},{7,6},{8,9},{9,8},{10,11... | collective-permute-start | bytes 208904 | tf_op jit(solution)/shard_map/ppermute | solution.py:619
  31.3 0.1 pad.34.clone
  31.4 2.2 %collective-permute-done.11 = f32[17,8,128]{2,1,0:T(8,128)S(1)} collective-permute-done((f32[17,8,128]{2,1,0:T(8,128)S(1)}, f32[17,8,128]{2,1,0:T(8,128)S(1)}, u32[]{:S(2)}, u32[]{:S(2)}) %collective-permute-start.11) | collective-permute-done | bytes 69664 | tf_op jit(solution)/shard_map/ppermute | solution.py:619
  33.7 0.1 fusion.3
  33.9 0.5 collective-permute-start.14
  34.4 0.9 %collective-permute-start.16 = (f32[8,128]{1,0:T(8,128)S(1)}, f32[8,128]{1,0:T(8,128)S(1)}, u32[]{:S(2)}, u32[]{:S(2)}) collective-permute-start(f32[8,128]{1,0:T(8,128)S(1)} %bitcast.71), channel_id=1, source_target_pairs={{0,20},{1,21},{2,22},{3,23},{4,16},{5,17},{6,18},{7,19},{8,28},{9,... | collective-permute-start | bytes 12296 | tf_op jit(solution)/shard_map/ppermute | solution.py:630
  35.2 1.7 %collective-permute-start.15 = (f32[8,128]{1,0:T(8,128)S(1)}, f32[8,128]{1,0:T(8,128)S(1)}, u32[]{:S(2)}, u32[]{:S(2)}) collective-permute-start(f32[8,128]{1,0:T(8,128)S(1)} %bitcast.72), channel_id=1, source_target_pairs={{0,16},{1,17},{2,18},{3,19},{4,20},{5,21},{6,22},{7,23},{8,24},{9,... | collective-permute-start | bytes 12296 | tf_op jit(solution)/shard_map/ppermute | solution.py:630
  36.9 0.5 collective-permute-done.16
  37.4 1.5 %collective-permute-done.15 = f32[8,128]{1,0:T(8,128)S(1)} collective-permute-done((f32[8,128]{1,0:T(8,128)S(1)}, f32[8,128]{1,0:T(8,128)S(1)}, u32[]{:S(2)}, u32[]{:S(2)}) %collective-permute-start.15) | collective-permute-done | bytes 4128 | tf_op jit(solution)/shard_map/ppermute | solution.py:630
  38.9 0.4 collective-permute-done.14.refs_4_
  39.3 1.9 %second_solve.1 = (f32[8,8,8,128]{3,2,1,0:T(8,128)S(1)}, f32[10,112,128]{2,1,0:T(8,128)S(1)}, f32[10,2,8,128]{3,2,1,0:T(8,128)S(1)}, f32[10,2,8,128]{3,2,1,0:T(8...) custom-call(f32[8,8,8,128]{3,2,1,0:T(8,128)S(1)} %get-tuple-element.53.refs_0_, ...), custom_call_target="tpu_custom_call" | custom-call | tf_op jit(solution)/shard_map/second_solve/pallas_call | solution.py:592
  41.2 2.1 %collective-permute-start.17 = (f32[10,2,8,128]{3,2,1,0:T(8,128)S(1)}, f32[10,2,8,128]{3,2,1,0:T(8,128)S(1)}, u32[]{:S(2)}, u32[]{:S(2)}) collective-permute-start(f32[10,2,8,128]{3,2,1,0:T(8,128)S(1)} %get-tuple-element.63), channel_id=1, source_target_pairs={{0,1},{1,0},{2,3},{3,2},{4,5},{5,4},{6,7},{7,6},{8,9},{9,8},{10,11... | collective-permute-start | bytes 245768 | tf_op jit(solution)/shard_map/ppermute | solution.py:619
  43.3 1.5 %collective-permute-start.20 = (f32[8,128]{1,0:T(8,128)S(1)}, f32[8,128]{1,0:T(8,128)S(1)}, u32[]{:S(2)}, u32[]{:S(2)}) collective-permute-start(f32[8,128]{1,0:T(8,128)S(1)} %fusion.23), channel_id=1, source_target_pairs={{0,2},{1,3},{2,0},{3,1},{4,6},{5,7},{6,4},{7,5},{8,10},{9,11},{10,... | collective-permute-start | bytes 12296 | tf_op jit(solution)/shard_map/ppermute | solution.py:630
  44.9 3.0 %collective-permute-done.20 = f32[8,128]{1,0:T(8,128)S(1)} collective-permute-done((f32[8,128]{1,0:T(8,128)S(1)}, f32[8,128]{1,0:T(8,128)S(1)}, u32[]{:S(2)}, u32[]{:S(2)}) %collective-permute-start.20) | collective-permute-done | bytes 4128 | tf_op jit(solution)/shard_map/ppermute | solution.py:630
  48.0 0.1 fusion.11
  48.1 1.1 %collective-permute-start.21 = (f32[17,8,128]{2,1,0:T(8,128)S(1)}, f32[17,8,128]{2,1,0:T(8,128)S(1)}, u32[]{:S(2)}, u32[]{:S(2)}) collective-permute-start(f32[17,8,128]{2,1,0:T(8,128)S(1)} %pad_maximum_fusion.4), channel_id=1, source_target_pairs={{0,28},{1,29},{2,30},{3,31},{4,8},{5,9},{6,10},{7,11},{8,4},{9,5},... | collective-permute-start | bytes 208904 | tf_op jit(solution)/shard_map/ppermute | solution.py:620
  49.1 0.6 collective-permute-start.19
  49.7 3.5 %collective-permute-done.21 = f32[17,8,128]{2,1,0:T(8,128)S(1)} collective-permute-done((f32[17,8,128]{2,1,0:T(8,128)S(1)}, f32[17,8,128]{2,1,0:T(8,128)S(1)}, u32[]{:S(2)}, u32[]{:S(2)}) %collective-permute-start.21) | collective-permute-done | bytes 69664 | tf_op jit(solution)/shard_map/ppermute | solution.py:620
  53.3 1.5 %second_apply.1 = (f32[8,8,8,128]{3,2,1,0:T(8,128)S(1)}, f32[8,8,8,128]{3,2,1,0:T(8,128)S(1)}, f32[8,8,128]{2,1,0:T(8,128)S(1)}, f32[8,8,128]{2,1,0:T(8,128)S(1)...) custom-call(f32[10,112,128]{2,1,0:T(8,128)S(1)} %get-tuple-element.62.refs_0_, ...), custom_call_target="tpu_custom_call" | custom-call | tf_op jit(solution)/shard_map/second_apply/pallas_call | solution.py:592
  54.9 1.6 %collective-permute-start.22 = (f32[8,8,128]{2,1,0:T(8,128)S(1)}, f32[8,8,128]{2,1,0:T(8,128)S(1)}, u32[]{:S(2)}, u32[]{:S(2)}) collective-permute-start(f32[8,8,128]{2,1,0:T(8,128)S(1)} %get-tuple-element.71), channel_id=1, source_target_pairs={{0,1},{1,0},{2,3},{3,2},{4,5},{5,4},{6,7},{7,6},{8,9},{9,8},{10,11... | collective-permute-start | bytes 98312 | tf_op jit(solution)/shard_map/ppermute | solution.py:619
  56.5 3.0 %all-to-all-start = ((f32[32,4,128]{2,1,0:T(4,128)}), f32[32,4,128]{2,1,0:T(4,128)S(1)}, u32[]{:S(2)}, u32[]{:S(2)}) async-start(f32[32,4,128]{2,1,0:T(4,128)} %get-tuple-element.75), calls=%async_computation | async-start | bytes 131072 | tf_op jit(solution)/shard_map/all_to_all | solution.py:656
  59.6 0.1 fusion.15
  59.7 2.4 %collective-permute-start.25 = (f32[8,8,128]{2,1,0:T(8,128)S(1)}, f32[8,8,128]{2,1,0:T(8,128)S(1)}, u32[]{:S(2)}, u32[]{:S(2)}) collective-permute-start(f32[8,8,128]{2,1,0:T(8,128)S(1)} %get-tuple-element.121), channel_id=1, source_target_pairs={{0,28},{1,29},{2,30},{3,31},{4,8},{5,9},{6,10},{7,11},{8,4},{9,5},... | collective-permute-start | bytes 98312 | tf_op jit(solution)/shard_map/ppermute | solution.py:620
  62.1 1.9 %collective-permute-done.25.refs_9_ = f32[8,8,128]{2,1,0:T(8,128)S(1)} collective-permute-done((f32[8,8,128]{2,1,0:T(8,128)S(1)}, f32[8,8,128]{2,1,0:T(8,128)S(1)}, u32[]{:S(2)}, u32[]{:S(2)}) %collective-permute-start.25) | collective-permute-done | bytes 32800 | tf_op jit(solution)/shard_map/ppermute | solution.py:620
  64.1 3.0 %all-to-all-done.refs_11_ = f32[32,4,128]{2,1,0:T(4,128)S(1)} async-done(((f32[32,4,128]{2,1,0:T(4,128)}), f32[32,4,128]{2,1,0:T(4,128)S(1)}, u32[]{:S(2)}, u32[]{:S(2)}) %all-to-all-start) | async-done | bytes 65568 | tf_op jit(solution)/shard_map/all_to_all | solution.py:656
  67.0 1.1 %final.1 = (f32[8,8,8,128]{3,2,1,0:T(8,128)}, f32[8,8,8,128]{3,2,1,0:T(8,128)}, f32[8,8,8,128]{3,2,1,0:T(8,128)}, f32[2]{0:T(128)}) custom-call(f32[8,8,8,128]{3,2,1,0:T(8,128)S(1)} %bitcast.59, f32[8,8,8,128]{3,2,1,0:T(8,128)S(1)} %bitcast.55, f32[8,8,8,128]{3,2,1,0:T(8,128)S(1)} %get-tuple-element.60.refs_9_.refs_2_, ...), custom_call_target="tpu_custom_call" | custom-call | tf_op jit(solution)/shard_map/final/pallas_call | solution.py:592
  (80 shorter events, 0.6 us)
Async XLA Ops:
  0.6 1.0 %copy-start = (f32[1,1,8,8,8,128]{5,4,3,2,1,0:T(8,128)S(1)}, f32[1,1,8,8,8,128]{5,4,3,2,1,0:T(8,128)}, u32[]{:S(2)}) copy-start(f32[1,1,8,8,8,128]{5,4,3,2,1,0:T(8,128)} %param.12) | copy-start | bytes 786436
  1.6 14.7 %copy-start.2 = (f32[10,104,128]{2,1,0:T(8,128)S(1)}, f32[10,104,128]{2,1,0:T(8,128)}, u32[]{:S(2)}) copy-start(f32[10,104,128]{2,1,0:T(8,128)} %constant.57.clone.refs_7_) | copy-start | bytes 1597444
  1.7 8.1 %collective-permute-start.1 = (f32[8,8,128]{2,1,0:T(8,128)S(1)}, f32[8,8,128]{2,1,0:T(8,128)S(1)}, u32[]{:S(2)}, u32[]{:S(2)}) collective-permute-start(f32[8,8,128]{2,1,0:T(8,128)S(1)} %get-tuple-element.43), channel_id=1, source_target_pairs={{0,4},{1,2},{2,1},{3,7},{4,0},{5,6},{6,5},{7,3},{8,12},{9,10},{10,... | collective-permute-start | bytes 98312 | tf_op jit(solution)/shard_map/ppermute | solution.py:620
  2.2 6.1 %collective-permute-start = (f32[9,8,128]{2,1,0:T(8,128)S(1)}, f32[9,8,128]{2,1,0:T(8,128)S(1)}, u32[]{:S(2)}, u32[]{:S(2)}) collective-permute-start(f32[9,8,128]{2,1,0:T(8,128)S(1)} %get-tuple-element.42), channel_id=1, source_target_pairs={{0,1},{1,0},{2,3},{3,2},{4,5},{5,4},{6,7},{7,6},{8,9},{9,8},{10,11... | collective-permute-start | bytes 110600 | tf_op jit(solution)/shard_map/ppermute | solution.py:619
  8.3 8.1 %copy-start.1 = (f32[1,1,8,8,8,128]{5,4,3,2,1,0:T(8,128)S(1)}, f32[1,1,8,8,8,128]{5,4,3,2,1,0:T(8,128)}, u32[]{:S(2)}) copy-start(f32[1,1,8,8,8,128]{5,4,3,2,1,0:T(8,128)} %param.12) | copy-start | bytes 786436
  8.3 4.7 %collective-permute-start.5 = (f32[8,128]{1,0:T(8,128)S(1)}, f32[8,128]{1,0:T(8,128)S(1)}, u32[]{:S(2)}, u32[]{:S(2)}) collective-permute-start(f32[8,128]{1,0:T(8,128)S(1)} %bitcast.69), channel_id=1, source_target_pairs={{0,20},{1,21},{2,22},{3,23},{4,16},{5,17},{6,18},{7,19},{8,28},{9,... | collective-permute-start | bytes 12296 | tf_op jit(solution)/shard_map/ppermute | solution.py:630
  8.3 4.7 %collective-permute-start.4 = (f32[8,128]{1,0:T(8,128)S(1)}, f32[8,128]{1,0:T(8,128)S(1)}, u32[]{:S(2)}, u32[]{:S(2)}) collective-permute-start(f32[8,128]{1,0:T(8,128)S(1)} %bitcast.70), channel_id=1, source_target_pairs={{0,16},{1,17},{2,18},{3,19},{4,20},{5,21},{6,22},{7,23},{8,24},{9,... | collective-permute-start | bytes 12296 | tf_op jit(solution)/shard_map/ppermute | solution.py:630
  9.9 6.4 %copy-start.4 = (f32[112,104]{1,0:T(8,128)S(1)}, f32[112,104]{1,0:T(8,128)}, u32[]{:S(2)}) copy-start(f32[112,104]{1,0:T(8,128)} %constant.56.clone.refs_6_) | copy-start | bytes 139780
  9.9 4.4 %collective-permute-start.3 = (f32[10,8,128]{2,1,0:T(8,128)S(1)}, f32[10,8,128]{2,1,0:T(8,128)S(1)}, u32[]{:S(2)}, u32[]{:S(2)}) collective-permute-start(f32[10,8,128]{2,1,0:T(8,128)S(1)} %get-tuple-element.96), channel_id=1, source_target_pairs={{0,28},{1,29},{2,30},{3,31},{4,8},{5,9},{6,10},{7,11},{8,4},{9,5},... | collective-permute-start | bytes 122888 | tf_op jit(solution)/shard_map/ppermute | solution.py:620
  12.3 2.0 %collective-permute-start.2 = (f32[11,8,128]{2,1,0:T(8,128)S(1)}, f32[11,8,128]{2,1,0:T(8,128)S(1)}, u32[]{:S(2)}, u32[]{:S(2)}) collective-permute-start(f32[11,8,128]{2,1,0:T(8,128)S(1)} %pad_maximum_fusion.9), channel_id=1, source_target_pairs={{0,4},{1,5},{2,6},{3,7},{4,0},{5,1},{6,2},{7,3},{8,12},{9,13},{10,... | collective-permute-start | bytes 135176 | tf_op jit(solution)/shard_map/ppermute | solution.py:619
  13.0 3.3 %copy-start.5 = (f32[104,112]{1,0:T(8,128)S(1)}, f32[104,112]{1,0:T(8,128)}, u32[]{:S(2)}) copy-start(f32[104,112]{1,0:T(8,128)} %constant.55.clone.refs_5_) | copy-start | bytes 139780
  14.3 5.4 %collective-permute-start.9 = (f32[8,128]{1,0:T(8,128)S(1)}, f32[8,128]{1,0:T(8,128)S(1)}, u32[]{:S(2)}, u32[]{:S(2)}) collective-permute-start(f32[8,128]{1,0:T(8,128)S(1)} %fusion.25), channel_id=1, source_target_pairs={{0,2},{1,3},{2,0},{3,1},{4,6},{5,7},{6,4},{7,5},{8,10},{9,11},{10,... | collective-permute-start | bytes 12296 | tf_op jit(solution)/shard_map/ppermute | solution.py:630
  18.2 4.5 %collective-permute-start.6 = (f32[10,2,8,128]{3,2,1,0:T(8,128)S(1)}, f32[10,2,8,128]{3,2,1,0:T(8,128)S(1)}, u32[]{:S(2)}, u32[]{:S(2)}) collective-permute-start(f32[10,2,8,128]{3,2,1,0:T(8,128)S(1)} %get-tuple-element.47), channel_id=1, source_target_pairs={{0,1},{1,0},{2,3},{3,2},{4,5},{5,4},{6,7},{7,6},{8,9},{9,8},{10,11... | collective-permute-start | bytes 245768 | tf_op jit(solution)/shard_map/ppermute | solution.py:619
  19.5 3.2 %collective-permute-start.7 = (f32[10,2,8,128]{3,2,1,0:T(8,128)S(1)}, f32[10,2,8,128]{3,2,1,0:T(8,128)S(1)}, u32[]{:S(2)}, u32[]{:S(2)}) collective-permute-start(f32[10,2,8,128]{3,2,1,0:T(8,128)S(1)} %get-tuple-element.48), channel_id=1, source_target_pairs={{0,4},{1,2},{2,1},{3,7},{4,0},{5,6},{6,5},{7,3},{8,12},{9,10},{10,... | collective-permute-start | bytes 245768 | tf_op jit(solution)/shard_map/ppermute | solution.py:620
  22.9 1.0 %copy-start.8 = (f32[32,128]{1,0:T(8,128)S(1)}, f32[32,128]{1,0:T(8,128)}, u32[]{:S(2)}) copy-start(f32[32,128]{1,0:T(8,128)} %constant.54.clone) | copy-start | bytes 49156
  22.9 1.0 %copy-start.9 = (f32[32]{0:T(128)S(1)}, f32[32]{0:T(128)}, u32[]{:S(2)}) copy-start(f32[32]{0:T(128)} %constant.68) | copy-start | bytes 388
  22.9 4.7 %collective-permute-start.10 = (f32[17,8,128]{2,1,0:T(8,128)S(1)}, f32[17,8,128]{2,1,0:T(8,128)S(1)}, u32[]{:S(2)}, u32[]{:S(2)}) collective-permute-start(f32[17,8,128]{2,1,0:T(8,128)S(1)} %pad_maximum_fusion.3), channel_id=1, source_target_pairs={{0,28},{1,29},{2,30},{3,31},{4,8},{5,9},{6,10},{7,11},{8,4},{9,5},... | collective-permute-start | bytes 208904 | tf_op jit(solution)/shard_map/ppermute | solution.py:620
  24.0 3.6 %collective-permute-start.8 = (f32[2,8,8,128]{3,2,1,0:T(8,128)S(1)}, f32[2,8,8,128]{3,2,1,0:T(8,128)S(1)}, u32[]{:S(2)}, u32[]{:S(2)}) collective-permute-start(f32[2,8,8,128]{3,2,1,0:T(8,128)S(1)} %get-tuple-element.105), channel_id=1, source_target_pairs={{0,4},{1,5},{2,6},{3,7},{4,0},{5,1},{6,2},{7,3},{8,12},{9,13},{10,... | collective-permute-start | bytes 196616 | tf_op jit(solution)/shard_map/ppermute | solution.py:619
  27.6 0.8 %copy-start.6 = (f32[9,8,128]{2,1,0:T(8,128)S(1)}, f32[9,8,128]{2,1,0:T(8,128)}, u32[]{:S(2)}) copy-start(f32[9,8,128]{2,1,0:T(8,128)} %constant.58.clone.refs_9_.refs_11_) | copy-start | bytes 110596
  27.7 0.8 %copy-start.7 = (s32[1,1,128]{2,1,0:T(1,128)S(1)}, s32[1,1,128]{2,1,0:T(1,128)}, u32[]{:S(2)}) copy-start(s32[1,1,128]{2,1,0:T(1,128)} %param.13) | copy-start | bytes 1540
  29.3 4.3 %collective-permute-start.11 = (f32[17,8,128]{2,1,0:T(8,128)S(1)}, f32[17,8,128]{2,1,0:T(8,128)S(1)}, u32[]{:S(2)}, u32[]{:S(2)}) collective-permute-start(f32[17,8,128]{2,1,0:T(8,128)S(1)} %get-tuple-element.54), channel_id=1, source_target_pairs={{0,1},{1,0},{2,3},{3,2},{4,5},{5,4},{6,7},{7,6},{8,9},{9,8},{10,11... | collective-permute-start | bytes 208904 | tf_op jit(solution)/shard_map/ppermute | solution.py:619
  31.3 2.3 %collective-permute-start.12 = (f32[16,8,128]{2,1,0:T(8,128)S(1)}, f32[16,8,128]{2,1,0:T(8,128)S(1)}, u32[]{:S(2)}, u32[]{:S(2)}) collective-permute-start(f32[16,8,128]{2,1,0:T(8,128)S(1)} %get-tuple-element.55), channel_id=1, source_target_pairs={{0,4},{1,2},{2,1},{3,7},{4,0},{5,6},{6,5},{7,3},{8,12},{9,10},{10,... | collective-permute-start | bytes 196616 | tf_op jit(solution)/shard_map/ppermute | solution.py:620
  33.8 5.5 %collective-permute-start.13 = (f32[21,8,128]{2,1,0:T(8,128)S(1)}, f32[21,8,128]{2,1,0:T(8,128)S(1)}, u32[]{:S(2)}, u32[]{:S(2)}) collective-permute-start(f32[21,8,128]{2,1,0:T(8,128)S(1)} %pad_maximum_fusion), channel_id=1, source_target_pairs={{0,4},{1,5},{2,6},{3,7},{4,0},{5,1},{6,2},{7,3},{8,12},{9,13},{10,... | collective-permute-start | bytes 258056 | tf_op jit(solution)/shard_map/ppermute | solution.py:619
  33.9 5.4 %collective-permute-start.14 = (f32[2,10,8,128]{3,2,1,0:T(8,128)S(1)}, f32[2,10,8,128]{3,2,1,0:T(8,128)S(1)}, u32[]{:S(2)}, u32[]{:S(2)}) collective-permute-start(f32[2,10,8,128]{3,2,1,0:T(8,128)S(1)} %get-tuple-element.102), channel_id=1, source_target_pairs={{0,28},{1,29},{2,30},{3,31},{4,8},{5,9},{6,10},{7,11},{8,4},{9,5},... | collective-permute-start | bytes 245768 | tf_op jit(solution)/shard_map/ppermute | solution.py:620
  34.4 3.0 %collective-permute-start.16 = (f32[8,128]{1,0:T(8,128)S(1)}, f32[8,128]{1,0:T(8,128)S(1)}, u32[]{:S(2)}, u32[]{:S(2)}) collective-permute-start(f32[8,128]{1,0:T(8,128)S(1)} %bitcast.71), channel_id=1, source_target_pairs={{0,20},{1,21},{2,22},{3,23},{4,16},{5,17},{6,18},{7,19},{8,28},{9,... | collective-permute-start | bytes 12296 | tf_op jit(solution)/shard_map/ppermute | solution.py:630
  35.2 3.6 %collective-permute-start.15 = (f32[8,128]{1,0:T(8,128)S(1)}, f32[8,128]{1,0:T(8,128)S(1)}, u32[]{:S(2)}, u32[]{:S(2)}) collective-permute-start(f32[8,128]{1,0:T(8,128)S(1)} %bitcast.72), channel_id=1, source_target_pairs={{0,16},{1,17},{2,18},{3,19},{4,20},{5,21},{6,22},{7,23},{8,24},{9,... | collective-permute-start | bytes 12296 | tf_op jit(solution)/shard_map/ppermute | solution.py:630
  41.2 6.7 %collective-permute-start.17 = (f32[10,2,8,128]{3,2,1,0:T(8,128)S(1)}, f32[10,2,8,128]{3,2,1,0:T(8,128)S(1)}, u32[]{:S(2)}, u32[]{:S(2)}) collective-permute-start(f32[10,2,8,128]{3,2,1,0:T(8,128)S(1)} %get-tuple-element.63), channel_id=1, source_target_pairs={{0,1},{1,0},{2,3},{3,2},{4,5},{5,4},{6,7},{7,6},{8,9},{9,8},{10,11... | collective-permute-start | bytes 245768 | tf_op jit(solution)/shard_map/ppermute | solution.py:619
  43.3 4.6 %collective-permute-start.18 = (f32[10,2,8,128]{3,2,1,0:T(8,128)S(1)}, f32[10,2,8,128]{3,2,1,0:T(8,128)S(1)}, u32[]{:S(2)}, u32[]{:S(2)}) collective-permute-start(f32[10,2,8,128]{3,2,1,0:T(8,128)S(1)} %get-tuple-element.64), channel_id=1, source_target_pairs={{0,4},{1,2},{2,1},{3,7},{4,0},{5,6},{6,5},{7,3},{8,12},{9,10},{10,... | collective-permute-start | bytes 245768 | tf_op jit(solution)/shard_map/ppermute | solution.py:620
  43.3 4.6 %collective-permute-start.20 = (f32[8,128]{1,0:T(8,128)S(1)}, f32[8,128]{1,0:T(8,128)S(1)}, u32[]{:S(2)}, u32[]{:S(2)}) collective-permute-start(f32[8,128]{1,0:T(8,128)S(1)} %fusion.23), channel_id=1, source_target_pairs={{0,2},{1,3},{2,0},{3,1},{4,6},{5,7},{6,4},{7,5},{8,10},{9,11},{10,... | collective-permute-start | bytes 12296 | tf_op jit(solution)/shard_map/ppermute | solution.py:630
  48.1 5.2 %collective-permute-start.21 = (f32[17,8,128]{2,1,0:T(8,128)S(1)}, f32[17,8,128]{2,1,0:T(8,128)S(1)}, u32[]{:S(2)}, u32[]{:S(2)}) collective-permute-start(f32[17,8,128]{2,1,0:T(8,128)S(1)} %pad_maximum_fusion.4), channel_id=1, source_target_pairs={{0,28},{1,29},{2,30},{3,31},{4,8},{5,9},{6,10},{7,11},{8,4},{9,5},... | collective-permute-start | bytes 208904 | tf_op jit(solution)/shard_map/ppermute | solution.py:620
  49.1 4.1 %collective-permute-start.19 = (f32[2,8,8,128]{3,2,1,0:T(8,128)S(1)}, f32[2,8,8,128]{3,2,1,0:T(8,128)S(1)}, u32[]{:S(2)}, u32[]{:S(2)}) collective-permute-start(f32[2,8,8,128]{3,2,1,0:T(8,128)S(1)} %get-tuple-element.101), channel_id=1, source_target_pairs={{0,4},{1,5},{2,6},{3,7},{4,0},{5,1},{6,2},{7,3},{8,12},{9,13},{10,... | collective-permute-start | bytes 196616 | tf_op jit(solution)/shard_map/ppermute | solution.py:619
  54.8 12.2 %copy-start.3 = (f32[1,1,8,8,8,128]{5,4,3,2,1,0:T(8,128)S(1)}, f32[1,1,8,8,8,128]{5,4,3,2,1,0:T(8,128)}, u32[]{:S(2)}) copy-start(f32[1,1,8,8,8,128]{5,4,3,2,1,0:T(8,128)} %param.11) | copy-start | bytes 786436
  54.9 4.7 %collective-permute-start.22 = (f32[8,8,128]{2,1,0:T(8,128)S(1)}, f32[8,8,128]{2,1,0:T(8,128)S(1)}, u32[]{:S(2)}, u32[]{:S(2)}) collective-permute-start(f32[8,8,128]{2,1,0:T(8,128)S(1)} %get-tuple-element.71), channel_id=1, source_target_pairs={{0,1},{1,0},{2,3},{3,2},{4,5},{5,4},{6,7},{7,6},{8,9},{9,8},{10,11... | collective-permute-start | bytes 98312 | tf_op jit(solution)/shard_map/ppermute | solution.py:619
  56.4 3.1 %collective-permute-start.23 = (f32[8,8,128]{2,1,0:T(8,128)S(1)}, f32[8,8,128]{2,1,0:T(8,128)S(1)}, u32[]{:S(2)}, u32[]{:S(2)}) collective-permute-start(f32[8,8,128]{2,1,0:T(8,128)S(1)} %get-tuple-element.72), channel_id=1, source_target_pairs={{0,4},{1,2},{2,1},{3,7},{4,0},{5,6},{6,5},{7,3},{8,12},{9,10},{10,... | collective-permute-start | bytes 98312 | tf_op jit(solution)/shard_map/ppermute | solution.py:620
  56.5 10.5 %all-to-all-start = ((f32[32,4,128]{2,1,0:T(4,128)}), f32[32,4,128]{2,1,0:T(4,128)S(1)}, u32[]{:S(2)}, u32[]{:S(2)}) async-start(f32[32,4,128]{2,1,0:T(4,128)} %get-tuple-element.75), calls=%async_computation | async-start | bytes 131072 | tf_op jit(solution)/shard_map/all_to_all | solution.py:656
  59.7 4.4 %collective-permute-start.25 = (f32[8,8,128]{2,1,0:T(8,128)S(1)}, f32[8,8,128]{2,1,0:T(8,128)S(1)}, u32[]{:S(2)}, u32[]{:S(2)}) collective-permute-start(f32[8,8,128]{2,1,0:T(8,128)S(1)} %get-tuple-element.121), channel_id=1, source_target_pairs={{0,28},{1,29},{2,30},{3,31},{4,8},{5,9},{6,10},{7,11},{8,4},{9,5},... | collective-permute-start | bytes 98312 | tf_op jit(solution)/shard_map/ppermute | solution.py:620
  62.1 1.9 %collective-permute-start.24 = (f32[8,8,128]{2,1,0:T(8,128)S(1)}, f32[8,8,128]{2,1,0:T(8,128)S(1)}, u32[]{:S(2)}, u32[]{:S(2)}) collective-permute-start(f32[8,8,128]{2,1,0:T(8,128)S(1)} %get-tuple-element.122), channel_id=1, source_target_pairs={{0,4},{1,5},{2,6},{3,7},{4,0},{5,1},{6,2},{7,3},{8,12},{9,13},{10,... | collective-permute-start | bytes 98312 | tf_op jit(solution)/shard_map/ppermute | solution.py:619

commit v4 on v3

--- a/solution.py
+++ b/solution.py
@@ -18,6 +18,7 @@
 shift_mass = 0.1
 mean_porosity = 0.7
 exact_mode = lax.Precision.HIGHEST
+plane_mode = lax.Precision.HIGH
 
 
 def legendre_columns(node_set, degree):
@@ -102,6 +103,10 @@
 WEIGHTS, DERIVATIVE = gll_tables()
 STIFF = DERIVATIVE.T @ (WEIGHTS[:, None] * DERIVATIVE)
 BASIS, EIGEN = schwarz_tables()
+PARITY = {
+    sign: [mode for mode in range(EXT) if BASIS[0, mode] * BASIS[EXT - 1, mode] * sign > 0]
+    for sign in (1, -1)
+}
 
 
 def plane_tables():
@@ -126,13 +131,12 @@
     )
 
 
-def tile_tables():
-    table = np.zeros((NODES + 1, NODES, 128))
-    table[0] = WEIGHTS[:, None]
-    for shift in range(NODES):
-        for k in range(NODES):
-            table[1 + shift, k] = STIFF[k, (k - shift) % NODES]
-    return table.astype(np.float32)
+def row_tile(values):
+    row = lax.broadcasted_iota(jnp.int32, (NODES, 128), 0)
+    tile = jnp.full((NODES, 128), float(values[0]), jnp.float32)
+    for k in range(1, NODES):
+        tile = jnp.where(row == k, float(values[k]), tile)
+    return tile
 
 
 def share_table(count):
@@ -316,37 +320,45 @@
     return jnp.concatenate([ref[a] for a in range(EXT)], axis=1)
 
 
-def local_solve(x_ref, h_ref, forward_ref, back_ref, inverse_ref, part_ref):
+def local_solve(x_ref, forward_ref, back_ref, inverse_ref, part_ref):
     zero = jnp.zeros((6, 128), jnp.float32)
     for a in range(EXT):
         x_ref[a, 80:90] = shift_up(x_ref[a, pl.ds(6, EXT, stride=NODES), :])
         x_ref[a, 96:106] = shift_down(x_ref[a, pl.ds(1, EXT, stride=NODES), :])
         x_ref[a, 90:96] = zero
         x_ref[a, 106:112] = zero
+    half = EXT // 2
+    for block in range(ROWS // 8):
+        rows = pl.ds(block * 8, 8)
+        low = [x_ref[a, rows] for a in range(half)]
+        high = [x_ref[EXT - 1 - a, rows] for a in range(half)]
+        folded = {1: [x + y for x, y in zip(low, high)], -1: [x - y for x, y in zip(low, high)]}
+        for sign in (1, -1):
+            for mode in PARITY[sign]:
+                total = folded[sign][0] * float(BASIS[0, mode])
+                for a in range(1, half):
+                    total = total + folded[sign][a] * float(BASIS[a, mode])
+                x_ref[mode, rows] = total
     spectrum = jnp.dot(
-        forward_ref[...], planes(x_ref), precision=exact_mode, preferred_element_type=jnp.float32
+        forward_ref[...], planes(x_ref), precision=plane_mode, preferred_element_type=jnp.float32
+    ) * planes(inverse_ref)
+    values = jnp.dot(
+        back_ref[...], spectrum, precision=plane_mode, preferred_element_type=jnp.float32
     )
-    for a in range(EXT):
-        h_ref[a] = spectrum[:, a * 128 : (a + 1) * 128]
-    for block in range(MODES // 8):
+    for block in range(ROWS // 8):
         rows = pl.ds(block * 8, 8)
-        values = [h_ref[a, rows] for a in range(EXT)]
-        modes = []
-        for mode in range(EXT):
-            total = values[0] * float(BASIS[0, mode])
-            for a in range(1, EXT):
-                total = total + values[a] * float(BASIS[a, mode])
-            modes.append(total * inverse_ref[mode, rows])
-        for a in range(EXT):
-            total = modes[0] * float(BASIS[a, 0])
-            for mode in range(1, EXT):
-                total = total + modes[mode] * float(BASIS[a, mode])
-            h_ref[a, rows] = total
-    values = jnp.dot(
-        back_ref[...], planes(h_ref), precision=exact_mode, preferred_element_type=jnp.float32
-    )
-    for a in range(EXT):
-        part_ref[a] = values[:, a * 128 : (a + 1) * 128]
+        modes = [values[block * 8 : block * 8 + 8, m * 128 : (m + 1) * 128] for m in range(EXT)]
+        back = {}
+        for sign in (1, -1):
+            for a in range(half):
+                total = None
+                for mode in PARITY[sign]:
+                    term = modes[mode] * float(BASIS[a, mode])
+                    total = term if total is None else total + term
+                back[(sign, a)] = total
+        for a in range(half):
+            part_ref[a, rows] = back[(1, a)] + back[(-1, a)]
+            part_ref[EXT - 1 - a, rows] = back[(1, a)] - back[(-1, a)]
     for a in range(EXT):
 
         def layer(k):
@@ -371,9 +383,10 @@
 
 
 def first_solve_kernel(
-    counts, r_ref, ry_first, ry_second, rx_first, rx_second, forward_ref, back_ref, inverse_ref,
-    part_ref, sy_first, sy_second, fx_first, fx_second, x_ref, h_ref,
+    counts, r_ref, grains_ref, ry_first, ry_second, rx_first, rx_second, forward_ref, back_ref,
+    inverse_ref, part_ref, sy_first, sy_second, fx_first, fx_second, porosity_ref, x_ref,
 ):
+    porosity_ref[...] = 1.0 - 0.6 * grains_ref[...].astype(jnp.float32) / MOST_GRAINS
     side_x, side_y = Sides("gx", counts[0]), Sides("gy", counts[1])
     x_ref[0, 0:80] = side_x.low(rx_first[...], rx_second[...]).reshape(80, 128)
     x_ref[EXT - 1, 0:80] = side_x.high(rx_first[...], rx_second[...]).reshape(80, 128)
@@ -381,13 +394,13 @@
         x_ref[a + 1, 0:8] = side_y.low(ry_first[a], ry_second[a])
         x_ref[a + 1, 8:72] = r_ref[a].reshape(64, 128)
         x_ref[a + 1, 72:80] = side_y.high(ry_first[a], ry_second[a])
-    local_solve(x_ref, h_ref, forward_ref, back_ref, inverse_ref, part_ref)
+    local_solve(x_ref, forward_ref, back_ref, inverse_ref, part_ref)
     send_parts(part_ref, side_x, side_y, sy_first, sy_second, fx_first, fx_second)
 
 
 def second_solve_kernel(
     counts, u_ref, ry_first, ry_second, rx_first, rx_second, forward_ref, back_ref, inverse_ref,
-    q_ref, part_ref, sy_first, sy_second, fx_first, fx_second, x_ref, h_ref,
+    q_ref, part_ref, sy_first, sy_second, fx_first, fx_second, x_ref,
 ):
     side_x, side_y = Sides("gx", counts[0]), Sides("gy", counts[1])
     low_x = side_x.low(rx_first[...], rx_second[...])
@@ -415,7 +428,7 @@
             x_ref[a + 1, b * 8 : b * 8 + 8] = value
             if 0 < b < EXT - 1:
                 q_ref[a, b - 1] = value
-    local_solve(x_ref, h_ref, forward_ref, back_ref, inverse_ref, part_ref)
+    local_solve(x_ref, forward_ref, back_ref, inverse_ref, part_ref)
     send_parts(part_ref, side_x, side_y, sy_first, sy_second, fx_first, fx_second)
 
 
@@ -441,20 +454,20 @@
     return result
 
 
-def porosity_row(grains_ref):
-    return 1.0 - 0.6 * grains_ref[...].astype(jnp.float32) / MOST_GRAINS
-
-
-def apply_tiles(z_ref, u_ref, y_ref, tiles_ref, por):
+def apply_tiles(z_ref, u_ref, y_ref, por):
+    weight_tile = row_tile(WEIGHTS)
+    stiff_tiles = [
+        row_tile([STIFF[k, (k - shift) % NODES] for k in range(NODES)]) for shift in range(NODES)
+    ]
     for a in range(NODES):
         for b in range(NODES):
-            y_ref[a, b] = z_ref[a, b] * tiles_ref[0]
+            y_ref[a, b] = z_ref[a, b] * weight_tile
     for a in range(NODES):
         for b in range(NODES):
             z = z_ref[a, b]
-            third = z * tiles_ref[1]
+            third = z * stiff_tiles[0]
             for shift in range(1, NODES):
-                third = third + pltpu.roll(z, shift, 0) * tiles_ref[1 + shift]
+                third = third + pltpu.roll(z, shift, 0) * stiff_tiles[shift]
             first = y_ref[0, b] * float(STIFF[a, 0] * WEIGHTS[b])
             second = y_ref[a, 0] * float(STIFF[b, 0] * WEIGHTS[a])
             for other in range(1, NODES):
@@ -475,8 +488,8 @@
 
 
 def first_apply_kernel(
-    counts, part_ref, ry_first, ry_second, rx_first, rx_second, sum_ref, lift_ref, grains_ref,
-    r_ref, tiles_ref, z_ref, u_ref, sy_first, sy_second, fx_first, fx_second, y_ref,
+    counts, part_ref, ry_first, ry_second, rx_first, rx_second, sum_ref, lift_ref, porosity_ref,
+    r_ref, z_ref, u_ref, sy_first, sy_second, fx_first, fx_second, y_ref,
 ):
     side_x, side_y = Sides("gx", counts[0]), Sides("gy", counts[1])
     field = lifted_rows(counts, row_of(counts, sum_ref), lift_ref)
@@ -487,7 +500,7 @@
         term = scaled(value * r_ref[a, b], axis_factor(a, side_x), axis_factor(b, side_y))
         inner = term if inner is None else inner + term
     inner = inner * multiplicity_tile()
-    apply_tiles(z_ref, u_ref, y_ref, tiles_ref, porosity_row(grains_ref))
+    apply_tiles(z_ref, u_ref, y_ref, porosity_ref[...])
     sums = {}
     curvature = None
     for a in range(NODES):
@@ -511,8 +524,8 @@
 
 
 def second_apply_kernel(
-    counts, part_ref, ry_first, ry_second, rx_first, rx_second, sum_ref, lift_ref, grains_ref,
-    r_ref, q_ref, z_ref, tiles_ref, z1_ref, u_ref, sy_first, sy_second, fx_first, fx_second, stats_ref, y_ref,
+    counts, part_ref, ry_first, ry_second, rx_first, rx_second, sum_ref, lift_ref, porosity_ref,
+    r_ref, q_ref, z_ref, z1_ref, u_ref, sy_first, sy_second, fx_first, fx_second, stats_ref, y_ref,
 ):
     side_x, side_y = Sides("gx", counts[0]), Sides("gy", counts[1])
     summed = row_of(counts, sum_ref)
@@ -527,7 +540,7 @@
         term = scaled(next_z * next_r, axis_factor(a, side_x), axis_factor(b, side_y))
         inner = term if inner is None else inner + term
     inner = inner * multiplicity_tile()
-    apply_tiles(z1_ref, u_ref, y_ref, tiles_ref, porosity_row(grains_ref))
+    apply_tiles(z1_ref, u_ref, y_ref, porosity_ref[...])
     own = None
     cross = None
     for a in range(NODES):
@@ -546,6 +559,15 @@
     low, high = u_ref[0], u_ref[NODES - 1]
     fx_first[...] = side_x.send_first(low, high)
     fx_second[...] = side_x.send_second(low, high)
+
+
+def prepare_kernel(counts, sol_ref, r_ref, q_ref, z_ref, sum_ref, sol_out, r_out):
+    summed = row_of(counts, sum_ref)
+    step = row_value(counts, summed, 0) / row_value(counts, summed, 1)
+    for a in range(NODES):
+        for b in range(NODES):
+            sol_out[a, b] = sol_ref[a, b] + step * z_ref[a, b]
+            r_out[a, b] = r_ref[a, b] - step * q_ref[a, b]
 
 
 def final_kernel(
@@ -578,8 +600,14 @@
             direction = z1_ref[a, b] + ratio * z
             image = image + ratio * q
             d_out[a, b] = direction
-            sol_out[a, b] = sol_ref[a, b] + first_step * z + second_step * direction
-            r_out[a, b] = r_ref[a, b] - first_step * q - second_step * image
+            sol_out[a, b] = sol_ref[a, b] + second_step * direction
+            r_out[a, b] = r_ref[a, b] - second_step * image
+
+
+COSTS = {
+    "start": 100, "first_solve": 1300, "second_solve": 1300, "first_apply": 800,
+    "second_apply": 800, "prepare": 20000, "final": 500,
+}
 
 
 def call(kernel, counts, name, shapes, scratch, *operands):
@@ -597,6 +625,9 @@
         out_specs=[pl.BlockSpec(memory_space=space(shape)) for shape in shapes],
         scratch_shapes=[pltpu.VMEM(shape, jnp.float32) for shape in scratch],
         compiler_params=pltpu.CompilerParams(vmem_limit_bytes=24 * 1024 * 1024),
+        cost_estimate=pl.CostEstimate(
+            flops=COSTS[name] * 1000000, bytes_accessed=COSTS[name] * 3000, transcendentals=0
+        ),
     )(*operands)
 
 
@@ -683,7 +714,6 @@
 
 def shards_of(counts):
     forward_np, back_np, inverse_np = plane_tables()
-    tiles_np = tile_tables()
 
     def shards(solution, residual, grain_counts):
         shard_shape = solution.shape
@@ -693,7 +723,6 @@
         lift = own_lift(lift_tables(counts, block[-1]))
         grains = grain_counts.reshape(1, 128)
         plane = [jnp.asarray(table) for table in (forward_np, back_np, inverse_np)]
-        tiles = jnp.asarray(tiles_np)
         side_x, side_y = Sides("gx", counts[0]), Sides("gy", counts[1])
         row = (counts[0] * counts[1], 4, 128)
         face = (NODES, NODES, 128)
@@ -702,7 +731,7 @@
             (EXT, 2, NODES, 128), (EXT, 2, NODES, 128),
             (2, EXT, NODES, 128), (2, EXT, NODES, 128),
         ]
-        solve_scratch = [(EXT, ROWS, 128), (EXT, MODES, 128)]
+        solve_scratch = [(EXT, ROWS, 128)]
 
         y_first, y_second = call(
             start_kernel, counts, "start", [(NODES + 1,) + face[1:], face], [], residual
@@ -722,14 +751,13 @@
             counts, 0, carry(side_x.send_first(low_face, high_face), running),
             side_x.send_second(low_face, high_face),
         )
-        rx, far = lax.optimization_barrier((rx, running.far((4, 0), (5, 0))))
         rx_first, tile = carried(rx[0], low_face.shape)
-        for value in [tile] + far:
-            running.add(value)
+        running.add(tile)
         rx = (rx_first, rx[1])
-        part, y_first, y_second, *fx = call(
-            first_solve_kernel, counts, "first_solve", part_shapes, solve_scratch,
-            residual, *ry, *rx, *plane,
+        far = running.far((0, 2))
+        part, y_first, y_second, *fx, porosity = call(
+            first_solve_kernel, counts, "first_solve", part_shapes + [(1, 128)], solve_scratch,
+            residual, grains, *ry, *rx, *plane,
         )
 
         def spread_faces(fx, ry):
@@ -744,9 +772,12 @@
                 fx[1][:, 1:-1] + side_x.send_second(*both),
             )
 
-        def trade_spread(y_first, y_second, fx, running):
+        def trade_spread(y_first, y_second, fx, running, far):
+            y_first, far = lax.optimization_barrier((y_first, far))
+            for value in far:
+                running.add(value)
             ry = trade(counts, 1, y_first, y_second)
-            for value in running.far((0, 2)):
+            for value in running.far((4, 0)):
                 running.add(value)
             first, second = spread_faces(fx, ry)
             rx = trade(counts, 0, first, carry(second, running))
@@ -754,13 +785,13 @@
             running.add(tile)
             return ry, (rx[0], rx_second)
 
-        ry, rx = trade_spread(y_first, y_second, fx, running)
+        ry, rx = trade_spread(y_first, y_second, fx, running, far)
         z, u, y_first, y_second, *fx = call(
             first_apply_kernel, counts, "first_apply",
             [block, block, (2 * NODES + 1, NODES, 128), (2 * NODES, NODES, 128),
              (2, NODES, NODES, 128), (2, NODES, NODES, 128)],
             [block],
-            part, *ry, *rx, running.value, lift, grains, residual, tiles,
+            part, *ry, *rx, running.value, lift, porosity, residual,
         )
         running = RunningSum(counts, y_first[-1])
         ry = trade(counts, 1, y_first, y_second)
@@ -779,23 +810,28 @@
         first = jnp.pad(fx[0], pads) + side_x.send_first(*both)
         second = jnp.pad(fx[1], pads) + side_x.send_second(*both)
         rx = trade(counts, 0, carry(first, running), second)
-        rx, far = lax.optimization_barrier((rx, running.far((4, 0), (5, 0))))
         rx_first, tile = carried(rx[0], first.shape)
-        for value in [tile] + far:
-            running.add(value)
+        running.add(tile)
         rx = (rx_first, rx[1])
+        far = running.far((0, 2))
         q, part, y_first, y_second, *fx = call(
             second_solve_kernel, counts, "second_solve", [block] + part_shapes, solve_scratch,
             u, *ry, *rx, *plane,
         )
-        ry, rx = trade_spread(y_first, y_second, fx, running)
+        ry, rx = trade_spread(y_first, y_second, fx, running, far)
         z1, u, y_first, y_second, *fx, stats = call(
             second_apply_kernel, counts, "second_apply",
             [block, block, face, face, face, face, row],
             [block],
-            part, *ry, *rx, running.value, lift, grains, residual, q, z, tiles,
-        )
-        ry = trade(counts, 1, y_first, y_second)
+            part, *ry, *rx, running.value, lift, porosity, residual, q, z,
+        )
+        next_solution, next_residual = call(
+            prepare_kernel, counts, "prepare", [block] * 2, [],
+            solution, residual, q, z, running.value,
+        )
+        ry, next_solution, next_residual = lax.optimization_barrier(
+            (trade(counts, 1, y_first, y_second), next_solution, next_residual)
+        )
         low_y, high_y = side_y.low(*ry), side_y.high(*ry)
 
         def edge_rows(index):
@@ -809,7 +845,7 @@
         last_stats = gather_stats(stats)
         solution_out, residual_out, direction, steps = call(
             final_kernel, counts, "final", [block] * 3 + [(2,)], [],
-            solution, residual, q, z, z1, u, *ry, *rx, running.value, last_stats,
+            next_solution, next_residual, q, z, z1, u, *ry, *rx, running.value, last_stats,
         )
         return (
             solution_out.reshape(shard_shape),

time: 68.4 us -> 65.4 us (0.956)
  waiting for transfers between devices: 24.5 us -> 21.2 us
  Pallas kernels: 7.47 us -> 6.06 us
  starting transfers between devices: 31 us -> 32.3 us
    ppermute x10, starting transfers between devices: 12.5 us -> 15.6 us  [trade(): lax.ppermute(first, AXES, swap_pairs(counts, axis, 0))]
    all_to_all x1, waiting for transfers between devices: 2.99 us -> 0.01 us  [gather_stats(): return lax.all_to_all(stats, AXES, 0, 0)]
    ppermute x6 -> x4, waiting for transfers between devices: 5.03 us -> 2.92 us  [trade_far(): return lax.ppermute(value, AXES, pairs)]
    pallas_call x6 -> x7, Pallas kernels: 7.47 us -> 6.06 us  [call(): pl.pallas_call(body, name=name, out_shape=[jax.ShapeDtypeStruct(shape, jn...]
    ppermute x10, waiting for transfers between devices: 6.46 us -> 7.72 us  [trade(): lax.ppermute(first, AXES, swap_pairs(counts, axis, 0))]
    ppermute x10, starting transfers between devices: 7.84 us -> 6.63 us  [trade(): lax.ppermute(second, AXES, swap_pairs(counts, axis, 1))]
    ppermute x6 -> x4, starting transfers between devices: 7.63 us -> 7.47 us  [trade_far(): return lax.ppermute(value, AXES, pairs)]
    unnamed x20 -> x18, local copies, waits for them, and re-layouts: 1.72 us -> 1.86 us
  transfers between devices with their start and end apart: 27 -> 25, of which waited for: 12 -> 11; matrix products, arithmetic and copies ran while one was open for 3% -> 3% of each run, Pallas kernels for 3% -> 4%
where the time goes in v4:
time: 65.4 us; the launch traced here: 64.9 us
  starting transfers between devices  32.3 us (49%)
  waiting for transfers between devices  21.2 us (32%)
  Pallas kernels  6.06 us (9%)
  local copies, waits for them, and re-layouts  3.62 us (6%)
  between operations  1.03 us (2%)
    ppermute x10, starting transfers between devices, trade(): lax.ppermute(first, AXES, swap_pairs(counts, axis, 0))  15.6 us
    ppermute x10, waiting for transfers between devices, trade(): lax.ppermute(second, AXES, swap_pairs(counts, axis, 1))  10.5 us
    ppermute x10, waiting for transfers between devices, trade(): lax.ppermute(first, AXES, swap_pairs(counts, axis, 0))  7.72 us
    ppermute x4, starting transfers between devices, trade_far(): return lax.ppermute(value, AXES, pairs)  7.47 us
    ppermute x10, starting transfers between devices, trade(): lax.ppermute(second, AXES, swap_pairs(counts, axis, 1))  6.63 us
    pallas_call x7, Pallas kernels, call(): pl.pallas_call(body, name=name, out_shape=[jax.ShapeDtypeStruct(shape, jn...  6.06 us
    ppermute x4, waiting for transfers between devices, trade_far(): return lax.ppermute(value, AXES, pairs)  2.92 us
    all_to_all x1, starting transfers between devices, gather_stats(): return lax.all_to_all(stats, AXES, 0, 0)  2.63 us
  transfers between devices with their start and end apart: 25, of which 11 were waited for; matrix products, arithmetic and copies ran while one was open for 3% of the time, Pallas kernels for 4%

profile of v4, /device:TPU:0, one launch (start us, length us, event | category | flops | bytes accessed | tf_op | source)
XLA Modules:
  0.0 64.9 jit_solution(3781498766674442530)
XLA Ops:
  0.6 0.9 %copy-done = f32[1,1,8,8,8,128]{5,4,3,2,1,0:T(8,128)S(1)} copy-done((f32[1,1,8,8,8,128]{5,4,3,2,1,0:T(8,128)S(1)}, f32[1,1,8,8,8,128]{5,4,3,2,1,0:T(8,128)}, u32[]{:S(2)}) %copy-start) | copy-done | bytes 262168
  1.6 0.1 start.1
  1.7 0.5 collective-permute-start.1
  2.2 4.1 %collective-permute-start = (f32[9,8,128]{2,1,0:T(8,128)S(1)}, f32[9,8,128]{2,1,0:T(8,128)S(1)}, u32[]{:S(2)}, u32[]{:S(2)}) collective-permute-start(f32[9,8,128]{2,1,0:T(8,128)S(1)} %get-tuple-element.45), channel_id=1, source_target_pairs={{0,1},{1,0},{2,3},{3,2},{4,5},{5,4},{6,7},{7,6},{8,9},{9,8},{10,11... | collective-permute-start | bytes 110600 | tf_op jit(solution)/shard_map/ppermute | solution.py:650
  6.3 0.7 %dynamic-slice_bitcast_fusion.1 = f32[3,8]{1,0:T(4,128)S(1)} fusion(f32[8,3,8]{2,1,0:T(4,128)} %constant.49.clone, s32[]{:T(128)S(6)} %select_n.192), kind=kLoop, calls=%fused_computation.59 | loop fusion | bytes 196 | tf_op jit(solution)/shard_map/mul | solution.py:710
  7.0 1.2 %collective-permute-done = f32[9,8,128]{2,1,0:T(8,128)S(1)} collective-permute-done((f32[9,8,128]{2,1,0:T(8,128)S(1)}, f32[9,8,128]{2,1,0:T(8,128)S(1)}, u32[]{:S(2)}, u32[]{:S(2)}) %collective-permute-start) | collective-permute-done | bytes 36896 | tf_op jit(solution)/shard_map/ppermute | solution.py:650
  8.4 0.7 %dynamic-slice_bitcast_fusion = f32[3,4]{1,0:T(4,128)S(1)} fusion(f32[4,3,4]{2,1,0:T(4,128)} %constant.50.clone, s32[]{:T(128)S(6)} %select_n.193), kind=kLoop, calls=%fused_computation.58 | loop fusion | bytes 100 | tf_op jit(solution)/shard_map/mul | solution.py:710
  9.1 2.5 %collective-permute-start.3 = (f32[10,8,128]{2,1,0:T(8,128)S(1)}, f32[10,8,128]{2,1,0:T(8,128)S(1)}, u32[]{:S(2)}, u32[]{:S(2)}) collective-permute-start(f32[10,8,128]{2,1,0:T(8,128)S(1)} %get-tuple-element.102), channel_id=1, source_target_pairs={{0,28},{1,29},{2,30},{3,31},{4,8},{5,9},{6,10},{7,11},{8,4},{9,5},... | collective-permute-start | bytes 122888 | tf_op jit(solution)/shard_map/ppermute | solution.py:651
  11.7 1.9 %collective-permute-start.4 = (f32[8,128]{1,0:T(8,128)S(1)}, f32[8,128]{1,0:T(8,128)S(1)}, u32[]{:S(2)}, u32[]{:S(2)}) collective-permute-start(f32[8,128]{1,0:T(8,128)S(1)} %fusion.23), channel_id=1, source_target_pairs={{0,2},{1,3},{2,0},{3,1},{4,6},{5,7},{6,4},{7,5},{8,10},{9,11},{10,... | collective-permute-start | bytes 12296 | tf_op jit(solution)/shard_map/ppermute | solution.py:661
  13.6 0.6 copy-done.3
  14.3 1.1 %first_solve.1 = (f32[10,112,128]{2,1,0:T(8,128)S(1)}, f32[10,2,8,128]{3,2,1,0:T(8,128)S(1)}, f32[10,2,8,128]{3,2,1,0:T(8,128)S(1)}, f32[2,10,8,128]{3,2,1,0:T(8...) custom-call(f32[8,8,8,128]{3,2,1,0:T(8,128)S(1)} %bitcast.47, s32[1,128]{1,0:T(1,128)S(1)} %bitcast.52, ...), custom_call_target="tpu_custom_call" | custom-call | flops 1300000000 | bytes 3900000 | tf_op jit(solution)/shard_map/first_solve/pallas_call | solution.py:620
  15.5 0.7 %collective-permute-done.4 = f32[8,128]{1,0:T(8,128)S(1)} collective-permute-done((f32[8,128]{1,0:T(8,128)S(1)}, f32[8,128]{1,0:T(8,128)S(1)}, u32[]{:S(2)}, u32[]{:S(2)}) %collective-permute-start.4) | collective-permute-done | bytes 4128 | tf_op jit(solution)/shard_map/ppermute | solution.py:661
  16.2 0.9 %collective-permute-start.8 = (f32[8,128]{1,0:T(8,128)S(1)}, f32[8,128]{1,0:T(8,128)S(1)}, u32[]{:S(2)}, u32[]{:S(2)}) collective-permute-start(f32[8,128]{1,0:T(8,128)S(1)} %add.83), channel_id=1, source_target_pairs={{0,16},{1,17},{2,18},{3,19},{4,20},{5,21},{6,22},{7,23},{8,24},{9,... | collective-permute-start | bytes 12296 | tf_op jit(solution)/shard_map/ppermute | solution.py:661
  17.1 2.4 %collective-permute-start.5 = (f32[10,2,8,128]{3,2,1,0:T(8,128)S(1)}, f32[10,2,8,128]{3,2,1,0:T(8,128)S(1)}, u32[]{:S(2)}, u32[]{:S(2)}) collective-permute-start(f32[10,2,8,128]{3,2,1,0:T(8,128)S(1)} %get-tuple-element.49), channel_id=1, source_target_pairs={{0,1},{1,0},{2,3},{3,2},{4,5},{5,4},{6,7},{7,6},{8,9},{9,8},{10,11... | collective-permute-start | bytes 245768 | tf_op jit(solution)/shard_map/ppermute | solution.py:650
  19.5 0.1 mul.37
  19.7 0.1 collective-permute-done.8
  19.8 2.1 %collective-permute-done.5.refs_1_ = f32[10,2,8,128]{3,2,1,0:T(8,128)S(1)} collective-permute-done((f32[10,2,8,128]{3,2,1,0:T(8,128)S(1)}, f32[10,2,8,128]{3,2,1,0:T(8,128)S(1)}, u32[]{:S(2)}, u32[]{:S(2)}) %collective-permute-start.5) | collective-permute-done | bytes 81952 | tf_op jit(solution)/shard_map/ppermute | solution.py:650
  21.9 0.1 fusion.7
  22.1 0.4 collective-permute-start.9
  22.5 0.3 copy-done.7
  22.7 0.1 fusion.18
  22.9 1.0 %collective-permute-start.7 = (f32[2,8,8,128]{3,2,1,0:T(8,128)S(1)}, f32[2,8,8,128]{3,2,1,0:T(8,128)S(1)}, u32[]{:S(2)}, u32[]{:S(2)}) collective-permute-start(f32[2,8,8,128]{3,2,1,0:T(8,128)S(1)} %get-tuple-element.111), channel_id=1, source_target_pairs={{0,4},{1,5},{2,6},{3,7},{4,0},{5,1},{6,2},{7,3},{8,12},{9,13},{10,... | collective-permute-start | bytes 196616 | tf_op jit(solution)/shard_map/ppermute | solution.py:650
  23.9 2.8 %collective-permute-done.9 = f32[17,8,128]{2,1,0:T(8,128)S(1)} collective-permute-done((f32[17,8,128]{2,1,0:T(8,128)S(1)}, f32[17,8,128]{2,1,0:T(8,128)S(1)}, u32[]{:S(2)}, u32[]{:S(2)}) %collective-permute-start.9) | collective-permute-done | bytes 69664 | tf_op jit(solution)/shard_map/ppermute | solution.py:651
  26.8 0.9 %first_apply.1 = (f32[8,8,8,128]{3,2,1,0:T(8,128)S(1)}, f32[8,8,8,128]{3,2,1,0:T(8,128)S(1)}, f32[17,8,128]{2,1,0:T(8,128)S(1)}, f32[16,8,128]{2,1,0:T(8,128)S(1...) custom-call(f32[10,112,128]{2,1,0:T(8,128)S(1)} %get-tuple-element.47.refs_0_, ...), custom_call_target="tpu_custom_call" | custom-call | flops 800000000 | bytes 2400000 | tf_op jit(solution)/shard_map/first_apply/pallas_call | solution.py:620
  27.7 2.0 %collective-permute-start.10 = (f32[17,8,128]{2,1,0:T(8,128)S(1)}, f32[17,8,128]{2,1,0:T(8,128)S(1)}, u32[]{:S(2)}, u32[]{:S(2)}) collective-permute-start(f32[17,8,128]{2,1,0:T(8,128)S(1)} %get-tuple-element.56), channel_id=1, source_target_pairs={{0,1},{1,0},{2,3},{3,2},{4,5},{5,4},{6,7},{7,6},{8,9},{9,8},{10,11... | collective-permute-start | bytes 208904 | tf_op jit(solution)/shard_map/ppermute | solution.py:650
  29.7 0.1 pad.34.clone
  29.8 2.2 %collective-permute-done.10 = f32[17,8,128]{2,1,0:T(8,128)S(1)} collective-permute-done((f32[17,8,128]{2,1,0:T(8,128)S(1)}, f32[17,8,128]{2,1,0:T(8,128)S(1)}, u32[]{:S(2)}, u32[]{:S(2)}) %collective-permute-start.10) | collective-permute-done | bytes 69664 | tf_op jit(solution)/shard_map/ppermute | solution.py:650
  32.1 0.1 fusion.3
  32.3 1.5 %collective-permute-start.13 = (f32[2,10,8,128]{3,2,1,0:T(8,128)S(1)}, f32[2,10,8,128]{3,2,1,0:T(8,128)S(1)}, u32[]{:S(2)}, u32[]{:S(2)}) collective-permute-start(f32[2,10,8,128]{3,2,1,0:T(8,128)S(1)} %get-tuple-element.108), channel_id=1, source_target_pairs={{0,28},{1,29},{2,30},{3,31},{4,8},{5,9},{6,10},{7,11},{8,4},{9,5},... | collective-permute-start | bytes 245768 | tf_op jit(solution)/shard_map/ppermute | solution.py:651
  33.7 3.2 %collective-permute-start.14 = (f32[8,128]{1,0:T(8,128)S(1)}, f32[8,128]{1,0:T(8,128)S(1)}, u32[]{:S(2)}, u32[]{:S(2)}) collective-permute-start(f32[8,128]{1,0:T(8,128)S(1)} %fusion.21), channel_id=1, source_target_pairs={{0,2},{1,3},{2,0},{3,1},{4,6},{5,7},{6,4},{7,5},{8,10},{9,11},{10,... | collective-permute-start | bytes 12296 | tf_op jit(solution)/shard_map/ppermute | solution.py:661
  36.9 0.7 %collective-permute-done.13.refs_4_ = f32[2,10,8,128]{3,2,1,0:T(8,128)S(1)} collective-permute-done((f32[2,10,8,128]{3,2,1,0:T(8,128)S(1)}, f32[2,10,8,128]{3,2,1,0:T(8,128)S(1)}, u32[]{:S(2)}, u32[]{:S(2)}) %collective-permute-start.13) | collective-permute-done | bytes 81952 | tf_op jit(solution)/shard_map/ppermute | solution.py:651
  37.6 1.2 %second_solve.1 = (f32[8,8,8,128]{3,2,1,0:T(8,128)S(1)}, f32[10,112,128]{2,1,0:T(8,128)S(1)}, f32[10,2,8,128]{3,2,1,0:T(8,128)S(1)}, f32[10,2,8,128]{3,2,1,0:T(8...) custom-call(f32[8,8,8,128]{3,2,1,0:T(8,128)S(1)} %get-tuple-element.55.refs_0_, ...), custom_call_target="tpu_custom_call" | custom-call | flops 1300000000 | bytes 3900000 | tf_op jit(solution)/shard_map/second_solve/pallas_call | solution.py:620
  38.8 0.1 collective-permute-start.16
  38.9 3.6 %collective-permute-start.15 = (f32[10,2,8,128]{3,2,1,0:T(8,128)S(1)}, f32[10,2,8,128]{3,2,1,0:T(8,128)S(1)}, u32[]{:S(2)}, u32[]{:S(2)}) collective-permute-start(f32[10,2,8,128]{3,2,1,0:T(8,128)S(1)} %get-tuple-element.62), channel_id=1, source_target_pairs={{0,1},{1,0},{2,3},{3,2},{4,5},{5,4},{6,7},{7,6},{8,9},{9,8},{10,11... | collective-permute-start | bytes 245768 | tf_op jit(solution)/shard_map/ppermute | solution.py:650
  42.5 1.5 %collective-permute-start.18 = (f32[8,128]{1,0:T(8,128)S(1)}, f32[8,128]{1,0:T(8,128)S(1)}, u32[]{:S(2)}, u32[]{:S(2)}) collective-permute-start(f32[8,128]{1,0:T(8,128)S(1)} %add.95), channel_id=1, source_target_pairs={{0,16},{1,17},{2,18},{3,19},{4,20},{5,21},{6,22},{7,23},{8,24},{9,... | collective-permute-start | bytes 12296 | tf_op jit(solution)/shard_map/ppermute | solution.py:661
  44.0 2.1 %collective-permute-done.18 = f32[8,128]{1,0:T(8,128)S(1)} collective-permute-done((f32[8,128]{1,0:T(8,128)S(1)}, f32[8,128]{1,0:T(8,128)S(1)}, u32[]{:S(2)}, u32[]{:S(2)}) %collective-permute-start.18) | collective-permute-done | bytes 4128 | tf_op jit(solution)/shard_map/ppermute | solution.py:661
  46.2 0.1 fusion.11
  46.5 4.5 %collective-permute-done.19 = f32[17,8,128]{2,1,0:T(8,128)S(1)} collective-permute-done((f32[17,8,128]{2,1,0:T(8,128)S(1)}, f32[17,8,128]{2,1,0:T(8,128)S(1)}, u32[]{:S(2)}, u32[]{:S(2)}) %collective-permute-start.19) | collective-permute-done | bytes 69664 | tf_op jit(solution)/shard_map/ppermute | solution.py:651
  51.0 1.6 %second_apply.1 = (f32[8,8,8,128]{3,2,1,0:T(8,128)S(1)}, f32[8,8,8,128]{3,2,1,0:T(8,128)S(1)}, f32[8,8,128]{2,1,0:T(8,128)S(1)}, f32[8,8,128]{2,1,0:T(8,128)S(1)...) custom-call(f32[10,112,128]{2,1,0:T(8,128)S(1)} %get-tuple-element.60.refs_0_, ...), custom_call_target="tpu_custom_call" | custom-call | flops 800000000 | bytes 2400000 | tf_op jit(solution)/shard_map/second_apply/pallas_call | solution.py:620
  52.6 2.6 %all-to-all-start = ((f32[32,4,128]{2,1,0:T(4,128)}), f32[32,4,128]{2,1,0:T(4,128)S(1)}, u32[]{:S(2)}, u32[]{:S(2)}) async-start(f32[32,4,128]{2,1,0:T(4,128)} %get-tuple-element.81), calls=%async_computation | async-start | bytes 131072 | tf_op jit(solution)/shard_map/all_to_all | solution.py:687
  55.2 1.8 %collective-permute-start.20 = (f32[8,8,128]{2,1,0:T(8,128)S(1)}, f32[8,8,128]{2,1,0:T(8,128)S(1)}, u32[]{:S(2)}, u32[]{:S(2)}) collective-permute-start(f32[8,8,128]{2,1,0:T(8,128)S(1)} %get-tuple-element.69), channel_id=1, source_target_pairs={{0,1},{1,0},{2,3},{3,2},{4,5},{5,4},{6,7},{7,6},{8,9},{9,8},{10,11... | collective-permute-start | bytes 98312 | tf_op jit(solution)/shard_map/ppermute | solution.py:650
  57.1 0.1 prepare.1
  57.2 2.2 %collective-permute-done.20.refs_6_ = f32[8,8,128]{2,1,0:T(8,128)S(1)} collective-permute-done((f32[8,8,128]{2,1,0:T(8,128)S(1)}, f32[8,8,128]{2,1,0:T(8,128)S(1)}, u32[]{:S(2)}, u32[]{:S(2)}) %collective-permute-start.20) | collective-permute-done | bytes 32800 | tf_op jit(solution)/shard_map/ppermute | solution.py:650
  59.4 0.1 fusion.15
  59.5 1.5 %collective-permute-start.23 = (f32[8,8,128]{2,1,0:T(8,128)S(1)}, f32[8,8,128]{2,1,0:T(8,128)S(1)}, u32[]{:S(2)}, u32[]{:S(2)}) collective-permute-start(f32[8,8,128]{2,1,0:T(8,128)S(1)} %get-tuple-element.127), channel_id=1, source_target_pairs={{0,28},{1,29},{2,30},{3,31},{4,8},{5,9},{6,10},{7,11},{8,4},{9,5},... | collective-permute-start | bytes 98312 | tf_op jit(solution)/shard_map/ppermute | solution.py:651
  61.0 0.4 collective-permute-start.22
  61.4 2.5 %collective-permute-done.23.refs_9_ = f32[8,8,128]{2,1,0:T(8,128)S(1)} collective-permute-done((f32[8,8,128]{2,1,0:T(8,128)S(1)}, f32[8,8,128]{2,1,0:T(8,128)S(1)}, u32[]{:S(2)}, u32[]{:S(2)}) %collective-permute-start.23) | collective-permute-done | bytes 32800 | tf_op jit(solution)/shard_map/ppermute | solution.py:651
  63.8 1.0 %final.1 = (f32[8,8,8,128]{3,2,1,0:T(8,128)}, f32[8,8,8,128]{3,2,1,0:T(8,128)}, f32[8,8,8,128]{3,2,1,0:T(8,128)}, f32[2]{0:T(128)}) custom-call(f32[8,8,8,128]{3,2,1,0:T(8,128)S(1)} %get-tuple-element.73.refs_0_, f32[8,8,8,128]{3,2,1,0:T(8,128)S(1)} %get-tuple-element.74.refs_1_, f32[8,8,8,128]{3,2,1,0:T(8,128)S(1)} %get-tuple-element.67.refs_9_.refs_2_, ...), custom_call_target="tpu_custom_call" | custom-call | flops 500000000 | bytes 1500000 | tf_op jit(solution)/shard_map/final/pallas_call | solution.py:620
  (77 shorter events, 0.8 us)
Async XLA Ops:
  0.6 1.0 %copy-start = (f32[1,1,8,8,8,128]{5,4,3,2,1,0:T(8,128)S(1)}, f32[1,1,8,8,8,128]{5,4,3,2,1,0:T(8,128)}, u32[]{:S(2)}) copy-start(f32[1,1,8,8,8,128]{5,4,3,2,1,0:T(8,128)} %param.11) | copy-start | bytes 786436
  1.6 12.0 %copy-start.4 = (f32[10,104,128]{2,1,0:T(8,128)S(1)}, f32[10,104,128]{2,1,0:T(8,128)}, u32[]{:S(2)}) copy-start(f32[10,104,128]{2,1,0:T(8,128)} %constant.55.clone.refs_8_.refs_7_) | copy-start | bytes 1597444
  1.7 5.3 %collective-permute-start.1 = (f32[8,8,128]{2,1,0:T(8,128)S(1)}, f32[8,8,128]{2,1,0:T(8,128)S(1)}, u32[]{:S(2)}, u32[]{:S(2)}) collective-permute-start(f32[8,8,128]{2,1,0:T(8,128)S(1)} %get-tuple-element.46), channel_id=1, source_target_pairs={{0,4},{1,2},{2,1},{3,7},{4,0},{5,6},{6,5},{7,3},{8,12},{9,10},{10,... | collective-permute-start | bytes 98312 | tf_op jit(solution)/shard_map/ppermute | solution.py:651
  2.2 6.1 %collective-permute-start = (f32[9,8,128]{2,1,0:T(8,128)S(1)}, f32[9,8,128]{2,1,0:T(8,128)S(1)}, u32[]{:S(2)}, u32[]{:S(2)}) collective-permute-start(f32[9,8,128]{2,1,0:T(8,128)S(1)} %get-tuple-element.45), channel_id=1, source_target_pairs={{0,1},{1,0},{2,3},{3,2},{4,5},{5,4},{6,7},{7,6},{8,9},{9,8},{10,11... | collective-permute-start | bytes 110600 | tf_op jit(solution)/shard_map/ppermute | solution.py:650
  7.0 6.6 %copy-start.1 = (f32[1,1,8,8,8,128]{5,4,3,2,1,0:T(8,128)S(1)}, f32[1,1,8,8,8,128]{5,4,3,2,1,0:T(8,128)}, u32[]{:S(2)}) copy-start(f32[1,1,8,8,8,128]{5,4,3,2,1,0:T(8,128)} %param.11) | copy-start | bytes 786436
  8.3 5.3 %copy-start.6 = (f32[104,112]{1,0:T(8,128)S(1)}, f32[104,112]{1,0:T(8,128)}, u32[]{:S(2)}) copy-start(f32[104,112]{1,0:T(8,128)} %constant.53.clone.refs_6_.refs_5_) | copy-start | bytes 139780
  8.3 5.3 %copy-start.5 = (f32[112,104]{1,0:T(8,128)S(1)}, f32[112,104]{1,0:T(8,128)}, u32[]{:S(2)}) copy-start(f32[112,104]{1,0:T(8,128)} %constant.54.clone.refs_7_.refs_6_) | copy-start | bytes 139780
  8.4 3.3 %collective-permute-start.2 = (f32[11,8,128]{2,1,0:T(8,128)S(1)}, f32[11,8,128]{2,1,0:T(8,128)S(1)}, u32[]{:S(2)}, u32[]{:S(2)}) collective-permute-start(f32[11,8,128]{2,1,0:T(8,128)S(1)} %pad_maximum_fusion.9), channel_id=1, source_target_pairs={{0,4},{1,5},{2,6},{3,7},{4,0},{5,1},{6,2},{7,3},{8,12},{9,13},{10,... | collective-permute-start | bytes 135176 | tf_op jit(solution)/shard_map/ppermute | solution.py:650
  9.1 4.5 %collective-permute-start.3 = (f32[10,8,128]{2,1,0:T(8,128)S(1)}, f32[10,8,128]{2,1,0:T(8,128)S(1)}, u32[]{:S(2)}, u32[]{:S(2)}) collective-permute-start(f32[10,8,128]{2,1,0:T(8,128)S(1)} %get-tuple-element.102), channel_id=1, source_target_pairs={{0,28},{1,29},{2,30},{3,31},{4,8},{5,9},{6,10},{7,11},{8,4},{9,5},... | collective-permute-start | bytes 122888 | tf_op jit(solution)/shard_map/ppermute | solution.py:651
  11.7 4.5 %collective-permute-start.4 = (f32[8,128]{1,0:T(8,128)S(1)}, f32[8,128]{1,0:T(8,128)S(1)}, u32[]{:S(2)}, u32[]{:S(2)}) collective-permute-start(f32[8,128]{1,0:T(8,128)S(1)} %fusion.23), channel_id=1, source_target_pairs={{0,2},{1,3},{2,0},{3,1},{4,6},{5,7},{6,4},{7,5},{8,10},{9,11},{10,... | collective-permute-start | bytes 12296 | tf_op jit(solution)/shard_map/ppermute | solution.py:661
  13.6 0.7 %copy-start.3 = (s32[1,1,128]{2,1,0:T(1,128)S(1)}, s32[1,1,128]{2,1,0:T(1,128)}, u32[]{:S(2)}) copy-start(s32[1,1,128]{2,1,0:T(1,128)} %param.12) | copy-start | bytes 1540
  15.4 4.4 %collective-permute-start.6 = (f32[10,2,8,128]{3,2,1,0:T(8,128)S(1)}, f32[10,2,8,128]{3,2,1,0:T(8,128)S(1)}, u32[]{:S(2)}, u32[]{:S(2)}) collective-permute-start(f32[10,2,8,128]{3,2,1,0:T(8,128)S(1)} %get-tuple-element.50), channel_id=1, source_target_pairs={{0,4},{1,2},{2,1},{3,7},{4,0},{5,6},{6,5},{7,3},{8,12},{9,10},{10,... | collective-permute-start | bytes 245768 | tf_op jit(solution)/shard_map/ppermute | solution.py:651
  16.2 3.6 %collective-permute-start.8 = (f32[8,128]{1,0:T(8,128)S(1)}, f32[8,128]{1,0:T(8,128)S(1)}, u32[]{:S(2)}, u32[]{:S(2)}) collective-permute-start(f32[8,128]{1,0:T(8,128)S(1)} %add.83), channel_id=1, source_target_pairs={{0,16},{1,17},{2,18},{3,19},{4,20},{5,21},{6,22},{7,23},{8,24},{9,... | collective-permute-start | bytes 12296 | tf_op jit(solution)/shard_map/ppermute | solution.py:661
  17.1 4.8 %collective-permute-start.5 = (f32[10,2,8,128]{3,2,1,0:T(8,128)S(1)}, f32[10,2,8,128]{3,2,1,0:T(8,128)S(1)}, u32[]{:S(2)}, u32[]{:S(2)}) collective-permute-start(f32[10,2,8,128]{3,2,1,0:T(8,128)S(1)} %get-tuple-element.49), channel_id=1, source_target_pairs={{0,1},{1,0},{2,3},{3,2},{4,5},{5,4},{6,7},{7,6},{8,9},{9,8},{10,11... | collective-permute-start | bytes 245768 | tf_op jit(solution)/shard_map/ppermute | solution.py:650
  22.0 0.7 %copy-start.7 = (f32[32,128]{1,0:T(8,128)S(1)}, f32[32,128]{1,0:T(8,128)}, u32[]{:S(2)}) copy-start(f32[32,128]{1,0:T(8,128)} %constant.52.clone) | copy-start | bytes 49156
  22.0 0.7 %copy-start.8 = (f32[32]{0:T(128)S(1)}, f32[32]{0:T(128)}, u32[]{:S(2)}) copy-start(f32[32]{0:T(128)} %constant.65) | copy-start | bytes 388
  22.1 4.7 %collective-permute-start.9 = (f32[17,8,128]{2,1,0:T(8,128)S(1)}, f32[17,8,128]{2,1,0:T(8,128)S(1)}, u32[]{:S(2)}, u32[]{:S(2)}) collective-permute-start(f32[17,8,128]{2,1,0:T(8,128)S(1)} %pad_maximum_fusion.3), channel_id=1, source_target_pairs={{0,28},{1,29},{2,30},{3,31},{4,8},{5,9},{6,10},{7,11},{8,4},{9,5},... | collective-permute-start | bytes 208904 | tf_op jit(solution)/shard_map/ppermute | solution.py:651
  22.9 3.9 %collective-permute-start.7 = (f32[2,8,8,128]{3,2,1,0:T(8,128)S(1)}, f32[2,8,8,128]{3,2,1,0:T(8,128)S(1)}, u32[]{:S(2)}, u32[]{:S(2)}) collective-permute-start(f32[2,8,8,128]{3,2,1,0:T(8,128)S(1)} %get-tuple-element.111), channel_id=1, source_target_pairs={{0,4},{1,5},{2,6},{3,7},{4,0},{5,1},{6,2},{7,3},{8,12},{9,13},{10,... | collective-permute-start | bytes 196616 | tf_op jit(solution)/shard_map/ppermute | solution.py:650
  27.7 4.3 %collective-permute-start.10 = (f32[17,8,128]{2,1,0:T(8,128)S(1)}, f32[17,8,128]{2,1,0:T(8,128)S(1)}, u32[]{:S(2)}, u32[]{:S(2)}) collective-permute-start(f32[17,8,128]{2,1,0:T(8,128)S(1)} %get-tuple-element.56), channel_id=1, source_target_pairs={{0,1},{1,0},{2,3},{3,2},{4,5},{5,4},{6,7},{7,6},{8,9},{9,8},{10,11... | collective-permute-start | bytes 208904 | tf_op jit(solution)/shard_map/ppermute | solution.py:650
  29.7 2.3 %collective-permute-start.11 = (f32[16,8,128]{2,1,0:T(8,128)S(1)}, f32[16,8,128]{2,1,0:T(8,128)S(1)}, u32[]{:S(2)}, u32[]{:S(2)}) collective-permute-start(f32[16,8,128]{2,1,0:T(8,128)S(1)} %get-tuple-element.57), channel_id=1, source_target_pairs={{0,4},{1,2},{2,1},{3,7},{4,0},{5,6},{6,5},{7,3},{8,12},{9,10},{10,... | collective-permute-start | bytes 196616 | tf_op jit(solution)/shard_map/ppermute | solution.py:651
  32.2 1.5 %collective-permute-start.12 = (f32[21,8,128]{2,1,0:T(8,128)S(1)}, f32[21,8,128]{2,1,0:T(8,128)S(1)}, u32[]{:S(2)}, u32[]{:S(2)}) collective-permute-start(f32[21,8,128]{2,1,0:T(8,128)S(1)} %pad_maximum_fusion), channel_id=1, source_target_pairs={{0,4},{1,5},{2,6},{3,7},{4,0},{5,1},{6,2},{7,3},{8,12},{9,13},{10,... | collective-permute-start | bytes 258056 | tf_op jit(solution)/shard_map/ppermute | solution.py:650
  32.3 5.3 %collective-permute-start.13 = (f32[2,10,8,128]{3,2,1,0:T(8,128)S(1)}, f32[2,10,8,128]{3,2,1,0:T(8,128)S(1)}, u32[]{:S(2)}, u32[]{:S(2)}) collective-permute-start(f32[2,10,8,128]{3,2,1,0:T(8,128)S(1)} %get-tuple-element.108), channel_id=1, source_target_pairs={{0,28},{1,29},{2,30},{3,31},{4,8},{5,9},{6,10},{7,11},{8,4},{9,5},... | collective-permute-start | bytes 245768 | tf_op jit(solution)/shard_map/ppermute | solution.py:651
  33.7 5.2 %collective-permute-start.14 = (f32[8,128]{1,0:T(8,128)S(1)}, f32[8,128]{1,0:T(8,128)S(1)}, u32[]{:S(2)}, u32[]{:S(2)}) collective-permute-start(f32[8,128]{1,0:T(8,128)S(1)} %fusion.21), channel_id=1, source_target_pairs={{0,2},{1,3},{2,0},{3,1},{4,6},{5,7},{6,4},{7,5},{8,10},{9,11},{10,... | collective-permute-start | bytes 12296 | tf_op jit(solution)/shard_map/ppermute | solution.py:661
  38.8 7.4 %collective-permute-start.16 = (f32[10,2,8,128]{3,2,1,0:T(8,128)S(1)}, f32[10,2,8,128]{3,2,1,0:T(8,128)S(1)}, u32[]{:S(2)}, u32[]{:S(2)}) collective-permute-start(f32[10,2,8,128]{3,2,1,0:T(8,128)S(1)} %get-tuple-element.63), channel_id=1, source_target_pairs={{0,4},{1,2},{2,1},{3,7},{4,0},{5,6},{6,5},{7,3},{8,12},{9,10},{10,... | collective-permute-start | bytes 245768 | tf_op jit(solution)/shard_map/ppermute | solution.py:651
  38.9 7.2 %collective-permute-start.15 = (f32[10,2,8,128]{3,2,1,0:T(8,128)S(1)}, f32[10,2,8,128]{3,2,1,0:T(8,128)S(1)}, u32[]{:S(2)}, u32[]{:S(2)}) collective-permute-start(f32[10,2,8,128]{3,2,1,0:T(8,128)S(1)} %get-tuple-element.62), channel_id=1, source_target_pairs={{0,1},{1,0},{2,3},{3,2},{4,5},{5,4},{6,7},{7,6},{8,9},{9,8},{10,11... | collective-permute-start | bytes 245768 | tf_op jit(solution)/shard_map/ppermute | solution.py:650
  42.5 3.6 %collective-permute-start.18 = (f32[8,128]{1,0:T(8,128)S(1)}, f32[8,128]{1,0:T(8,128)S(1)}, u32[]{:S(2)}, u32[]{:S(2)}) collective-permute-start(f32[8,128]{1,0:T(8,128)S(1)} %add.95), channel_id=1, source_target_pairs={{0,16},{1,17},{2,18},{3,19},{4,20},{5,21},{6,22},{7,23},{8,24},{9,... | collective-permute-start | bytes 12296 | tf_op jit(solution)/shard_map/ppermute | solution.py:661
  46.3 4.7 %collective-permute-start.19 = (f32[17,8,128]{2,1,0:T(8,128)S(1)}, f32[17,8,128]{2,1,0:T(8,128)S(1)}, u32[]{:S(2)}, u32[]{:S(2)}) collective-permute-start(f32[17,8,128]{2,1,0:T(8,128)S(1)} %pad_maximum_fusion.4), channel_id=1, source_target_pairs={{0,28},{1,29},{2,30},{3,31},{4,8},{5,9},{6,10},{7,11},{8,4},{9,5},... | collective-permute-start | bytes 208904 | tf_op jit(solution)/shard_map/ppermute | solution.py:651
  46.5 4.6 %collective-permute-start.17 = (f32[2,8,8,128]{3,2,1,0:T(8,128)S(1)}, f32[2,8,8,128]{3,2,1,0:T(8,128)S(1)}, u32[]{:S(2)}, u32[]{:S(2)}) collective-permute-start(f32[2,8,8,128]{3,2,1,0:T(8,128)S(1)} %get-tuple-element.107), channel_id=1, source_target_pairs={{0,4},{1,5},{2,6},{3,7},{4,0},{5,1},{6,2},{7,3},{8,12},{9,13},{10,... | collective-permute-start | bytes 196616 | tf_op jit(solution)/shard_map/ppermute | solution.py:650
  51.0 6.0 %copy-start.2 = (f32[1,1,8,8,8,128]{5,4,3,2,1,0:T(8,128)S(1)}, f32[1,1,8,8,8,128]{5,4,3,2,1,0:T(8,128)}, u32[]{:S(2)}) copy-start(f32[1,1,8,8,8,128]{5,4,3,2,1,0:T(8,128)} %param.10) | copy-start | bytes 786436
  52.6 11.2 %all-to-all-start = ((f32[32,4,128]{2,1,0:T(4,128)}), f32[32,4,128]{2,1,0:T(4,128)S(1)}, u32[]{:S(2)}, u32[]{:S(2)}) async-start(f32[32,4,128]{2,1,0:T(4,128)} %get-tuple-element.81), calls=%async_computation | async-start | bytes 131072 | tf_op jit(solution)/shard_map/all_to_all | solution.py:687
  55.2 4.2 %collective-permute-start.20 = (f32[8,8,128]{2,1,0:T(8,128)S(1)}, f32[8,8,128]{2,1,0:T(8,128)S(1)}, u32[]{:S(2)}, u32[]{:S(2)}) collective-permute-start(f32[8,8,128]{2,1,0:T(8,128)S(1)} %get-tuple-element.69), channel_id=1, source_target_pairs={{0,1},{1,0},{2,3},{3,2},{4,5},{5,4},{6,7},{7,6},{8,9},{9,8},{10,11... | collective-permute-start | bytes 98312 | tf_op jit(solution)/shard_map/ppermute | solution.py:650
  57.1 2.3 %collective-permute-start.21 = (f32[8,8,128]{2,1,0:T(8,128)S(1)}, f32[8,8,128]{2,1,0:T(8,128)S(1)}, u32[]{:S(2)}, u32[]{:S(2)}) collective-permute-start(f32[8,8,128]{2,1,0:T(8,128)S(1)} %get-tuple-element.70), channel_id=1, source_target_pairs={{0,4},{1,2},{2,1},{3,7},{4,0},{5,6},{6,5},{7,3},{8,12},{9,10},{10,... | collective-permute-start | bytes 98312 | tf_op jit(solution)/shard_map/ppermute | solution.py:651
  59.5 4.3 %collective-permute-start.23 = (f32[8,8,128]{2,1,0:T(8,128)S(1)}, f32[8,8,128]{2,1,0:T(8,128)S(1)}, u32[]{:S(2)}, u32[]{:S(2)}) collective-permute-start(f32[8,8,128]{2,1,0:T(8,128)S(1)} %get-tuple-element.127), channel_id=1, source_target_pairs={{0,28},{1,29},{2,30},{3,31},{4,8},{5,9},{6,10},{7,11},{8,4},{9,5},... | collective-permute-start | bytes 98312 | tf_op jit(solution)/shard_map/ppermute | solution.py:651
  61.0 2.8 %collective-permute-start.22 = (f32[8,8,128]{2,1,0:T(8,128)S(1)}, f32[8,8,128]{2,1,0:T(8,128)S(1)}, u32[]{:S(2)}, u32[]{:S(2)}) collective-permute-start(f32[8,8,128]{2,1,0:T(8,128)S(1)} %get-tuple-element.128), channel_id=1, source_target_pairs={{0,4},{1,5},{2,6},{3,7},{4,0},{5,1},{6,2},{7,3},{8,12},{9,13},{10,... | collective-permute-start | bytes 98312 | tf_op jit(solution)/shard_map/ppermute | solution.py:650

commit v5 on v4

--- a/solution.py
+++ b/solution.py
@@ -299,21 +299,27 @@
     return [sums[(i, j)] for i in range(3) for j in range(3)]
 
 
+def shared_class_tiles(field_ref, side_x, side_y):
+    tile = multiplicity_tile()
+    sums = {}
+    for a in range(NODES):
+        for b in range(NODES):
+            add_to(sums, (class_of(a), class_of(b)), field_ref[a, b])
+    for (i, j), value in sums.items():
+        a, b = (0, 1, NODES - 1)[i], (0, 1, NODES - 1)[j]
+        sums[(i, j)] = scaled(value * tile, axis_factor(a, side_x), axis_factor(b, side_y))
+    return class_tiles(sums)
+
+
 def start_kernel(counts, r_ref, sy_first, sy_second):
     side_x, side_y = Sides("gx", counts[0]), Sides("gy", counts[1])
-    tile = multiplicity_tile()
     for a in range(NODES):
         low, high = r_ref[a, 1], r_ref[a, NODES - 2]
         sy_first[a] = side_y.send_first(low, high)
         sy_second[a] = side_y.send_second(low, high)
-    sums = {}
-    for a in range(NODES):
-        for b in range(NODES):
-            add_to(sums, (class_of(a), class_of(b)), r_ref[a, b])
-    for (i, j), value in sums.items():
-        a, b = (0, 1, NODES - 1)[i], (0, 1, NODES - 1)[j]
-        sums[(i, j)] = scaled(value * tile, axis_factor(a, side_x), axis_factor(b, side_y))
-    sy_first[NODES] = summed_row(counts, class_tiles(sums), side_x, side_y)
+    sy_first[NODES] = summed_row(
+        counts, shared_class_tiles(r_ref, side_x, side_y), side_x, side_y
+    )
 
 
 def planes(ref):
@@ -374,8 +380,8 @@
 def send_parts(part_ref, side_x, side_y, sy_first, sy_second, fx_first, fx_second):
     for a in range(EXT):
         low, high = part_ref[a, 0:16], part_ref[a, 64:80]
-        sy_first[a] = side_y.send_first(low, high).reshape(2, NODES, 128)
-        sy_second[a] = side_y.send_second(low, high).reshape(2, NODES, 128)
+        sy_first[2 * a : 2 * a + 2] = side_y.send_first(low, high).reshape(2, NODES, 128)
+        sy_second[2 * a : 2 * a + 2] = side_y.send_second(low, high).reshape(2, NODES, 128)
     for layer in range(2):
         low, high = part_ref[layer, 0:80], part_ref[NODES + layer, 0:80]
         fx_first[layer] = side_x.send_first(low, high).reshape(EXT, NODES, 128)
@@ -383,10 +389,11 @@
 
 
 def first_solve_kernel(
-    counts, r_ref, grains_ref, ry_first, ry_second, rx_first, rx_second, forward_ref, back_ref,
-    inverse_ref, part_ref, sy_first, sy_second, fx_first, fx_second, porosity_ref, x_ref,
+    counts, r_ref, porosity_ref, ry_first, ry_second, rx_first, rx_second, forward_ref, back_ref,
+    inverse_ref, part_ref, sy_first, sy_second, fx_first, fx_second, x_ref,
 ):
-    porosity_ref[...] = 1.0 - 0.6 * grains_ref[...].astype(jnp.float32) / MOST_GRAINS
+    for send in (sy_first, sy_second):
+        send[2 * EXT] = jnp.broadcast_to(porosity_ref[...], (NODES, 128))
     side_x, side_y = Sides("gx", counts[0]), Sides("gy", counts[1])
     x_ref[0, 0:80] = side_x.low(rx_first[...], rx_second[...]).reshape(80, 128)
     x_ref[EXT - 1, 0:80] = side_x.high(rx_first[...], rx_second[...]).reshape(80, 128)
@@ -403,10 +410,48 @@
     q_ref, part_ref, sy_first, sy_second, fx_first, fx_second, x_ref,
 ):
     side_x, side_y = Sides("gx", counts[0]), Sides("gy", counts[1])
+    extend_image(
+        u_ref, ry_first, ry_second, rx_first, rx_second, side_x, side_y, q_ref, x_ref, None
+    )
+    local_solve(x_ref, forward_ref, back_ref, inverse_ref, part_ref)
+    send_parts(part_ref, side_x, side_y, sy_first, sy_second, fx_first, fx_second)
+
+
+def late_solve_kernel(
+    counts, u_ref, ry_first, ry_second, rx_first, rx_second, columns_ref, lift_ref, sum_ref,
+    forward_ref, back_ref, inverse_ref, q_ref, part_ref, sy_first, sy_second, fx_first, fx_second,
+    field_ref, x_ref, table_ref,
+):
+    side_x, side_y = Sides("gx", counts[0]), Sides("gy", counts[1])
+    table_ref[...] = jnp.broadcast_to(
+        jnp.sum(lift_ref[...] * sum_ref[0:1], axis=1, keepdims=True), table_ref.shape
+    )
+    fields = near_fields(counts, table_ref, side_x, side_y)
+    own = fields[(1, 1)]
+    field_ref[...] = jnp.concatenate(
+        [own[i][j] for i in range(3) for j in range(3)] + [jnp.zeros((7, 128), jnp.float32)]
+    )
+    image = LiftedImage(fields, columns_ref)
+    extend_image(
+        u_ref, ry_first, ry_second, rx_first, rx_second, side_x, side_y, q_ref, x_ref, image
+    )
+    local_solve(x_ref, forward_ref, back_ref, inverse_ref, part_ref)
+    send_parts(part_ref, side_x, side_y, sy_first, sy_second, fx_first, fx_second)
+
+
+def extend_image(
+    u_ref, ry_first, ry_second, rx_first, rx_second, side_x, side_y, q_ref, x_ref, image
+):
     low_x = side_x.low(rx_first[...], rx_second[...])
     high_x = side_x.high(rx_first[...], rx_second[...])
-    x_ref[0, 0:80] = low_x[0].reshape(80, 128)
-    x_ref[EXT - 1, 0:80] = high_x[1].reshape(80, 128)
+
+    def lifted(value, a, b):
+        return value if image is None else value + image.at(a - 1, b - 1)
+
+    for b in range(EXT):
+        rows = pl.ds(b * 8, 8)
+        x_ref[0, rows] = lifted(low_x[0, b], 0, b)
+        x_ref[EXT - 1, rows] = lifted(high_x[1, b], EXT - 1, b)
     for a in range(NODES):
         low_y = side_y.low(ry_first[a], ry_second[a])
         high_y = side_y.high(ry_first[a], ry_second[a])
@@ -425,11 +470,10 @@
                 value = value + low_x[1, b]
             if a == NODES - 1:
                 value = value + high_x[0, b]
+            value = lifted(value, a + 1, b)
             x_ref[a + 1, b * 8 : b * 8 + 8] = value
             if 0 < b < EXT - 1:
                 q_ref[a, b - 1] = value
-    local_solve(x_ref, forward_ref, back_ref, inverse_ref, part_ref)
-    send_parts(part_ref, side_x, side_y, sy_first, sy_second, fx_first, fx_second)
 
 
 def collect_parts(part_ref, ry_first, ry_second, rx_first, rx_second, side_x, side_y, field):
@@ -449,8 +493,10 @@
                 value = value + low_x[a, b]
             if a >= NODES - 2:
                 value = value + high_x[a - (NODES - 2), b]
-            node_class = 3 * class_of(a) + class_of(b)
-            result[(a, b)] = value + field[node_class : node_class + 1, :]
+            if field is not None:
+                node_class = 3 * class_of(a) + class_of(b)
+                value = value + field[node_class : node_class + 1, :]
+            result[(a, b)] = value
     return result
 
 
@@ -489,7 +535,7 @@
 
 def first_apply_kernel(
     counts, part_ref, ry_first, ry_second, rx_first, rx_second, sum_ref, lift_ref, porosity_ref,
-    r_ref, z_ref, u_ref, sy_first, sy_second, fx_first, fx_second, y_ref,
+    r_ref, z_ref, u_ref, sy_first, sy_second, fx_first, fx_second, tile_ref, y_ref,
 ):
     side_x, side_y = Sides("gx", counts[0]), Sides("gy", counts[1])
     field = lifted_rows(counts, row_of(counts, sum_ref), lift_ref)
@@ -510,17 +556,9 @@
             term = value * z_ref[a, b]
             curvature = term if curvature is None else curvature + term
     tiles = class_tiles(sums) + [inner, curvature]
-    sy_first[2 * NODES] = summed_row(counts, tiles, side_x, side_y)
+    tile_ref[...] = summed_row(counts, tiles, side_x, side_y)
     sum_column(u_ref)
-    for a in range(NODES):
-        for layer in range(2):
-            low, high = u_ref[a, layer], u_ref[a, NODES - 2 + layer]
-            sy_first[2 * a + layer] = side_y.send_first(low, high)
-            sy_second[2 * a + layer] = side_y.send_second(low, high)
-    for layer in range(2):
-        low, high = u_ref[layer], u_ref[NODES - 2 + layer]
-        fx_first[layer] = side_x.send_first(low, high)
-        fx_second[layer] = side_x.send_second(low, high)
+    send_layers(u_ref, side_x, side_y, sy_first, sy_second, fx_first, fx_second)
 
 
 def second_apply_kernel(
@@ -561,6 +599,259 @@
     fx_second[...] = side_x.send_second(low, high)
 
 
+def send_layers(u_ref, side_x, side_y, sy_first, sy_second, fx_first, fx_second):
+    for a in range(NODES):
+        for layer in range(2):
+            low, high = u_ref[a, layer], u_ref[a, NODES - 2 + layer]
+            sy_first[2 * a + layer] = side_y.send_first(low, high)
+            sy_second[2 * a + layer] = side_y.send_second(low, high)
+    for layer in range(2):
+        low, high = u_ref[layer], u_ref[NODES - 2 + layer]
+        fx_first[layer] = side_x.send_first(low, high)
+        fx_second[layer] = side_x.send_second(low, high)
+
+
+def early_apply_kernel(
+    counts, part_ref, ry_first, ry_second, rx_first, rx_second, porosity_ref,
+    z_ref, u_ref, sy_first, sy_second, fx_first, fx_second, y_ref,
+):
+    side_x, side_y = Sides("gx", counts[0]), Sides("gy", counts[1])
+    z = collect_parts(part_ref, ry_first, ry_second, rx_first, rx_second, side_x, side_y, None)
+    for (a, b), value in z.items():
+        z_ref[a, b] = value
+    apply_tiles(z_ref, u_ref, y_ref, porosity_ref[...])
+    sum_column(u_ref)
+    send_layers(u_ref, side_x, side_y, sy_first, sy_second, fx_first, fx_second)
+
+
+def late_apply_kernel(
+    counts, part_ref, ry_first, ry_second, rx_first, rx_second, porosity_ref, r_ref, q_ref,
+    schwarz_ref, field_ref, z_ref, w_ref, u_ref, sy_first, sy_second, fx_first, fx_second,
+    stats_ref, y_ref,
+):
+    side_x, side_y = Sides("gx", counts[0]), Sides("gy", counts[1])
+    w = collect_parts(part_ref, ry_first, ry_second, rx_first, rx_second, side_x, side_y, None)
+    inner = first_inner = first_curvature = None
+    for (a, b), value in w.items():
+        w_ref[a, b] = value
+        node_class = 3 * class_of(a) + class_of(b)
+        z = schwarz_ref[a, b] + field_ref[node_class : node_class + 1, :]
+        z_ref[a, b] = z
+        q = q_ref[a, b]
+        factors = (axis_factor(a, side_x), axis_factor(b, side_y))
+        terms = [scaled(t, *factors) for t in (value * q, z * r_ref[a, b], z * q)]
+        if inner is None:
+            inner, first_inner, first_curvature = terms
+        else:
+            inner, first_inner, first_curvature = (
+                inner + terms[0], first_inner + terms[1], first_curvature + terms[2]
+            )
+    tile = multiplicity_tile()
+    inner, first_inner, first_curvature = inner * tile, first_inner * tile, first_curvature * tile
+    porosity = porosity_ref[...]
+    apply_tiles(w_ref, u_ref, y_ref, porosity)
+    sums = {}
+    own = None
+    for a in range(NODES):
+        for b in range(NODES):
+            value = u_ref[a, b]
+            add_to(sums, (class_of(a), class_of(b)), value)
+            term = value * w_ref[a, b]
+            own = term if own is None else own + term
+    total = counts[0] * counts[1]
+    tiles = class_tiles(sums) + [inner, own, porosity]
+    first_tiles = shared_class_tiles(q_ref, side_x, side_y) + [first_inner, first_curvature]
+    row = summed_row(counts, first_tiles, side_x, side_y)[0:1] + pltpu.roll(
+        summed_row(counts, tiles, side_x, side_y), total + 2, 1
+    )[0:1]
+    for index in range(stats_ref.shape[0]):
+        stats_ref[index] = jnp.broadcast_to(row, stats_ref.shape[1:])
+    sum_column(u_ref)
+    for a in range(NODES):
+        low, high = u_ref[a, 0], u_ref[a, NODES - 1]
+        sy_first[a] = side_y.send_first(low, high)
+        sy_second[a] = side_y.send_second(low, high)
+    low, high = u_ref[0], u_ref[NODES - 1]
+    fx_first[...] = side_x.send_first(low, high)
+    fx_second[...] = side_x.send_second(low, high)
+
+
+def porosity_kernel(counts, low_ref, own_ref, high_ref, out_ref):
+    row = lax.broadcasted_iota(jnp.int32, (NODES, 128), 0)
+    weights = row_tile(WEIGHTS)
+    mass = shift_mass * weights / multiplicity_tile()
+    end = float(WEIGHTS[0])
+    for x, ref in enumerate((low_ref, own_ref, high_ref)):
+        for y in range(3):
+            porosity = ref[y : y + 1]
+            tile = porosity * weights
+            tile = tile + jnp.where(row == 0, end * shift_up(porosity), 0.0)
+            tile = tile + jnp.where(row == NODES - 1, end * shift_down(porosity), 0.0)
+            out_ref[3 * x + y] = tile
+            out_ref[9 + 3 * x + y] = jnp.where(porosity > 0.0, mass, 0.0)
+
+
+CLASS_STIFF = np.stack(
+    [STIFF[:, 0], STIFF[:, 1 : NODES - 1].sum(axis=1), STIFF[:, NODES - 1]], axis=1
+)
+CLASS_ENDS = np.stack(
+    [CLASS_STIFF[0], CLASS_STIFF[1 : NODES - 1].sum(axis=0), CLASS_STIFF[NODES - 1]]
+)
+CLASS_WEIGHTS = np.array([WEIGHTS[0], WEIGHTS[1 : NODES - 1].sum(), WEIGHTS[NODES - 1]])
+
+
+def combine(coefficients, values):
+    total = None
+    for coefficient, value in zip(coefficients, values):
+        term = value * float(coefficient)
+        total = term if total is None else total + term
+    return total
+
+
+def sharing(node):
+    return {
+        -1: [(0, NODES - 2)], 0: [(1, 0), (0, NODES - 1)],
+        NODES - 1: [(1, NODES - 1), (2, 0)], NODES: [(2, 1)],
+    }.get(node, [(1, node)])
+
+
+class LiftedImage:
+    def __init__(self, fields, columns_ref):
+        self.fields, self.columns, self.known = fields, columns_ref, {}
+
+    def along(self, column, place, other_class, axis):
+        key = (column, place, other_class, axis)
+        if key not in self.known:
+            field = self.fields[column]
+            line = [
+                field[i][other_class] if axis == 0 else field[other_class][i] for i in range(3)
+            ]
+            self.known[key] = combine(CLASS_STIFF[place], line)
+        return self.known[key]
+
+    def at(self, a, b):
+        total = None
+        for i, place_a in sharing(a):
+            for j, place_b in sharing(b):
+                class_a, class_b = class_of(place_a), class_of(place_b)
+                stiff = self.along((i, j), place_a, class_b, 0) * float(WEIGHTS[place_b])
+                stiff = stiff + self.along((i, j), place_b, class_a, 1) * float(WEIGHTS[place_a])
+                mass = self.fields[(i, j)][class_a][class_b]
+                mass = mass * float(WEIGHTS[place_a] * WEIGHTS[place_b])
+                term = stiff * self.columns[3 * i + j] + mass * self.columns[9 + 3 * i + j]
+                total = term if total is None else total + term
+        return total
+
+
+def near_fields(counts, table_ref, side_x, side_y):
+    total = counts[0] * counts[1]
+
+    def field_of(step_x, step_y):
+        x = jnp.clip(side_x.index + step_x, 0, counts[0] - 1)
+        y = jnp.clip(side_y.index + step_y, 0, counts[1] - 1)
+        place = x * counts[1] + y
+        return [
+            [table_ref[pl.ds((3 * i + j) * total + place, 1), :] for j in range(3)]
+            for i in range(3)
+        ]
+
+    return {(i, j): field_of(i - 1, j - 1) for i in range(3) for j in range(3)}
+
+
+def lifted_energy(counts, table_ref, porosity_sums, length):
+    total = counts[0] * counts[1]
+    field = [
+        [table_ref[pl.ds((3 * i + j) * total, total), :] for j in range(3)] for i in range(3)
+    ]
+
+    def line(values):
+        terms = []
+        for i, j in ((0, 1), (0, 2), (1, 2)):
+            difference = values[i] - values[j]
+            terms.append(difference * difference * float(-CLASS_ENDS[i, j]))
+        return terms[0] + terms[1] + terms[2]
+
+    stiff = None
+    mass = None
+    for i in range(3):
+        term = line(field[i]) * float(CLASS_WEIGHTS[i])
+        term = term + line([field[j][i] for j in range(3)]) * float(CLASS_WEIGHTS[i])
+        stiff = term if stiff is None else stiff + term
+        for j in range(3):
+            term = field[i][j] * field[i][j] * float(CLASS_WEIGHTS[i] * CLASS_WEIGHTS[j])
+            mass = term if mass is None else mass + term
+    energy = stiff * porosity_sums * 2.0 + mass * (shift_mass * 2.0 * length)
+    return jnp.sum(energy, axis=0, keepdims=True)
+
+
+def late_final_kernel(
+    counts, sol_ref, r_ref, q_ref, z_ref, w_ref, u_ref, ry_first, ry_second, rx_first, rx_second,
+    columns_ref, lift_ref, stats_ref, sol_out, r_out, d_out, steps_out, table_ref,
+):
+    side_x, side_y = Sides("gx", counts[0]), Sides("gy", counts[1])
+    total = counts[0] * counts[1]
+    stats = stats_ref[:, 0, :]
+    summed = jnp.sum(stats, axis=0, keepdims=True)
+    table_ref[...] = jnp.broadcast_to(
+        jnp.sum(lift_ref[...] * summed, axis=1, keepdims=True), table_ref.shape
+    )
+    column = lax.broadcasted_iota(jnp.int32, (total, 128), 0)
+    lane = lax.broadcasted_iota(jnp.int32, (total, 128), 1)
+    at = 2 * total + 2
+    porosity_sums = jnp.sum(
+        jnp.where(lane == at + 2, stats, 0.0), axis=1, keepdims=True
+    )
+    coarse = table_ref[pl.ds(4 * total, total), :]
+
+    def product(first):
+        chosen = jnp.where(lane == column + first, coarse * summed, 0.0)
+        return jnp.sum(jnp.sum(chosen, axis=0, keepdims=True), axis=1, keepdims=True)
+
+    def value(index):
+        return jnp.sum(jnp.where(lane[0:1] == index, summed, 0.0), axis=1, keepdims=True)
+
+    first_inner, first_curvature = value(total), value(total + 1)
+    cross = value(at) + product(0)
+    energy = value(at + 1) + 2.0 * product(total + 2) + lifted_energy(
+        counts, table_ref, porosity_sums, sol_ref.shape[-1]
+    )
+    first_step = first_inner / first_curvature
+    second_inner = first_step * first_step * cross - first_inner
+    ratio = second_inner / first_inner
+    mixed = first_curvature - first_step * cross
+    own = first_curvature - 2.0 * first_step * cross + first_step * first_step * energy
+    second_step = second_inner / (own + ratio * (2.0 * mixed + ratio * first_curvature))
+    first_step, second_step, ratio = (
+        jnp.broadcast_to(scalar[:, 0:1], (1, 128)) for scalar in (first_step, second_step, ratio)
+    )
+    steps_out[0] = first_step[0, 0]
+    steps_out[1] = second_step[0, 0]
+
+    fields = near_fields(counts, table_ref, side_x, side_y)
+    lifted_image = LiftedImage(fields, columns_ref)
+    low_x = side_x.low(rx_first[...], rx_second[...])
+    high_x = side_x.high(rx_first[...], rx_second[...])
+    for a in range(NODES):
+        for b in range(NODES):
+            image = u_ref[a, b]
+            if b == 0:
+                image = image + side_y.low(ry_first[a], ry_second[a])
+            if b == NODES - 1:
+                image = image + side_y.high(ry_first[a], ry_second[a])
+            if a == 0:
+                image = image + low_x[b]
+            if a == NODES - 1:
+                image = image + high_x[b]
+            lifted = fields[(1, 1)][class_of(a)][class_of(b)]
+            image = image + lifted_image.at(a, b)
+            z, q = z_ref[a, b], q_ref[a, b]
+            direction = z - first_step * (w_ref[a, b] + lifted) + ratio * z
+            image = q - first_step * image + ratio * q
+            d_out[a, b] = direction
+            sol_out[a, b] = sol_ref[a, b] + first_step * z + second_step * direction
+            r_out[a, b] = r_ref[a, b] - first_step * q - second_step * image
+
+
 def prepare_kernel(counts, sol_ref, r_ref, q_ref, z_ref, sum_ref, sol_out, r_out):
     summed = row_of(counts, sum_ref)
     step = row_value(counts, summed, 0) / row_value(counts, summed, 1)
@@ -606,7 +897,7 @@
 
 COSTS = {
     "start": 100, "first_solve": 1300, "second_solve": 1300, "first_apply": 800,
-    "second_apply": 800, "prepare": 20000, "final": 500,
+    "second_apply": 800, "prepare": 20000, "final": 500, "late_apply": 800, "porosity": 20000, "late_final": 800,
 }
 
 
@@ -662,9 +953,9 @@
 
 
 class RunningSum:
-    def __init__(self, counts, tile):
+    def __init__(self, counts, tile, carried):
         self.counts = counts
-        self.carried = counts == (8, 4)
+        self.carried = carried
         self.value = tile if self.carried else lax.psum(tile, AXES)
 
     def add(self, received):
@@ -703,6 +994,18 @@
     return [table.astype(np.float32) for table in (modes_x, modes_y, 1.0 / divisor, to_modes)]
 
 
+def all_lift(counts, column_length):
+    modes_x, modes_y, inverse, to_modes = lift_tables(counts, column_length)
+    total = counts[0] * counts[1]
+    lift = np.einsum(
+        "xia,yjb,ab,abl->ijxyl", *(
+            table.astype(np.float64)
+            for table in (modes_x, modes_y, inverse, to_modes.reshape(inverse.shape + (-1,)))
+        ),
+    )
+    return jnp.asarray(lift.reshape(9 * total, -1).astype(np.float32))
+
+
 def own_lift(tables):
     modes_x, modes_y, inverse, to_modes = [jnp.asarray(table) for table in tables]
     own_x = lax.dynamic_index_in_dim(modes_x, lax.axis_index("gx"), 0, keepdims=False)
@@ -721,22 +1024,26 @@
         solution = solution.reshape(block)
         residual = residual.reshape(block)
         lift = own_lift(lift_tables(counts, block[-1]))
-        grains = grain_counts.reshape(1, 128)
+        late = counts == (8, 4)
+        every_lift = all_lift(counts, block[-1]) if late else None
+        porosity = 1.0 - 0.6 * grain_counts.reshape(1, 128).astype(jnp.float32) / MOST_GRAINS
         plane = [jnp.asarray(table) for table in (forward_np, back_np, inverse_np)]
         side_x, side_y = Sides("gx", counts[0]), Sides("gy", counts[1])
         row = (counts[0] * counts[1], 4, 128)
         face = (NODES, NODES, 128)
         part_shapes = [
             (EXT, ROWS, 128),
-            (EXT, 2, NODES, 128), (EXT, 2, NODES, 128),
+            (2 * EXT, NODES, 128), (2 * EXT, NODES, 128),
             (2, EXT, NODES, 128), (2, EXT, NODES, 128),
         ]
+        first_shapes = list(part_shapes)
+        first_shapes[1:3] = [(2 * EXT + 1, NODES, 128)] * 2
         solve_scratch = [(EXT, ROWS, 128)]
 
         y_first, y_second = call(
             start_kernel, counts, "start", [(NODES + 1,) + face[1:], face], [], residual
         )
-        running = RunningSum(counts, y_first[-1])
+        running = RunningSum(counts, y_first[-1], late)
         ry = trade(counts, 1, y_first, y_second)
         ry_first, tile = carried(ry[0], face)
         running.add(tile)
@@ -754,10 +1061,9 @@
         rx_first, tile = carried(rx[0], low_face.shape)
         running.add(tile)
         rx = (rx_first, rx[1])
-        far = running.far((0, 2))
-        part, y_first, y_second, *fx, porosity = call(
-            first_solve_kernel, counts, "first_solve", part_shapes + [(1, 128)], solve_scratch,
-            residual, grains, *ry, *rx, *plane,
+        part, y_first, y_second, *fx = call(
+            first_solve_kernel, counts, "first_solve", first_shapes, solve_scratch,
+            residual, porosity, *ry, *rx, *plane,
         )
 
         def spread_faces(fx, ry):
@@ -772,33 +1078,62 @@
                 fx[1][:, 1:-1] + side_x.send_second(*both),
             )
 
-        def trade_spread(y_first, y_second, fx, running, far):
-            y_first, far = lax.optimization_barrier((y_first, far))
-            for value in far:
-                running.add(value)
+        def trade_y(y_first, y_second, shape):
+            count = math.prod(shape[:-2])
             ry = trade(counts, 1, y_first, y_second)
-            for value in running.far((4, 0)):
-                running.add(value)
-            first, second = spread_faces(fx, ry)
-            rx = trade(counts, 0, first, carry(second, running))
-            rx_second, tile = carried(rx[1], second.shape)
-            running.add(tile)
-            return ry, (rx[0], rx_second)
-
-        ry, rx = trade_spread(y_first, y_second, fx, running, far)
-        z, u, y_first, y_second, *fx = call(
-            first_apply_kernel, counts, "first_apply",
-            [block, block, (2 * NODES + 1, NODES, 128), (2 * NODES, NODES, 128),
-             (2, NODES, NODES, 128), (2, NODES, NODES, 128)],
-            [block],
-            part, *ry, *rx, running.value, lift, porosity, residual,
+            faces = [value[:count].reshape(shape) for value in ry]
+            return faces, [value[count:] for value in ry]
+
+        ext_face = (EXT, 2, NODES, 128)
+        two = (NODES, 2, NODES, 128)
+        tiles = (-1, NODES, 128)
+        middle = jnp.broadcast_to(porosity, (1, NODES, 128))
+        if late:
+            y_second = jnp.concatenate([y_second, running.value[None]])
+            ry, rows = trade_y(y_first, y_second, ext_face)
+            inner_y = (side_y.index > 0) & (side_y.index < counts[1] - 1)
+            running.add(jnp.where(inner_y, rows[1][1], 0.0))
+        else:
+            ry, rows = trade_y(y_first, y_second, ext_face)
+        three = jnp.concatenate(
+            [
+                side[0, 0:1]
+                for side in (
+                    side_y.low(rows[0][:1], rows[1][:1]), middle,
+                    side_y.high(rows[0][:1], rows[1][:1]),
+                )
+            ]
+            + [jnp.zeros((NODES - 3, 128), jnp.float32)]
         )
-        running = RunningSum(counts, y_first[-1])
-        ry = trade(counts, 1, y_first, y_second)
-        two = (NODES, 2, NODES, 128)
-        ry_first, tile = carried(ry[0], two)
-        running.add(tile)
-        ry = (ry_first, ry[1].reshape(two))
+        first, second = spread_faces(fx, ry)
+        rx = trade(
+            counts, 0, jnp.concatenate([first.reshape(tiles), three[None]]),
+            jnp.concatenate([second.reshape(tiles), three[None], running.value[None]]),
+        )
+        count = 2 * NODES
+        threes = [value[count] for value in rx]
+        running.add(rx[1][count + 1])
+        rx = [value[:count].reshape(first.shape) for value in rx]
+        if late:
+            z, u, y_first, y_second, *fx = call(
+                early_apply_kernel, counts, "first_apply",
+                [block, block, (2 * NODES, NODES, 128), (2 * NODES, NODES, 128),
+                 (2, NODES, NODES, 128), (2, NODES, NODES, 128)],
+                [block],
+                part, *ry, *rx, porosity,
+            )
+            y_first = jnp.concatenate([y_first, running.value[None]])
+        else:
+            z, u, y_first, y_second, *fx, tile = call(
+                first_apply_kernel, counts, "first_apply",
+                [block, block, (2 * NODES, NODES, 128), (2 * NODES, NODES, 128),
+                 (2, NODES, NODES, 128), (2, NODES, NODES, 128), (NODES, 128)],
+                [block],
+                part, *ry, *rx, running.value, lift, porosity, residual,
+            )
+        ry, rows = trade_y(y_first, y_second, two)
+        if late:
+            running.value = jnp.where(inner_y, running.value, rows[0][0])
         low_y, high_y = side_y.low(*ry), side_y.high(*ry)
 
         def image_faces(index):
@@ -807,46 +1142,75 @@
 
         pads = ((0, 0), (1, 1), (0, 0), (0, 0))
         both = (image_faces(slice(0, 2)), image_faces(slice(NODES - 2, NODES)))
-        first = jnp.pad(fx[0], pads) + side_x.send_first(*both)
-        second = jnp.pad(fx[1], pads) + side_x.send_second(*both)
-        rx = trade(counts, 0, carry(first, running), second)
-        rx_first, tile = carried(rx[0], first.shape)
-        running.add(tile)
-        rx = (rx_first, rx[1])
-        far = running.far((0, 2))
-        q, part, y_first, y_second, *fx = call(
-            second_solve_kernel, counts, "second_solve", [block] + part_shapes, solve_scratch,
-            u, *ry, *rx, *plane,
+        rx = trade(
+            counts, 0,
+            jnp.pad(fx[0], pads) + side_x.send_first(*both),
+            jnp.pad(fx[1], pads) + side_x.send_second(*both),
         )
-        ry, rx = trade_spread(y_first, y_second, fx, running, far)
-        z1, u, y_first, y_second, *fx, stats = call(
-            second_apply_kernel, counts, "second_apply",
-            [block, block, face, face, face, face, row],
-            [block],
-            part, *ry, *rx, running.value, lift, porosity, residual, q, z,
-        )
-        next_solution, next_residual = call(
-            prepare_kernel, counts, "prepare", [block] * 2, [],
-            solution, residual, q, z, running.value,
-        )
-        ry, next_solution, next_residual = lax.optimization_barrier(
-            (trade(counts, 1, y_first, y_second), next_solution, next_residual)
-        )
-        low_y, high_y = side_y.low(*ry), side_y.high(*ry)
-
-        def edge_rows(index):
-            middle = jnp.zeros((NODES - 2, NODES, 128), jnp.float32)
-            return jnp.concatenate([low_y[index][None], middle, high_y[index][None]])
-
-        both = (edge_rows(0), edge_rows(NODES - 1))
-        rx = trade(
-            counts, 0, fx[0] + side_x.send_first(*both), fx[1] + side_x.send_second(*both)
-        )
-        last_stats = gather_stats(stats)
-        solution_out, residual_out, direction, steps = call(
-            final_kernel, counts, "final", [block] * 3 + [(2,)], [],
-            next_solution, next_residual, q, z, z1, u, *ry, *rx, running.value, last_stats,
-        )
+        if late:
+            (columns,) = call(
+                porosity_kernel, counts, "porosity", [(18, NODES, 128)], [],
+                side_x.low(*threes), three, side_x.high(*threes),
+            )
+            rx, far, columns = lax.optimization_barrier((rx, running.far((4, 0)), columns))
+            for value in far:
+                running.add(value)
+            table = (9 * counts[0] * counts[1], 128)
+            q, part, y_first, y_second, *fx, field = call(
+                late_solve_kernel, counts, "second_solve", [block] + part_shapes + [(16, 128)],
+                solve_scratch + [table],
+                u, *ry, *rx, columns, every_lift, running.value, *plane,
+            )
+        else:
+            q, part, y_first, y_second, *fx = call(
+                second_solve_kernel, counts, "second_solve", [block] + part_shapes, solve_scratch,
+                u, *ry, *rx, *plane,
+            )
+        ry, _ = trade_y(y_first, y_second, ext_face)
+        rx = trade(counts, 0, *spread_faces(fx, ry))
+
+        def trade_edges(y_first, y_second, fx, beside):
+            ry, beside = lax.optimization_barrier((trade(counts, 1, y_first, y_second), beside))
+            low_y, high_y = side_y.low(*ry), side_y.high(*ry)
+
+            def edge_rows(index):
+                middle = jnp.zeros((NODES - 2, NODES, 128), jnp.float32)
+                return jnp.concatenate([low_y[index][None], middle, high_y[index][None]])
+
+            both = (edge_rows(0), edge_rows(NODES - 1))
+            rx = trade(
+                counts, 0, fx[0] + side_x.send_first(*both), fx[1] + side_x.send_second(*both)
+            )
+            return ry, rx, beside
+
+        if late:
+            z, w, u, y_first, y_second, *fx, stats = call(
+                late_apply_kernel, counts, "late_apply",
+                [block, block, block, face, face, face, face, row], [block],
+                part, *ry, *rx, porosity, residual, q, z, field,
+            )
+            ry, rx, _ = trade_edges(y_first, y_second, fx, [])
+            solution_out, residual_out, direction, steps = call(
+                late_final_kernel, counts, "late_final", [block] * 3 + [(2,)], [table],
+                solution, residual, q, z, w, u, *ry, *rx, columns, every_lift,
+                gather_stats(stats),
+            )
+        else:
+            summed = lax.psum(tile, AXES)
+            z1, u, y_first, y_second, *fx, stats = call(
+                second_apply_kernel, counts, "second_apply",
+                [block, block, face, face, face, face, row], [block],
+                part, *ry, *rx, summed, lift, porosity, residual, q, z,
+            )
+            nexts = call(
+                prepare_kernel, counts, "prepare", [block] * 2, [],
+                solution, residual, q, z, summed,
+            )
+            ry, rx, nexts = trade_edges(y_first, y_second, fx, nexts)
+            solution_out, residual_out, direction, steps = call(
+                final_kernel, counts, "final", [block] * 3 + [(2,)], [],
+                *nexts, q, z, z1, u, *ry, *rx, summed, gather_stats(stats),
+            )
         return (
             solution_out.reshape(shard_shape),
             residual_out.reshape(shard_shape),

time: 65.4 us -> 63.4 us (0.969)
  starting transfers between devices: 32.3 us -> 25.8 us
  waiting for transfers between devices: 21.2 us -> 27.5 us
  local copies, waits for them, and re-layouts: 3.62 us -> 1.9 us
    ppermute x4 -> x1, starting transfers between devices: 7.47 us -> 0.85 us  [trade_far(): return lax.ppermute(value, AXES, pairs)]
    all_to_all x1, waiting for transfers between devices: 0.01 us -> 2.99 us  [gather_stats(): return lax.all_to_all(stats, AXES, 0, 0)]
    ppermute x10, waiting for transfers between devices: 7.72 us -> 10.5 us  [trade(): lax.ppermute(first, AXES, swap_pairs(counts, axis, 0))]
    ppermute x10, waiting for transfers between devices: 10.5 us -> 12.7 us  [trade(): lax.ppermute(second, AXES, swap_pairs(counts, axis, 1))]
    ppermute x10, starting transfers between devices: 15.6 us -> 13.4 us  [trade(): lax.ppermute(first, AXES, swap_pairs(counts, axis, 0))]
    ppermute x4 -> x1, waiting for transfers between devices: 2.92 us -> 1.28 us  [trade_far(): return lax.ppermute(value, AXES, pairs)]
    ppermute x10, starting transfers between devices: 6.63 us -> 8.2 us  [trade(): lax.ppermute(second, AXES, swap_pairs(counts, axis, 1))]
    mul x3 -> x0, local copies, waits for them, and re-layouts: 1.45 us -> none  [own_lift(): own_x[:, None, :, None] * own_y[None, :, None, :] * inverse[None, None]]
  transfers between devices with their start and end apart: 25 -> 22, of which waited for: 11 -> 12; matrix products, arithmetic and copies ran while one was open for 3% -> 1% of each run, Pallas kernels for 4% -> 0%
where the time goes in v5:
time: 63.4 us; the launch traced here: 63.2 us
  waiting for transfers between devices  27.5 us (43%)
  starting transfers between devices  25.8 us (41%)
  Pallas kernels  6.47 us (10%)
  local copies, waits for them, and re-layouts  1.9 us (3%)
  between operations  0.99 us (2%)
    ppermute x10, starting transfers between devices, trade(): lax.ppermute(first, AXES, swap_pairs(counts, axis, 0))  13.4 us
    ppermute x10, waiting for transfers between devices, trade(): lax.ppermute(second, AXES, swap_pairs(counts, axis, 1))  12.7 us
    ppermute x10, waiting for transfers between devices, trade(): lax.ppermute(first, AXES, swap_pairs(counts, axis, 0))  10.5 us
    ppermute x10, starting transfers between devices, trade(): lax.ppermute(second, AXES, swap_pairs(counts, axis, 1))  8.2 us
    pallas_call x7, Pallas kernels, call(): pl.pallas_call(body, name=name, out_shape=[jax.ShapeDtypeStruct(shape, jn...  6.47 us
    all_to_all x1, starting transfers between devices, gather_stats(): return lax.all_to_all(stats, AXES, 0, 0)  3.38 us
    all_to_all x1, waiting for transfers between devices, gather_stats(): return lax.all_to_all(stats, AXES, 0, 0)  2.99 us
    unnamed x16, local copies, waits for them, and re-layouts  1.51 us
  transfers between devices with their start and end apart: 22, of which 12 were waited for; matrix products, arithmetic and copies ran while one was open for 1% of the time, Pallas kernels for 0%

profile of v5, /device:TPU:0, one launch (start us, length us, event | category | flops | bytes accessed | tf_op | source)
XLA Modules:
  0.0 63.2 jit_solution(3011290956849148244)
XLA Ops:
  0.6 0.9 %copy-done = f32[1,1,8,8,8,128]{5,4,3,2,1,0:T(8,128)S(1)} copy-done((f32[1,1,8,8,8,128]{5,4,3,2,1,0:T(8,128)S(1)}, f32[1,1,8,8,8,128]{5,4,3,2,1,0:T(8,128)}, u32[]{:S(2)}) %copy-start) | copy-done | bytes 262168
  1.6 0.1 start.1
  1.7 0.5 collective-permute-start.1
  2.2 4.1 %collective-permute-start = (f32[9,8,128]{2,1,0:T(8,128)S(1)}, f32[9,8,128]{2,1,0:T(8,128)S(1)}, u32[]{:S(2)}, u32[]{:S(2)}) collective-permute-start(f32[9,8,128]{2,1,0:T(8,128)S(1)} %get-tuple-element.42), channel_id=1, source_target_pairs={{0,1},{1,0},{2,3},{3,2},{4,5},{5,4},{6,7},{7,6},{8,9},{9,8},{10,11... | collective-permute-start | bytes 110600 | tf_op jit(solution)/shard_map/ppermute | solution.py:941
  6.3 1.9 %collective-permute-done = f32[9,8,128]{2,1,0:T(8,128)S(1)} collective-permute-done((f32[9,8,128]{2,1,0:T(8,128)S(1)}, f32[9,8,128]{2,1,0:T(8,128)S(1)}, u32[]{:S(2)}, u32[]{:S(2)}) %collective-permute-start) | collective-permute-done | bytes 36896 | tf_op jit(solution)/shard_map/ppermute | solution.py:941
  8.4 0.1 collective-permute-start.2
  8.4 0.5 copy-done.7
  9.0 2.0 %collective-permute-start.3 = (f32[10,8,128]{2,1,0:T(8,128)S(1)}, f32[10,8,128]{2,1,0:T(8,128)S(1)}, u32[]{:S(2)}, u32[]{:S(2)}) collective-permute-start(f32[10,8,128]{2,1,0:T(8,128)S(1)} %get-tuple-element.101), channel_id=1, source_target_pairs={{0,28},{1,29},{2,30},{3,31},{4,8},{5,9},{6,10},{7,11},{8,4},{9,5},... | collective-permute-start | bytes 122888 | tf_op jit(solution)/shard_map/ppermute | solution.py:942
  11.0 2.5 %collective-permute-done.3.refs_5_ = f32[10,8,128]{2,1,0:T(8,128)S(1)} collective-permute-done((f32[10,8,128]{2,1,0:T(8,128)S(1)}, f32[10,8,128]{2,1,0:T(8,128)S(1)}, u32[]{:S(2)}, u32[]{:S(2)}) %collective-permute-start.3) | collective-permute-done | bytes 40992 | tf_op jit(solution)/shard_map/ppermute | solution.py:942
  13.6 1.1 %first_solve.1 = (f32[10,112,128]{2,1,0:T(8,128)S(1)}, f32[21,8,128]{2,1,0:T(8,128)S(1)}, f32[21,8,128]{2,1,0:T(8,128)S(1)}, f32[2,10,8,128]{3,2,1,0:T(8,128)S(1)}, f32[2,10,8,128]{3,2,1,0:T(8,128)S(1)}) custom-call(f32[8,8,8,128]{3,2,1,0:T(8,128)S(1)} %bitcast.48, f32[1,128]{1,0:T(1,128)S(1)} %subtract_bitcast_fusion.refs_1_.refs_5_, ...), custom_call_target="tpu_custom_call" | custom-call | flops 1300000000 | bytes 3900000 | tf_op jit(solution)/shard_map/first_solve/pallas_call | solution.py:911
  14.7 0.1 collective-permute-start.5
  14.8 2.5 %collective-permute-start.4 = (f32[21,8,128]{2,1,0:T(8,128)S(1)}, f32[21,8,128]{2,1,0:T(8,128)S(1)}, u32[]{:S(2)}, u32[]{:S(2)}) collective-permute-start(f32[21,8,128]{2,1,0:T(8,128)S(1)} %get-tuple-element.45), channel_id=1, source_target_pairs={{0,1},{1,0},{2,3},{3,2},{4,5},{5,4},{6,7},{7,6},{8,9},{9,8},{10,11... | collective-permute-start | bytes 258056 | tf_op jit(solution)/shard_map/ppermute | solution.py:941
  17.3 0.1 pad.42.clone
  17.3 0.1 pad.37.clone
  17.4 2.3 %collective-permute-done.4 = f32[21,8,128]{2,1,0:T(8,128)S(1)} collective-permute-done((f32[21,8,128]{2,1,0:T(8,128)S(1)}, f32[21,8,128]{2,1,0:T(8,128)S(1)}, u32[]{:S(2)}, u32[]{:S(2)}) %collective-permute-start.4) | collective-permute-done | bytes 86048 | tf_op jit(solution)/shard_map/ppermute | solution.py:941
  19.9 0.1 maximum_maximum_fusion
  19.9 0.1 fusion.7
  20.0 1.4 %collective-permute-start.7 = (f32[18,8,128]{2,1,0:T(8,128)S(1)}, f32[18,8,128]{2,1,0:T(8,128)S(1)}, u32[]{:S(2)}, u32[]{:S(2)}) collective-permute-start(f32[18,8,128]{2,1,0:T(8,128)S(1)} %pad_maximum_fusion.3), channel_id=1, source_target_pairs={{0,28},{1,29},{2,30},{3,31},{4,8},{5,9},{6,10},{7,11},{8,4},{9,5},... | collective-permute-start | bytes 221192 | tf_op jit(solution)/shard_map/ppermute | solution.py:942
  21.5 0.2 collective-permute-start.6
  21.7 1.0 %collective-permute-done.6 = f32[17,8,128]{2,1,0:T(8,128)S(1)} collective-permute-done((f32[17,8,128]{2,1,0:T(8,128)S(1)}, f32[17,8,128]{2,1,0:T(8,128)S(1)}, u32[]{:S(2)}, u32[]{:S(2)}) %collective-permute-start.6) | collective-permute-done | bytes 69664 | tf_op jit(solution)/shard_map/ppermute | solution.py:941
  22.8 2.6 %collective-permute-done.7 = f32[18,8,128]{2,1,0:T(8,128)S(1)} collective-permute-done((f32[18,8,128]{2,1,0:T(8,128)S(1)}, f32[18,8,128]{2,1,0:T(8,128)S(1)}, u32[]{:S(2)}, u32[]{:S(2)}) %collective-permute-start.7) | collective-permute-done | bytes 73760 | tf_op jit(solution)/shard_map/ppermute | solution.py:942
  25.3 0.7 %first_apply.1 = (f32[8,8,8,128]{3,2,1,0:T(8,128)S(1)}, f32[8,8,8,128]{3,2,1,0:T(8,128)S(1)}, f32[16,8,128]{2,1,0:T(8,128)S(1)}, f32[16,8,128]{2,1,0:T(8,128)S(1...) custom-call(f32[10,112,128]{2,1,0:T(8,128)S(1)} %get-tuple-element.44.refs_0_, ...), custom_call_target="tpu_custom_call" | custom-call | flops 800000000 | bytes 2400000 | tf_op jit(solution)/shard_map/first_apply/pallas_call | solution.py:911
  26.1 1.8 %collective-permute-start.8 = (f32[17,8,128]{2,1,0:T(8,128)S(1)}, f32[17,8,128]{2,1,0:T(8,128)S(1)}, u32[]{:S(2)}, u32[]{:S(2)}) collective-permute-start(f32[17,8,128]{2,1,0:T(8,128)S(1)} %pad_maximum_fusion.5), channel_id=1, source_target_pairs={{0,1},{1,0},{2,3},{3,2},{4,5},{5,4},{6,7},{7,6},{8,9},{9,8},{10,11... | collective-permute-start | bytes 208904 | tf_op jit(solution)/shard_map/ppermute | solution.py:941
  27.9 0.1 pad.25.clone
  28.0 2.5 %collective-permute-done.8 = f32[17,8,128]{2,1,0:T(8,128)S(1)} collective-permute-done((f32[17,8,128]{2,1,0:T(8,128)S(1)}, f32[17,8,128]{2,1,0:T(8,128)S(1)}, u32[]{:S(2)}, u32[]{:S(2)}) %collective-permute-start.8) | collective-permute-done | bytes 69664 | tf_op jit(solution)/shard_map/ppermute | solution.py:941
  30.5 0.9 %collective-permute-start.12 = (f32[8,128]{1,0:T(8,128)S(1)}, f32[8,128]{1,0:T(8,128)S(1)}, u32[]{:S(2)}, u32[]{:S(2)}) collective-permute-start(f32[8,128]{1,0:T(8,128)S(1)} %fusion.18), channel_id=1, source_target_pairs={{0,16},{1,17},{2,18},{3,19},{4,20},{5,21},{6,22},{7,23},{8,24},{9,... | collective-permute-start | bytes 12296 | tf_op jit(solution)/shard_map/ppermute | solution.py:952
  31.4 0.1 fusion.3
  31.5 1.0 %collective-permute-start.11 = (f32[2,10,8,128]{3,2,1,0:T(8,128)S(1)}, f32[2,10,8,128]{3,2,1,0:T(8,128)S(1)}, u32[]{:S(2)}, u32[]{:S(2)}) collective-permute-start(f32[2,10,8,128]{3,2,1,0:T(8,128)S(1)} %get-tuple-element.108), channel_id=1, source_target_pairs={{0,28},{1,29},{2,30},{3,31},{4,8},{5,9},{6,10},{7,11},{8,4},{9,5},... | collective-permute-start | bytes 245768 | tf_op jit(solution)/shard_map/ppermute | solution.py:942
  32.5 0.2 collective-permute-start.10
  32.7 0.1 porosity.1.refs_5_.refs_10_
  32.8 1.3 %collective-permute-done.12 = f32[8,128]{1,0:T(8,128)S(1)} collective-permute-done((f32[8,128]{1,0:T(8,128)S(1)}, f32[8,128]{1,0:T(8,128)S(1)}, u32[]{:S(2)}, u32[]{:S(2)}) %collective-permute-start.12) | collective-permute-done | bytes 4128 | tf_op jit(solution)/shard_map/ppermute | solution.py:952
  34.1 2.4 %collective-permute-done.11.refs_4_ = f32[2,10,8,128]{3,2,1,0:T(8,128)S(1)} collective-permute-done((f32[2,10,8,128]{3,2,1,0:T(8,128)S(1)}, f32[2,10,8,128]{3,2,1,0:T(8,128)S(1)}, u32[]{:S(2)}, u32[]{:S(2)}) %collective-permute-start.11) | collective-permute-done | bytes 81952 | tf_op jit(solution)/shard_map/ppermute | solution.py:942
  36.5 1.5 %second_solve.1 = (f32[8,8,8,128]{3,2,1,0:T(8,128)S(1)}, f32[10,112,128]{2,1,0:T(8,128)S(1)}, f32[20,8,128]{2,1,0:T(8,128)S(1)}, f32[20,8,128]{2,1,0:T(8,128)S(1...) custom-call(f32[8,8,8,128]{3,2,1,0:T(8,128)S(1)} %get-tuple-element.49.refs_0_, ...), custom_call_target="tpu_custom_call" | custom-call | flops 1300000000 | bytes 3900000 | tf_op jit(solution)/shard_map/second_solve/pallas_call | solution.py:911
  38.0 1.8 %collective-permute-start.13 = (f32[20,8,128]{2,1,0:T(8,128)S(1)}, f32[20,8,128]{2,1,0:T(8,128)S(1)}, u32[]{:S(2)}, u32[]{:S(2)}) collective-permute-start(f32[20,8,128]{2,1,0:T(8,128)S(1)} %get-tuple-element.60), channel_id=1, source_target_pairs={{0,1},{1,0},{2,3},{3,2},{4,5},{5,4},{6,7},{7,6},{8,9},{9,8},{10,11... | collective-permute-start | bytes 245768 | tf_op jit(solution)/shard_map/ppermute | solution.py:941
  39.9 2.7 %collective-permute-done.13 = f32[20,8,128]{2,1,0:T(8,128)S(1)} collective-permute-done((f32[20,8,128]{2,1,0:T(8,128)S(1)}, f32[20,8,128]{2,1,0:T(8,128)S(1)}, u32[]{:S(2)}, u32[]{:S(2)}) %collective-permute-start.13) | collective-permute-done | bytes 81952 | tf_op jit(solution)/shard_map/ppermute | solution.py:941
  42.6 0.1 fusion.11
  42.7 0.7 %collective-permute-start.16 = (f32[2,8,8,128]{3,2,1,0:T(8,128)S(1)}, f32[2,8,8,128]{3,2,1,0:T(8,128)S(1)}, u32[]{:S(2)}, u32[]{:S(2)}) collective-permute-start(f32[2,8,8,128]{3,2,1,0:T(8,128)S(1)} %get-tuple-element.106), channel_id=1, source_target_pairs={{0,28},{1,29},{2,30},{3,31},{4,8},{5,9},{6,10},{7,11},{8,4},{9,5},... | collective-permute-start | bytes 196616 | tf_op jit(solution)/shard_map/ppermute | solution.py:942
  43.4 0.6 collective-permute-start.15
  44.0 3.3 %collective-permute-done.16.refs_4_ = f32[2,8,8,128]{3,2,1,0:T(8,128)S(1)} collective-permute-done((f32[2,8,8,128]{3,2,1,0:T(8,128)S(1)}, f32[2,8,8,128]{3,2,1,0:T(8,128)S(1)}, u32[]{:S(2)}, u32[]{:S(2)}) %collective-permute-start.16) | collective-permute-done | bytes 65568 | tf_op jit(solution)/shard_map/ppermute | solution.py:942
  47.3 1.5 %late_apply.1 = (f32[8,8,8,128]{3,2,1,0:T(8,128)S(1)}, f32[8,8,8,128]{3,2,1,0:T(8,128)S(1)}, f32[8,8,8,128]{3,2,1,0:T(8,128)S(1)}, f32[8,8,128]{2,1,0:T(8,128)S(...) custom-call(f32[10,112,128]{2,1,0:T(8,128)S(1)} %get-tuple-element.5, ...), custom_call_target="tpu_custom_call" | custom-call | flops 800000000 | bytes 2400000 | tf_op jit(solution)/shard_map/late_apply/pallas_call | solution.py:911
  48.9 2.0 %collective-permute-start.17 = (f32[8,8,128]{2,1,0:T(8,128)S(1)}, f32[8,8,128]{2,1,0:T(8,128)S(1)}, u32[]{:S(2)}, u32[]{:S(2)}) collective-permute-start(f32[8,8,128]{2,1,0:T(8,128)S(1)} %get-tuple-element.69), channel_id=1, source_target_pairs={{0,1},{1,0},{2,3},{3,2},{4,5},{5,4},{6,7},{7,6},{8,9},{9,8},{10,11... | collective-permute-start | bytes 98312 | tf_op jit(solution)/shard_map/ppermute | solution.py:941
  50.9 0.1 pad.13.clone
  51.0 3.4 %all-to-all-start = ((f32[32,4,128]{2,1,0:T(4,128)}), f32[32,4,128]{2,1,0:T(4,128)S(1)}, u32[]{:S(2)}, u32[]{:S(2)}) async-start(f32[32,4,128]{2,1,0:T(4,128)} %get-tuple-element.75), calls=%async_computation | async-start | bytes 131072 | tf_op jit(solution)/shard_map/all_to_all | solution.py:978
  54.4 0.1 fusion.15
  54.5 2.4 %collective-permute-start.20 = (f32[8,8,128]{2,1,0:T(8,128)S(1)}, f32[8,8,128]{2,1,0:T(8,128)S(1)}, u32[]{:S(2)}, u32[]{:S(2)}) collective-permute-start(f32[8,8,128]{2,1,0:T(8,128)S(1)} %get-tuple-element.127), channel_id=1, source_target_pairs={{0,28},{1,29},{2,30},{3,31},{4,8},{5,9},{6,10},{7,11},{8,4},{9,5},... | collective-permute-start | bytes 98312 | tf_op jit(solution)/shard_map/ppermute | solution.py:942
  56.9 1.9 %collective-permute-done.20.refs_9_ = f32[8,8,128]{2,1,0:T(8,128)S(1)} collective-permute-done((f32[8,8,128]{2,1,0:T(8,128)S(1)}, f32[8,8,128]{2,1,0:T(8,128)S(1)}, u32[]{:S(2)}, u32[]{:S(2)}) %collective-permute-start.20) | collective-permute-done | bytes 32800 | tf_op jit(solution)/shard_map/ppermute | solution.py:942
  58.9 3.0 %all-to-all-done.refs_12_ = f32[32,4,128]{2,1,0:T(4,128)S(1)} async-done(((f32[32,4,128]{2,1,0:T(4,128)}), f32[32,4,128]{2,1,0:T(4,128)S(1)}, u32[]{:S(2)}, u32[]{:S(2)}) %all-to-all-start) | async-done | bytes 65568 | tf_op jit(solution)/shard_map/all_to_all | solution.py:978
  61.8 1.4 %late_final.1 = (f32[8,8,8,128]{3,2,1,0:T(8,128)}, f32[8,8,8,128]{3,2,1,0:T(8,128)}, f32[8,8,8,128]{3,2,1,0:T(8,128)}, f32[2]{0:T(128)}) custom-call(f32[8,8,8,128]{3,2,1,0:T(8,128)S(1)} %bitcast.51, f32[8,8,8,128]{3,2,1,0:T(8,128)S(1)} %bitcast.50, f32[8,8,8,128]{3,2,1,0:T(8,128)S(1)} %get-tuple-element.58.refs_7_.refs_2_, ...), custom_call_target="tpu_custom_call" | custom-call | flops 800000000 | bytes 2400000 | tf_op jit(solution)/shard_map/late_final/pallas_call | solution.py:911
  (67 shorter events, 0.3 us)
Async XLA Ops:
  0.6 1.0 %copy-start = (f32[1,1,8,8,8,128]{5,4,3,2,1,0:T(8,128)S(1)}, f32[1,1,8,8,8,128]{5,4,3,2,1,0:T(8,128)}, u32[]{:S(2)}) copy-start(f32[1,1,8,8,8,128]{5,4,3,2,1,0:T(8,128)} %param.8) | copy-start | bytes 786436
  1.6 12.0 %copy-start.3 = (f32[10,104,128]{2,1,0:T(8,128)S(1)}, f32[10,104,128]{2,1,0:T(8,128)}, u32[]{:S(2)}) copy-start(f32[10,104,128]{2,1,0:T(8,128)} %constant.46.clone.refs_8_.refs_10_) | copy-start | bytes 1597444
  1.7 4.6 %collective-permute-start.1 = (f32[8,8,128]{2,1,0:T(8,128)S(1)}, f32[8,8,128]{2,1,0:T(8,128)S(1)}, u32[]{:S(2)}, u32[]{:S(2)}) collective-permute-start(f32[8,8,128]{2,1,0:T(8,128)S(1)} %get-tuple-element.43), channel_id=1, source_target_pairs={{0,4},{1,2},{2,1},{3,7},{4,0},{5,6},{6,5},{7,3},{8,12},{9,10},{10,... | collective-permute-start | bytes 98312 | tf_op jit(solution)/shard_map/ppermute | solution.py:942
  2.2 6.1 %collective-permute-start = (f32[9,8,128]{2,1,0:T(8,128)S(1)}, f32[9,8,128]{2,1,0:T(8,128)S(1)}, u32[]{:S(2)}, u32[]{:S(2)}) collective-permute-start(f32[9,8,128]{2,1,0:T(8,128)S(1)} %get-tuple-element.42), channel_id=1, source_target_pairs={{0,1},{1,0},{2,3},{3,2},{4,5},{5,4},{6,7},{7,6},{8,9},{9,8},{10,11... | collective-permute-start | bytes 110600 | tf_op jit(solution)/shard_map/ppermute | solution.py:941
  6.3 7.2 %copy-start.1 = (f32[1,1,8,8,8,128]{5,4,3,2,1,0:T(8,128)S(1)}, f32[1,1,8,8,8,128]{5,4,3,2,1,0:T(8,128)}, u32[]{:S(2)}) copy-start(f32[1,1,8,8,8,128]{5,4,3,2,1,0:T(8,128)} %param.8) | copy-start | bytes 786436
  8.3 0.7 %copy-start.7 = (s32[1,1,128]{2,1,0:T(1,128)S(1)}, s32[1,1,128]{2,1,0:T(1,128)}, u32[]{:S(2)}) copy-start(s32[1,1,128]{2,1,0:T(1,128)} %param.9) | copy-start | bytes 1540
  8.3 5.2 %copy-start.6 = (f32[104,112]{1,0:T(8,128)S(1)}, f32[104,112]{1,0:T(8,128)}, u32[]{:S(2)}) copy-start(f32[104,112]{1,0:T(8,128)} %constant.44.clone.refs_6_.refs_8_) | copy-start | bytes 139780
  8.4 5.2 %copy-start.5 = (f32[112,104]{1,0:T(8,128)S(1)}, f32[112,104]{1,0:T(8,128)}, u32[]{:S(2)}) copy-start(f32[112,104]{1,0:T(8,128)} %constant.45.clone.refs_7_.refs_9_) | copy-start | bytes 139780
  8.4 2.6 %collective-permute-start.2 = (f32[11,8,128]{2,1,0:T(8,128)S(1)}, f32[11,8,128]{2,1,0:T(8,128)S(1)}, u32[]{:S(2)}, u32[]{:S(2)}) collective-permute-start(f32[11,8,128]{2,1,0:T(8,128)S(1)} %pad_maximum_fusion.10), channel_id=1, source_target_pairs={{0,4},{1,5},{2,6},{3,7},{4,0},{5,1},{6,2},{7,3},{8,12},{9,13},{10,... | collective-permute-start | bytes 135176 | tf_op jit(solution)/shard_map/ppermute | solution.py:941
  9.0 4.6 %collective-permute-start.3 = (f32[10,8,128]{2,1,0:T(8,128)S(1)}, f32[10,8,128]{2,1,0:T(8,128)S(1)}, u32[]{:S(2)}, u32[]{:S(2)}) collective-permute-start(f32[10,8,128]{2,1,0:T(8,128)S(1)} %get-tuple-element.101), channel_id=1, source_target_pairs={{0,28},{1,29},{2,30},{3,31},{4,8},{5,9},{6,10},{7,11},{8,4},{9,5},... | collective-permute-start | bytes 122888 | tf_op jit(solution)/shard_map/ppermute | solution.py:942
  14.7 5.0 %collective-permute-start.5 = (f32[22,8,128]{2,1,0:T(8,128)S(1)}, f32[22,8,128]{2,1,0:T(8,128)S(1)}, u32[]{:S(2)}, u32[]{:S(2)}) collective-permute-start(f32[22,8,128]{2,1,0:T(8,128)S(1)} %pad_maximum_fusion), channel_id=1, source_target_pairs={{0,4},{1,2},{2,1},{3,7},{4,0},{5,6},{6,5},{7,3},{8,12},{9,10},{10,... | collective-permute-start | bytes 270344 | tf_op jit(solution)/shard_map/ppermute | solution.py:942
  14.8 4.9 %collective-permute-start.4 = (f32[21,8,128]{2,1,0:T(8,128)S(1)}, f32[21,8,128]{2,1,0:T(8,128)S(1)}, u32[]{:S(2)}, u32[]{:S(2)}) collective-permute-start(f32[21,8,128]{2,1,0:T(8,128)S(1)} %get-tuple-element.45), channel_id=1, source_target_pairs={{0,1},{1,0},{2,3},{3,2},{4,5},{5,4},{6,7},{7,6},{8,9},{9,8},{10,11... | collective-permute-start | bytes 258056 | tf_op jit(solution)/shard_map/ppermute | solution.py:941
  20.0 5.3 %collective-permute-start.7 = (f32[18,8,128]{2,1,0:T(8,128)S(1)}, f32[18,8,128]{2,1,0:T(8,128)S(1)}, u32[]{:S(2)}, u32[]{:S(2)}) collective-permute-start(f32[18,8,128]{2,1,0:T(8,128)S(1)} %pad_maximum_fusion.3), channel_id=1, source_target_pairs={{0,28},{1,29},{2,30},{3,31},{4,8},{5,9},{6,10},{7,11},{8,4},{9,5},... | collective-permute-start | bytes 221192 | tf_op jit(solution)/shard_map/ppermute | solution.py:942
  21.5 1.3 %collective-permute-start.6 = (f32[17,8,128]{2,1,0:T(8,128)S(1)}, f32[17,8,128]{2,1,0:T(8,128)S(1)}, u32[]{:S(2)}, u32[]{:S(2)}) collective-permute-start(f32[17,8,128]{2,1,0:T(8,128)S(1)} %pad_maximum_fusion.4), channel_id=1, source_target_pairs={{0,4},{1,5},{2,6},{3,7},{4,0},{5,1},{6,2},{7,3},{8,12},{9,13},{10,... | collective-permute-start | bytes 208904 | tf_op jit(solution)/shard_map/ppermute | solution.py:941
  26.1 4.4 %collective-permute-start.8 = (f32[17,8,128]{2,1,0:T(8,128)S(1)}, f32[17,8,128]{2,1,0:T(8,128)S(1)}, u32[]{:S(2)}, u32[]{:S(2)}) collective-permute-start(f32[17,8,128]{2,1,0:T(8,128)S(1)} %pad_maximum_fusion.5), channel_id=1, source_target_pairs={{0,1},{1,0},{2,3},{3,2},{4,5},{5,4},{6,7},{7,6},{8,9},{9,8},{10,11... | collective-permute-start | bytes 208904 | tf_op jit(solution)/shard_map/ppermute | solution.py:941
  28.0 3.4 %collective-permute-start.9 = (f32[16,8,128]{2,1,0:T(8,128)S(1)}, f32[16,8,128]{2,1,0:T(8,128)S(1)}, u32[]{:S(2)}, u32[]{:S(2)}) collective-permute-start(f32[16,8,128]{2,1,0:T(8,128)S(1)} %get-tuple-element.51), channel_id=1, source_target_pairs={{0,4},{1,2},{2,1},{3,7},{4,0},{5,6},{6,5},{7,3},{8,12},{9,10},{10,... | collective-permute-start | bytes 196616 | tf_op jit(solution)/shard_map/ppermute | solution.py:942
  30.5 3.6 %collective-permute-start.12 = (f32[8,128]{1,0:T(8,128)S(1)}, f32[8,128]{1,0:T(8,128)S(1)}, u32[]{:S(2)}, u32[]{:S(2)}) collective-permute-start(f32[8,128]{1,0:T(8,128)S(1)} %fusion.18), channel_id=1, source_target_pairs={{0,16},{1,17},{2,18},{3,19},{4,20},{5,21},{6,22},{7,23},{8,24},{9,... | collective-permute-start | bytes 12296 | tf_op jit(solution)/shard_map/ppermute | solution.py:952
  31.5 5.0 %collective-permute-start.11 = (f32[2,10,8,128]{3,2,1,0:T(8,128)S(1)}, f32[2,10,8,128]{3,2,1,0:T(8,128)S(1)}, u32[]{:S(2)}, u32[]{:S(2)}) collective-permute-start(f32[2,10,8,128]{3,2,1,0:T(8,128)S(1)} %get-tuple-element.108), channel_id=1, source_target_pairs={{0,28},{1,29},{2,30},{3,31},{4,8},{5,9},{6,10},{7,11},{8,4},{9,5},... | collective-permute-start | bytes 245768 | tf_op jit(solution)/shard_map/ppermute | solution.py:942
  32.5 4.0 %collective-permute-start.10 = (f32[2,10,8,128]{3,2,1,0:T(8,128)S(1)}, f32[2,10,8,128]{3,2,1,0:T(8,128)S(1)}, u32[]{:S(2)}, u32[]{:S(2)}) collective-permute-start(f32[2,10,8,128]{3,2,1,0:T(8,128)S(1)} %get-tuple-element.109), channel_id=1, source_target_pairs={{0,4},{1,5},{2,6},{3,7},{4,0},{5,1},{6,2},{7,3},{8,12},{9,13},{10,... | collective-permute-start | bytes 245768 | tf_op jit(solution)/shard_map/ppermute | solution.py:941
  32.7 3.8 %copy-start.4 = (f32[288,128]{1,0:T(8,128)S(1)}, f32[288,128]{1,0:T(8,128)}, u32[]{:S(2)}) copy-start(f32[288,128]{1,0:T(8,128)} %constant.43.clone.refs_6_.refs_11_) | copy-start | bytes 442372
  38.0 4.5 %collective-permute-start.13 = (f32[20,8,128]{2,1,0:T(8,128)S(1)}, f32[20,8,128]{2,1,0:T(8,128)S(1)}, u32[]{:S(2)}, u32[]{:S(2)}) collective-permute-start(f32[20,8,128]{2,1,0:T(8,128)S(1)} %get-tuple-element.60), channel_id=1, source_target_pairs={{0,1},{1,0},{2,3},{3,2},{4,5},{5,4},{6,7},{7,6},{8,9},{9,8},{10,11... | collective-permute-start | bytes 245768 | tf_op jit(solution)/shard_map/ppermute | solution.py:941
  39.8 2.7 %collective-permute-start.14 = (f32[20,8,128]{2,1,0:T(8,128)S(1)}, f32[20,8,128]{2,1,0:T(8,128)S(1)}, u32[]{:S(2)}, u32[]{:S(2)}) collective-permute-start(f32[20,8,128]{2,1,0:T(8,128)S(1)} %get-tuple-element.61), channel_id=1, source_target_pairs={{0,4},{1,2},{2,1},{3,7},{4,0},{5,6},{6,5},{7,3},{8,12},{9,10},{10,... | collective-permute-start | bytes 245768 | tf_op jit(solution)/shard_map/ppermute | solution.py:942
  42.7 4.7 %collective-permute-start.16 = (f32[2,8,8,128]{3,2,1,0:T(8,128)S(1)}, f32[2,8,8,128]{3,2,1,0:T(8,128)S(1)}, u32[]{:S(2)}, u32[]{:S(2)}) collective-permute-start(f32[2,8,8,128]{3,2,1,0:T(8,128)S(1)} %get-tuple-element.106), channel_id=1, source_target_pairs={{0,28},{1,29},{2,30},{3,31},{4,8},{5,9},{6,10},{7,11},{8,4},{9,5},... | collective-permute-start | bytes 196616 | tf_op jit(solution)/shard_map/ppermute | solution.py:942
  43.4 3.9 %collective-permute-start.15 = (f32[2,8,8,128]{3,2,1,0:T(8,128)S(1)}, f32[2,8,8,128]{3,2,1,0:T(8,128)S(1)}, u32[]{:S(2)}, u32[]{:S(2)}) collective-permute-start(f32[2,8,8,128]{3,2,1,0:T(8,128)S(1)} %get-tuple-element.107), channel_id=1, source_target_pairs={{0,4},{1,5},{2,6},{3,7},{4,0},{5,1},{6,2},{7,3},{8,12},{9,13},{10,... | collective-permute-start | bytes 196616 | tf_op jit(solution)/shard_map/ppermute | solution.py:941
  48.9 13.0 %copy-start.2 = (f32[1,1,8,8,8,128]{5,4,3,2,1,0:T(8,128)S(1)}, f32[1,1,8,8,8,128]{5,4,3,2,1,0:T(8,128)}, u32[]{:S(2)}) copy-start(f32[1,1,8,8,8,128]{5,4,3,2,1,0:T(8,128)} %param.7) | copy-start | bytes 786436
  48.9 5.5 %collective-permute-start.17 = (f32[8,8,128]{2,1,0:T(8,128)S(1)}, f32[8,8,128]{2,1,0:T(8,128)S(1)}, u32[]{:S(2)}, u32[]{:S(2)}) collective-permute-start(f32[8,8,128]{2,1,0:T(8,128)S(1)} %get-tuple-element.69), channel_id=1, source_target_pairs={{0,1},{1,0},{2,3},{3,2},{4,5},{5,4},{6,7},{7,6},{8,9},{9,8},{10,11... | collective-permute-start | bytes 98312 | tf_op jit(solution)/shard_map/ppermute | solution.py:941
  50.9 3.5 %collective-permute-start.18 = (f32[8,8,128]{2,1,0:T(8,128)S(1)}, f32[8,8,128]{2,1,0:T(8,128)S(1)}, u32[]{:S(2)}, u32[]{:S(2)}) collective-permute-start(f32[8,8,128]{2,1,0:T(8,128)S(1)} %get-tuple-element.70), channel_id=1, source_target_pairs={{0,4},{1,2},{2,1},{3,7},{4,0},{5,6},{6,5},{7,3},{8,12},{9,10},{10,... | collective-permute-start | bytes 98312 | tf_op jit(solution)/shard_map/ppermute | solution.py:942
  51.0 10.9 %all-to-all-start = ((f32[32,4,128]{2,1,0:T(4,128)}), f32[32,4,128]{2,1,0:T(4,128)S(1)}, u32[]{:S(2)}, u32[]{:S(2)}) async-start(f32[32,4,128]{2,1,0:T(4,128)} %get-tuple-element.75), calls=%async_computation | async-start | bytes 131072 | tf_op jit(solution)/shard_map/all_to_all | solution.py:978
  54.5 4.4 %collective-permute-start.20 = (f32[8,8,128]{2,1,0:T(8,128)S(1)}, f32[8,8,128]{2,1,0:T(8,128)S(1)}, u32[]{:S(2)}, u32[]{:S(2)}) collective-permute-start(f32[8,8,128]{2,1,0:T(8,128)S(1)} %get-tuple-element.127), channel_id=1, source_target_pairs={{0,28},{1,29},{2,30},{3,31},{4,8},{5,9},{6,10},{7,11},{8,4},{9,5},... | collective-permute-start | bytes 98312 | tf_op jit(solution)/shard_map/ppermute | solution.py:942
  56.9 1.9 %collective-permute-start.19 = (f32[8,8,128]{2,1,0:T(8,128)S(1)}, f32[8,8,128]{2,1,0:T(8,128)S(1)}, u32[]{:S(2)}, u32[]{:S(2)}) collective-permute-start(f32[8,8,128]{2,1,0:T(8,128)S(1)} %get-tuple-element.128), channel_id=1, source_target_pairs={{0,4},{1,5},{2,6},{3,7},{4,0},{5,1},{6,2},{7,3},{8,12},{9,13},{10,... | collective-permute-start | bytes 98312 | tf_op jit(solution)/shard_map/ppermute | solution.py:941

commit v6 on v5

--- a/solution.py
+++ b/solution.py
@@ -625,9 +625,9 @@
 
 
 def late_apply_kernel(
-    counts, part_ref, ry_first, ry_second, rx_first, rx_second, porosity_ref, r_ref, q_ref,
-    schwarz_ref, field_ref, z_ref, w_ref, u_ref, sy_first, sy_second, fx_first, fx_second,
-    stats_ref, y_ref,
+    counts, part_ref, ry_first, ry_second, rx_first, rx_second, porosity_ref, low_ref, own_ref,
+    high_ref, r_ref, q_ref, schwarz_ref, field_ref, w_ref, u_ref, sy_first, sy_second, fx_first, fx_second, stats_ref,
+    y_ref,
 ):
     side_x, side_y = Sides("gx", counts[0]), Sides("gy", counts[1])
     w = collect_parts(part_ref, ry_first, ry_second, rx_first, rx_second, side_x, side_y, None)
@@ -636,7 +636,6 @@
         w_ref[a, b] = value
         node_class = 3 * class_of(a) + class_of(b)
         z = schwarz_ref[a, b] + field_ref[node_class : node_class + 1, :]
-        z_ref[a, b] = z
         q = q_ref[a, b]
         factors = (axis_factor(a, side_x), axis_factor(b, side_y))
         terms = [scaled(t, *factors) for t in (value * q, z * r_ref[a, b], z * q)]
@@ -667,13 +666,65 @@
     for index in range(stats_ref.shape[0]):
         stats_ref[index] = jnp.broadcast_to(row, stats_ref.shape[1:])
     sum_column(u_ref)
+    near = [[ref[y : y + 1] for y in range(3)] for ref in (low_ref, own_ref, high_ref)]
+    send_corners(
+        u_ref, w_ref, y_ref, near, side_x, side_y, sy_first, sy_second, fx_first, fx_second
+    )
+
+
+def sum_tile(tile):
+    row = lax.broadcasted_iota(jnp.int32, (NODES, 128), 0)
+    below = jnp.where(row == 0, pltpu.roll(shift_up(tile), 1, 0), 0.0)
+    above = jnp.where(row == NODES - 1, pltpu.roll(shift_down(tile), NODES - 1, 0), 0.0)
+    return tile + below + above
+
+
+def send_corners(
+    u_ref, w_ref, y_ref, near, side_x, side_y, sy_first, sy_second, fx_first, fx_second
+):
+    ends = (0, NODES - 1)
+
+    def along_x(end, b):
+        return combine(STIFF[end] * WEIGHTS[b], [y_ref[a, b] for a in range(NODES)])
+
+    def along_y(end, a):
+        return combine(STIFF[end] * WEIGHTS[a], [y_ref[a, b] for b in range(NODES)])
+
     for a in range(NODES):
         low, high = u_ref[a, 0], u_ref[a, NODES - 1]
         sy_first[a] = side_y.send_first(low, high)
         sy_second[a] = side_y.send_second(low, high)
-    low, high = u_ref[0], u_ref[NODES - 1]
-    fx_first[...] = side_x.send_first(low, high)
-    fx_second[...] = side_x.send_second(low, high)
+        low, high = u_ref[0, a], u_ref[NODES - 1, a]
+        fx_first[a] = side_x.send_first(low, high)
+        fx_second[a] = side_x.send_second(low, high)
+    for place, node in enumerate(ends):
+        low, high = (sum_tile(near[2 * place][1] * along_y(end, node)) for end in ends)
+        sy_first[NODES + place] = side_y.send_first(low, high)
+        sy_second[NODES + place] = side_y.send_second(low, high)
+        low, high = (sum_tile(near[1][2 * place] * along_x(end, node)) for end in ends)
+        fx_first[NODES + place] = side_x.send_first(low, high)
+        fx_second[NODES + place] = side_x.send_second(low, high)
+    weight = float(WEIGHTS[0] * WEIGHTS[0])
+    for i, a in enumerate(ends):
+        for j, b in enumerate(ends):
+            porosity = near[2 * i][2 * j]
+            value = w_ref[a, b]
+            third = None
+            for shift in range(NODES):
+                turned = value if shift == 0 else pltpu.roll(value, shift, 0)
+                term = turned * row_tile([STIFF[k, (k - shift) % NODES] for k in range(NODES)])
+                third = term if third is None else third + term
+            mass = jnp.where(porosity > 0.0, shift_mass * y_ref[a, b], 0.0)
+            u_ref[a, b] = u_ref[a, b] + weight * sum_tile(porosity * third + mass)
+
+
+def prepare_late_kernel(counts, sol_ref, r_ref, schwarz_ref, field_ref, z_ref, sol_out, r_out):
+    for a in range(NODES):
+        for b in range(NODES):
+            node_class = 3 * class_of(a) + class_of(b)
+            z_ref[a, b] = schwarz_ref[a, b] + field_ref[node_class : node_class + 1, :]
+            sol_out[a, b] = sol_ref[a, b]
+            r_out[a, b] = r_ref[a, b]
 
 
 def porosity_kernel(counts, low_ref, own_ref, high_ref, out_ref):
@@ -831,6 +882,11 @@
     lifted_image = LiftedImage(fields, columns_ref)
     low_x = side_x.low(rx_first[...], rx_second[...])
     high_x = side_x.high(rx_first[...], rx_second[...])
+    corner_y = {}
+    for place in range(2):
+        tiles = ry_first[NODES + place], ry_second[NODES + place]
+        corner_y[(place > 0, False)] = side_y.low(*tiles)
+        corner_y[(place > 0, True)] = side_y.high(*tiles)
     for a in range(NODES):
         for b in range(NODES):
             image = u_ref[a, b]
@@ -842,6 +898,9 @@
                 image = image + low_x[b]
             if a == NODES - 1:
                 image = image + high_x[b]
+            if a in (0, NODES - 1) and b in (0, NODES - 1):
+                from_x = low_x if a == 0 else high_x
+                image = image + from_x[NODES + (b > 0)] + corner_y[(a > 0, b > 0)]
             lifted = fields[(1, 1)][class_of(a)][class_of(b)]
             image = image + lifted_image.at(a, b)
             z, q = z_ref[a, b], q_ref[a, b]
@@ -1148,10 +1207,8 @@
             jnp.pad(fx[1], pads) + side_x.send_second(*both),
         )
         if late:
-            (columns,) = call(
-                porosity_kernel, counts, "porosity", [(18, NODES, 128)], [],
-                side_x.low(*threes), three, side_x.high(*threes),
-            )
+            near = (side_x.low(*threes), three, side_x.high(*threes))
+            (columns,) = call(porosity_kernel, counts, "porosity", [(18, NODES, 128)], [], *near)
             rx, far, columns = lax.optimization_barrier((rx, running.far((4, 0)), columns))
             for value in far:
                 running.add(value)
@@ -1184,12 +1241,19 @@
             return ry, rx, beside
 
         if late:
-            z, w, u, y_first, y_second, *fx, stats = call(
+            w, u, y_first, y_second, *fx, stats = call(
                 late_apply_kernel, counts, "late_apply",
-                [block, block, block, face, face, face, face, row], [block],
-                part, *ry, *rx, porosity, residual, q, z, field,
-            )
-            ry, rx, _ = trade_edges(y_first, y_second, fx, [])
+                [block, block] + [(NODES + 2, NODES, 128)] * 4 + [row], [block],
+                part, *ry, *rx, porosity, *near, residual, q, z, field,
+            )
+            z, w = lax.optimization_barrier((z, w))
+            nexts = call(
+                prepare_late_kernel, counts, "prepare", [block] * 3, [],
+                solution, residual, z, field,
+            )
+            ry, rx, (z, solution, residual) = lax.optimization_barrier(
+                (trade(counts, 1, y_first, y_second), trade(counts, 0, *fx), nexts)
+            )
             solution_out, residual_out, direction, steps = call(
                 late_final_kernel, counts, "late_final", [block] * 3 + [(2,)], [table],
                 solution, residual, q, z, w, u, *ry, *rx, columns, every_lift,

time: 63.4 us -> 62.2 us (0.981)
  waiting for transfers between devices: 27.5 us -> 26 us
    all_to_all x1, waiting for transfers between devices: 2.99 us -> 0.7 us  [gather_stats(): return lax.all_to_all(stats, AXES, 0, 0)]
    ppermute x10, waiting for transfers between devices: 12.7 us -> 13.5 us  [trade(): lax.ppermute(second, AXES, swap_pairs(counts, axis, 1))]
    pallas_call x7 -> x8, Pallas kernels: 6.47 us -> 6.65 us  [call(): pl.pallas_call(body, name=name, out_shape=[jax.ShapeDtypeStruct(shape, jn...]
where the time goes in v6:
time: 62.2 us; the launch traced here: 62 us
  starting transfers between devices  26.1 us (42%)
  waiting for transfers between devices  26 us (42%)
  Pallas kernels  6.65 us (11%)
  local copies, waits for them, and re-layouts  1.82 us (3%)
  between operations  0.97 us (2%)
    ppermute x10, starting transfers between devices, trade(): lax.ppermute(first, AXES, swap_pairs(counts, axis, 0))  13.7 us
    ppermute x10, waiting for transfers between devices, trade(): lax.ppermute(second, AXES, swap_pairs(counts, axis, 1))  13.5 us
    ppermute x10, waiting for transfers between devices, trade(): lax.ppermute(first, AXES, swap_pairs(counts, axis, 0))  10.5 us
    ppermute x10, starting transfers between devices, trade(): lax.ppermute(second, AXES, swap_pairs(counts, axis, 1))  7.72 us
    pallas_call x8, Pallas kernels, call(): pl.pallas_call(body, name=name, out_shape=[jax.ShapeDtypeStruct(shape, jn...  6.65 us
    all_to_all x1, starting transfers between devices, gather_stats(): return lax.all_to_all(stats, AXES, 0, 0)  3.82 us
    unnamed x16, local copies, waits for them, and re-layouts  1.51 us
    ppermute x1, waiting for transfers between devices, trade_far(): return lax.ppermute(value, AXES, pairs)  1.28 us
  transfers between devices with their start and end apart: 22, of which 12 were waited for; matrix products, arithmetic and copies ran while one was open for 1% of the time, Pallas kernels for 0%

profile of v6, /device:TPU:0, one launch (start us, length us, event | category | flops | bytes accessed | tf_op | source)
XLA Modules:
  0.0 62.0 jit_solution(8490304214054948122)
XLA Ops:
  0.6 0.9 %copy-done = f32[1,1,8,8,8,128]{5,4,3,2,1,0:T(8,128)S(1)} copy-done((f32[1,1,8,8,8,128]{5,4,3,2,1,0:T(8,128)S(1)}, f32[1,1,8,8,8,128]{5,4,3,2,1,0:T(8,128)}, u32[]{:S(2)}) %copy-start) | copy-done | bytes 262168
  1.6 0.1 start.1
  1.7 0.5 collective-permute-start.1
  2.2 4.1 %collective-permute-start = (f32[9,8,128]{2,1,0:T(8,128)S(1)}, f32[9,8,128]{2,1,0:T(8,128)S(1)}, u32[]{:S(2)}, u32[]{:S(2)}) collective-permute-start(f32[9,8,128]{2,1,0:T(8,128)S(1)} %get-tuple-element.51), channel_id=1, source_target_pairs={{0,1},{1,0},{2,3},{3,2},{4,5},{5,4},{6,7},{7,6},{8,9},{9,8},{10,11... | collective-permute-start | bytes 110600 | tf_op jit(solution)/shard_map/ppermute | solution.py:1000
  6.3 1.9 %collective-permute-done = f32[9,8,128]{2,1,0:T(8,128)S(1)} collective-permute-done((f32[9,8,128]{2,1,0:T(8,128)S(1)}, f32[9,8,128]{2,1,0:T(8,128)S(1)}, u32[]{:S(2)}, u32[]{:S(2)}) %collective-permute-start) | collective-permute-done | bytes 36896 | tf_op jit(solution)/shard_map/ppermute | solution.py:1000
  8.4 0.1 collective-permute-start.2
  8.4 0.5 copy-done.7
  9.0 2.0 %collective-permute-start.3 = (f32[10,8,128]{2,1,0:T(8,128)S(1)}, f32[10,8,128]{2,1,0:T(8,128)S(1)}, u32[]{:S(2)}, u32[]{:S(2)}) collective-permute-start(f32[10,8,128]{2,1,0:T(8,128)S(1)} %get-tuple-element.119), channel_id=1, source_target_pairs={{0,28},{1,29},{2,30},{3,31},{4,8},{5,9},{6,10},{7,11},{8,4},{9,5},... | collective-permute-start | bytes 122888 | tf_op jit(solution)/shard_map/ppermute | solution.py:1001
  11.0 2.5 %collective-permute-done.3.refs_5_ = f32[10,8,128]{2,1,0:T(8,128)S(1)} collective-permute-done((f32[10,8,128]{2,1,0:T(8,128)S(1)}, f32[10,8,128]{2,1,0:T(8,128)S(1)}, u32[]{:S(2)}, u32[]{:S(2)}) %collective-permute-start.3) | collective-permute-done | bytes 40992 | tf_op jit(solution)/shard_map/ppermute | solution.py:1001
  13.6 1.1 %first_solve.1 = (f32[10,112,128]{2,1,0:T(8,128)S(1)}, f32[21,8,128]{2,1,0:T(8,128)S(1)}, f32[21,8,128]{2,1,0:T(8,128)S(1)}, f32[2,10,8,128]{3,2,1,0:T(8,128)S(1)}, f32[2,10,8,128]{3,2,1,0:T(8,128)S(1)}) custom-call(f32[8,8,8,128]{3,2,1,0:T(8,128)S(1)} %bitcast.48, f32[1,128]{1,0:T(1,128)S(1)} %subtract_bitcast_fusion.refs_1_.refs_5_, ...), custom_call_target="tpu_custom_call" | custom-call | flops 1300000000 | bytes 3900000 | tf_op jit(solution)/shard_map/first_solve/pallas_call | solution.py:970
  14.7 0.1 collective-permute-start.5
  14.8 2.5 %collective-permute-start.4 = (f32[21,8,128]{2,1,0:T(8,128)S(1)}, f32[21,8,128]{2,1,0:T(8,128)S(1)}, u32[]{:S(2)}, u32[]{:S(2)}) collective-permute-start(f32[21,8,128]{2,1,0:T(8,128)S(1)} %get-tuple-element.54), channel_id=1, source_target_pairs={{0,1},{1,0},{2,3},{3,2},{4,5},{5,4},{6,7},{7,6},{8,9},{9,8},{10,11... | collective-permute-start | bytes 258056 | tf_op jit(solution)/shard_map/ppermute | solution.py:1000
  17.3 0.1 pad.36.clone
  17.3 0.1 pad.31.clone
  17.4 2.3 %collective-permute-done.4 = f32[21,8,128]{2,1,0:T(8,128)S(1)} collective-permute-done((f32[21,8,128]{2,1,0:T(8,128)S(1)}, f32[21,8,128]{2,1,0:T(8,128)S(1)}, u32[]{:S(2)}, u32[]{:S(2)}) %collective-permute-start.4) | collective-permute-done | bytes 86048 | tf_op jit(solution)/shard_map/ppermute | solution.py:1000
  19.9 0.1 maximum_maximum_fusion
  19.9 0.1 fusion.7
  20.0 1.4 %collective-permute-start.7 = (f32[18,8,128]{2,1,0:T(8,128)S(1)}, f32[18,8,128]{2,1,0:T(8,128)S(1)}, u32[]{:S(2)}, u32[]{:S(2)}) collective-permute-start(f32[18,8,128]{2,1,0:T(8,128)S(1)} %pad_maximum_fusion.3), channel_id=1, source_target_pairs={{0,28},{1,29},{2,30},{3,31},{4,8},{5,9},{6,10},{7,11},{8,4},{9,5},... | collective-permute-start | bytes 221192 | tf_op jit(solution)/shard_map/ppermute | solution.py:1001
  21.5 0.2 collective-permute-start.6
  21.7 1.0 %collective-permute-done.6 = f32[17,8,128]{2,1,0:T(8,128)S(1)} collective-permute-done((f32[17,8,128]{2,1,0:T(8,128)S(1)}, f32[17,8,128]{2,1,0:T(8,128)S(1)}, u32[]{:S(2)}, u32[]{:S(2)}) %collective-permute-start.6) | collective-permute-done | bytes 69664 | tf_op jit(solution)/shard_map/ppermute | solution.py:1000
  22.8 2.6 %collective-permute-done.7 = f32[18,8,128]{2,1,0:T(8,128)S(1)} collective-permute-done((f32[18,8,128]{2,1,0:T(8,128)S(1)}, f32[18,8,128]{2,1,0:T(8,128)S(1)}, u32[]{:S(2)}, u32[]{:S(2)}) %collective-permute-start.7) | collective-permute-done | bytes 73760 | tf_op jit(solution)/shard_map/ppermute | solution.py:1001
  25.3 0.7 %first_apply.1 = (f32[8,8,8,128]{3,2,1,0:T(8,128)S(1)}, f32[8,8,8,128]{3,2,1,0:T(8,128)S(1)}, f32[16,8,128]{2,1,0:T(8,128)S(1)}, f32[16,8,128]{2,1,0:T(8,128)S(1...) custom-call(f32[10,112,128]{2,1,0:T(8,128)S(1)} %get-tuple-element.53.refs_0_, ...), custom_call_target="tpu_custom_call" | custom-call | flops 800000000 | bytes 2400000 | tf_op jit(solution)/shard_map/first_apply/pallas_call | solution.py:970
  26.1 1.8 %collective-permute-start.8 = (f32[17,8,128]{2,1,0:T(8,128)S(1)}, f32[17,8,128]{2,1,0:T(8,128)S(1)}, u32[]{:S(2)}, u32[]{:S(2)}) collective-permute-start(f32[17,8,128]{2,1,0:T(8,128)S(1)} %pad_maximum_fusion.5), channel_id=1, source_target_pairs={{0,1},{1,0},{2,3},{3,2},{4,5},{5,4},{6,7},{7,6},{8,9},{9,8},{10,11... | collective-permute-start | bytes 208904 | tf_op jit(solution)/shard_map/ppermute | solution.py:1000
  27.9 0.1 pad.19.clone
  28.0 2.5 %collective-permute-done.8 = f32[17,8,128]{2,1,0:T(8,128)S(1)} collective-permute-done((f32[17,8,128]{2,1,0:T(8,128)S(1)}, f32[17,8,128]{2,1,0:T(8,128)S(1)}, u32[]{:S(2)}, u32[]{:S(2)}) %collective-permute-start.8) | collective-permute-done | bytes 69664 | tf_op jit(solution)/shard_map/ppermute | solution.py:1000
  30.5 0.9 %collective-permute-start.12 = (f32[8,128]{1,0:T(8,128)S(1)}, f32[8,128]{1,0:T(8,128)S(1)}, u32[]{:S(2)}, u32[]{:S(2)}) collective-permute-start(f32[8,128]{1,0:T(8,128)S(1)} %fusion.14), channel_id=1, source_target_pairs={{0,16},{1,17},{2,18},{3,19},{4,20},{5,21},{6,22},{7,23},{8,24},{9,... | collective-permute-start | bytes 12296 | tf_op jit(solution)/shard_map/ppermute | solution.py:1011
  31.4 0.1 fusion.3
  31.5 1.0 %collective-permute-start.11 = (f32[2,10,8,128]{3,2,1,0:T(8,128)S(1)}, f32[2,10,8,128]{3,2,1,0:T(8,128)S(1)}, u32[]{:S(2)}, u32[]{:S(2)}) collective-permute-start(f32[2,10,8,128]{3,2,1,0:T(8,128)S(1)} %get-tuple-element.126), channel_id=1, source_target_pairs={{0,28},{1,29},{2,30},{3,31},{4,8},{5,9},{6,10},{7,11},{8,4},{9,5},... | collective-permute-start | bytes 245768 | tf_op jit(solution)/shard_map/ppermute | solution.py:1001
  32.5 0.2 collective-permute-start.10
  32.7 0.1 porosity.1.refs_5_.refs_10_
  32.8 1.3 %collective-permute-done.12 = f32[8,128]{1,0:T(8,128)S(1)} collective-permute-done((f32[8,128]{1,0:T(8,128)S(1)}, f32[8,128]{1,0:T(8,128)S(1)}, u32[]{:S(2)}, u32[]{:S(2)}) %collective-permute-start.12) | collective-permute-done | bytes 4128 | tf_op jit(solution)/shard_map/ppermute | solution.py:1011
  34.1 2.4 %collective-permute-done.11.refs_4_ = f32[2,10,8,128]{3,2,1,0:T(8,128)S(1)} collective-permute-done((f32[2,10,8,128]{3,2,1,0:T(8,128)S(1)}, f32[2,10,8,128]{3,2,1,0:T(8,128)S(1)}, u32[]{:S(2)}, u32[]{:S(2)}) %collective-permute-start.11) | collective-permute-done | bytes 81952 | tf_op jit(solution)/shard_map/ppermute | solution.py:1001
  36.5 1.5 %second_solve.1 = (f32[8,8,8,128]{3,2,1,0:T(8,128)S(1)}, f32[10,112,128]{2,1,0:T(8,128)S(1)}, f32[20,8,128]{2,1,0:T(8,128)S(1)}, f32[20,8,128]{2,1,0:T(8,128)S(1...) custom-call(f32[8,8,8,128]{3,2,1,0:T(8,128)S(1)} %get-tuple-element.58.refs_0_, ...), custom_call_target="tpu_custom_call" | custom-call | flops 1300000000 | bytes 3900000 | tf_op jit(solution)/shard_map/second_solve/pallas_call | solution.py:970
  38.0 1.8 %collective-permute-start.13 = (f32[20,8,128]{2,1,0:T(8,128)S(1)}, f32[20,8,128]{2,1,0:T(8,128)S(1)}, u32[]{:S(2)}, u32[]{:S(2)}) collective-permute-start(f32[20,8,128]{2,1,0:T(8,128)S(1)} %get-tuple-element.68), channel_id=1, source_target_pairs={{0,1},{1,0},{2,3},{3,2},{4,5},{5,4},{6,7},{7,6},{8,9},{9,8},{10,11... | collective-permute-start | bytes 245768 | tf_op jit(solution)/shard_map/ppermute | solution.py:1000
  39.9 2.7 %collective-permute-done.13 = f32[20,8,128]{2,1,0:T(8,128)S(1)} collective-permute-done((f32[20,8,128]{2,1,0:T(8,128)S(1)}, f32[20,8,128]{2,1,0:T(8,128)S(1)}, u32[]{:S(2)}, u32[]{:S(2)}) %collective-permute-start.13) | collective-permute-done | bytes 81952 | tf_op jit(solution)/shard_map/ppermute | solution.py:1000
  42.6 0.1 fusion.11
  42.7 0.7 %collective-permute-start.16 = (f32[2,8,8,128]{3,2,1,0:T(8,128)S(1)}, f32[2,8,8,128]{3,2,1,0:T(8,128)S(1)}, u32[]{:S(2)}, u32[]{:S(2)}) collective-permute-start(f32[2,8,8,128]{3,2,1,0:T(8,128)S(1)} %get-tuple-element.124), channel_id=1, source_target_pairs={{0,28},{1,29},{2,30},{3,31},{4,8},{5,9},{6,10},{7,11},{8,4},{9,5},... | collective-permute-start | bytes 196616 | tf_op jit(solution)/shard_map/ppermute | solution.py:1001
  43.4 0.6 collective-permute-start.15
  44.0 3.3 %collective-permute-done.16.refs_4_ = f32[2,8,8,128]{3,2,1,0:T(8,128)S(1)} collective-permute-done((f32[2,8,8,128]{3,2,1,0:T(8,128)S(1)}, f32[2,8,8,128]{3,2,1,0:T(8,128)S(1)}, u32[]{:S(2)}, u32[]{:S(2)}) %collective-permute-start.16) | collective-permute-done | bytes 65568 | tf_op jit(solution)/shard_map/ppermute | solution.py:1001
  47.3 1.6 %late_apply.1 = (f32[8,8,8,128]{3,2,1,0:T(8,128)S(1)}, f32[8,8,8,128]{3,2,1,0:T(8,128)S(1)}, f32[10,8,128]{2,1,0:T(8,128)S(1)}, f32[10,8,128]{2,1,0:T(8,128)S(1)...) custom-call(f32[10,112,128]{2,1,0:T(8,128)S(1)} %get-tuple-element.67.refs_0_, ...), custom_call_target="tpu_custom_call" | custom-call | flops 800000000 | bytes 2400000 | tf_op jit(solution)/shard_map/late_apply/pallas_call | solution.py:970
  49.0 3.8 %all-to-all-start = ((f32[32,4,128]{2,1,0:T(4,128)}), f32[32,4,128]{2,1,0:T(4,128)S(1)}, u32[]{:S(2)}, u32[]{:S(2)}) async-start(f32[32,4,128]{2,1,0:T(4,128)} %get-tuple-element.93), calls=%async_computation | async-start | bytes 131072 | tf_op jit(solution)/shard_map/all_to_all | solution.py:1037
  52.8 1.8 %collective-permute-start.17 = (f32[10,8,128]{2,1,0:T(8,128)S(1)}, f32[10,8,128]{2,1,0:T(8,128)S(1)}, u32[]{:S(2)}, u32[]{:S(2)}) collective-permute-start(f32[10,8,128]{2,1,0:T(8,128)S(1)} %get-tuple-element.75), channel_id=1, source_target_pairs={{0,1},{1,0},{2,3},{3,2},{4,5},{5,4},{6,7},{7,6},{8,9},{9,8},{10,11... | collective-permute-start | bytes 122888 | tf_op jit(solution)/shard_map/ppermute | solution.py:1000
  54.6 0.5 collective-permute-start.19
  55.1 2.0 %collective-permute-start.20 = (f32[10,8,128]{2,1,0:T(8,128)S(1)}, f32[10,8,128]{2,1,0:T(8,128)S(1)}, u32[]{:S(2)}, u32[]{:S(2)}) collective-permute-start(f32[10,8,128]{2,1,0:T(8,128)S(1)} %get-tuple-element.78), channel_id=1, source_target_pairs={{0,28},{1,29},{2,30},{3,31},{4,8},{5,9},{6,10},{7,11},{8,4},{9,5},... | collective-permute-start | bytes 122888 | tf_op jit(solution)/shard_map/ppermute | solution.py:1001
  57.1 0.1 prepare.1
  57.2 2.7 %collective-permute-done.20.refs_9_ = f32[10,8,128]{2,1,0:T(8,128)S(1)} collective-permute-done((f32[10,8,128]{2,1,0:T(8,128)S(1)}, f32[10,8,128]{2,1,0:T(8,128)S(1)}, u32[]{:S(2)}, u32[]{:S(2)}) %collective-permute-start.20) | collective-permute-done | bytes 40992 | tf_op jit(solution)/shard_map/ppermute | solution.py:1001
  59.9 0.7 %all-to-all-done.refs_12_ = f32[32,4,128]{2,1,0:T(4,128)S(1)} async-done(((f32[32,4,128]{2,1,0:T(4,128)}), f32[32,4,128]{2,1,0:T(4,128)S(1)}, u32[]{:S(2)}, u32[]{:S(2)}) %all-to-all-start) | async-done | bytes 65568 | tf_op jit(solution)/shard_map/all_to_all | solution.py:1037
  60.6 1.4 %late_final.1 = (f32[8,8,8,128]{3,2,1,0:T(8,128)}, f32[8,8,8,128]{3,2,1,0:T(8,128)}, f32[8,8,8,128]{3,2,1,0:T(8,128)}, f32[2]{0:T(128)}) custom-call(f32[8,8,8,128]{3,2,1,0:T(8,128)S(1)} %get-tuple-element.84.refs_0_, f32[8,8,8,128]{3,2,1,0:T(8,128)S(1)} %get-tuple-element.85.refs_1_, f32[8,8,8,128]{3,2,1,0:T(8,128)S(1)} %get-tuple-element.72.refs_10_.refs_2_, ...), custom_call_target="tpu_custom_call" | custom-call | flops 800000000 | bytes 2400000 | tf_op jit(solution)/shard_map/late_final/pallas_call | solution.py:970
  (63 shorter events, 0.3 us)
Async XLA Ops:
  0.6 1.0 %copy-start = (f32[1,1,8,8,8,128]{5,4,3,2,1,0:T(8,128)S(1)}, f32[1,1,8,8,8,128]{5,4,3,2,1,0:T(8,128)}, u32[]{:S(2)}) copy-start(f32[1,1,8,8,8,128]{5,4,3,2,1,0:T(8,128)} %param.8) | copy-start | bytes 786436
  1.6 12.0 %copy-start.3 = (f32[10,104,128]{2,1,0:T(8,128)S(1)}, f32[10,104,128]{2,1,0:T(8,128)}, u32[]{:S(2)}) copy-start(f32[10,104,128]{2,1,0:T(8,128)} %constant.45.clone.refs_8_.refs_10_) | copy-start | bytes 1597444
  1.7 4.6 %collective-permute-start.1 = (f32[8,8,128]{2,1,0:T(8,128)S(1)}, f32[8,8,128]{2,1,0:T(8,128)S(1)}, u32[]{:S(2)}, u32[]{:S(2)}) collective-permute-start(f32[8,8,128]{2,1,0:T(8,128)S(1)} %get-tuple-element.52), channel_id=1, source_target_pairs={{0,4},{1,2},{2,1},{3,7},{4,0},{5,6},{6,5},{7,3},{8,12},{9,10},{10,... | collective-permute-start | bytes 98312 | tf_op jit(solution)/shard_map/ppermute | solution.py:1001
  2.2 6.1 %collective-permute-start = (f32[9,8,128]{2,1,0:T(8,128)S(1)}, f32[9,8,128]{2,1,0:T(8,128)S(1)}, u32[]{:S(2)}, u32[]{:S(2)}) collective-permute-start(f32[9,8,128]{2,1,0:T(8,128)S(1)} %get-tuple-element.51), channel_id=1, source_target_pairs={{0,1},{1,0},{2,3},{3,2},{4,5},{5,4},{6,7},{7,6},{8,9},{9,8},{10,11... | collective-permute-start | bytes 110600 | tf_op jit(solution)/shard_map/ppermute | solution.py:1000
  6.3 7.2 %copy-start.1 = (f32[1,1,8,8,8,128]{5,4,3,2,1,0:T(8,128)S(1)}, f32[1,1,8,8,8,128]{5,4,3,2,1,0:T(8,128)}, u32[]{:S(2)}) copy-start(f32[1,1,8,8,8,128]{5,4,3,2,1,0:T(8,128)} %param.8) | copy-start | bytes 786436
  8.3 0.7 %copy-start.7 = (s32[1,1,128]{2,1,0:T(1,128)S(1)}, s32[1,1,128]{2,1,0:T(1,128)}, u32[]{:S(2)}) copy-start(s32[1,1,128]{2,1,0:T(1,128)} %param.9) | copy-start | bytes 1540
  8.3 5.2 %copy-start.6 = (f32[104,112]{1,0:T(8,128)S(1)}, f32[104,112]{1,0:T(8,128)}, u32[]{:S(2)}) copy-start(f32[104,112]{1,0:T(8,128)} %constant.43.clone.refs_6_.refs_8_) | copy-start | bytes 139780
  8.4 5.2 %copy-start.5 = (f32[112,104]{1,0:T(8,128)S(1)}, f32[112,104]{1,0:T(8,128)}, u32[]{:S(2)}) copy-start(f32[112,104]{1,0:T(8,128)} %constant.44.clone.refs_7_.refs_9_) | copy-start | bytes 139780
  8.4 2.6 %collective-permute-start.2 = (f32[11,8,128]{2,1,0:T(8,128)S(1)}, f32[11,8,128]{2,1,0:T(8,128)S(1)}, u32[]{:S(2)}, u32[]{:S(2)}) collective-permute-start(f32[11,8,128]{2,1,0:T(8,128)S(1)} %pad_maximum_fusion.10), channel_id=1, source_target_pairs={{0,4},{1,5},{2,6},{3,7},{4,0},{5,1},{6,2},{7,3},{8,12},{9,13},{10,... | collective-permute-start | bytes 135176 | tf_op jit(solution)/shard_map/ppermute | solution.py:1000
  9.0 4.6 %collective-permute-start.3 = (f32[10,8,128]{2,1,0:T(8,128)S(1)}, f32[10,8,128]{2,1,0:T(8,128)S(1)}, u32[]{:S(2)}, u32[]{:S(2)}) collective-permute-start(f32[10,8,128]{2,1,0:T(8,128)S(1)} %get-tuple-element.119), channel_id=1, source_target_pairs={{0,28},{1,29},{2,30},{3,31},{4,8},{5,9},{6,10},{7,11},{8,4},{9,5},... | collective-permute-start | bytes 122888 | tf_op jit(solution)/shard_map/ppermute | solution.py:1001
  14.7 5.0 %collective-permute-start.5 = (f32[22,8,128]{2,1,0:T(8,128)S(1)}, f32[22,8,128]{2,1,0:T(8,128)S(1)}, u32[]{:S(2)}, u32[]{:S(2)}) collective-permute-start(f32[22,8,128]{2,1,0:T(8,128)S(1)} %pad_maximum_fusion), channel_id=1, source_target_pairs={{0,4},{1,2},{2,1},{3,7},{4,0},{5,6},{6,5},{7,3},{8,12},{9,10},{10,... | collective-permute-start | bytes 270344 | tf_op jit(solution)/shard_map/ppermute | solution.py:1001
  14.8 4.9 %collective-permute-start.4 = (f32[21,8,128]{2,1,0:T(8,128)S(1)}, f32[21,8,128]{2,1,0:T(8,128)S(1)}, u32[]{:S(2)}, u32[]{:S(2)}) collective-permute-start(f32[21,8,128]{2,1,0:T(8,128)S(1)} %get-tuple-element.54), channel_id=1, source_target_pairs={{0,1},{1,0},{2,3},{3,2},{4,5},{5,4},{6,7},{7,6},{8,9},{9,8},{10,11... | collective-permute-start | bytes 258056 | tf_op jit(solution)/shard_map/ppermute | solution.py:1000
  20.0 5.3 %collective-permute-start.7 = (f32[18,8,128]{2,1,0:T(8,128)S(1)}, f32[18,8,128]{2,1,0:T(8,128)S(1)}, u32[]{:S(2)}, u32[]{:S(2)}) collective-permute-start(f32[18,8,128]{2,1,0:T(8,128)S(1)} %pad_maximum_fusion.3), channel_id=1, source_target_pairs={{0,28},{1,29},{2,30},{3,31},{4,8},{5,9},{6,10},{7,11},{8,4},{9,5},... | collective-permute-start | bytes 221192 | tf_op jit(solution)/shard_map/ppermute | solution.py:1001
  21.5 1.3 %collective-permute-start.6 = (f32[17,8,128]{2,1,0:T(8,128)S(1)}, f32[17,8,128]{2,1,0:T(8,128)S(1)}, u32[]{:S(2)}, u32[]{:S(2)}) collective-permute-start(f32[17,8,128]{2,1,0:T(8,128)S(1)} %pad_maximum_fusion.4), channel_id=1, source_target_pairs={{0,4},{1,5},{2,6},{3,7},{4,0},{5,1},{6,2},{7,3},{8,12},{9,13},{10,... | collective-permute-start | bytes 208904 | tf_op jit(solution)/shard_map/ppermute | solution.py:1000
  26.1 4.4 %collective-permute-start.8 = (f32[17,8,128]{2,1,0:T(8,128)S(1)}, f32[17,8,128]{2,1,0:T(8,128)S(1)}, u32[]{:S(2)}, u32[]{:S(2)}) collective-permute-start(f32[17,8,128]{2,1,0:T(8,128)S(1)} %pad_maximum_fusion.5), channel_id=1, source_target_pairs={{0,1},{1,0},{2,3},{3,2},{4,5},{5,4},{6,7},{7,6},{8,9},{9,8},{10,11... | collective-permute-start | bytes 208904 | tf_op jit(solution)/shard_map/ppermute | solution.py:1000
  28.0 3.4 %collective-permute-start.9 = (f32[16,8,128]{2,1,0:T(8,128)S(1)}, f32[16,8,128]{2,1,0:T(8,128)S(1)}, u32[]{:S(2)}, u32[]{:S(2)}) collective-permute-start(f32[16,8,128]{2,1,0:T(8,128)S(1)} %get-tuple-element.60), channel_id=1, source_target_pairs={{0,4},{1,2},{2,1},{3,7},{4,0},{5,6},{6,5},{7,3},{8,12},{9,10},{10,... | collective-permute-start | bytes 196616 | tf_op jit(solution)/shard_map/ppermute | solution.py:1001
  30.5 3.6 %collective-permute-start.12 = (f32[8,128]{1,0:T(8,128)S(1)}, f32[8,128]{1,0:T(8,128)S(1)}, u32[]{:S(2)}, u32[]{:S(2)}) collective-permute-start(f32[8,128]{1,0:T(8,128)S(1)} %fusion.14), channel_id=1, source_target_pairs={{0,16},{1,17},{2,18},{3,19},{4,20},{5,21},{6,22},{7,23},{8,24},{9,... | collective-permute-start | bytes 12296 | tf_op jit(solution)/shard_map/ppermute | solution.py:1011
  31.5 5.0 %collective-permute-start.11 = (f32[2,10,8,128]{3,2,1,0:T(8,128)S(1)}, f32[2,10,8,128]{3,2,1,0:T(8,128)S(1)}, u32[]{:S(2)}, u32[]{:S(2)}) collective-permute-start(f32[2,10,8,128]{3,2,1,0:T(8,128)S(1)} %get-tuple-element.126), channel_id=1, source_target_pairs={{0,28},{1,29},{2,30},{3,31},{4,8},{5,9},{6,10},{7,11},{8,4},{9,5},... | collective-permute-start | bytes 245768 | tf_op jit(solution)/shard_map/ppermute | solution.py:1001
  32.5 4.0 %collective-permute-start.10 = (f32[2,10,8,128]{3,2,1,0:T(8,128)S(1)}, f32[2,10,8,128]{3,2,1,0:T(8,128)S(1)}, u32[]{:S(2)}, u32[]{:S(2)}) collective-permute-start(f32[2,10,8,128]{3,2,1,0:T(8,128)S(1)} %get-tuple-element.127), channel_id=1, source_target_pairs={{0,4},{1,5},{2,6},{3,7},{4,0},{5,1},{6,2},{7,3},{8,12},{9,13},{10,... | collective-permute-start | bytes 245768 | tf_op jit(solution)/shard_map/ppermute | solution.py:1000
  32.7 3.8 %copy-start.4 = (f32[288,128]{1,0:T(8,128)S(1)}, f32[288,128]{1,0:T(8,128)}, u32[]{:S(2)}) copy-start(f32[288,128]{1,0:T(8,128)} %constant.42.clone.refs_6_.refs_11_) | copy-start | bytes 442372
  38.0 4.5 %collective-permute-start.13 = (f32[20,8,128]{2,1,0:T(8,128)S(1)}, f32[20,8,128]{2,1,0:T(8,128)S(1)}, u32[]{:S(2)}, u32[]{:S(2)}) collective-permute-start(f32[20,8,128]{2,1,0:T(8,128)S(1)} %get-tuple-element.68), channel_id=1, source_target_pairs={{0,1},{1,0},{2,3},{3,2},{4,5},{5,4},{6,7},{7,6},{8,9},{9,8},{10,11... | collective-permute-start | bytes 245768 | tf_op jit(solution)/shard_map/ppermute | solution.py:1000
  39.8 2.7 %collective-permute-start.14 = (f32[20,8,128]{2,1,0:T(8,128)S(1)}, f32[20,8,128]{2,1,0:T(8,128)S(1)}, u32[]{:S(2)}, u32[]{:S(2)}) collective-permute-start(f32[20,8,128]{2,1,0:T(8,128)S(1)} %get-tuple-element.69), channel_id=1, source_target_pairs={{0,4},{1,2},{2,1},{3,7},{4,0},{5,6},{6,5},{7,3},{8,12},{9,10},{10,... | collective-permute-start | bytes 245768 | tf_op jit(solution)/shard_map/ppermute | solution.py:1001
  42.7 4.7 %collective-permute-start.16 = (f32[2,8,8,128]{3,2,1,0:T(8,128)S(1)}, f32[2,8,8,128]{3,2,1,0:T(8,128)S(1)}, u32[]{:S(2)}, u32[]{:S(2)}) collective-permute-start(f32[2,8,8,128]{3,2,1,0:T(8,128)S(1)} %get-tuple-element.124), channel_id=1, source_target_pairs={{0,28},{1,29},{2,30},{3,31},{4,8},{5,9},{6,10},{7,11},{8,4},{9,5},... | collective-permute-start | bytes 196616 | tf_op jit(solution)/shard_map/ppermute | solution.py:1001
  43.4 3.9 %collective-permute-start.15 = (f32[2,8,8,128]{3,2,1,0:T(8,128)S(1)}, f32[2,8,8,128]{3,2,1,0:T(8,128)S(1)}, u32[]{:S(2)}, u32[]{:S(2)}) collective-permute-start(f32[2,8,8,128]{3,2,1,0:T(8,128)S(1)} %get-tuple-element.125), channel_id=1, source_target_pairs={{0,4},{1,5},{2,6},{3,7},{4,0},{5,1},{6,2},{7,3},{8,12},{9,13},{10,... | collective-permute-start | bytes 196616 | tf_op jit(solution)/shard_map/ppermute | solution.py:1000
  47.3 9.8 %copy-start.2 = (f32[1,1,8,8,8,128]{5,4,3,2,1,0:T(8,128)S(1)}, f32[1,1,8,8,8,128]{5,4,3,2,1,0:T(8,128)}, u32[]{:S(2)}) copy-start(f32[1,1,8,8,8,128]{5,4,3,2,1,0:T(8,128)} %param.7) | copy-start | bytes 786436
  49.0 11.7 %all-to-all-start = ((f32[32,4,128]{2,1,0:T(4,128)}), f32[32,4,128]{2,1,0:T(4,128)S(1)}, u32[]{:S(2)}, u32[]{:S(2)}) async-start(f32[32,4,128]{2,1,0:T(4,128)} %get-tuple-element.93), calls=%async_computation | async-start | bytes 131072 | tf_op jit(solution)/shard_map/all_to_all | solution.py:1037
  52.8 4.4 %collective-permute-start.17 = (f32[10,8,128]{2,1,0:T(8,128)S(1)}, f32[10,8,128]{2,1,0:T(8,128)S(1)}, u32[]{:S(2)}, u32[]{:S(2)}) collective-permute-start(f32[10,8,128]{2,1,0:T(8,128)S(1)} %get-tuple-element.75), channel_id=1, source_target_pairs={{0,1},{1,0},{2,3},{3,2},{4,5},{5,4},{6,7},{7,6},{8,9},{9,8},{10,11... | collective-permute-start | bytes 122888 | tf_op jit(solution)/shard_map/ppermute | solution.py:1000
  54.6 2.6 %collective-permute-start.18 = (f32[10,8,128]{2,1,0:T(8,128)S(1)}, f32[10,8,128]{2,1,0:T(8,128)S(1)}, u32[]{:S(2)}, u32[]{:S(2)}) collective-permute-start(f32[10,8,128]{2,1,0:T(8,128)S(1)} %get-tuple-element.76), channel_id=1, source_target_pairs={{0,4},{1,2},{2,1},{3,7},{4,0},{5,6},{6,5},{7,3},{8,12},{9,10},{10,... | collective-permute-start | bytes 122888 | tf_op jit(solution)/shard_map/ppermute | solution.py:1001
  54.6 2.6 %collective-permute-start.19 = (f32[10,8,128]{2,1,0:T(8,128)S(1)}, f32[10,8,128]{2,1,0:T(8,128)S(1)}, u32[]{:S(2)}, u32[]{:S(2)}) collective-permute-start(f32[10,8,128]{2,1,0:T(8,128)S(1)} %get-tuple-element.77), channel_id=1, source_target_pairs={{0,4},{1,5},{2,6},{3,7},{4,0},{5,1},{6,2},{7,3},{8,12},{9,13},{10,... | collective-permute-start | bytes 122888 | tf_op jit(solution)/shard_map/ppermute | solution.py:1000
  55.1 4.8 %collective-permute-start.20 = (f32[10,8,128]{2,1,0:T(8,128)S(1)}, f32[10,8,128]{2,1,0:T(8,128)S(1)}, u32[]{:S(2)}, u32[]{:S(2)}) collective-permute-start(f32[10,8,128]{2,1,0:T(8,128)S(1)} %get-tuple-element.78), channel_id=1, source_target_pairs={{0,28},{1,29},{2,30},{3,31},{4,8},{5,9},{6,10},{7,11},{8,4},{9,5},... | collective-permute-start | bytes 122888 | tf_op jit(solution)/shard_map/ppermute | solution.py:1001

commit v7 on v6

--- a/solution.py
+++ b/solution.py
@@ -14,6 +14,8 @@
 ROWS = 112
 MODES = 104
 AXES = ("gx", "gy")
+EDGE = (0, 1, EXT - 2, EXT - 1)
+INNER = tuple(range(2, EXT - 2))
 
 shift_mass = 0.1
 mean_porosity = 0.7
@@ -124,11 +126,17 @@
                 mean_porosity * (EIGEN + EIGEN[mode_b] + EIGEN[mode_c]) + shift_mass
             )
     lanes = np.repeat(inverse.T[:, :, None], 128, axis=2)
-    return (
-        forward.astype(np.float32),
-        forward.T.astype(np.float32).copy(),
-        lanes.astype(np.float32),
-    )
+    back = forward.T
+    tables = [
+        np.concatenate([back[[8 * b + k for b in layers for k in range(NODES)]]]
+                       + [pad_rows(back[[at + b for b in layers]], 8) for at in (80, 96)])
+        for layers in (EDGE, INNER)
+    ]
+    return tuple(table.astype(np.float32) for table in (forward, *tables, lanes))
+
+
+def pad_rows(table, count):
+    return np.pad(table, ((0, -len(table) % count), (0, 0)))
 
 
 def row_tile(values):
@@ -326,7 +334,7 @@
     return jnp.concatenate([ref[a] for a in range(EXT)], axis=1)
 
 
-def local_solve(x_ref, forward_ref, back_ref, inverse_ref, part_ref):
+def to_spectrum(x_ref, forward_ref, inverse_ref):
     zero = jnp.zeros((6, 128), jnp.float32)
     for a in range(EXT):
         x_ref[a, 80:90] = shift_up(x_ref[a, pl.ds(6, EXT, stride=NODES), :])
@@ -348,10 +356,15 @@
     spectrum = jnp.dot(
         forward_ref[...], planes(x_ref), precision=plane_mode, preferred_element_type=jnp.float32
     ) * planes(inverse_ref)
+    return spectrum
+
+
+def from_spectrum(spectrum, back_ref, part_ref, count):
+    half = EXT // 2
     values = jnp.dot(
         back_ref[...], spectrum, precision=plane_mode, preferred_element_type=jnp.float32
     )
-    for block in range(ROWS // 8):
+    for block in range(part_ref.shape[1] // 8):
         rows = pl.ds(block * 8, 8)
         modes = [values[block * 8 : block * 8 + 8, m * 128 : (m + 1) * 128] for m in range(EXT)]
         back = {}
@@ -365,32 +378,53 @@
         for a in range(half):
             part_ref[a, rows] = back[(1, a)] + back[(-1, a)]
             part_ref[EXT - 1 - a, rows] = back[(1, a)] - back[(-1, a)]
+    below, above = NODES * count, NODES * count + 8
     for a in range(EXT):
 
         def layer(k):
-            return (a, pl.ds(k, EXT, stride=NODES), slice(None))
+            return (a, pl.ds(k, count, stride=NODES), slice(None))
 
         bottom, top = part_ref[layer(0)], part_ref[layer(NODES - 1)]
         part_ref[layer(0)] = bottom + shift_up(top)
         part_ref[layer(NODES - 1)] = top + shift_down(bottom)
-        part_ref[layer(1)] = part_ref[layer(1)] + shift_up(part_ref[a, 96:106])
-        part_ref[layer(NODES - 2)] = part_ref[layer(NODES - 2)] + shift_down(part_ref[a, 80:90])
-
-
-def send_parts(part_ref, side_x, side_y, sy_first, sy_second, fx_first, fx_second):
+        part_ref[layer(1)] = part_ref[layer(1)] + shift_up(part_ref[a, above : above + count])
+        part_ref[layer(NODES - 2)] = part_ref[layer(NODES - 2)] + shift_down(
+            part_ref[a, below : below + count]
+        )
+
+
+def solve_edges(
+    x_ref, forward_ref, back_ref, inverse_ref, spectrum_ref, edge_ref, sy_first, sy_second,
+    side_y, part_ref,
+):
+    spectrum = to_spectrum(x_ref, forward_ref, inverse_ref)
+    spectrum_ref[...] = spectrum
+    from_spectrum(spectrum, back_ref, part_ref, len(EDGE))
     for a in range(EXT):
-        low, high = part_ref[a, 0:16], part_ref[a, 64:80]
+        low, high = part_ref[a, 0:16], part_ref[a, 16:32]
         sy_first[2 * a : 2 * a + 2] = side_y.send_first(low, high).reshape(2, NODES, 128)
         sy_second[2 * a : 2 * a + 2] = side_y.send_second(low, high).reshape(2, NODES, 128)
+        edge_ref[a] = part_ref[a, 8:24]
+
+
+def rest_kernel(
+    counts, spectrum_ref, edge_ref, back_ref, part_ref, fx_first, fx_second, inner_ref
+):
+    side_x = Sides("gx", counts[0])
+    from_spectrum(spectrum_ref[...], back_ref, inner_ref, len(INNER))
+    for a in range(EXT):
+        part_ref[a, 0:8] = edge_ref[a, 0:8]
+        part_ref[a, 8:56] = inner_ref[a, 0:48]
+        part_ref[a, 56:64] = edge_ref[a, 8:16]
     for layer in range(2):
-        low, high = part_ref[layer, 0:80], part_ref[NODES + layer, 0:80]
-        fx_first[layer] = side_x.send_first(low, high).reshape(EXT, NODES, 128)
-        fx_second[layer] = side_x.send_second(low, high).reshape(EXT, NODES, 128)
+        low, high = part_ref[layer], part_ref[NODES + layer]
+        fx_first[layer] = side_x.send_first(low, high).reshape(NODES, NODES, 128)
+        fx_second[layer] = side_x.send_second(low, high).reshape(NODES, NODES, 128)
 
 
 def first_solve_kernel(
     counts, r_ref, porosity_ref, ry_first, ry_second, rx_first, rx_second, forward_ref, back_ref,
-    inverse_ref, part_ref, sy_first, sy_second, fx_first, fx_second, x_ref,
+    inverse_ref, spectrum_ref, edge_ref, sy_first, sy_second, x_ref, part_ref,
 ):
     for send in (sy_first, sy_second):
         send[2 * EXT] = jnp.broadcast_to(porosity_ref[...], (NODES, 128))
@@ -401,26 +435,30 @@
         x_ref[a + 1, 0:8] = side_y.low(ry_first[a], ry_second[a])
         x_ref[a + 1, 8:72] = r_ref[a].reshape(64, 128)
         x_ref[a + 1, 72:80] = side_y.high(ry_first[a], ry_second[a])
-    local_solve(x_ref, forward_ref, back_ref, inverse_ref, part_ref)
-    send_parts(part_ref, side_x, side_y, sy_first, sy_second, fx_first, fx_second)
+    solve_edges(
+        x_ref, forward_ref, back_ref, inverse_ref, spectrum_ref, edge_ref, sy_first, sy_second,
+        side_y, part_ref,
+    )
 
 
 def second_solve_kernel(
-    counts, u_ref, ry_first, ry_second, rx_first, rx_second, forward_ref, back_ref, inverse_ref,
-    q_ref, part_ref, sy_first, sy_second, fx_first, fx_second, x_ref,
+    counts, edge_ref, inner_ref, ry_first, ry_second, rx_first, rx_second, forward_ref, back_ref,
+    inverse_ref, q_ref, spectrum_ref, layers_ref, sy_first, sy_second, x_ref, part_ref,
 ):
     side_x, side_y = Sides("gx", counts[0]), Sides("gy", counts[1])
     extend_image(
-        u_ref, ry_first, ry_second, rx_first, rx_second, side_x, side_y, q_ref, x_ref, None
-    )
-    local_solve(x_ref, forward_ref, back_ref, inverse_ref, part_ref)
-    send_parts(part_ref, side_x, side_y, sy_first, sy_second, fx_first, fx_second)
+        edge_ref, inner_ref, ry_first, ry_second, rx_first, rx_second, side_x, side_y, q_ref, x_ref, None
+    )
+    solve_edges(
+        x_ref, forward_ref, back_ref, inverse_ref, spectrum_ref, layers_ref, sy_first, sy_second,
+        side_y, part_ref,
+    )
 
 
 def late_solve_kernel(
-    counts, u_ref, ry_first, ry_second, rx_first, rx_second, columns_ref, lift_ref, sum_ref,
-    forward_ref, back_ref, inverse_ref, q_ref, part_ref, sy_first, sy_second, fx_first, fx_second,
-    field_ref, x_ref, table_ref,
+    counts, edge_ref, inner_ref, ry_first, ry_second, rx_first, rx_second, columns_ref, lift_ref,
+    sum_ref, forward_ref, back_ref, inverse_ref, q_ref, spectrum_ref, layers_ref, sy_first,
+    sy_second, field_ref, x_ref, part_ref, table_ref,
 ):
     side_x, side_y = Sides("gx", counts[0]), Sides("gy", counts[1])
     table_ref[...] = jnp.broadcast_to(
@@ -433,14 +471,23 @@
     )
     image = LiftedImage(fields, columns_ref)
     extend_image(
-        u_ref, ry_first, ry_second, rx_first, rx_second, side_x, side_y, q_ref, x_ref, image
-    )
-    local_solve(x_ref, forward_ref, back_ref, inverse_ref, part_ref)
-    send_parts(part_ref, side_x, side_y, sy_first, sy_second, fx_first, fx_second)
+        edge_ref, inner_ref, ry_first, ry_second, rx_first, rx_second, side_x, side_y, q_ref, x_ref, image
+    )
+    solve_edges(
+        x_ref, forward_ref, back_ref, inverse_ref, spectrum_ref, layers_ref, sy_first, sy_second,
+        side_y, part_ref,
+    )
+
+
+def layer_of(edge_ref, inner_ref, a, b):
+    if 2 <= b < NODES - 2:
+        return inner_ref[a, b - 2]
+    return edge_ref[a, b if b < 2 else b - (NODES - 4)]
 
 
 def extend_image(
-    u_ref, ry_first, ry_second, rx_first, rx_second, side_x, side_y, q_ref, x_ref, image
+    edge_ref, inner_ref, ry_first, ry_second, rx_first, rx_second, side_x, side_y, q_ref, x_ref,
+    image,
 ):
     low_x = side_x.low(rx_first[...], rx_second[...])
     high_x = side_x.high(rx_first[...], rx_second[...])
@@ -457,7 +504,7 @@
         high_y = side_y.high(ry_first[a], ry_second[a])
         rows = [low_y[0]]
         for b in range(NODES):
-            value = u_ref[a, b]
+            value = layer_of(edge_ref, inner_ref, a, b)
             if b == 0:
                 value = value + low_y[1]
             if b == NODES - 1:
@@ -484,7 +531,7 @@
         low_y = side_y.low(ry_first[a + 1], ry_second[a + 1])
         high_y = side_y.high(ry_first[a + 1], ry_second[a + 1])
         for b in range(NODES):
-            value = part_ref[a + 1, (b + 1) * 8 : (b + 2) * 8]
+            value = part_ref[a + 1, b * 8 : (b + 1) * 8]
             if b < 2:
                 value = value + low_y[b]
             if b >= NODES - 2:
@@ -500,7 +547,7 @@
     return result
 
 
-def apply_tiles(z_ref, u_ref, y_ref, por):
+def apply_tiles(z_ref, u_ref, y_ref, por, layers=range(NODES)):
     weight_tile = row_tile(WEIGHTS)
     stiff_tiles = [
         row_tile([STIFF[k, (k - shift) % NODES] for k in range(NODES)]) for shift in range(NODES)
@@ -509,7 +556,7 @@
         for b in range(NODES):
             y_ref[a, b] = z_ref[a, b] * weight_tile
     for a in range(NODES):
-        for b in range(NODES):
+        for place, b in enumerate(layers):
             z = z_ref[a, b]
             third = z * stiff_tiles[0]
             for shift in range(1, NODES):
@@ -520,7 +567,7 @@
                 first = first + y_ref[other, b] * float(STIFF[a, other] * WEIGHTS[b])
                 second = second + y_ref[a, other] * float(STIFF[b, other] * WEIGHTS[a])
             weight = float(WEIGHTS[a] * WEIGHTS[b])
-            u_ref[a, b] = por * (third * weight + first + second) + y_ref[a, b] * (
+            u_ref[a, place] = por * (third * weight + first + second) + y_ref[a, b] * (
                 shift_mass * weight
             )
 
@@ -613,15 +660,33 @@
 
 def early_apply_kernel(
     counts, part_ref, ry_first, ry_second, rx_first, rx_second, porosity_ref,
-    z_ref, u_ref, sy_first, sy_second, fx_first, fx_second, y_ref,
+    z_ref, edge_ref, sy_first, sy_second, y_ref,
 ):
     side_x, side_y = Sides("gx", counts[0]), Sides("gy", counts[1])
     z = collect_parts(part_ref, ry_first, ry_second, rx_first, rx_second, side_x, side_y, None)
     for (a, b), value in z.items():
         z_ref[a, b] = value
-    apply_tiles(z_ref, u_ref, y_ref, porosity_ref[...])
-    sum_column(u_ref)
-    send_layers(u_ref, side_x, side_y, sy_first, sy_second, fx_first, fx_second)
+    apply_tiles(z_ref, edge_ref, y_ref, porosity_ref[...], (0, 1, NODES - 2, NODES - 1))
+    sum_column(edge_ref)
+    for a in range(NODES):
+        for layer in range(2):
+            low, high = edge_ref[a, layer], edge_ref[a, 2 + layer]
+            sy_first[2 * a + layer] = side_y.send_first(low, high)
+            sy_second[2 * a + layer] = side_y.send_second(low, high)
+
+
+def rest_apply_kernel(
+    counts, z_ref, edge_ref, porosity_ref, inner_ref, fx_first, fx_second, y_ref
+):
+    side_x = Sides("gx", counts[0])
+    apply_tiles(z_ref, inner_ref, y_ref, porosity_ref[...], range(2, NODES - 2))
+    sum_column(inner_ref)
+    for layer in range(2):
+        for b in range(NODES):
+            low = layer_of(edge_ref, inner_ref, layer, b)
+            high = layer_of(edge_ref, inner_ref, NODES - 2 + layer, b)
+            fx_first[layer, b] = side_x.send_first(low, high)
+            fx_second[layer, b] = side_x.send_second(low, high)
 
 
 def late_apply_kernel(
@@ -955,8 +1020,9 @@
 
 
 COSTS = {
-    "start": 100, "first_solve": 1300, "second_solve": 1300, "first_apply": 800,
-    "second_apply": 800, "prepare": 20000, "final": 500, "late_apply": 800, "porosity": 20000, "late_final": 800,
+    "start": 100, "first_solve": 900, "second_solve": 900, "rest_of_solve": 600,
+    "first_apply": 500, "rest_of_apply": 400, "second_apply": 800, "prepare": 20000,
+    "final": 500, "late_apply": 800, "porosity": 20000, "late_final": 800,
 }
 
 
@@ -1075,7 +1141,7 @@
 
 
 def shards_of(counts):
-    forward_np, back_np, inverse_np = plane_tables()
+    forward_np, back_edge_np, back_inner_np, inverse_np = plane_tables()
 
     def shards(solution, residual, grain_counts):
         shard_shape = solution.shape
@@ -1086,18 +1152,21 @@
         late = counts == (8, 4)
         every_lift = all_lift(counts, block[-1]) if late else None
         porosity = 1.0 - 0.6 * grain_counts.reshape(1, 128).astype(jnp.float32) / MOST_GRAINS
-        plane = [jnp.asarray(table) for table in (forward_np, back_np, inverse_np)]
+        plane = [jnp.asarray(table) for table in (forward_np, back_edge_np, inverse_np)]
+        back_inner = jnp.asarray(back_inner_np)
         side_x, side_y = Sides("gx", counts[0]), Sides("gy", counts[1])
         row = (counts[0] * counts[1], 4, 128)
         face = (NODES, NODES, 128)
-        part_shapes = [
-            (EXT, ROWS, 128),
-            (2 * EXT, NODES, 128), (2 * EXT, NODES, 128),
-            (2, EXT, NODES, 128), (2, EXT, NODES, 128),
-        ]
-        first_shapes = list(part_shapes)
-        first_shapes[1:3] = [(2 * EXT + 1, NODES, 128)] * 2
-        solve_scratch = [(EXT, ROWS, 128)]
+        sends = [(2 * EXT, NODES, 128)] * 2
+        solve_shapes = [(MODES, EXT * 128), (EXT, 2 * NODES, 128)]
+        solve_scratch = [(EXT, ROWS, 128), (EXT, len(back_edge_np), 128)]
+
+        def rest_of_solve(spectrum, edges):
+            return call(
+                rest_kernel, counts, "rest_of_solve",
+                [(EXT, NODES * NODES, 128)] + [(2, NODES, NODES, 128)] * 2,
+                [(EXT, len(back_inner_np), 128)], spectrum, edges, back_inner,
+            )
 
         y_first, y_second = call(
             start_kernel, counts, "start", [(NODES + 1,) + face[1:], face], [], residual
@@ -1120,10 +1189,12 @@
         rx_first, tile = carried(rx[0], low_face.shape)
         running.add(tile)
         rx = (rx_first, rx[1])
-        part, y_first, y_second, *fx = call(
-            first_solve_kernel, counts, "first_solve", first_shapes, solve_scratch,
+        spectrum, edges, y_first, y_second = call(
+            first_solve_kernel, counts, "first_solve",
+            solve_shapes + [(2 * EXT + 1, NODES, 128)] * 2, solve_scratch,
             residual, porosity, *ry, *rx, *plane,
         )
+        part, *fx = rest_of_solve(spectrum, edges)
 
         def spread_faces(fx, ry):
             low_y, high_y = side_y.low(*ry), side_y.high(*ry)
@@ -1133,8 +1204,8 @@
                 for at in (slice(0, 2), slice(8, 10))
             ]
             return (
-                fx[0][:, 1:-1] + side_x.send_first(*both),
-                fx[1][:, 1:-1] + side_x.send_second(*both),
+                fx[0] + side_x.send_first(*both),
+                fx[1] + side_x.send_second(*both),
             )
 
         def trade_y(y_first, y_second, shape):
@@ -1174,12 +1245,16 @@
         running.add(rx[1][count + 1])
         rx = [value[:count].reshape(first.shape) for value in rx]
         if late:
-            z, u, y_first, y_second, *fx = call(
+            half = (NODES, NODES // 2, NODES, 128)
+            z, u_edge, y_first, y_second = call(
                 early_apply_kernel, counts, "first_apply",
-                [block, block, (2 * NODES, NODES, 128), (2 * NODES, NODES, 128),
-                 (2, NODES, NODES, 128), (2, NODES, NODES, 128)],
-                [block],
+                [block, half, (2 * NODES, NODES, 128), (2 * NODES, NODES, 128)], [block],
                 part, *ry, *rx, porosity,
+            )
+            u_inner, *fx = call(
+                rest_apply_kernel, counts, "rest_of_apply",
+                [half, (2, NODES, NODES, 128), (2, NODES, NODES, 128)], [block],
+                z, u_edge, porosity,
             )
             y_first = jnp.concatenate([y_first, running.value[None]])
         else:
@@ -1190,6 +1265,8 @@
                 [block],
                 part, *ry, *rx, running.value, lift, porosity, residual,
             )
+            u_edge = jnp.concatenate([u[:, :2], u[:, -2:]], axis=1)
+            u_inner = u[:, 2:-2]
         ry, rows = trade_y(y_first, y_second, two)
         if late:
             running.value = jnp.where(inner_y, running.value, rows[0][0])
@@ -1213,16 +1290,17 @@
             for value in far:
                 running.add(value)
             table = (9 * counts[0] * counts[1], 128)
-            q, part, y_first, y_second, *fx, field = call(
-                late_solve_kernel, counts, "second_solve", [block] + part_shapes + [(16, 128)],
-                solve_scratch + [table],
-                u, *ry, *rx, columns, every_lift, running.value, *plane,
+            q, spectrum, edges, y_first, y_second, field = call(
+                late_solve_kernel, counts, "second_solve",
+                [block] + solve_shapes + sends + [(16, 128)], solve_scratch + [table],
+                u_edge, u_inner, *ry, *rx, columns, every_lift, running.value, *plane,
             )
         else:
-            q, part, y_first, y_second, *fx = call(
-                second_solve_kernel, counts, "second_solve", [block] + part_shapes, solve_scratch,
-                u, *ry, *rx, *plane,
-            )
+            q, spectrum, edges, y_first, y_second = call(
+                second_solve_kernel, counts, "second_solve", [block] + solve_shapes + sends,
+                solve_scratch, u_edge, u_inner, *ry, *rx, *plane,
+            )
+        part, *fx = rest_of_solve(spectrum, edges)
         ry, _ = trade_y(y_first, y_second, ext_face)
         rx = trade(counts, 0, *spread_faces(fx, ry))
 

time: 62.2 us -> 61.6 us (level)
  waiting for transfers between devices: 26 us -> 24.6 us
  Pallas kernels: 6.65 us -> 7.33 us
    ppermute x10, waiting for transfers between devices: 10.5 us -> 9.09 us  [trade(): lax.ppermute(first, AXES, swap_pairs(counts, axis, 0))]
    pallas_call x8 -> x11, Pallas kernels: 6.65 us -> 7.33 us  [call(): pl.pallas_call(body, name=name, out_shape=[jax.ShapeDtypeStruct(shape, jn...]
    unnamed x16 -> x18, local copies, waits for them, and re-layouts: 1.51 us -> 1.52 us
  transfers between devices with their start and end apart: 22 -> 22, of which waited for: 12 -> 12; matrix products, arithmetic and copies ran while one was open for 1% -> 1% of each run, Pallas kernels for 0% -> 2%
where the time goes in v7:
time: 61.6 us; the launch traced here: 61.3 us
  starting transfers between devices  26.1 us (42%)
  waiting for transfers between devices  24.6 us (40%)
  Pallas kernels  7.33 us (12%)
  local copies, waits for them, and re-layouts  1.83 us (3%)
  between operations  0.98 us (2%)
    ppermute x10, starting transfers between devices, trade(): lax.ppermute(first, AXES, swap_pairs(counts, axis, 0))  13.7 us
    ppermute x10, waiting for transfers between devices, trade(): lax.ppermute(second, AXES, swap_pairs(counts, axis, 1))  13.5 us
    ppermute x10, waiting for transfers between devices, trade(): lax.ppermute(first, AXES, swap_pairs(counts, axis, 0))  9.09 us
    ppermute x10, starting transfers between devices, trade(): lax.ppermute(second, AXES, swap_pairs(counts, axis, 1))  7.72 us
    pallas_call x11, Pallas kernels, call(): pl.pallas_call(body, name=name, out_shape=[jax.ShapeDtypeStruct(shape, jn...  7.33 us
    all_to_all x1, starting transfers between devices, gather_stats(): return lax.all_to_all(stats, AXES, 0, 0)  3.82 us
    unnamed x18, local copies, waits for them, and re-layouts  1.52 us
    ppermute x1, waiting for transfers between devices, trade_far(): return lax.ppermute(value, AXES, pairs)  1.27 us
  transfers between devices with their start and end apart: 22, of which 12 were waited for; matrix products, arithmetic and copies ran while one was open for 1% of the time, Pallas kernels for 2%

profile of v7, /device:TPU:0, one launch (start us, length us, event | category | flops | bytes accessed | tf_op | source)
XLA Modules:
  0.0 61.3 jit_solution(3898484378050952877)
XLA Ops:
  0.6 0.9 %copy-done = f32[1,1,8,8,8,128]{5,4,3,2,1,0:T(8,128)S(1)} copy-done((f32[1,1,8,8,8,128]{5,4,3,2,1,0:T(8,128)S(1)}, f32[1,1,8,8,8,128]{5,4,3,2,1,0:T(8,128)}, u32[]{:S(2)}) %copy-start) | copy-done | bytes 262168
  1.6 0.1 start.1
  1.7 0.5 collective-permute-start.1
  2.2 4.1 %collective-permute-start = (f32[9,8,128]{2,1,0:T(8,128)S(1)}, f32[9,8,128]{2,1,0:T(8,128)S(1)}, u32[]{:S(2)}, u32[]{:S(2)}) collective-permute-start(f32[9,8,128]{2,1,0:T(8,128)S(1)} %get-tuple-element.56), channel_id=1, source_target_pairs={{0,1},{1,0},{2,3},{3,2},{4,5},{5,4},{6,7},{7,6},{8,9},{9,8},{10,11... | collective-permute-start | bytes 110600 | tf_op jit(solution)/shard_map/ppermute | solution.py:1066
  6.3 1.9 %collective-permute-done = f32[9,8,128]{2,1,0:T(8,128)S(1)} collective-permute-done((f32[9,8,128]{2,1,0:T(8,128)S(1)}, f32[9,8,128]{2,1,0:T(8,128)S(1)}, u32[]{:S(2)}, u32[]{:S(2)}) %collective-permute-start) | collective-permute-done | bytes 36896 | tf_op jit(solution)/shard_map/ppermute | solution.py:1066
  8.4 0.5 copy-done.8
  9.0 2.0 %collective-permute-start.3 = (f32[10,8,128]{2,1,0:T(8,128)S(1)}, f32[10,8,128]{2,1,0:T(8,128)S(1)}, u32[]{:S(2)}, u32[]{:S(2)}) collective-permute-start(f32[10,8,128]{2,1,0:T(8,128)S(1)} %get-tuple-element.129), channel_id=1, source_target_pairs={{0,28},{1,29},{2,30},{3,31},{4,8},{5,9},{6,10},{7,11},{8,4},{9,5},... | collective-permute-start | bytes 122888 | tf_op jit(solution)/shard_map/ppermute | solution.py:1067
  11.0 2.5 %collective-permute-done.3.refs_5_ = f32[10,8,128]{2,1,0:T(8,128)S(1)} collective-permute-done((f32[10,8,128]{2,1,0:T(8,128)S(1)}, f32[10,8,128]{2,1,0:T(8,128)S(1)}, u32[]{:S(2)}, u32[]{:S(2)}) %collective-permute-start.3) | collective-permute-done | bytes 40992 | tf_op jit(solution)/shard_map/ppermute | solution.py:1067
  13.6 0.9 %first_solve.1 = (f32[104,1280]{1,0:T(8,128)S(1)}, f32[10,16,128]{2,1,0:T(8,128)S(1)}, f32[21,8,128]{2,1,0:T(8,128)S(1)}, f32[21,8,128]{2,1,0:T(8,128)S(1)}) custom-call(f32[8,8,8,128]{3,2,1,0:T(8,128)S(1)} %bitcast.48, f32[1,128]{1,0:T(1,128)S(1)} %subtract_bitcast_fusion.refs_1_.refs_5_.refs_2_, f32[8,8,128]{2,1,0:T(8,128)S(1)} %get-tuple-element.144.refs_2_, ...), custom_call_target="tpu_custom_call" | custom-call | flops 900000000 | bytes 2700000 | tf_op jit(solution)/shard_map/first_solve/pallas_call | solution.py:1036
  14.6 2.5 %collective-permute-start.4 = (f32[21,8,128]{2,1,0:T(8,128)S(1)}, f32[21,8,128]{2,1,0:T(8,128)S(1)}, u32[]{:S(2)}, u32[]{:S(2)}) collective-permute-start(f32[21,8,128]{2,1,0:T(8,128)S(1)} %get-tuple-element.61), channel_id=1, source_target_pairs={{0,1},{1,0},{2,3},{3,2},{4,5},{5,4},{6,7},{7,6},{8,9},{9,8},{10,11... | collective-permute-start | bytes 258056 | tf_op jit(solution)/shard_map/ppermute | solution.py:1066
  17.1 0.1 pad.36.clone
  17.2 0.1 pad.31.clone
  17.3 0.5 rest_of_solve.2
  17.7 1.9 %collective-permute-done.4 = f32[21,8,128]{2,1,0:T(8,128)S(1)} collective-permute-done((f32[21,8,128]{2,1,0:T(8,128)S(1)}, f32[21,8,128]{2,1,0:T(8,128)S(1)}, u32[]{:S(2)}, u32[]{:S(2)}) %collective-permute-start.4) | collective-permute-done | bytes 86048 | tf_op jit(solution)/shard_map/ppermute | solution.py:1066
  19.7 0.1 maximum_maximum_fusion
  19.8 0.1 fusion.7
  19.9 1.4 %collective-permute-start.7 = (f32[18,8,128]{2,1,0:T(8,128)S(1)}, f32[18,8,128]{2,1,0:T(8,128)S(1)}, u32[]{:S(2)}, u32[]{:S(2)}) collective-permute-start(f32[18,8,128]{2,1,0:T(8,128)S(1)} %pad_maximum_fusion.3), channel_id=1, source_target_pairs={{0,28},{1,29},{2,30},{3,31},{4,8},{5,9},{6,10},{7,11},{8,4},{9,5},... | collective-permute-start | bytes 221192 | tf_op jit(solution)/shard_map/ppermute | solution.py:1067
  21.3 0.2 collective-permute-start.6
  21.6 1.0 %collective-permute-done.6 = f32[17,8,128]{2,1,0:T(8,128)S(1)} collective-permute-done((f32[17,8,128]{2,1,0:T(8,128)S(1)}, f32[17,8,128]{2,1,0:T(8,128)S(1)}, u32[]{:S(2)}, u32[]{:S(2)}) %collective-permute-start.6) | collective-permute-done | bytes 69664 | tf_op jit(solution)/shard_map/ppermute | solution.py:1066
  22.6 2.6 %collective-permute-done.7 = f32[18,8,128]{2,1,0:T(8,128)S(1)} collective-permute-done((f32[18,8,128]{2,1,0:T(8,128)S(1)}, f32[18,8,128]{2,1,0:T(8,128)S(1)}, u32[]{:S(2)}, u32[]{:S(2)}) %collective-permute-start.7) | collective-permute-done | bytes 73760 | tf_op jit(solution)/shard_map/ppermute | solution.py:1067
  25.2 0.4 first_apply.1
  25.6 1.8 %collective-permute-start.8 = (f32[17,8,128]{2,1,0:T(8,128)S(1)}, f32[17,8,128]{2,1,0:T(8,128)S(1)}, u32[]{:S(2)}, u32[]{:S(2)}) collective-permute-start(f32[17,8,128]{2,1,0:T(8,128)S(1)} %pad_maximum_fusion.5), channel_id=1, source_target_pairs={{0,1},{1,0},{2,3},{3,2},{4,5},{5,4},{6,7},{7,6},{8,9},{9,8},{10,11... | collective-permute-start | bytes 208904 | tf_op jit(solution)/shard_map/ppermute | solution.py:1066
  27.4 0.1 pad.19.clone
  27.5 0.4 rest_of_apply.1
  27.9 2.1 %collective-permute-done.8 = f32[17,8,128]{2,1,0:T(8,128)S(1)} collective-permute-done((f32[17,8,128]{2,1,0:T(8,128)S(1)}, f32[17,8,128]{2,1,0:T(8,128)S(1)}, u32[]{:S(2)}, u32[]{:S(2)}) %collective-permute-start.8) | collective-permute-done | bytes 69664 | tf_op jit(solution)/shard_map/ppermute | solution.py:1066
  30.0 0.9 %collective-permute-start.12 = (f32[8,128]{1,0:T(8,128)S(1)}, f32[8,128]{1,0:T(8,128)S(1)}, u32[]{:S(2)}, u32[]{:S(2)}) collective-permute-start(f32[8,128]{1,0:T(8,128)S(1)} %fusion.14), channel_id=1, source_target_pairs={{0,16},{1,17},{2,18},{3,19},{4,20},{5,21},{6,22},{7,23},{8,24},{9,... | collective-permute-start | bytes 12296 | tf_op jit(solution)/shard_map/ppermute | solution.py:1077
  30.9 0.1 fusion.3
  31.0 1.0 %collective-permute-start.11 = (f32[2,10,8,128]{3,2,1,0:T(8,128)S(1)}, f32[2,10,8,128]{3,2,1,0:T(8,128)S(1)}, u32[]{:S(2)}, u32[]{:S(2)}) collective-permute-start(f32[2,10,8,128]{3,2,1,0:T(8,128)S(1)} %get-tuple-element.136), channel_id=1, source_target_pairs={{0,28},{1,29},{2,30},{3,31},{4,8},{5,9},{6,10},{7,11},{8,4},{9,5},... | collective-permute-start | bytes 245768 | tf_op jit(solution)/shard_map/ppermute | solution.py:1067
  32.0 0.3 collective-permute-start.10
  32.3 0.1 porosity.1.refs_6_.refs_10_
  32.3 1.3 %collective-permute-done.12 = f32[8,128]{1,0:T(8,128)S(1)} collective-permute-done((f32[8,128]{1,0:T(8,128)S(1)}, f32[8,128]{1,0:T(8,128)S(1)}, u32[]{:S(2)}, u32[]{:S(2)}) %collective-permute-start.12) | collective-permute-done | bytes 4128 | tf_op jit(solution)/shard_map/ppermute | solution.py:1077
  33.6 2.4 %collective-permute-done.11.refs_5_ = f32[2,10,8,128]{3,2,1,0:T(8,128)S(1)} collective-permute-done((f32[2,10,8,128]{3,2,1,0:T(8,128)S(1)}, f32[2,10,8,128]{3,2,1,0:T(8,128)S(1)}, u32[]{:S(2)}, u32[]{:S(2)}) %collective-permute-start.11) | collective-permute-done | bytes 81952 | tf_op jit(solution)/shard_map/ppermute | solution.py:1067
  36.0 1.3 %second_solve.1 = (f32[8,8,8,128]{3,2,1,0:T(8,128)S(1)}, f32[104,1280]{1,0:T(8,128)S(1)}, f32[10,16,128]{2,1,0:T(8,128)S(1)}, f32[20,8,128]{2,1,0:T(8,128)S(1)},...) custom-call(f32[8,4,8,128]{3,2,1,0:T(8,128)S(1)} %get-tuple-element.65.refs_1_.refs_0_, ...), custom_call_target="tpu_custom_call" | custom-call | flops 900000000 | bytes 2700000 | tf_op jit(solution)/shard_map/second_solve/pallas_call | solution.py:1036
  37.4 1.8 %collective-permute-start.13 = (f32[20,8,128]{2,1,0:T(8,128)S(1)}, f32[20,8,128]{2,1,0:T(8,128)S(1)}, u32[]{:S(2)}, u32[]{:S(2)}) collective-permute-start(f32[20,8,128]{2,1,0:T(8,128)S(1)} %get-tuple-element.79), channel_id=1, source_target_pairs={{0,1},{1,0},{2,3},{3,2},{4,5},{5,4},{6,7},{7,6},{8,9},{9,8},{10,11... | collective-permute-start | bytes 245768 | tf_op jit(solution)/shard_map/ppermute | solution.py:1066
  39.2 0.5 rest_of_solve.3
  39.7 2.2 %collective-permute-done.13 = f32[20,8,128]{2,1,0:T(8,128)S(1)} collective-permute-done((f32[20,8,128]{2,1,0:T(8,128)S(1)}, f32[20,8,128]{2,1,0:T(8,128)S(1)}, u32[]{:S(2)}, u32[]{:S(2)}) %collective-permute-start.13) | collective-permute-done | bytes 81952 | tf_op jit(solution)/shard_map/ppermute | solution.py:1066
  41.9 0.1 fusion.11
  42.0 0.8 %collective-permute-start.16 = (f32[2,8,8,128]{3,2,1,0:T(8,128)S(1)}, f32[2,8,8,128]{3,2,1,0:T(8,128)S(1)}, u32[]{:S(2)}, u32[]{:S(2)}) collective-permute-start(f32[2,8,8,128]{3,2,1,0:T(8,128)S(1)} %get-tuple-element.134), channel_id=1, source_target_pairs={{0,28},{1,29},{2,30},{3,31},{4,8},{5,9},{6,10},{7,11},{8,4},{9,5},... | collective-permute-start | bytes 196616 | tf_op jit(solution)/shard_map/ppermute | solution.py:1067
  42.8 0.5 collective-permute-start.15
  43.4 3.3 %collective-permute-done.16.refs_4_ = f32[2,8,8,128]{3,2,1,0:T(8,128)S(1)} collective-permute-done((f32[2,8,8,128]{3,2,1,0:T(8,128)S(1)}, f32[2,8,8,128]{3,2,1,0:T(8,128)S(1)}, u32[]{:S(2)}, u32[]{:S(2)}) %collective-permute-start.16) | collective-permute-done | bytes 65568 | tf_op jit(solution)/shard_map/ppermute | solution.py:1067
  46.7 1.6 %late_apply.1 = (f32[8,8,8,128]{3,2,1,0:T(8,128)S(1)}, f32[8,8,8,128]{3,2,1,0:T(8,128)S(1)}, f32[10,8,128]{2,1,0:T(8,128)S(1)}, f32[10,8,128]{2,1,0:T(8,128)S(1)...) custom-call(f32[10,64,128]{2,1,0:T(8,128)S(1)} %get-tuple-element.78.refs_0_, ...), custom_call_target="tpu_custom_call" | custom-call | flops 800000000 | bytes 2400000 | tf_op jit(solution)/shard_map/late_apply/pallas_call | solution.py:1036
  48.3 3.8 %all-to-all-start = ((f32[32,4,128]{2,1,0:T(4,128)}), f32[32,4,128]{2,1,0:T(4,128)S(1)}, u32[]{:S(2)}, u32[]{:S(2)}) async-start(f32[32,4,128]{2,1,0:T(4,128)} %get-tuple-element.103), calls=%async_computation | async-start | bytes 131072 | tf_op jit(solution)/shard_map/all_to_all | solution.py:1103
  52.1 1.8 %collective-permute-start.17 = (f32[10,8,128]{2,1,0:T(8,128)S(1)}, f32[10,8,128]{2,1,0:T(8,128)S(1)}, u32[]{:S(2)}, u32[]{:S(2)}) collective-permute-start(f32[10,8,128]{2,1,0:T(8,128)S(1)} %get-tuple-element.85), channel_id=1, source_target_pairs={{0,1},{1,0},{2,3},{3,2},{4,5},{5,4},{6,7},{7,6},{8,9},{9,8},{10,11... | collective-permute-start | bytes 122888 | tf_op jit(solution)/shard_map/ppermute | solution.py:1066
  54.0 0.5 collective-permute-start.19
  54.5 2.0 %collective-permute-start.20 = (f32[10,8,128]{2,1,0:T(8,128)S(1)}, f32[10,8,128]{2,1,0:T(8,128)S(1)}, u32[]{:S(2)}, u32[]{:S(2)}) collective-permute-start(f32[10,8,128]{2,1,0:T(8,128)S(1)} %get-tuple-element.88), channel_id=1, source_target_pairs={{0,28},{1,29},{2,30},{3,31},{4,8},{5,9},{6,10},{7,11},{8,4},{9,5},... | collective-permute-start | bytes 122888 | tf_op jit(solution)/shard_map/ppermute | solution.py:1067
  56.5 2.7 %collective-permute-done.20.refs_9_ = f32[10,8,128]{2,1,0:T(8,128)S(1)} collective-permute-done((f32[10,8,128]{2,1,0:T(8,128)S(1)}, f32[10,8,128]{2,1,0:T(8,128)S(1)}, u32[]{:S(2)}, u32[]{:S(2)}) %collective-permute-start.20) | collective-permute-done | bytes 40992 | tf_op jit(solution)/shard_map/ppermute | solution.py:1067
  59.3 0.7 %all-to-all-done.refs_12_ = f32[32,4,128]{2,1,0:T(4,128)S(1)} async-done(((f32[32,4,128]{2,1,0:T(4,128)}), f32[32,4,128]{2,1,0:T(4,128)S(1)}, u32[]{:S(2)}, u32[]{:S(2)}) %all-to-all-start) | async-done | bytes 65568 | tf_op jit(solution)/shard_map/all_to_all | solution.py:1103
  60.0 1.4 %late_final.1 = (f32[8,8,8,128]{3,2,1,0:T(8,128)}, f32[8,8,8,128]{3,2,1,0:T(8,128)}, f32[8,8,8,128]{3,2,1,0:T(8,128)}, f32[2]{0:T(128)}) custom-call(f32[8,8,8,128]{3,2,1,0:T(8,128)S(1)} %get-tuple-element.94.refs_0_, f32[8,8,8,128]{3,2,1,0:T(8,128)S(1)} %get-tuple-element.95.refs_1_, f32[8,8,8,128]{3,2,1,0:T(8,128)S(1)} %get-tuple-element.83.refs_10_.refs_2_, ...), custom_call_target="tpu_custom_call" | custom-call | flops 800000000 | bytes 2400000 | tf_op jit(solution)/shard_map/late_final/pallas_call | solution.py:1036
  (68 shorter events, 0.5 us)
Async XLA Ops:
  0.6 1.0 %copy-start = (f32[1,1,8,8,8,128]{5,4,3,2,1,0:T(8,128)S(1)}, f32[1,1,8,8,8,128]{5,4,3,2,1,0:T(8,128)}, u32[]{:S(2)}) copy-start(f32[1,1,8,8,8,128]{5,4,3,2,1,0:T(8,128)} %param.9) | copy-start | bytes 786436
  1.6 12.0 %copy-start.3 = (f32[10,104,128]{2,1,0:T(8,128)S(1)}, f32[10,104,128]{2,1,0:T(8,128)}, u32[]{:S(2)}) copy-start(f32[10,104,128]{2,1,0:T(8,128)} %constant.47.clone.refs_8_.refs_11_) | copy-start | bytes 1597444
  1.7 4.6 %collective-permute-start.1 = (f32[8,8,128]{2,1,0:T(8,128)S(1)}, f32[8,8,128]{2,1,0:T(8,128)S(1)}, u32[]{:S(2)}, u32[]{:S(2)}) collective-permute-start(f32[8,8,128]{2,1,0:T(8,128)S(1)} %get-tuple-element.57), channel_id=1, source_target_pairs={{0,4},{1,2},{2,1},{3,7},{4,0},{5,6},{6,5},{7,3},{8,12},{9,10},{10,... | collective-permute-start | bytes 98312 | tf_op jit(solution)/shard_map/ppermute | solution.py:1067
  2.2 6.1 %collective-permute-start = (f32[9,8,128]{2,1,0:T(8,128)S(1)}, f32[9,8,128]{2,1,0:T(8,128)S(1)}, u32[]{:S(2)}, u32[]{:S(2)}) collective-permute-start(f32[9,8,128]{2,1,0:T(8,128)S(1)} %get-tuple-element.56), channel_id=1, source_target_pairs={{0,1},{1,0},{2,3},{3,2},{4,5},{5,4},{6,7},{7,6},{8,9},{9,8},{10,11... | collective-permute-start | bytes 110600 | tf_op jit(solution)/shard_map/ppermute | solution.py:1066
  6.3 7.2 %copy-start.1 = (f32[1,1,8,8,8,128]{5,4,3,2,1,0:T(8,128)S(1)}, f32[1,1,8,8,8,128]{5,4,3,2,1,0:T(8,128)}, u32[]{:S(2)}) copy-start(f32[1,1,8,8,8,128]{5,4,3,2,1,0:T(8,128)} %param.9) | copy-start | bytes 786436
  8.3 0.7 %copy-start.8 = (s32[1,1,128]{2,1,0:T(1,128)S(1)}, s32[1,1,128]{2,1,0:T(1,128)}, u32[]{:S(2)}) copy-start(s32[1,1,128]{2,1,0:T(1,128)} %param.10) | copy-start | bytes 1540
  8.3 5.2 %copy-start.5 = (f32[104,112]{1,0:T(8,128)S(1)}, f32[104,112]{1,0:T(8,128)}, u32[]{:S(2)}) copy-start(f32[104,112]{1,0:T(8,128)} %constant.45.clone.refs_6_.refs_9_) | copy-start | bytes 139780
  8.4 2.6 %collective-permute-start.2 = (f32[11,8,128]{2,1,0:T(8,128)S(1)}, f32[11,8,128]{2,1,0:T(8,128)S(1)}, u32[]{:S(2)}, u32[]{:S(2)}) collective-permute-start(f32[11,8,128]{2,1,0:T(8,128)S(1)} %pad_maximum_fusion.10), channel_id=1, source_target_pairs={{0,4},{1,5},{2,6},{3,7},{4,0},{5,1},{6,2},{7,3},{8,12},{9,13},{10,... | collective-permute-start | bytes 135176 | tf_op jit(solution)/shard_map/ppermute | solution.py:1066
  9.0 4.6 %collective-permute-start.3 = (f32[10,8,128]{2,1,0:T(8,128)S(1)}, f32[10,8,128]{2,1,0:T(8,128)S(1)}, u32[]{:S(2)}, u32[]{:S(2)}) collective-permute-start(f32[10,8,128]{2,1,0:T(8,128)S(1)} %get-tuple-element.129), channel_id=1, source_target_pairs={{0,28},{1,29},{2,30},{3,31},{4,8},{5,9},{6,10},{7,11},{8,4},{9,5},... | collective-permute-start | bytes 122888 | tf_op jit(solution)/shard_map/ppermute | solution.py:1067
  11.0 2.6 %copy-start.7 = (f32[48,104]{1,0:T(8,128)S(1)}, f32[48,104]{1,0:T(8,128)}, u32[]{:S(2)}) copy-start(f32[48,104]{1,0:T(8,128)} %constant.46.clone.refs_7_.refs_10_) | copy-start | bytes 59908
  14.5 2.7 %copy-start.6 = (f32[64,104]{1,0:T(8,128)S(1)}, f32[64,104]{1,0:T(8,128)}, u32[]{:S(2)}) copy-start(f32[64,104]{1,0:T(8,128)} %constant.48.clone.refs_2_) | copy-start | bytes 79876
  14.6 5.0 %collective-permute-start.5 = (f32[22,8,128]{2,1,0:T(8,128)S(1)}, f32[22,8,128]{2,1,0:T(8,128)S(1)}, u32[]{:S(2)}, u32[]{:S(2)}) collective-permute-start(f32[22,8,128]{2,1,0:T(8,128)S(1)} %pad_maximum_fusion), channel_id=1, source_target_pairs={{0,4},{1,2},{2,1},{3,7},{4,0},{5,6},{6,5},{7,3},{8,12},{9,10},{10,... | collective-permute-start | bytes 270344 | tf_op jit(solution)/shard_map/ppermute | solution.py:1067
  14.6 4.9 %collective-permute-start.4 = (f32[21,8,128]{2,1,0:T(8,128)S(1)}, f32[21,8,128]{2,1,0:T(8,128)S(1)}, u32[]{:S(2)}, u32[]{:S(2)}) collective-permute-start(f32[21,8,128]{2,1,0:T(8,128)S(1)} %get-tuple-element.61), channel_id=1, source_target_pairs={{0,1},{1,0},{2,3},{3,2},{4,5},{5,4},{6,7},{7,6},{8,9},{9,8},{10,11... | collective-permute-start | bytes 258056 | tf_op jit(solution)/shard_map/ppermute | solution.py:1066
  19.9 5.3 %collective-permute-start.7 = (f32[18,8,128]{2,1,0:T(8,128)S(1)}, f32[18,8,128]{2,1,0:T(8,128)S(1)}, u32[]{:S(2)}, u32[]{:S(2)}) collective-permute-start(f32[18,8,128]{2,1,0:T(8,128)S(1)} %pad_maximum_fusion.3), channel_id=1, source_target_pairs={{0,28},{1,29},{2,30},{3,31},{4,8},{5,9},{6,10},{7,11},{8,4},{9,5},... | collective-permute-start | bytes 221192 | tf_op jit(solution)/shard_map/ppermute | solution.py:1067
  21.3 1.3 %collective-permute-start.6 = (f32[17,8,128]{2,1,0:T(8,128)S(1)}, f32[17,8,128]{2,1,0:T(8,128)S(1)}, u32[]{:S(2)}, u32[]{:S(2)}) collective-permute-start(f32[17,8,128]{2,1,0:T(8,128)S(1)} %pad_maximum_fusion.4), channel_id=1, source_target_pairs={{0,4},{1,5},{2,6},{3,7},{4,0},{5,1},{6,2},{7,3},{8,12},{9,13},{10,... | collective-permute-start | bytes 208904 | tf_op jit(solution)/shard_map/ppermute | solution.py:1066
  25.6 4.4 %collective-permute-start.8 = (f32[17,8,128]{2,1,0:T(8,128)S(1)}, f32[17,8,128]{2,1,0:T(8,128)S(1)}, u32[]{:S(2)}, u32[]{:S(2)}) collective-permute-start(f32[17,8,128]{2,1,0:T(8,128)S(1)} %pad_maximum_fusion.5), channel_id=1, source_target_pairs={{0,1},{1,0},{2,3},{3,2},{4,5},{5,4},{6,7},{7,6},{8,9},{9,8},{10,11... | collective-permute-start | bytes 208904 | tf_op jit(solution)/shard_map/ppermute | solution.py:1066
  27.5 3.4 %collective-permute-start.9 = (f32[16,8,128]{2,1,0:T(8,128)S(1)}, f32[16,8,128]{2,1,0:T(8,128)S(1)}, u32[]{:S(2)}, u32[]{:S(2)}) collective-permute-start(f32[16,8,128]{2,1,0:T(8,128)S(1)} %get-tuple-element.69), channel_id=1, source_target_pairs={{0,4},{1,2},{2,1},{3,7},{4,0},{5,6},{6,5},{7,3},{8,12},{9,10},{10,... | collective-permute-start | bytes 196616 | tf_op jit(solution)/shard_map/ppermute | solution.py:1067
  30.0 3.6 %collective-permute-start.12 = (f32[8,128]{1,0:T(8,128)S(1)}, f32[8,128]{1,0:T(8,128)S(1)}, u32[]{:S(2)}, u32[]{:S(2)}) collective-permute-start(f32[8,128]{1,0:T(8,128)S(1)} %fusion.14), channel_id=1, source_target_pairs={{0,16},{1,17},{2,18},{3,19},{4,20},{5,21},{6,22},{7,23},{8,24},{9,... | collective-permute-start | bytes 12296 | tf_op jit(solution)/shard_map/ppermute | solution.py:1077
  31.0 5.0 %collective-permute-start.11 = (f32[2,10,8,128]{3,2,1,0:T(8,128)S(1)}, f32[2,10,8,128]{3,2,1,0:T(8,128)S(1)}, u32[]{:S(2)}, u32[]{:S(2)}) collective-permute-start(f32[2,10,8,128]{3,2,1,0:T(8,128)S(1)} %get-tuple-element.136), channel_id=1, source_target_pairs={{0,28},{1,29},{2,30},{3,31},{4,8},{5,9},{6,10},{7,11},{8,4},{9,5},... | collective-permute-start | bytes 245768 | tf_op jit(solution)/shard_map/ppermute | solution.py:1067
  32.0 4.1 %collective-permute-start.10 = (f32[2,10,8,128]{3,2,1,0:T(8,128)S(1)}, f32[2,10,8,128]{3,2,1,0:T(8,128)S(1)}, u32[]{:S(2)}, u32[]{:S(2)}) collective-permute-start(f32[2,10,8,128]{3,2,1,0:T(8,128)S(1)} %get-tuple-element.137), channel_id=1, source_target_pairs={{0,4},{1,5},{2,6},{3,7},{4,0},{5,1},{6,2},{7,3},{8,12},{9,13},{10,... | collective-permute-start | bytes 245768 | tf_op jit(solution)/shard_map/ppermute | solution.py:1066
  32.2 3.8 %copy-start.4 = (f32[288,128]{1,0:T(8,128)S(1)}, f32[288,128]{1,0:T(8,128)}, u32[]{:S(2)}) copy-start(f32[288,128]{1,0:T(8,128)} %constant.44.clone.refs_7_.refs_11_) | copy-start | bytes 442372
  37.4 4.5 %collective-permute-start.13 = (f32[20,8,128]{2,1,0:T(8,128)S(1)}, f32[20,8,128]{2,1,0:T(8,128)S(1)}, u32[]{:S(2)}, u32[]{:S(2)}) collective-permute-start(f32[20,8,128]{2,1,0:T(8,128)S(1)} %get-tuple-element.79), channel_id=1, source_target_pairs={{0,1},{1,0},{2,3},{3,2},{4,5},{5,4},{6,7},{7,6},{8,9},{9,8},{10,11... | collective-permute-start | bytes 245768 | tf_op jit(solution)/shard_map/ppermute | solution.py:1066
  39.2 2.7 %collective-permute-start.14 = (f32[20,8,128]{2,1,0:T(8,128)S(1)}, f32[20,8,128]{2,1,0:T(8,128)S(1)}, u32[]{:S(2)}, u32[]{:S(2)}) collective-permute-start(f32[20,8,128]{2,1,0:T(8,128)S(1)} %get-tuple-element.80), channel_id=1, source_target_pairs={{0,4},{1,2},{2,1},{3,7},{4,0},{5,6},{6,5},{7,3},{8,12},{9,10},{10,... | collective-permute-start | bytes 245768 | tf_op jit(solution)/shard_map/ppermute | solution.py:1067
  42.0 4.7 %collective-permute-start.16 = (f32[2,8,8,128]{3,2,1,0:T(8,128)S(1)}, f32[2,8,8,128]{3,2,1,0:T(8,128)S(1)}, u32[]{:S(2)}, u32[]{:S(2)}) collective-permute-start(f32[2,8,8,128]{3,2,1,0:T(8,128)S(1)} %get-tuple-element.134), channel_id=1, source_target_pairs={{0,28},{1,29},{2,30},{3,31},{4,8},{5,9},{6,10},{7,11},{8,4},{9,5},... | collective-permute-start | bytes 196616 | tf_op jit(solution)/shard_map/ppermute | solution.py:1067
  42.8 3.8 %collective-permute-start.15 = (f32[2,8,8,128]{3,2,1,0:T(8,128)S(1)}, f32[2,8,8,128]{3,2,1,0:T(8,128)S(1)}, u32[]{:S(2)}, u32[]{:S(2)}) collective-permute-start(f32[2,8,8,128]{3,2,1,0:T(8,128)S(1)} %get-tuple-element.135), channel_id=1, source_target_pairs={{0,4},{1,5},{2,6},{3,7},{4,0},{5,1},{6,2},{7,3},{8,12},{9,13},{10,... | collective-permute-start | bytes 196616 | tf_op jit(solution)/shard_map/ppermute | solution.py:1066
  46.7 9.8 %copy-start.2 = (f32[1,1,8,8,8,128]{5,4,3,2,1,0:T(8,128)S(1)}, f32[1,1,8,8,8,128]{5,4,3,2,1,0:T(8,128)}, u32[]{:S(2)}) copy-start(f32[1,1,8,8,8,128]{5,4,3,2,1,0:T(8,128)} %param.8) | copy-start | bytes 786436
  48.3 11.7 %all-to-all-start = ((f32[32,4,128]{2,1,0:T(4,128)}), f32[32,4,128]{2,1,0:T(4,128)S(1)}, u32[]{:S(2)}, u32[]{:S(2)}) async-start(f32[32,4,128]{2,1,0:T(4,128)} %get-tuple-element.103), calls=%async_computation | async-start | bytes 131072 | tf_op jit(solution)/shard_map/all_to_all | solution.py:1103
  52.1 4.4 %collective-permute-start.17 = (f32[10,8,128]{2,1,0:T(8,128)S(1)}, f32[10,8,128]{2,1,0:T(8,128)S(1)}, u32[]{:S(2)}, u32[]{:S(2)}) collective-permute-start(f32[10,8,128]{2,1,0:T(8,128)S(1)} %get-tuple-element.85), channel_id=1, source_target_pairs={{0,1},{1,0},{2,3},{3,2},{4,5},{5,4},{6,7},{7,6},{8,9},{9,8},{10,11... | collective-permute-start | bytes 122888 | tf_op jit(solution)/shard_map/ppermute | solution.py:1066
  54.0 2.6 %collective-permute-start.18 = (f32[10,8,128]{2,1,0:T(8,128)S(1)}, f32[10,8,128]{2,1,0:T(8,128)S(1)}, u32[]{:S(2)}, u32[]{:S(2)}) collective-permute-start(f32[10,8,128]{2,1,0:T(8,128)S(1)} %get-tuple-element.86), channel_id=1, source_target_pairs={{0,4},{1,2},{2,1},{3,7},{4,0},{5,6},{6,5},{7,3},{8,12},{9,10},{10,... | collective-permute-start | bytes 122888 | tf_op jit(solution)/shard_map/ppermute | solution.py:1067
  54.0 2.6 %collective-permute-start.19 = (f32[10,8,128]{2,1,0:T(8,128)S(1)}, f32[10,8,128]{2,1,0:T(8,128)S(1)}, u32[]{:S(2)}, u32[]{:S(2)}) collective-permute-start(f32[10,8,128]{2,1,0:T(8,128)S(1)} %get-tuple-element.87), channel_id=1, source_target_pairs={{0,4},{1,5},{2,6},{3,7},{4,0},{5,1},{6,2},{7,3},{8,12},{9,13},{10,... | collective-permute-start | bytes 122888 | tf_op jit(solution)/shard_map/ppermute | solution.py:1066
  54.5 4.8 %collective-permute-start.20 = (f32[10,8,128]{2,1,0:T(8,128)S(1)}, f32[10,8,128]{2,1,0:T(8,128)S(1)}, u32[]{:S(2)}, u32[]{:S(2)}) collective-permute-start(f32[10,8,128]{2,1,0:T(8,128)S(1)} %get-tuple-element.88), channel_id=1, source_target_pairs={{0,28},{1,29},{2,30},{3,31},{4,8},{5,9},{6,10},{7,11},{8,4},{9,5},... | collective-permute-start | bytes 122888 | tf_op jit(solution)/shard_map/ppermute | solution.py:1067

commit v8 on v7

--- a/solution.py
+++ b/solution.py
@@ -423,11 +423,12 @@
 
 
 def first_solve_kernel(
-    counts, r_ref, porosity_ref, ry_first, ry_second, rx_first, rx_second, forward_ref, back_ref,
+    counts, r_ref, porosity_ref, sum_ref, ry_first, ry_second, rx_first, rx_second, forward_ref, back_ref,
     inverse_ref, spectrum_ref, edge_ref, sy_first, sy_second, x_ref, part_ref,
 ):
+    row = lax.broadcasted_iota(jnp.int32, (NODES, 128), 0)
     for send in (sy_first, sy_second):
-        send[2 * EXT] = jnp.broadcast_to(porosity_ref[...], (NODES, 128))
+        send[2 * EXT] = jnp.where(row == 0, sum_ref[...], porosity_ref[...])
     side_x, side_y = Sides("gx", counts[0]), Sides("gy", counts[1])
     x_ref[0, 0:80] = side_x.low(rx_first[...], rx_second[...]).reshape(80, 128)
     x_ref[EXT - 1, 0:80] = side_x.high(rx_first[...], rx_second[...]).reshape(80, 128)
@@ -659,7 +660,7 @@
 
 
 def early_apply_kernel(
-    counts, part_ref, ry_first, ry_second, rx_first, rx_second, porosity_ref,
+    counts, part_ref, ry_first, ry_second, rx_first, rx_second, porosity_ref, sum_ref,
     z_ref, edge_ref, sy_first, sy_second, y_ref,
 ):
     side_x, side_y = Sides("gx", counts[0]), Sides("gy", counts[1])
@@ -673,6 +674,7 @@
             low, high = edge_ref[a, layer], edge_ref[a, 2 + layer]
             sy_first[2 * a + layer] = side_y.send_first(low, high)
             sy_second[2 * a + layer] = side_y.send_second(low, high)
+    sy_first[2 * NODES] = sum_ref[...]
 
 
 def rest_apply_kernel(
@@ -731,7 +733,7 @@
     for index in range(stats_ref.shape[0]):
         stats_ref[index] = jnp.broadcast_to(row, stats_ref.shape[1:])
     sum_column(u_ref)
-    near = [[ref[y : y + 1] for y in range(3)] for ref in (low_ref, own_ref, high_ref)]
+    near = [[ref[y + 1 : y + 2] for y in range(3)] for ref in (low_ref, own_ref, high_ref)]
     send_corners(
         u_ref, w_ref, y_ref, near, side_x, side_y, sy_first, sy_second, fx_first, fx_second
     )
@@ -799,7 +801,7 @@
     end = float(WEIGHTS[0])
     for x, ref in enumerate((low_ref, own_ref, high_ref)):
         for y in range(3):
-            porosity = ref[y : y + 1]
+            porosity = ref[y + 1 : y + 2]
             tile = porosity * weights
             tile = tile + jnp.where(row == 0, end * shift_up(porosity), 0.0)
             tile = tile + jnp.where(row == NODES - 1, end * shift_down(porosity), 0.0)
@@ -1047,13 +1049,14 @@
     )(*operands)
 
 
-def swap_pairs(counts, axis, parity):
+def swap_pairs(counts, axis, parity, ring):
     count_x, count_y = counts
     pairs = []
     for x in range(count_x):
         for y in range(count_y):
             if axis == 0:
-                to = ((x + 1 if x % 2 == parity else x - 1) % count_x, y)
+                other = x + 1 if x % 2 == parity else x - 1
+                to = (other % count_x, y) if ring or 0 <= other < count_x else (x, y ^ 1)
             else:
                 other = y + 1 if y % 2 == parity else y - 1
                 to = (x, other) if 0 <= other < count_y else (x ^ 1, y)
@@ -1061,10 +1064,10 @@
     return pairs
 
 
-def trade(counts, axis, first, second):
+def trade(counts, axis, first, second, ring=False):
     return (
-        lax.ppermute(first, AXES, swap_pairs(counts, axis, 0)),
-        lax.ppermute(second, AXES, swap_pairs(counts, axis, 1)),
+        lax.ppermute(first, AXES, swap_pairs(counts, axis, 0, ring)),
+        lax.ppermute(second, AXES, swap_pairs(counts, axis, 1, ring)),
     )
 
 
@@ -1192,7 +1195,7 @@
         spectrum, edges, y_first, y_second = call(
             first_solve_kernel, counts, "first_solve",
             solve_shapes + [(2 * EXT + 1, NODES, 128)] * 2, solve_scratch,
-            residual, porosity, *ry, *rx, *plane,
+            residual, porosity, running.value, *ry, *rx, *plane,
         )
         part, *fx = rest_of_solve(spectrum, edges)
 
@@ -1217,46 +1220,37 @@
         ext_face = (EXT, 2, NODES, 128)
         two = (NODES, 2, NODES, 128)
         tiles = (-1, NODES, 128)
-        middle = jnp.broadcast_to(porosity, (1, NODES, 128))
-        if late:
-            y_second = jnp.concatenate([y_second, running.value[None]])
-            ry, rows = trade_y(y_first, y_second, ext_face)
-            inner_y = (side_y.index > 0) & (side_y.index < counts[1] - 1)
-            running.add(jnp.where(inner_y, rows[1][1], 0.0))
-        else:
-            ry, rows = trade_y(y_first, y_second, ext_face)
+        ry, rows = trade_y(y_first, y_second, ext_face)
+        rows = [value[0] for value in rows]
+        inner_y = (side_y.index > 0) & (side_y.index < counts[1] - 1)
         three = jnp.concatenate(
             [
-                side[0, 0:1]
-                for side in (
-                    side_y.low(rows[0][:1], rows[1][:1]), middle,
-                    side_y.high(rows[0][:1], rows[1][:1]),
-                )
+                running.value[0:1] + jnp.where(inner_y, rows[1][0:1], 0.0),
+                side_y.low(*rows)[1:2], porosity, side_y.high(*rows)[1:2],
+                jnp.zeros((NODES - 4, 128), jnp.float32),
             ]
-            + [jnp.zeros((NODES - 3, 128), jnp.float32)]
         )
-        first, second = spread_faces(fx, ry)
-        rx = trade(
-            counts, 0, jnp.concatenate([first.reshape(tiles), three[None]]),
-            jnp.concatenate([second.reshape(tiles), three[None], running.value[None]]),
+        first, second = (
+            jnp.concatenate([faces.reshape(tiles), three[None]]) for faces in spread_faces(fx, ry)
         )
+        rx = trade(counts, 0, first, second, ring=True)
         count = 2 * NODES
         threes = [value[count] for value in rx]
-        running.add(rx[1][count + 1])
-        rx = [value[:count].reshape(first.shape) for value in rx]
+        rx = [value[:count].reshape((2, NODES, NODES, 128)) for value in rx]
+        if late:
+            running.value = three + threes[1]
         if late:
             half = (NODES, NODES // 2, NODES, 128)
             z, u_edge, y_first, y_second = call(
                 early_apply_kernel, counts, "first_apply",
-                [block, half, (2 * NODES, NODES, 128), (2 * NODES, NODES, 128)], [block],
-                part, *ry, *rx, porosity,
+                [block, half, (2 * NODES + 1, NODES, 128), (2 * NODES, NODES, 128)], [block],
+                part, *ry, *rx, porosity, running.value,
             )
             u_inner, *fx = call(
                 rest_apply_kernel, counts, "rest_of_apply",
                 [half, (2, NODES, NODES, 128), (2, NODES, NODES, 128)], [block],
                 z, u_edge, porosity,
             )
-            y_first = jnp.concatenate([y_first, running.value[None]])
         else:
             z, u, y_first, y_second, *fx, tile = call(
                 first_apply_kernel, counts, "first_apply",

time: 61.6 us -> 60.6 us (0.984)
  waiting for transfers between devices: 24.6 us -> 20.8 us
  starting transfers between devices: 26.1 us -> 29.2 us
    ppermute x20, waiting for transfers between devices: 22.6 us -> 19.7 us  [the longest x10 12.1 us: trade(): lax.ppermute(second, AXES, swap_pairs(counts, axis, 1, ring))]
    ppermute x20, starting transfers between devices: 21.4 us -> 23.7 us  [the longest x10 13.6 us: trade(): lax.ppermute(first, AXES, swap_pairs(counts, axis, 0, ring))]
    ppermute x1, waiting for transfers between devices: 1.27 us -> 0.06 us  [trade_far(): return lax.ppermute(value, AXES, pairs)]
  transfers between devices with their start and end apart: 22 -> 22, of which waited for: 12 -> 11; matrix products, arithmetic and copies ran while one was open for 1% -> 0% of each run, Pallas kernels for 2% -> 2%
where the time goes in v8:
time: 60.6 us; the launch traced here: 60.4 us
  starting transfers between devices  29.2 us (48%)
  waiting for transfers between devices  20.8 us (34%)
  Pallas kernels  7.29 us (12%)
  local copies, waits for them, and re-layouts  1.79 us (3%)
  between operations  0.98 us (2%)
    ppermute x10, starting transfers between devices, trade(): lax.ppermute(first, AXES, swap_pairs(counts, axis, 0, ring))  13.6 us
    ppermute x10, waiting for transfers between devices, trade(): lax.ppermute(second, AXES, swap_pairs(counts, axis, 1, ring))  12.1 us
    ppermute x10, starting transfers between devices, trade(): lax.ppermute(second, AXES, swap_pairs(counts, axis, 1, ring))  10.1 us
    ppermute x10, waiting for transfers between devices, trade(): lax.ppermute(first, AXES, swap_pairs(counts, axis, 0, ring))  7.59 us
    pallas_call x11, Pallas kernels, call(): pl.pallas_call(body, name=name, out_shape=[jax.ShapeDtypeStruct(shape, jn...  7.29 us
    all_to_all x1, starting transfers between devices, gather_stats(): return lax.all_to_all(stats, AXES, 0, 0)  4.3 us
    unnamed x18, local copies, waits for them, and re-layouts  1.52 us
  transfers between devices with their start and end apart: 22, of which 11 were waited for; matrix products, arithmetic and copies ran while one was open for 0% of the time, Pallas kernels for 2%

profile of v8, /device:TPU:0, one launch (start us, length us, event | category | flops | bytes accessed | tf_op | source)
XLA Modules:
  0.0 60.4 jit_solution(8000232318516813350)
XLA Ops:
  0.6 0.9 %copy-done = f32[1,1,8,8,8,128]{5,4,3,2,1,0:T(8,128)S(1)} copy-done((f32[1,1,8,8,8,128]{5,4,3,2,1,0:T(8,128)S(1)}, f32[1,1,8,8,8,128]{5,4,3,2,1,0:T(8,128)}, u32[]{:S(2)}) %copy-start) | copy-done | bytes 262168
  1.6 0.1 start.1
  1.7 0.5 collective-permute-start.1
  2.2 4.1 %collective-permute-start = (f32[9,8,128]{2,1,0:T(8,128)S(1)}, f32[9,8,128]{2,1,0:T(8,128)S(1)}, u32[]{:S(2)}, u32[]{:S(2)}) collective-permute-start(f32[9,8,128]{2,1,0:T(8,128)S(1)} %get-tuple-element.56), channel_id=1, source_target_pairs={{0,1},{1,0},{2,3},{3,2},{4,5},{5,4},{6,7},{7,6},{8,9},{9,8},{10,11... | collective-permute-start | bytes 110600 | tf_op jit(solution)/shard_map/ppermute | solution.py:1069
  6.3 1.9 %collective-permute-done = f32[9,8,128]{2,1,0:T(8,128)S(1)} collective-permute-done((f32[9,8,128]{2,1,0:T(8,128)S(1)}, f32[9,8,128]{2,1,0:T(8,128)S(1)}, u32[]{:S(2)}, u32[]{:S(2)}) %collective-permute-start) | collective-permute-done | bytes 36896 | tf_op jit(solution)/shard_map/ppermute | solution.py:1069
  8.3 0.0 copy-start.8
  8.3 0.0 copy-start.5
  8.4 0.1 collective-permute-start.2
  8.4 0.5 copy-done.8
  9.0 2.0 %collective-permute-start.3 = (f32[10,8,128]{2,1,0:T(8,128)S(1)}, f32[10,8,128]{2,1,0:T(8,128)S(1)}, u32[]{:S(2)}, u32[]{:S(2)}) collective-permute-start(f32[10,8,128]{2,1,0:T(8,128)S(1)} %get-tuple-element.128), channel_id=1, source_target_pairs={{0,1},{1,0},{2,3},{3,2},{4,8},{5,9},{6,10},{7,11},{8,4},{9,5},{10,... | collective-permute-start | bytes 122888 | tf_op jit(solution)/shard_map/ppermute | solution.py:1070
  11.0 2.0 %collective-permute-done.3.refs_6_ = f32[10,8,128]{2,1,0:T(8,128)S(1)} collective-permute-done((f32[10,8,128]{2,1,0:T(8,128)S(1)}, f32[10,8,128]{2,1,0:T(8,128)S(1)}, u32[]{:S(2)}, u32[]{:S(2)}) %collective-permute-start.3) | collective-permute-done | bytes 40992 | tf_op jit(solution)/shard_map/ppermute | solution.py:1070
  13.0 0.0 copy-start.6
  13.0 0.9 %first_solve.1 = (f32[104,1280]{1,0:T(8,128)S(1)}, f32[10,16,128]{2,1,0:T(8,128)S(1)}, f32[21,8,128]{2,1,0:T(8,128)S(1)}, f32[21,8,128]{2,1,0:T(8,128)S(1)}) custom-call(f32[8,8,8,128]{3,2,1,0:T(8,128)S(1)} %bitcast.63, f32[1,128]{1,0:T(1,128)S(1)} %subtract_bitcast_fusion.refs_1_.refs_5_.refs_2_, f32[8,128]{1,0:T(8,128)S(1)} %bitcast.66, ...), custom_call_target="tpu_custom_call" | custom-call | flops 900000000 | bytes 2700000 | tf_op jit(solution)/shard_map/first_solve/pallas_call | solution.py:1038
  14.0 2.1 %collective-permute-start.4 = (f32[21,8,128]{2,1,0:T(8,128)S(1)}, f32[21,8,128]{2,1,0:T(8,128)S(1)}, u32[]{:S(2)}, u32[]{:S(2)}) collective-permute-start(f32[21,8,128]{2,1,0:T(8,128)S(1)} %get-tuple-element.61), channel_id=1, source_target_pairs={{0,1},{1,0},{2,3},{3,2},{4,5},{5,4},{6,7},{7,6},{8,9},{9,8},{10,11... | collective-permute-start | bytes 258056 | tf_op jit(solution)/shard_map/ppermute | solution.py:1069
  16.1 0.1 pad.29.clone
  16.1 0.5 rest_of_solve.2
  16.6 1.9 %collective-permute-done.4 = f32[21,8,128]{2,1,0:T(8,128)S(1)} collective-permute-done((f32[21,8,128]{2,1,0:T(8,128)S(1)}, f32[21,8,128]{2,1,0:T(8,128)S(1)}, u32[]{:S(2)}, u32[]{:S(2)}) %collective-permute-start.4) | collective-permute-done | bytes 86048 | tf_op jit(solution)/shard_map/ppermute | solution.py:1069
  18.7 0.1 fusion.7
  18.8 0.9 %collective-permute-start.7 = (f32[17,8,128]{2,1,0:T(8,128)S(1)}, f32[17,8,128]{2,1,0:T(8,128)S(1)}, u32[]{:S(2)}, u32[]{:S(2)}) collective-permute-start(f32[17,8,128]{2,1,0:T(8,128)S(1)} %get-tuple-element.148), channel_id=1, source_target_pairs={{0,28},{1,29},{2,30},{3,31},{4,8},{5,9},{6,10},{7,11},{8,4},{9,5},... | collective-permute-start | bytes 208904 | tf_op jit(solution)/shard_map/ppermute | solution.py:1070
  19.7 0.7 %collective-permute-start.6 = (f32[17,8,128]{2,1,0:T(8,128)S(1)}, f32[17,8,128]{2,1,0:T(8,128)S(1)}, u32[]{:S(2)}, u32[]{:S(2)}) collective-permute-start(f32[17,8,128]{2,1,0:T(8,128)S(1)} %get-tuple-element.149), channel_id=1, source_target_pairs={{0,4},{1,5},{2,6},{3,7},{4,0},{5,1},{6,2},{7,3},{8,12},{9,13},{10,... | collective-permute-start | bytes 208904 | tf_op jit(solution)/shard_map/ppermute | solution.py:1069
  20.4 3.8 %collective-permute-done.7 = f32[17,8,128]{2,1,0:T(8,128)S(1)} collective-permute-done((f32[17,8,128]{2,1,0:T(8,128)S(1)}, f32[17,8,128]{2,1,0:T(8,128)S(1)}, u32[]{:S(2)}, u32[]{:S(2)}) %collective-permute-start.7) | collective-permute-done | bytes 69664 | tf_op jit(solution)/shard_map/ppermute | solution.py:1070
  24.2 0.5 first_apply.1
  24.6 2.1 %collective-permute-start.8 = (f32[17,8,128]{2,1,0:T(8,128)S(1)}, f32[17,8,128]{2,1,0:T(8,128)S(1)}, u32[]{:S(2)}, u32[]{:S(2)}) collective-permute-start(f32[17,8,128]{2,1,0:T(8,128)S(1)} %get-tuple-element.68), channel_id=1, source_target_pairs={{0,1},{1,0},{2,3},{3,2},{4,5},{5,4},{6,7},{7,6},{8,9},{9,8},{10,11... | collective-permute-start | bytes 208904 | tf_op jit(solution)/shard_map/ppermute | solution.py:1069
  26.8 0.1 pad.19.clone
  26.9 0.4 rest_of_apply.1
  27.3 1.8 %collective-permute-done.8 = f32[17,8,128]{2,1,0:T(8,128)S(1)} collective-permute-done((f32[17,8,128]{2,1,0:T(8,128)S(1)}, f32[17,8,128]{2,1,0:T(8,128)S(1)}, u32[]{:S(2)}, u32[]{:S(2)}) %collective-permute-start.8) | collective-permute-done | bytes 69664 | tf_op jit(solution)/shard_map/ppermute | solution.py:1069
  29.1 1.2 %collective-permute-start.12 = (f32[8,128]{1,0:T(8,128)S(1)}, f32[8,128]{1,0:T(8,128)S(1)}, u32[]{:S(2)}, u32[]{:S(2)}) collective-permute-start(f32[8,128]{1,0:T(8,128)S(1)} %fusion.14), channel_id=1, source_target_pairs={{0,16},{1,17},{2,18},{3,19},{4,20},{5,21},{6,22},{7,23},{8,24},{9,... | collective-permute-start | bytes 12296 | tf_op jit(solution)/shard_map/ppermute | solution.py:1080
  30.3 0.1 fusion.3
  30.4 2.1 %collective-permute-start.11 = (f32[2,10,8,128]{3,2,1,0:T(8,128)S(1)}, f32[2,10,8,128]{3,2,1,0:T(8,128)S(1)}, u32[]{:S(2)}, u32[]{:S(2)}) collective-permute-start(f32[2,10,8,128]{3,2,1,0:T(8,128)S(1)} %get-tuple-element.135), channel_id=1, source_target_pairs={{0,1},{1,0},{2,3},{3,2},{4,8},{5,9},{6,10},{7,11},{8,4},{9,5},{10,... | collective-permute-start | bytes 245768 | tf_op jit(solution)/shard_map/ppermute | solution.py:1070
  32.5 0.1 porosity.1.refs_6_.refs_10_
  32.6 0.1 collective-permute-done.12
  32.7 2.3 %collective-permute-done.11.refs_5_ = f32[2,10,8,128]{3,2,1,0:T(8,128)S(1)} collective-permute-done((f32[2,10,8,128]{3,2,1,0:T(8,128)S(1)}, f32[2,10,8,128]{3,2,1,0:T(8,128)S(1)}, u32[]{:S(2)}, u32[]{:S(2)}) %collective-permute-start.11) | collective-permute-done | bytes 81952 | tf_op jit(solution)/shard_map/ppermute | solution.py:1070
  34.9 1.3 %second_solve.1 = (f32[8,8,8,128]{3,2,1,0:T(8,128)S(1)}, f32[104,1280]{1,0:T(8,128)S(1)}, f32[10,16,128]{2,1,0:T(8,128)S(1)}, f32[20,8,128]{2,1,0:T(8,128)S(1)},...) custom-call(f32[8,4,8,128]{3,2,1,0:T(8,128)S(1)} %get-tuple-element.65.refs_1_.refs_0_, ...), custom_call_target="tpu_custom_call" | custom-call | flops 900000000 | bytes 2700000 | tf_op jit(solution)/shard_map/second_solve/pallas_call | solution.py:1038
  36.3 2.1 %collective-permute-start.13 = (f32[20,8,128]{2,1,0:T(8,128)S(1)}, f32[20,8,128]{2,1,0:T(8,128)S(1)}, u32[]{:S(2)}, u32[]{:S(2)}) collective-permute-start(f32[20,8,128]{2,1,0:T(8,128)S(1)} %get-tuple-element.79), channel_id=1, source_target_pairs={{0,1},{1,0},{2,3},{3,2},{4,5},{5,4},{6,7},{7,6},{8,9},{9,8},{10,11... | collective-permute-start | bytes 245768 | tf_op jit(solution)/shard_map/ppermute | solution.py:1069
  38.4 0.5 rest_of_solve.3
  38.8 1.9 %collective-permute-done.13 = f32[20,8,128]{2,1,0:T(8,128)S(1)} collective-permute-done((f32[20,8,128]{2,1,0:T(8,128)S(1)}, f32[20,8,128]{2,1,0:T(8,128)S(1)}, u32[]{:S(2)}, u32[]{:S(2)}) %collective-permute-start.13) | collective-permute-done | bytes 81952 | tf_op jit(solution)/shard_map/ppermute | solution.py:1069
  40.8 0.1 fusion.11
  40.9 2.2 %collective-permute-start.16 = (f32[2,8,8,128]{3,2,1,0:T(8,128)S(1)}, f32[2,8,8,128]{3,2,1,0:T(8,128)S(1)}, u32[]{:S(2)}, u32[]{:S(2)}) collective-permute-start(f32[2,8,8,128]{3,2,1,0:T(8,128)S(1)} %get-tuple-element.133), channel_id=1, source_target_pairs={{0,1},{1,0},{2,3},{3,2},{4,8},{5,9},{6,10},{7,11},{8,4},{9,5},{10,... | collective-permute-start | bytes 196616 | tf_op jit(solution)/shard_map/ppermute | solution.py:1070
  43.1 2.2 %collective-permute-done.16.refs_4_ = f32[2,8,8,128]{3,2,1,0:T(8,128)S(1)} collective-permute-done((f32[2,8,8,128]{3,2,1,0:T(8,128)S(1)}, f32[2,8,8,128]{3,2,1,0:T(8,128)S(1)}, u32[]{:S(2)}, u32[]{:S(2)}) %collective-permute-start.16) | collective-permute-done | bytes 65568 | tf_op jit(solution)/shard_map/ppermute | solution.py:1070
  45.3 1.6 %late_apply.1 = (f32[8,8,8,128]{3,2,1,0:T(8,128)S(1)}, f32[8,8,8,128]{3,2,1,0:T(8,128)S(1)}, f32[10,8,128]{2,1,0:T(8,128)S(1)}, f32[10,8,128]{2,1,0:T(8,128)S(1)...) custom-call(f32[10,64,128]{2,1,0:T(8,128)S(1)} %get-tuple-element.78.refs_0_, ...), custom_call_target="tpu_custom_call" | custom-call | flops 800000000 | bytes 2400000 | tf_op jit(solution)/shard_map/late_apply/pallas_call | solution.py:1038
  46.9 4.3 %all-to-all-start = ((f32[32,4,128]{2,1,0:T(4,128)}), f32[32,4,128]{2,1,0:T(4,128)S(1)}, u32[]{:S(2)}, u32[]{:S(2)}) async-start(f32[32,4,128]{2,1,0:T(4,128)} %get-tuple-element.103), calls=%async_computation | async-start | bytes 131072 | tf_op jit(solution)/shard_map/all_to_all | solution.py:1106
  51.2 1.8 %collective-permute-start.17 = (f32[10,8,128]{2,1,0:T(8,128)S(1)}, f32[10,8,128]{2,1,0:T(8,128)S(1)}, u32[]{:S(2)}, u32[]{:S(2)}) collective-permute-start(f32[10,8,128]{2,1,0:T(8,128)S(1)} %get-tuple-element.85), channel_id=1, source_target_pairs={{0,1},{1,0},{2,3},{3,2},{4,5},{5,4},{6,7},{7,6},{8,9},{9,8},{10,11... | collective-permute-start | bytes 122888 | tf_op jit(solution)/shard_map/ppermute | solution.py:1069
  53.1 0.5 collective-permute-start.19
  53.6 2.5 %collective-permute-start.20 = (f32[10,8,128]{2,1,0:T(8,128)S(1)}, f32[10,8,128]{2,1,0:T(8,128)S(1)}, u32[]{:S(2)}, u32[]{:S(2)}) collective-permute-start(f32[10,8,128]{2,1,0:T(8,128)S(1)} %get-tuple-element.88), channel_id=1, source_target_pairs={{0,1},{1,0},{2,3},{3,2},{4,8},{5,9},{6,10},{7,11},{8,4},{9,5},{10,... | collective-permute-start | bytes 122888 | tf_op jit(solution)/shard_map/ppermute | solution.py:1070
  56.1 0.1 prepare.1
  56.2 1.9 %collective-permute-done.20.refs_9_ = f32[10,8,128]{2,1,0:T(8,128)S(1)} collective-permute-done((f32[10,8,128]{2,1,0:T(8,128)S(1)}, f32[10,8,128]{2,1,0:T(8,128)S(1)}, u32[]{:S(2)}, u32[]{:S(2)}) %collective-permute-start.20) | collective-permute-done | bytes 40992 | tf_op jit(solution)/shard_map/ppermute | solution.py:1070
  58.0 1.0 %all-to-all-done.refs_12_ = f32[32,4,128]{2,1,0:T(4,128)S(1)} async-done(((f32[32,4,128]{2,1,0:T(4,128)}), f32[32,4,128]{2,1,0:T(4,128)S(1)}, u32[]{:S(2)}, u32[]{:S(2)}) %all-to-all-start) | async-done | bytes 65568 | tf_op jit(solution)/shard_map/all_to_all | solution.py:1106
  59.1 1.3 %late_final.1 = (f32[8,8,8,128]{3,2,1,0:T(8,128)}, f32[8,8,8,128]{3,2,1,0:T(8,128)}, f32[8,8,8,128]{3,2,1,0:T(8,128)}, f32[2]{0:T(128)}) custom-call(f32[8,8,8,128]{3,2,1,0:T(8,128)S(1)} %get-tuple-element.94.refs_0_, f32[8,8,8,128]{3,2,1,0:T(8,128)S(1)} %get-tuple-element.95.refs_1_, f32[8,8,8,128]{3,2,1,0:T(8,128)S(1)} %get-tuple-element.83.refs_10_.refs_2_, ...), custom_call_target="tpu_custom_call" | custom-call | flops 800000000 | bytes 2400000 | tf_op jit(solution)/shard_map/late_final/pallas_call | solution.py:1038
  (65 shorter events, 0.3 us)
Async XLA Ops:
  0.6 1.0 %copy-start = (f32[1,1,8,8,8,128]{5,4,3,2,1,0:T(8,128)S(1)}, f32[1,1,8,8,8,128]{5,4,3,2,1,0:T(8,128)}, u32[]{:S(2)}) copy-start(f32[1,1,8,8,8,128]{5,4,3,2,1,0:T(8,128)} %param.9) | copy-start | bytes 786436
  1.6 11.4 %copy-start.3 = (f32[10,104,128]{2,1,0:T(8,128)S(1)}, f32[10,104,128]{2,1,0:T(8,128)}, u32[]{:S(2)}) copy-start(f32[10,104,128]{2,1,0:T(8,128)} %constant.47.clone.refs_9_.refs_11_) | copy-start | bytes 1597444
  1.7 4.6 %collective-permute-start.1 = (f32[8,8,128]{2,1,0:T(8,128)S(1)}, f32[8,8,128]{2,1,0:T(8,128)S(1)}, u32[]{:S(2)}, u32[]{:S(2)}) collective-permute-start(f32[8,8,128]{2,1,0:T(8,128)S(1)} %get-tuple-element.57), channel_id=1, source_target_pairs={{0,4},{1,2},{2,1},{3,7},{4,0},{5,6},{6,5},{7,3},{8,12},{9,10},{10,... | collective-permute-start | bytes 98312 | tf_op jit(solution)/shard_map/ppermute | solution.py:1070
  2.2 6.1 %collective-permute-start = (f32[9,8,128]{2,1,0:T(8,128)S(1)}, f32[9,8,128]{2,1,0:T(8,128)S(1)}, u32[]{:S(2)}, u32[]{:S(2)}) collective-permute-start(f32[9,8,128]{2,1,0:T(8,128)S(1)} %get-tuple-element.56), channel_id=1, source_target_pairs={{0,1},{1,0},{2,3},{3,2},{4,5},{5,4},{6,7},{7,6},{8,9},{9,8},{10,11... | collective-permute-start | bytes 110600 | tf_op jit(solution)/shard_map/ppermute | solution.py:1069
  6.3 6.7 %copy-start.1 = (f32[1,1,8,8,8,128]{5,4,3,2,1,0:T(8,128)S(1)}, f32[1,1,8,8,8,128]{5,4,3,2,1,0:T(8,128)}, u32[]{:S(2)}) copy-start(f32[1,1,8,8,8,128]{5,4,3,2,1,0:T(8,128)} %param.9) | copy-start | bytes 786436
  8.3 0.7 %copy-start.8 = (s32[1,1,128]{2,1,0:T(1,128)S(1)}, s32[1,1,128]{2,1,0:T(1,128)}, u32[]{:S(2)}) copy-start(s32[1,1,128]{2,1,0:T(1,128)} %param.10) | copy-start | bytes 1540
  8.3 4.6 %copy-start.5 = (f32[104,112]{1,0:T(8,128)S(1)}, f32[104,112]{1,0:T(8,128)}, u32[]{:S(2)}) copy-start(f32[104,112]{1,0:T(8,128)} %constant.45.clone.refs_7_.refs_9_) | copy-start | bytes 139780
  8.4 2.7 %collective-permute-start.2 = (f32[11,8,128]{2,1,0:T(8,128)S(1)}, f32[11,8,128]{2,1,0:T(8,128)S(1)}, u32[]{:S(2)}, u32[]{:S(2)}) collective-permute-start(f32[11,8,128]{2,1,0:T(8,128)S(1)} %pad_maximum_fusion.8), channel_id=1, source_target_pairs={{0,4},{1,5},{2,6},{3,7},{4,0},{5,1},{6,2},{7,3},{8,12},{9,13},{10,... | collective-permute-start | bytes 135176 | tf_op jit(solution)/shard_map/ppermute | solution.py:1069
  9.0 4.0 %collective-permute-start.3 = (f32[10,8,128]{2,1,0:T(8,128)S(1)}, f32[10,8,128]{2,1,0:T(8,128)S(1)}, u32[]{:S(2)}, u32[]{:S(2)}) collective-permute-start(f32[10,8,128]{2,1,0:T(8,128)S(1)} %get-tuple-element.128), channel_id=1, source_target_pairs={{0,1},{1,0},{2,3},{3,2},{4,8},{5,9},{6,10},{7,11},{8,4},{9,5},{10,... | collective-permute-start | bytes 122888 | tf_op jit(solution)/shard_map/ppermute | solution.py:1070
  11.0 2.0 %copy-start.7 = (f32[48,104]{1,0:T(8,128)S(1)}, f32[48,104]{1,0:T(8,128)}, u32[]{:S(2)}) copy-start(f32[48,104]{1,0:T(8,128)} %constant.46.clone.refs_8_.refs_10_) | copy-start | bytes 59908
  13.0 3.1 %copy-start.6 = (f32[64,104]{1,0:T(8,128)S(1)}, f32[64,104]{1,0:T(8,128)}, u32[]{:S(2)}) copy-start(f32[64,104]{1,0:T(8,128)} %constant.48.clone.refs_2_) | copy-start | bytes 79876
  14.0 4.6 %collective-permute-start.4 = (f32[21,8,128]{2,1,0:T(8,128)S(1)}, f32[21,8,128]{2,1,0:T(8,128)S(1)}, u32[]{:S(2)}, u32[]{:S(2)}) collective-permute-start(f32[21,8,128]{2,1,0:T(8,128)S(1)} %get-tuple-element.61), channel_id=1, source_target_pairs={{0,1},{1,0},{2,3},{3,2},{4,5},{5,4},{6,7},{7,6},{8,9},{9,8},{10,11... | collective-permute-start | bytes 258056 | tf_op jit(solution)/shard_map/ppermute | solution.py:1069
  16.1 2.5 %collective-permute-start.5 = (f32[21,8,128]{2,1,0:T(8,128)S(1)}, f32[21,8,128]{2,1,0:T(8,128)S(1)}, u32[]{:S(2)}, u32[]{:S(2)}) collective-permute-start(f32[21,8,128]{2,1,0:T(8,128)S(1)} %get-tuple-element.62), channel_id=1, source_target_pairs={{0,4},{1,2},{2,1},{3,7},{4,0},{5,6},{6,5},{7,3},{8,12},{9,10},{10,... | collective-permute-start | bytes 258056 | tf_op jit(solution)/shard_map/ppermute | solution.py:1070
  18.8 5.3 %collective-permute-start.7 = (f32[17,8,128]{2,1,0:T(8,128)S(1)}, f32[17,8,128]{2,1,0:T(8,128)S(1)}, u32[]{:S(2)}, u32[]{:S(2)}) collective-permute-start(f32[17,8,128]{2,1,0:T(8,128)S(1)} %get-tuple-element.148), channel_id=1, source_target_pairs={{0,28},{1,29},{2,30},{3,31},{4,8},{5,9},{6,10},{7,11},{8,4},{9,5},... | collective-permute-start | bytes 208904 | tf_op jit(solution)/shard_map/ppermute | solution.py:1070
  19.7 4.5 %collective-permute-start.6 = (f32[17,8,128]{2,1,0:T(8,128)S(1)}, f32[17,8,128]{2,1,0:T(8,128)S(1)}, u32[]{:S(2)}, u32[]{:S(2)}) collective-permute-start(f32[17,8,128]{2,1,0:T(8,128)S(1)} %get-tuple-element.149), channel_id=1, source_target_pairs={{0,4},{1,5},{2,6},{3,7},{4,0},{5,1},{6,2},{7,3},{8,12},{9,13},{10,... | collective-permute-start | bytes 208904 | tf_op jit(solution)/shard_map/ppermute | solution.py:1069
  24.6 4.4 %collective-permute-start.8 = (f32[17,8,128]{2,1,0:T(8,128)S(1)}, f32[17,8,128]{2,1,0:T(8,128)S(1)}, u32[]{:S(2)}, u32[]{:S(2)}) collective-permute-start(f32[17,8,128]{2,1,0:T(8,128)S(1)} %get-tuple-element.68), channel_id=1, source_target_pairs={{0,1},{1,0},{2,3},{3,2},{4,5},{5,4},{6,7},{7,6},{8,9},{9,8},{10,11... | collective-permute-start | bytes 208904 | tf_op jit(solution)/shard_map/ppermute | solution.py:1069
  26.8 3.4 %collective-permute-start.9 = (f32[16,8,128]{2,1,0:T(8,128)S(1)}, f32[16,8,128]{2,1,0:T(8,128)S(1)}, u32[]{:S(2)}, u32[]{:S(2)}) collective-permute-start(f32[16,8,128]{2,1,0:T(8,128)S(1)} %get-tuple-element.69), channel_id=1, source_target_pairs={{0,4},{1,2},{2,1},{3,7},{4,0},{5,6},{6,5},{7,3},{8,12},{9,10},{10,... | collective-permute-start | bytes 196616 | tf_op jit(solution)/shard_map/ppermute | solution.py:1070
  29.1 3.6 %collective-permute-start.12 = (f32[8,128]{1,0:T(8,128)S(1)}, f32[8,128]{1,0:T(8,128)S(1)}, u32[]{:S(2)}, u32[]{:S(2)}) collective-permute-start(f32[8,128]{1,0:T(8,128)S(1)} %fusion.14), channel_id=1, source_target_pairs={{0,16},{1,17},{2,18},{3,19},{4,20},{5,21},{6,22},{7,23},{8,24},{9,... | collective-permute-start | bytes 12296 | tf_op jit(solution)/shard_map/ppermute | solution.py:1080
  30.4 4.5 %collective-permute-start.11 = (f32[2,10,8,128]{3,2,1,0:T(8,128)S(1)}, f32[2,10,8,128]{3,2,1,0:T(8,128)S(1)}, u32[]{:S(2)}, u32[]{:S(2)}) collective-permute-start(f32[2,10,8,128]{3,2,1,0:T(8,128)S(1)} %get-tuple-element.135), channel_id=1, source_target_pairs={{0,1},{1,0},{2,3},{3,2},{4,8},{5,9},{6,10},{7,11},{8,4},{9,5},{10,... | collective-permute-start | bytes 245768 | tf_op jit(solution)/shard_map/ppermute | solution.py:1070
  32.5 2.4 %collective-permute-start.10 = (f32[2,10,8,128]{3,2,1,0:T(8,128)S(1)}, f32[2,10,8,128]{3,2,1,0:T(8,128)S(1)}, u32[]{:S(2)}, u32[]{:S(2)}) collective-permute-start(f32[2,10,8,128]{3,2,1,0:T(8,128)S(1)} %get-tuple-element.136), channel_id=1, source_target_pairs={{0,4},{1,5},{2,6},{3,7},{4,0},{5,1},{6,2},{7,3},{8,12},{9,13},{10,... | collective-permute-start | bytes 245768 | tf_op jit(solution)/shard_map/ppermute | solution.py:1069
  32.5 2.4 %copy-start.4 = (f32[288,128]{1,0:T(8,128)S(1)}, f32[288,128]{1,0:T(8,128)}, u32[]{:S(2)}) copy-start(f32[288,128]{1,0:T(8,128)} %constant.44.clone.refs_7_.refs_11_) | copy-start | bytes 442372
  36.3 4.5 %collective-permute-start.13 = (f32[20,8,128]{2,1,0:T(8,128)S(1)}, f32[20,8,128]{2,1,0:T(8,128)S(1)}, u32[]{:S(2)}, u32[]{:S(2)}) collective-permute-start(f32[20,8,128]{2,1,0:T(8,128)S(1)} %get-tuple-element.79), channel_id=1, source_target_pairs={{0,1},{1,0},{2,3},{3,2},{4,5},{5,4},{6,7},{7,6},{8,9},{9,8},{10,11... | collective-permute-start | bytes 245768 | tf_op jit(solution)/shard_map/ppermute | solution.py:1069
  38.4 2.4 %collective-permute-start.14 = (f32[20,8,128]{2,1,0:T(8,128)S(1)}, f32[20,8,128]{2,1,0:T(8,128)S(1)}, u32[]{:S(2)}, u32[]{:S(2)}) collective-permute-start(f32[20,8,128]{2,1,0:T(8,128)S(1)} %get-tuple-element.80), channel_id=1, source_target_pairs={{0,4},{1,2},{2,1},{3,7},{4,0},{5,6},{6,5},{7,3},{8,12},{9,10},{10,... | collective-permute-start | bytes 245768 | tf_op jit(solution)/shard_map/ppermute | solution.py:1070
  40.9 4.4 %collective-permute-start.16 = (f32[2,8,8,128]{3,2,1,0:T(8,128)S(1)}, f32[2,8,8,128]{3,2,1,0:T(8,128)S(1)}, u32[]{:S(2)}, u32[]{:S(2)}) collective-permute-start(f32[2,8,8,128]{3,2,1,0:T(8,128)S(1)} %get-tuple-element.133), channel_id=1, source_target_pairs={{0,1},{1,0},{2,3},{3,2},{4,8},{5,9},{6,10},{7,11},{8,4},{9,5},{10,... | collective-permute-start | bytes 196616 | tf_op jit(solution)/shard_map/ppermute | solution.py:1070
  43.1 2.2 %collective-permute-start.15 = (f32[2,8,8,128]{3,2,1,0:T(8,128)S(1)}, f32[2,8,8,128]{3,2,1,0:T(8,128)S(1)}, u32[]{:S(2)}, u32[]{:S(2)}) collective-permute-start(f32[2,8,8,128]{3,2,1,0:T(8,128)S(1)} %get-tuple-element.134), channel_id=1, source_target_pairs={{0,4},{1,5},{2,6},{3,7},{4,0},{5,1},{6,2},{7,3},{8,12},{9,13},{10,... | collective-permute-start | bytes 196616 | tf_op jit(solution)/shard_map/ppermute | solution.py:1069
  45.3 10.7 %copy-start.2 = (f32[1,1,8,8,8,128]{5,4,3,2,1,0:T(8,128)S(1)}, f32[1,1,8,8,8,128]{5,4,3,2,1,0:T(8,128)}, u32[]{:S(2)}) copy-start(f32[1,1,8,8,8,128]{5,4,3,2,1,0:T(8,128)} %param.8) | copy-start | bytes 786436
  46.9 12.1 %all-to-all-start = ((f32[32,4,128]{2,1,0:T(4,128)}), f32[32,4,128]{2,1,0:T(4,128)S(1)}, u32[]{:S(2)}, u32[]{:S(2)}) async-start(f32[32,4,128]{2,1,0:T(4,128)} %get-tuple-element.103), calls=%async_computation | async-start | bytes 131072 | tf_op jit(solution)/shard_map/all_to_all | solution.py:1106
  51.2 4.9 %collective-permute-start.17 = (f32[10,8,128]{2,1,0:T(8,128)S(1)}, f32[10,8,128]{2,1,0:T(8,128)S(1)}, u32[]{:S(2)}, u32[]{:S(2)}) collective-permute-start(f32[10,8,128]{2,1,0:T(8,128)S(1)} %get-tuple-element.85), channel_id=1, source_target_pairs={{0,1},{1,0},{2,3},{3,2},{4,5},{5,4},{6,7},{7,6},{8,9},{9,8},{10,11... | collective-permute-start | bytes 122888 | tf_op jit(solution)/shard_map/ppermute | solution.py:1069
  53.1 3.1 %collective-permute-start.18 = (f32[10,8,128]{2,1,0:T(8,128)S(1)}, f32[10,8,128]{2,1,0:T(8,128)S(1)}, u32[]{:S(2)}, u32[]{:S(2)}) collective-permute-start(f32[10,8,128]{2,1,0:T(8,128)S(1)} %get-tuple-element.86), channel_id=1, source_target_pairs={{0,4},{1,2},{2,1},{3,7},{4,0},{5,6},{6,5},{7,3},{8,12},{9,10},{10,... | collective-permute-start | bytes 122888 | tf_op jit(solution)/shard_map/ppermute | solution.py:1070
  53.1 3.1 %collective-permute-start.19 = (f32[10,8,128]{2,1,0:T(8,128)S(1)}, f32[10,8,128]{2,1,0:T(8,128)S(1)}, u32[]{:S(2)}, u32[]{:S(2)}) collective-permute-start(f32[10,8,128]{2,1,0:T(8,128)S(1)} %get-tuple-element.87), channel_id=1, source_target_pairs={{0,4},{1,5},{2,6},{3,7},{4,0},{5,1},{6,2},{7,3},{8,12},{9,13},{10,... | collective-permute-start | bytes 122888 | tf_op jit(solution)/shard_map/ppermute | solution.py:1069
  53.6 4.4 %collective-permute-start.20 = (f32[10,8,128]{2,1,0:T(8,128)S(1)}, f32[10,8,128]{2,1,0:T(8,128)S(1)}, u32[]{:S(2)}, u32[]{:S(2)}) collective-permute-start(f32[10,8,128]{2,1,0:T(8,128)S(1)} %get-tuple-element.88), channel_id=1, source_target_pairs={{0,1},{1,0},{2,3},{3,2},{4,8},{5,9},{6,10},{7,11},{8,4},{9,5},{10,... | collective-permute-start | bytes 122888 | tf_op jit(solution)/shard_map/ppermute | solution.py:1070

commit v9 on v8

--- a/solution.py
+++ b/solution.py
@@ -691,29 +691,35 @@
             fx_second[layer, b] = side_x.send_second(low, high)
 
 
+def first_sums_kernel(counts, r_ref, q_ref, schwarz_ref, field_ref, row_ref):
+    side_x, side_y = Sides("gx", counts[0]), Sides("gy", counts[1])
+    inner = curvature = None
+    for a in range(NODES):
+        for b in range(NODES):
+            node_class = 3 * class_of(a) + class_of(b)
+            z = schwarz_ref[a, b] + field_ref[node_class : node_class + 1, :]
+            factors = (axis_factor(a, side_x), axis_factor(b, side_y))
+            first, second = (scaled(z * ref[a, b], *factors) for ref in (r_ref, q_ref))
+            inner = first if inner is None else inner + first
+            curvature = second if curvature is None else curvature + second
+    tile = multiplicity_tile()
+    tiles = shared_class_tiles(q_ref, side_x, side_y) + [inner * tile, curvature * tile]
+    row_ref[...] = summed_row(counts, tiles, side_x, side_y)
+
+
 def late_apply_kernel(
     counts, part_ref, ry_first, ry_second, rx_first, rx_second, porosity_ref, low_ref, own_ref,
-    high_ref, r_ref, q_ref, schwarz_ref, field_ref, w_ref, u_ref, sy_first, sy_second, fx_first, fx_second, stats_ref,
+    high_ref, q_ref, first_ref, w_ref, u_ref, sy_first, sy_second, fx_first, fx_second, stats_ref,
     y_ref,
 ):
     side_x, side_y = Sides("gx", counts[0]), Sides("gy", counts[1])
     w = collect_parts(part_ref, ry_first, ry_second, rx_first, rx_second, side_x, side_y, None)
-    inner = first_inner = first_curvature = None
+    inner = None
     for (a, b), value in w.items():
         w_ref[a, b] = value
-        node_class = 3 * class_of(a) + class_of(b)
-        z = schwarz_ref[a, b] + field_ref[node_class : node_class + 1, :]
-        q = q_ref[a, b]
-        factors = (axis_factor(a, side_x), axis_factor(b, side_y))
-        terms = [scaled(t, *factors) for t in (value * q, z * r_ref[a, b], z * q)]
-        if inner is None:
-            inner, first_inner, first_curvature = terms
-        else:
-            inner, first_inner, first_curvature = (
-                inner + terms[0], first_inner + terms[1], first_curvature + terms[2]
-            )
-    tile = multiplicity_tile()
-    inner, first_inner, first_curvature = inner * tile, first_inner * tile, first_curvature * tile
+        term = scaled(value * q_ref[a, b], axis_factor(a, side_x), axis_factor(b, side_y))
+        inner = term if inner is None else inner + term
+    inner = inner * multiplicity_tile()
     porosity = porosity_ref[...]
     apply_tiles(w_ref, u_ref, y_ref, porosity)
     sums = {}
@@ -726,8 +732,7 @@
             own = term if own is None else own + term
     total = counts[0] * counts[1]
     tiles = class_tiles(sums) + [inner, own, porosity]
-    first_tiles = shared_class_tiles(q_ref, side_x, side_y) + [first_inner, first_curvature]
-    row = summed_row(counts, first_tiles, side_x, side_y)[0:1] + pltpu.roll(
+    row = first_ref[0:1] + pltpu.roll(
         summed_row(counts, tiles, side_x, side_y), total + 2, 1
     )[0:1]
     for index in range(stats_ref.shape[0]):
@@ -1024,7 +1029,7 @@
 COSTS = {
     "start": 100, "first_solve": 900, "second_solve": 900, "rest_of_solve": 600,
     "first_apply": 500, "rest_of_apply": 400, "second_apply": 800, "prepare": 20000,
-    "final": 500, "late_apply": 800, "porosity": 20000, "late_final": 800,
+    "final": 500, "late_apply": 800, "first_sums": 300, "porosity": 20000, "late_final": 800,
 }
 
 
@@ -1296,6 +1301,12 @@
             )
         part, *fx = rest_of_solve(spectrum, edges)
         ry, _ = trade_y(y_first, y_second, ext_face)
+        if late:
+            (first_row,) = call(
+                first_sums_kernel, counts, "first_sums", [(NODES, 128)], [],
+                residual, q, z, field,
+            )
+            ry, first_row = lax.optimization_barrier((ry, first_row))
         rx = trade(counts, 0, *spread_faces(fx, ry))
 
         def trade_edges(y_first, y_second, fx, beside):
@@ -1316,7 +1327,7 @@
             w, u, y_first, y_second, *fx, stats = call(
                 late_apply_kernel, counts, "late_apply",
                 [block, block] + [(NODES + 2, NODES, 128)] * 4 + [row], [block],
-                part, *ry, *rx, porosity, *near, residual, q, z, field,
+                part, *ry, *rx, porosity, *near, q, first_row,
             )
             z, w = lax.optimization_barrier((z, w))
             nexts = call(

time: 60.6 us -> 60.6 us (level)
    pallas_call x11 -> x12, Pallas kernels: 7.29 us -> 7.4 us  [call(): pl.pallas_call(body, name=name, out_shape=[jax.ShapeDtypeStruct(shape, jn...]
  transfers between devices with their start and end apart: 22 -> 22, of which waited for: 11 -> 11; matrix products, arithmetic and copies ran while one was open for 0% -> 0% of each run, Pallas kernels for 2% -> 3%
where the time goes in v9:
time: 60.6 us; the launch traced here: 60.3 us
  starting transfers between devices  29.2 us (48%)
  waiting for transfers between devices  20.6 us (34%)
  Pallas kernels  7.4 us (12%)
  local copies, waits for them, and re-layouts  1.79 us (3%)
  between operations  0.98 us (2%)
    ppermute x10, starting transfers between devices, trade(): lax.ppermute(first, AXES, swap_pairs(counts, axis, 0, ring))  13.6 us
    ppermute x10, waiting for transfers between devices, trade(): lax.ppermute(second, AXES, swap_pairs(counts, axis, 1, ring))  12.1 us
    ppermute x10, starting transfers between devices, trade(): lax.ppermute(second, AXES, swap_pairs(counts, axis, 1, ring))  10.1 us
    pallas_call x12, Pallas kernels, call(): pl.pallas_call(body, name=name, out_shape=[jax.ShapeDtypeStruct(shape, jn...  7.4 us
    ppermute x10, waiting for transfers between devices, trade(): lax.ppermute(first, AXES, swap_pairs(counts, axis, 0, ring))  7.4 us
    all_to_all x1, starting transfers between devices, gather_stats(): return lax.all_to_all(stats, AXES, 0, 0)  4.3 us
    unnamed x18, local copies, waits for them, and re-layouts  1.52 us
  transfers between devices with their start and end apart: 22, of which 11 were waited for; matrix products, arithmetic and copies ran while one was open for 0% of the time, Pallas kernels for 3%

profile of v9, /device:TPU:0, one launch (start us, length us, event | category | flops | bytes accessed | tf_op | source)
XLA Modules:
  0.0 60.3 jit_solution(12067030056465144256)
XLA Ops:
  0.6 0.9 %copy-done = f32[1,1,8,8,8,128]{5,4,3,2,1,0:T(8,128)S(1)} copy-done((f32[1,1,8,8,8,128]{5,4,3,2,1,0:T(8,128)S(1)}, f32[1,1,8,8,8,128]{5,4,3,2,1,0:T(8,128)}, u32[]{:S(2)}) %copy-start) | copy-done | bytes 262168
  1.6 0.1 start.1
  1.7 0.5 collective-permute-start.1
  2.2 4.1 %collective-permute-start = (f32[9,8,128]{2,1,0:T(8,128)S(1)}, f32[9,8,128]{2,1,0:T(8,128)S(1)}, u32[]{:S(2)}, u32[]{:S(2)}) collective-permute-start(f32[9,8,128]{2,1,0:T(8,128)S(1)} %get-tuple-element.59), channel_id=1, source_target_pairs={{0,1},{1,0},{2,3},{3,2},{4,5},{5,4},{6,7},{7,6},{8,9},{9,8},{10,11... | collective-permute-start | bytes 110600 | tf_op jit(solution)/shard_map/ppermute | solution.py:1074
  6.3 1.9 %collective-permute-done = f32[9,8,128]{2,1,0:T(8,128)S(1)} collective-permute-done((f32[9,8,128]{2,1,0:T(8,128)S(1)}, f32[9,8,128]{2,1,0:T(8,128)S(1)}, u32[]{:S(2)}, u32[]{:S(2)}) %collective-permute-start) | collective-permute-done | bytes 36896 | tf_op jit(solution)/shard_map/ppermute | solution.py:1074
  8.3 0.0 copy-start.5
  8.4 0.1 collective-permute-start.2
  8.4 0.5 copy-done.8
  9.0 2.0 %collective-permute-start.3 = (f32[10,8,128]{2,1,0:T(8,128)S(1)}, f32[10,8,128]{2,1,0:T(8,128)S(1)}, u32[]{:S(2)}, u32[]{:S(2)}) collective-permute-start(f32[10,8,128]{2,1,0:T(8,128)S(1)} %get-tuple-element.134), channel_id=1, source_target_pairs={{0,1},{1,0},{2,3},{3,2},{4,8},{5,9},{6,10},{7,11},{8,4},{9,5},{10,... | collective-permute-start | bytes 122888 | tf_op jit(solution)/shard_map/ppermute | solution.py:1075
  11.0 2.0 %collective-permute-done.3.refs_6_ = f32[10,8,128]{2,1,0:T(8,128)S(1)} collective-permute-done((f32[10,8,128]{2,1,0:T(8,128)S(1)}, f32[10,8,128]{2,1,0:T(8,128)S(1)}, u32[]{:S(2)}, u32[]{:S(2)}) %collective-permute-start.3) | collective-permute-done | bytes 40992 | tf_op jit(solution)/shard_map/ppermute | solution.py:1075
  13.0 0.0 copy-start.6
  13.0 0.9 %first_solve.1 = (f32[104,1280]{1,0:T(8,128)S(1)}, f32[10,16,128]{2,1,0:T(8,128)S(1)}, f32[21,8,128]{2,1,0:T(8,128)S(1)}, f32[21,8,128]{2,1,0:T(8,128)S(1)}) custom-call(f32[8,8,8,128]{3,2,1,0:T(8,128)S(1)} %bitcast.63, f32[1,128]{1,0:T(1,128)S(1)} %subtract_bitcast_fusion.refs_1_.refs_5_.refs_2_, f32[8,128]{1,0:T(8,128)S(1)} %bitcast.66, ...), custom_call_target="tpu_custom_call" | custom-call | flops 900000000 | bytes 2700000 | tf_op jit(solution)/shard_map/first_solve/pallas_call | solution.py:1043
  14.0 2.1 %collective-permute-start.4 = (f32[21,8,128]{2,1,0:T(8,128)S(1)}, f32[21,8,128]{2,1,0:T(8,128)S(1)}, u32[]{:S(2)}, u32[]{:S(2)}) collective-permute-start(f32[21,8,128]{2,1,0:T(8,128)S(1)} %get-tuple-element.64), channel_id=1, source_target_pairs={{0,1},{1,0},{2,3},{3,2},{4,5},{5,4},{6,7},{7,6},{8,9},{9,8},{10,11... | collective-permute-start | bytes 258056 | tf_op jit(solution)/shard_map/ppermute | solution.py:1074
  16.1 0.1 pad.29.clone
  16.1 0.5 rest_of_solve.2
  16.6 1.9 %collective-permute-done.4 = f32[21,8,128]{2,1,0:T(8,128)S(1)} collective-permute-done((f32[21,8,128]{2,1,0:T(8,128)S(1)}, f32[21,8,128]{2,1,0:T(8,128)S(1)}, u32[]{:S(2)}, u32[]{:S(2)}) %collective-permute-start.4) | collective-permute-done | bytes 86048 | tf_op jit(solution)/shard_map/ppermute | solution.py:1074
  18.7 0.1 fusion.7
  18.8 0.9 %collective-permute-start.7 = (f32[17,8,128]{2,1,0:T(8,128)S(1)}, f32[17,8,128]{2,1,0:T(8,128)S(1)}, u32[]{:S(2)}, u32[]{:S(2)}) collective-permute-start(f32[17,8,128]{2,1,0:T(8,128)S(1)} %get-tuple-element.154), channel_id=1, source_target_pairs={{0,28},{1,29},{2,30},{3,31},{4,8},{5,9},{6,10},{7,11},{8,4},{9,5},... | collective-permute-start | bytes 208904 | tf_op jit(solution)/shard_map/ppermute | solution.py:1075
  19.7 0.7 %collective-permute-start.6 = (f32[17,8,128]{2,1,0:T(8,128)S(1)}, f32[17,8,128]{2,1,0:T(8,128)S(1)}, u32[]{:S(2)}, u32[]{:S(2)}) collective-permute-start(f32[17,8,128]{2,1,0:T(8,128)S(1)} %get-tuple-element.155), channel_id=1, source_target_pairs={{0,4},{1,5},{2,6},{3,7},{4,0},{5,1},{6,2},{7,3},{8,12},{9,13},{10,... | collective-permute-start | bytes 208904 | tf_op jit(solution)/shard_map/ppermute | solution.py:1074
  20.4 3.8 %collective-permute-done.7 = f32[17,8,128]{2,1,0:T(8,128)S(1)} collective-permute-done((f32[17,8,128]{2,1,0:T(8,128)S(1)}, f32[17,8,128]{2,1,0:T(8,128)S(1)}, u32[]{:S(2)}, u32[]{:S(2)}) %collective-permute-start.7) | collective-permute-done | bytes 69664 | tf_op jit(solution)/shard_map/ppermute | solution.py:1075
  24.2 0.5 first_apply.1
  24.6 2.1 %collective-permute-start.8 = (f32[17,8,128]{2,1,0:T(8,128)S(1)}, f32[17,8,128]{2,1,0:T(8,128)S(1)}, u32[]{:S(2)}, u32[]{:S(2)}) collective-permute-start(f32[17,8,128]{2,1,0:T(8,128)S(1)} %get-tuple-element.71), channel_id=1, source_target_pairs={{0,1},{1,0},{2,3},{3,2},{4,5},{5,4},{6,7},{7,6},{8,9},{9,8},{10,11... | collective-permute-start | bytes 208904 | tf_op jit(solution)/shard_map/ppermute | solution.py:1074
  26.8 0.1 pad.19.clone
  26.9 0.4 rest_of_apply.1
  27.3 1.8 %collective-permute-done.8 = f32[17,8,128]{2,1,0:T(8,128)S(1)} collective-permute-done((f32[17,8,128]{2,1,0:T(8,128)S(1)}, f32[17,8,128]{2,1,0:T(8,128)S(1)}, u32[]{:S(2)}, u32[]{:S(2)}) %collective-permute-start.8) | collective-permute-done | bytes 69664 | tf_op jit(solution)/shard_map/ppermute | solution.py:1074
  29.1 1.2 %collective-permute-start.12 = (f32[8,128]{1,0:T(8,128)S(1)}, f32[8,128]{1,0:T(8,128)S(1)}, u32[]{:S(2)}, u32[]{:S(2)}) collective-permute-start(f32[8,128]{1,0:T(8,128)S(1)} %fusion.14), channel_id=1, source_target_pairs={{0,16},{1,17},{2,18},{3,19},{4,20},{5,21},{6,22},{7,23},{8,24},{9,... | collective-permute-start | bytes 12296 | tf_op jit(solution)/shard_map/ppermute | solution.py:1085
  30.3 0.1 fusion.3
  30.4 2.1 %collective-permute-start.11 = (f32[2,10,8,128]{3,2,1,0:T(8,128)S(1)}, f32[2,10,8,128]{3,2,1,0:T(8,128)S(1)}, u32[]{:S(2)}, u32[]{:S(2)}) collective-permute-start(f32[2,10,8,128]{3,2,1,0:T(8,128)S(1)} %get-tuple-element.141), channel_id=1, source_target_pairs={{0,1},{1,0},{2,3},{3,2},{4,8},{5,9},{6,10},{7,11},{8,4},{9,5},{10,... | collective-permute-start | bytes 245768 | tf_op jit(solution)/shard_map/ppermute | solution.py:1075
  32.5 0.1 porosity.1.refs_6_.refs_10_
  32.6 0.1 collective-permute-done.12
  32.7 2.3 %collective-permute-done.11.refs_5_ = f32[2,10,8,128]{3,2,1,0:T(8,128)S(1)} collective-permute-done((f32[2,10,8,128]{3,2,1,0:T(8,128)S(1)}, f32[2,10,8,128]{3,2,1,0:T(8,128)S(1)}, u32[]{:S(2)}, u32[]{:S(2)}) %collective-permute-start.11) | collective-permute-done | bytes 81952 | tf_op jit(solution)/shard_map/ppermute | solution.py:1075
  34.9 1.3 %second_solve.1 = (f32[8,8,8,128]{3,2,1,0:T(8,128)S(1)}, f32[104,1280]{1,0:T(8,128)S(1)}, f32[10,16,128]{2,1,0:T(8,128)S(1)}, f32[20,8,128]{2,1,0:T(8,128)S(1)},...) custom-call(f32[8,4,8,128]{3,2,1,0:T(8,128)S(1)} %get-tuple-element.68.refs_1_.refs_0_, ...), custom_call_target="tpu_custom_call" | custom-call | flops 900000000 | bytes 2700000 | tf_op jit(solution)/shard_map/second_solve/pallas_call | solution.py:1043
  36.3 2.1 %collective-permute-start.13 = (f32[20,8,128]{2,1,0:T(8,128)S(1)}, f32[20,8,128]{2,1,0:T(8,128)S(1)}, u32[]{:S(2)}, u32[]{:S(2)}) collective-permute-start(f32[20,8,128]{2,1,0:T(8,128)S(1)} %get-tuple-element.82), channel_id=1, source_target_pairs={{0,1},{1,0},{2,3},{3,2},{4,5},{5,4},{6,7},{7,6},{8,9},{9,8},{10,11... | collective-permute-start | bytes 245768 | tf_op jit(solution)/shard_map/ppermute | solution.py:1074
  38.4 0.2 first_sums.1.refs_10_
  38.6 0.5 rest_of_solve.3
  39.0 1.8 %collective-permute-done.13 = f32[20,8,128]{2,1,0:T(8,128)S(1)} collective-permute-done((f32[20,8,128]{2,1,0:T(8,128)S(1)}, f32[20,8,128]{2,1,0:T(8,128)S(1)}, u32[]{:S(2)}, u32[]{:S(2)}) %collective-permute-start.13) | collective-permute-done | bytes 81952 | tf_op jit(solution)/shard_map/ppermute | solution.py:1074
  40.8 0.1 fusion.11
  40.9 2.2 %collective-permute-start.16 = (f32[2,8,8,128]{3,2,1,0:T(8,128)S(1)}, f32[2,8,8,128]{3,2,1,0:T(8,128)S(1)}, u32[]{:S(2)}, u32[]{:S(2)}) collective-permute-start(f32[2,8,8,128]{3,2,1,0:T(8,128)S(1)} %get-tuple-element.139), channel_id=1, source_target_pairs={{0,1},{1,0},{2,3},{3,2},{4,8},{5,9},{6,10},{7,11},{8,4},{9,5},{10,... | collective-permute-start | bytes 196616 | tf_op jit(solution)/shard_map/ppermute | solution.py:1075
  43.1 2.2 %collective-permute-done.16.refs_4_ = f32[2,8,8,128]{3,2,1,0:T(8,128)S(1)} collective-permute-done((f32[2,8,8,128]{3,2,1,0:T(8,128)S(1)}, f32[2,8,8,128]{3,2,1,0:T(8,128)S(1)}, u32[]{:S(2)}, u32[]{:S(2)}) %collective-permute-start.16) | collective-permute-done | bytes 65568 | tf_op jit(solution)/shard_map/ppermute | solution.py:1075
  45.3 1.5 %late_apply.1 = (f32[8,8,8,128]{3,2,1,0:T(8,128)S(1)}, f32[8,8,8,128]{3,2,1,0:T(8,128)S(1)}, f32[10,8,128]{2,1,0:T(8,128)S(1)}, f32[10,8,128]{2,1,0:T(8,128)S(1)...) custom-call(f32[10,64,128]{2,1,0:T(8,128)S(1)} %get-tuple-element.81.refs_0_, ...), custom_call_target="tpu_custom_call" | custom-call | flops 800000000 | bytes 2400000 | tf_op jit(solution)/shard_map/late_apply/pallas_call | solution.py:1043
  46.9 4.3 %all-to-all-start = ((f32[32,4,128]{2,1,0:T(4,128)}), f32[32,4,128]{2,1,0:T(4,128)S(1)}, u32[]{:S(2)}, u32[]{:S(2)}) async-start(f32[32,4,128]{2,1,0:T(4,128)} %get-tuple-element.109), calls=%async_computation | async-start | bytes 131072 | tf_op jit(solution)/shard_map/all_to_all | solution.py:1111
  51.2 1.8 %collective-permute-start.17 = (f32[10,8,128]{2,1,0:T(8,128)S(1)}, f32[10,8,128]{2,1,0:T(8,128)S(1)}, u32[]{:S(2)}, u32[]{:S(2)}) collective-permute-start(f32[10,8,128]{2,1,0:T(8,128)S(1)} %get-tuple-element.91), channel_id=1, source_target_pairs={{0,1},{1,0},{2,3},{3,2},{4,5},{5,4},{6,7},{7,6},{8,9},{9,8},{10,11... | collective-permute-start | bytes 122888 | tf_op jit(solution)/shard_map/ppermute | solution.py:1074
  53.0 0.5 collective-permute-start.19
  53.5 2.5 %collective-permute-start.20 = (f32[10,8,128]{2,1,0:T(8,128)S(1)}, f32[10,8,128]{2,1,0:T(8,128)S(1)}, u32[]{:S(2)}, u32[]{:S(2)}) collective-permute-start(f32[10,8,128]{2,1,0:T(8,128)S(1)} %get-tuple-element.94), channel_id=1, source_target_pairs={{0,1},{1,0},{2,3},{3,2},{4,8},{5,9},{6,10},{7,11},{8,4},{9,5},{10,... | collective-permute-start | bytes 122888 | tf_op jit(solution)/shard_map/ppermute | solution.py:1075
  56.0 0.1 prepare.1
  56.1 1.9 %collective-permute-done.20.refs_9_ = f32[10,8,128]{2,1,0:T(8,128)S(1)} collective-permute-done((f32[10,8,128]{2,1,0:T(8,128)S(1)}, f32[10,8,128]{2,1,0:T(8,128)S(1)}, u32[]{:S(2)}, u32[]{:S(2)}) %collective-permute-start.20) | collective-permute-done | bytes 40992 | tf_op jit(solution)/shard_map/ppermute | solution.py:1075
  58.0 1.0 %all-to-all-done.refs_12_ = f32[32,4,128]{2,1,0:T(4,128)S(1)} async-done(((f32[32,4,128]{2,1,0:T(4,128)}), f32[32,4,128]{2,1,0:T(4,128)S(1)}, u32[]{:S(2)}, u32[]{:S(2)}) %all-to-all-start) | async-done | bytes 65568 | tf_op jit(solution)/shard_map/all_to_all | solution.py:1111
  59.0 1.3 %late_final.1 = (f32[8,8,8,128]{3,2,1,0:T(8,128)}, f32[8,8,8,128]{3,2,1,0:T(8,128)}, f32[8,8,8,128]{3,2,1,0:T(8,128)}, f32[2]{0:T(128)}) custom-call(f32[8,8,8,128]{3,2,1,0:T(8,128)S(1)} %get-tuple-element.100.refs_0_, f32[8,8,8,128]{3,2,1,0:T(8,128)S(1)} %get-tuple-element.101.refs_1_, f32[8,8,8,128]{3,2,1,0:T(8,128)S(1)} %get-tuple-element.84.refs_1_.refs_9_.refs_2_, ...), custom_call_target="tpu_custom_call" | custom-call | flops 800000000 | bytes 2400000 | tf_op jit(solution)/shard_map/late_final/pallas_call | solution.py:1043
  (66 shorter events, 0.3 us)
Async XLA Ops:
  0.6 1.0 %copy-start = (f32[1,1,8,8,8,128]{5,4,3,2,1,0:T(8,128)S(1)}, f32[1,1,8,8,8,128]{5,4,3,2,1,0:T(8,128)}, u32[]{:S(2)}) copy-start(f32[1,1,8,8,8,128]{5,4,3,2,1,0:T(8,128)} %param.9) | copy-start | bytes 786436
  1.6 11.4 %copy-start.3 = (f32[10,104,128]{2,1,0:T(8,128)S(1)}, f32[10,104,128]{2,1,0:T(8,128)}, u32[]{:S(2)}) copy-start(f32[10,104,128]{2,1,0:T(8,128)} %constant.47.clone.refs_9_.refs_11_) | copy-start | bytes 1597444
  1.7 4.6 %collective-permute-start.1 = (f32[8,8,128]{2,1,0:T(8,128)S(1)}, f32[8,8,128]{2,1,0:T(8,128)S(1)}, u32[]{:S(2)}, u32[]{:S(2)}) collective-permute-start(f32[8,8,128]{2,1,0:T(8,128)S(1)} %get-tuple-element.60), channel_id=1, source_target_pairs={{0,4},{1,2},{2,1},{3,7},{4,0},{5,6},{6,5},{7,3},{8,12},{9,10},{10,... | collective-permute-start | bytes 98312 | tf_op jit(solution)/shard_map/ppermute | solution.py:1075
  2.2 6.1 %collective-permute-start = (f32[9,8,128]{2,1,0:T(8,128)S(1)}, f32[9,8,128]{2,1,0:T(8,128)S(1)}, u32[]{:S(2)}, u32[]{:S(2)}) collective-permute-start(f32[9,8,128]{2,1,0:T(8,128)S(1)} %get-tuple-element.59), channel_id=1, source_target_pairs={{0,1},{1,0},{2,3},{3,2},{4,5},{5,4},{6,7},{7,6},{8,9},{9,8},{10,11... | collective-permute-start | bytes 110600 | tf_op jit(solution)/shard_map/ppermute | solution.py:1074
  6.3 6.7 %copy-start.1 = (f32[1,1,8,8,8,128]{5,4,3,2,1,0:T(8,128)S(1)}, f32[1,1,8,8,8,128]{5,4,3,2,1,0:T(8,128)}, u32[]{:S(2)}) copy-start(f32[1,1,8,8,8,128]{5,4,3,2,1,0:T(8,128)} %param.9) | copy-start | bytes 786436
  8.3 0.7 %copy-start.8 = (s32[1,1,128]{2,1,0:T(1,128)S(1)}, s32[1,1,128]{2,1,0:T(1,128)}, u32[]{:S(2)}) copy-start(s32[1,1,128]{2,1,0:T(1,128)} %param.10) | copy-start | bytes 1540
  8.3 4.6 %copy-start.5 = (f32[104,112]{1,0:T(8,128)S(1)}, f32[104,112]{1,0:T(8,128)}, u32[]{:S(2)}) copy-start(f32[104,112]{1,0:T(8,128)} %constant.45.clone.refs_7_.refs_9_) | copy-start | bytes 139780
  8.4 2.7 %collective-permute-start.2 = (f32[11,8,128]{2,1,0:T(8,128)S(1)}, f32[11,8,128]{2,1,0:T(8,128)S(1)}, u32[]{:S(2)}, u32[]{:S(2)}) collective-permute-start(f32[11,8,128]{2,1,0:T(8,128)S(1)} %pad_maximum_fusion.8), channel_id=1, source_target_pairs={{0,4},{1,5},{2,6},{3,7},{4,0},{5,1},{6,2},{7,3},{8,12},{9,13},{10,... | collective-permute-start | bytes 135176 | tf_op jit(solution)/shard_map/ppermute | solution.py:1074
  9.0 4.0 %collective-permute-start.3 = (f32[10,8,128]{2,1,0:T(8,128)S(1)}, f32[10,8,128]{2,1,0:T(8,128)S(1)}, u32[]{:S(2)}, u32[]{:S(2)}) collective-permute-start(f32[10,8,128]{2,1,0:T(8,128)S(1)} %get-tuple-element.134), channel_id=1, source_target_pairs={{0,1},{1,0},{2,3},{3,2},{4,8},{5,9},{6,10},{7,11},{8,4},{9,5},{10,... | collective-permute-start | bytes 122888 | tf_op jit(solution)/shard_map/ppermute | solution.py:1075
  11.0 2.0 %copy-start.7 = (f32[48,104]{1,0:T(8,128)S(1)}, f32[48,104]{1,0:T(8,128)}, u32[]{:S(2)}) copy-start(f32[48,104]{1,0:T(8,128)} %constant.46.clone.refs_8_.refs_10_) | copy-start | bytes 59908
  13.0 3.1 %copy-start.6 = (f32[64,104]{1,0:T(8,128)S(1)}, f32[64,104]{1,0:T(8,128)}, u32[]{:S(2)}) copy-start(f32[64,104]{1,0:T(8,128)} %constant.48.clone.refs_2_) | copy-start | bytes 79876
  14.0 4.6 %collective-permute-start.4 = (f32[21,8,128]{2,1,0:T(8,128)S(1)}, f32[21,8,128]{2,1,0:T(8,128)S(1)}, u32[]{:S(2)}, u32[]{:S(2)}) collective-permute-start(f32[21,8,128]{2,1,0:T(8,128)S(1)} %get-tuple-element.64), channel_id=1, source_target_pairs={{0,1},{1,0},{2,3},{3,2},{4,5},{5,4},{6,7},{7,6},{8,9},{9,8},{10,11... | collective-permute-start | bytes 258056 | tf_op jit(solution)/shard_map/ppermute | solution.py:1074
  16.1 2.5 %collective-permute-start.5 = (f32[21,8,128]{2,1,0:T(8,128)S(1)}, f32[21,8,128]{2,1,0:T(8,128)S(1)}, u32[]{:S(2)}, u32[]{:S(2)}) collective-permute-start(f32[21,8,128]{2,1,0:T(8,128)S(1)} %get-tuple-element.65), channel_id=1, source_target_pairs={{0,4},{1,2},{2,1},{3,7},{4,0},{5,6},{6,5},{7,3},{8,12},{9,10},{10,... | collective-permute-start | bytes 258056 | tf_op jit(solution)/shard_map/ppermute | solution.py:1075
  18.8 5.3 %collective-permute-start.7 = (f32[17,8,128]{2,1,0:T(8,128)S(1)}, f32[17,8,128]{2,1,0:T(8,128)S(1)}, u32[]{:S(2)}, u32[]{:S(2)}) collective-permute-start(f32[17,8,128]{2,1,0:T(8,128)S(1)} %get-tuple-element.154), channel_id=1, source_target_pairs={{0,28},{1,29},{2,30},{3,31},{4,8},{5,9},{6,10},{7,11},{8,4},{9,5},... | collective-permute-start | bytes 208904 | tf_op jit(solution)/shard_map/ppermute | solution.py:1075
  19.7 4.5 %collective-permute-start.6 = (f32[17,8,128]{2,1,0:T(8,128)S(1)}, f32[17,8,128]{2,1,0:T(8,128)S(1)}, u32[]{:S(2)}, u32[]{:S(2)}) collective-permute-start(f32[17,8,128]{2,1,0:T(8,128)S(1)} %get-tuple-element.155), channel_id=1, source_target_pairs={{0,4},{1,5},{2,6},{3,7},{4,0},{5,1},{6,2},{7,3},{8,12},{9,13},{10,... | collective-permute-start | bytes 208904 | tf_op jit(solution)/shard_map/ppermute | solution.py:1074
  24.6 4.4 %collective-permute-start.8 = (f32[17,8,128]{2,1,0:T(8,128)S(1)}, f32[17,8,128]{2,1,0:T(8,128)S(1)}, u32[]{:S(2)}, u32[]{:S(2)}) collective-permute-start(f32[17,8,128]{2,1,0:T(8,128)S(1)} %get-tuple-element.71), channel_id=1, source_target_pairs={{0,1},{1,0},{2,3},{3,2},{4,5},{5,4},{6,7},{7,6},{8,9},{9,8},{10,11... | collective-permute-start | bytes 208904 | tf_op jit(solution)/shard_map/ppermute | solution.py:1074
  26.8 3.4 %collective-permute-start.9 = (f32[16,8,128]{2,1,0:T(8,128)S(1)}, f32[16,8,128]{2,1,0:T(8,128)S(1)}, u32[]{:S(2)}, u32[]{:S(2)}) collective-permute-start(f32[16,8,128]{2,1,0:T(8,128)S(1)} %get-tuple-element.72), channel_id=1, source_target_pairs={{0,4},{1,2},{2,1},{3,7},{4,0},{5,6},{6,5},{7,3},{8,12},{9,10},{10,... | collective-permute-start | bytes 196616 | tf_op jit(solution)/shard_map/ppermute | solution.py:1075
  29.1 3.6 %collective-permute-start.12 = (f32[8,128]{1,0:T(8,128)S(1)}, f32[8,128]{1,0:T(8,128)S(1)}, u32[]{:S(2)}, u32[]{:S(2)}) collective-permute-start(f32[8,128]{1,0:T(8,128)S(1)} %fusion.14), channel_id=1, source_target_pairs={{0,16},{1,17},{2,18},{3,19},{4,20},{5,21},{6,22},{7,23},{8,24},{9,... | collective-permute-start | bytes 12296 | tf_op jit(solution)/shard_map/ppermute | solution.py:1085
  30.4 4.5 %collective-permute-start.11 = (f32[2,10,8,128]{3,2,1,0:T(8,128)S(1)}, f32[2,10,8,128]{3,2,1,0:T(8,128)S(1)}, u32[]{:S(2)}, u32[]{:S(2)}) collective-permute-start(f32[2,10,8,128]{3,2,1,0:T(8,128)S(1)} %get-tuple-element.141), channel_id=1, source_target_pairs={{0,1},{1,0},{2,3},{3,2},{4,8},{5,9},{6,10},{7,11},{8,4},{9,5},{10,... | collective-permute-start | bytes 245768 | tf_op jit(solution)/shard_map/ppermute | solution.py:1075
  32.5 2.4 %collective-permute-start.10 = (f32[2,10,8,128]{3,2,1,0:T(8,128)S(1)}, f32[2,10,8,128]{3,2,1,0:T(8,128)S(1)}, u32[]{:S(2)}, u32[]{:S(2)}) collective-permute-start(f32[2,10,8,128]{3,2,1,0:T(8,128)S(1)} %get-tuple-element.142), channel_id=1, source_target_pairs={{0,4},{1,5},{2,6},{3,7},{4,0},{5,1},{6,2},{7,3},{8,12},{9,13},{10,... | collective-permute-start | bytes 245768 | tf_op jit(solution)/shard_map/ppermute | solution.py:1074
  32.5 2.4 %copy-start.4 = (f32[288,128]{1,0:T(8,128)S(1)}, f32[288,128]{1,0:T(8,128)}, u32[]{:S(2)}) copy-start(f32[288,128]{1,0:T(8,128)} %constant.44.clone.refs_7_.refs_11_) | copy-start | bytes 442372
  36.3 4.5 %collective-permute-start.13 = (f32[20,8,128]{2,1,0:T(8,128)S(1)}, f32[20,8,128]{2,1,0:T(8,128)S(1)}, u32[]{:S(2)}, u32[]{:S(2)}) collective-permute-start(f32[20,8,128]{2,1,0:T(8,128)S(1)} %get-tuple-element.82), channel_id=1, source_target_pairs={{0,1},{1,0},{2,3},{3,2},{4,5},{5,4},{6,7},{7,6},{8,9},{9,8},{10,11... | collective-permute-start | bytes 245768 | tf_op jit(solution)/shard_map/ppermute | solution.py:1074
  38.4 2.4 %collective-permute-start.14 = (f32[20,8,128]{2,1,0:T(8,128)S(1)}, f32[20,8,128]{2,1,0:T(8,128)S(1)}, u32[]{:S(2)}, u32[]{:S(2)}) collective-permute-start(f32[20,8,128]{2,1,0:T(8,128)S(1)} %get-tuple-element.83), channel_id=1, source_target_pairs={{0,4},{1,2},{2,1},{3,7},{4,0},{5,6},{6,5},{7,3},{8,12},{9,10},{10,... | collective-permute-start | bytes 245768 | tf_op jit(solution)/shard_map/ppermute | solution.py:1075
  40.9 4.4 %collective-permute-start.16 = (f32[2,8,8,128]{3,2,1,0:T(8,128)S(1)}, f32[2,8,8,128]{3,2,1,0:T(8,128)S(1)}, u32[]{:S(2)}, u32[]{:S(2)}) collective-permute-start(f32[2,8,8,128]{3,2,1,0:T(8,128)S(1)} %get-tuple-element.139), channel_id=1, source_target_pairs={{0,1},{1,0},{2,3},{3,2},{4,8},{5,9},{6,10},{7,11},{8,4},{9,5},{10,... | collective-permute-start | bytes 196616 | tf_op jit(solution)/shard_map/ppermute | solution.py:1075
  43.1 2.2 %collective-permute-start.15 = (f32[2,8,8,128]{3,2,1,0:T(8,128)S(1)}, f32[2,8,8,128]{3,2,1,0:T(8,128)S(1)}, u32[]{:S(2)}, u32[]{:S(2)}) collective-permute-start(f32[2,8,8,128]{3,2,1,0:T(8,128)S(1)} %get-tuple-element.140), channel_id=1, source_target_pairs={{0,4},{1,5},{2,6},{3,7},{4,0},{5,1},{6,2},{7,3},{8,12},{9,13},{10,... | collective-permute-start | bytes 196616 | tf_op jit(solution)/shard_map/ppermute | solution.py:1074
  45.3 10.6 %copy-start.2 = (f32[1,1,8,8,8,128]{5,4,3,2,1,0:T(8,128)S(1)}, f32[1,1,8,8,8,128]{5,4,3,2,1,0:T(8,128)}, u32[]{:S(2)}) copy-start(f32[1,1,8,8,8,128]{5,4,3,2,1,0:T(8,128)} %param.8) | copy-start | bytes 786436
  46.9 12.1 %all-to-all-start = ((f32[32,4,128]{2,1,0:T(4,128)}), f32[32,4,128]{2,1,0:T(4,128)S(1)}, u32[]{:S(2)}, u32[]{:S(2)}) async-start(f32[32,4,128]{2,1,0:T(4,128)} %get-tuple-element.109), calls=%async_computation | async-start | bytes 131072 | tf_op jit(solution)/shard_map/all_to_all | solution.py:1111
  51.2 4.9 %collective-permute-start.17 = (f32[10,8,128]{2,1,0:T(8,128)S(1)}, f32[10,8,128]{2,1,0:T(8,128)S(1)}, u32[]{:S(2)}, u32[]{:S(2)}) collective-permute-start(f32[10,8,128]{2,1,0:T(8,128)S(1)} %get-tuple-element.91), channel_id=1, source_target_pairs={{0,1},{1,0},{2,3},{3,2},{4,5},{5,4},{6,7},{7,6},{8,9},{9,8},{10,11... | collective-permute-start | bytes 122888 | tf_op jit(solution)/shard_map/ppermute | solution.py:1074
  53.0 3.1 %collective-permute-start.18 = (f32[10,8,128]{2,1,0:T(8,128)S(1)}, f32[10,8,128]{2,1,0:T(8,128)S(1)}, u32[]{:S(2)}, u32[]{:S(2)}) collective-permute-start(f32[10,8,128]{2,1,0:T(8,128)S(1)} %get-tuple-element.92), channel_id=1, source_target_pairs={{0,4},{1,2},{2,1},{3,7},{4,0},{5,6},{6,5},{7,3},{8,12},{9,10},{10,... | collective-permute-start | bytes 122888 | tf_op jit(solution)/shard_map/ppermute | solution.py:1075
  53.0 3.1 %collective-permute-start.19 = (f32[10,8,128]{2,1,0:T(8,128)S(1)}, f32[10,8,128]{2,1,0:T(8,128)S(1)}, u32[]{:S(2)}, u32[]{:S(2)}) collective-permute-start(f32[10,8,128]{2,1,0:T(8,128)S(1)} %get-tuple-element.93), channel_id=1, source_target_pairs={{0,4},{1,5},{2,6},{3,7},{4,0},{5,1},{6,2},{7,3},{8,12},{9,13},{10,... | collective-permute-start | bytes 122888 | tf_op jit(solution)/shard_map/ppermute | solution.py:1074
  53.5 4.4 %collective-permute-start.20 = (f32[10,8,128]{2,1,0:T(8,128)S(1)}, f32[10,8,128]{2,1,0:T(8,128)S(1)}, u32[]{:S(2)}, u32[]{:S(2)}) collective-permute-start(f32[10,8,128]{2,1,0:T(8,128)S(1)} %get-tuple-element.94), channel_id=1, source_target_pairs={{0,1},{1,0},{2,3},{3,2},{4,8},{5,9},{6,10},{7,11},{8,4},{9,5},{10,... | collective-permute-start | bytes 122888 | tf_op jit(solution)/shard_map/ppermute | solution.py:1075

commit v10 on v9

--- a/solution.py
+++ b/solution.py
@@ -556,21 +556,34 @@
     for a in range(NODES):
         for b in range(NODES):
             y_ref[a, b] = z_ref[a, b] * weight_tile
-    for a in range(NODES):
+    half = NODES // 2
+
+    def contract(line, wanted):
+        even = [line[i] + line[NODES - 1 - i] for i in range(half)]
+        odd = [line[i] - line[NODES - 1 - i] for i in range(half)]
+        result = {}
+        for node in range(half):
+            if node in wanted:
+                mirrored = STIFF[node, ::-1]
+                both = combine(0.5 * (STIFF[node] + mirrored)[:half], even)
+                apart = combine(0.5 * (STIFF[node] - mirrored)[:half], odd)
+                result[node], result[NODES - 1 - node] = both + apart, both - apart
+        return result
+
+    for place, b in enumerate(layers):
+        first = contract([y_ref[a, b] for a in range(NODES)], range(NODES))
+        for a in range(NODES):
+            u_ref[a, place] = first[a] * float(WEIGHTS[b])
+    for a in range(NODES):
+        second = contract([y_ref[a, b] for b in range(NODES)], layers)
         for place, b in enumerate(layers):
             z = z_ref[a, b]
             third = z * stiff_tiles[0]
             for shift in range(1, NODES):
                 third = third + pltpu.roll(z, shift, 0) * stiff_tiles[shift]
-            first = y_ref[0, b] * float(STIFF[a, 0] * WEIGHTS[b])
-            second = y_ref[a, 0] * float(STIFF[b, 0] * WEIGHTS[a])
-            for other in range(1, NODES):
-                first = first + y_ref[other, b] * float(STIFF[a, other] * WEIGHTS[b])
-                second = second + y_ref[a, other] * float(STIFF[b, other] * WEIGHTS[a])
             weight = float(WEIGHTS[a] * WEIGHTS[b])
-            u_ref[a, place] = por * (third * weight + first + second) + y_ref[a, b] * (
-                shift_mass * weight
-            )
+            total = third * weight + u_ref[a, place] + second[b] * float(WEIGHTS[a])
+            u_ref[a, place] = por * total + y_ref[a, b] * (shift_mass * weight)
 
 
 def sum_column(u_ref):

time: 60.6 us -> 60.5 us (level)
  no operation moved by 1% of the time
where the time goes in v10:
time: 60.5 us; the launch traced here: 60.2 us
  starting transfers between devices  29.2 us (48%)
  waiting for transfers between devices  20.7 us (34%)
  Pallas kernels  7.27 us (12%)
  local copies, waits for them, and re-layouts  1.79 us (3%)
  between operations  0.98 us (2%)
    ppermute x10, starting transfers between devices, trade(): lax.ppermute(first, AXES, swap_pairs(counts, axis, 0, ring))  13.6 us
    ppermute x10, waiting for transfers between devices, trade(): lax.ppermute(second, AXES, swap_pairs(counts, axis, 1, ring))  12.1 us
    ppermute x10, starting transfers between devices, trade(): lax.ppermute(second, AXES, swap_pairs(counts, axis, 1, ring))  10.1 us
    ppermute x10, waiting for transfers between devices, trade(): lax.ppermute(first, AXES, swap_pairs(counts, axis, 0, ring))  7.44 us
    pallas_call x12, Pallas kernels, call(): pl.pallas_call(body, name=name, out_shape=[jax.ShapeDtypeStruct(shape, jn...  7.27 us
    all_to_all x1, starting transfers between devices, gather_stats(): return lax.all_to_all(stats, AXES, 0, 0)  4.3 us
    unnamed x18, local copies, waits for them, and re-layouts  1.52 us
  transfers between devices with their start and end apart: 22, of which 11 were waited for; matrix products, arithmetic and copies ran while one was open for 0% of the time, Pallas kernels for 3%

profile of v10, /device:TPU:0, one launch (start us, length us, event | category | flops | bytes accessed | tf_op | source)
XLA Modules:
  0.0 60.2 jit_solution(2490170533025087140)
XLA Ops:
  0.6 0.9 %copy-done = f32[1,1,8,8,8,128]{5,4,3,2,1,0:T(8,128)S(1)} copy-done((f32[1,1,8,8,8,128]{5,4,3,2,1,0:T(8,128)S(1)}, f32[1,1,8,8,8,128]{5,4,3,2,1,0:T(8,128)}, u32[]{:S(2)}) %copy-start) | copy-done | bytes 262168
  1.6 0.1 start.1
  1.7 0.5 collective-permute-start.1
  2.2 4.1 %collective-permute-start = (f32[9,8,128]{2,1,0:T(8,128)S(1)}, f32[9,8,128]{2,1,0:T(8,128)S(1)}, u32[]{:S(2)}, u32[]{:S(2)}) collective-permute-start(f32[9,8,128]{2,1,0:T(8,128)S(1)} %get-tuple-element.59), channel_id=1, source_target_pairs={{0,1},{1,0},{2,3},{3,2},{4,5},{5,4},{6,7},{7,6},{8,9},{9,8},{10,11... | collective-permute-start | bytes 110600 | tf_op jit(solution)/shard_map/ppermute | solution.py:1087
  6.3 1.9 %collective-permute-done = f32[9,8,128]{2,1,0:T(8,128)S(1)} collective-permute-done((f32[9,8,128]{2,1,0:T(8,128)S(1)}, f32[9,8,128]{2,1,0:T(8,128)S(1)}, u32[]{:S(2)}, u32[]{:S(2)}) %collective-permute-start) | collective-permute-done | bytes 36896 | tf_op jit(solution)/shard_map/ppermute | solution.py:1087
  8.3 0.0 copy-start.5
  8.4 0.1 collective-permute-start.2
  8.4 0.5 copy-done.8
  9.0 2.0 %collective-permute-start.3 = (f32[10,8,128]{2,1,0:T(8,128)S(1)}, f32[10,8,128]{2,1,0:T(8,128)S(1)}, u32[]{:S(2)}, u32[]{:S(2)}) collective-permute-start(f32[10,8,128]{2,1,0:T(8,128)S(1)} %get-tuple-element.134), channel_id=1, source_target_pairs={{0,1},{1,0},{2,3},{3,2},{4,8},{5,9},{6,10},{7,11},{8,4},{9,5},{10,... | collective-permute-start | bytes 122888 | tf_op jit(solution)/shard_map/ppermute | solution.py:1088
  11.0 2.0 %collective-permute-done.3.refs_6_ = f32[10,8,128]{2,1,0:T(8,128)S(1)} collective-permute-done((f32[10,8,128]{2,1,0:T(8,128)S(1)}, f32[10,8,128]{2,1,0:T(8,128)S(1)}, u32[]{:S(2)}, u32[]{:S(2)}) %collective-permute-start.3) | collective-permute-done | bytes 40992 | tf_op jit(solution)/shard_map/ppermute | solution.py:1088
  13.0 0.0 copy-start.6
  13.0 0.9 %first_solve.1 = (f32[104,1280]{1,0:T(8,128)S(1)}, f32[10,16,128]{2,1,0:T(8,128)S(1)}, f32[21,8,128]{2,1,0:T(8,128)S(1)}, f32[21,8,128]{2,1,0:T(8,128)S(1)}) custom-call(f32[8,8,8,128]{3,2,1,0:T(8,128)S(1)} %bitcast.63, f32[1,128]{1,0:T(1,128)S(1)} %subtract_bitcast_fusion.refs_1_.refs_5_.refs_2_, f32[8,128]{1,0:T(8,128)S(1)} %bitcast.66, ...), custom_call_target="tpu_custom_call" | custom-call | flops 900000000 | bytes 2700000 | tf_op jit(solution)/shard_map/first_solve/pallas_call | solution.py:1056
  14.0 2.1 %collective-permute-start.4 = (f32[21,8,128]{2,1,0:T(8,128)S(1)}, f32[21,8,128]{2,1,0:T(8,128)S(1)}, u32[]{:S(2)}, u32[]{:S(2)}) collective-permute-start(f32[21,8,128]{2,1,0:T(8,128)S(1)} %get-tuple-element.64), channel_id=1, source_target_pairs={{0,1},{1,0},{2,3},{3,2},{4,5},{5,4},{6,7},{7,6},{8,9},{9,8},{10,11... | collective-permute-start | bytes 258056 | tf_op jit(solution)/shard_map/ppermute | solution.py:1087
  16.1 0.1 pad.29.clone
  16.1 0.5 rest_of_solve.2
  16.6 1.9 %collective-permute-done.4 = f32[21,8,128]{2,1,0:T(8,128)S(1)} collective-permute-done((f32[21,8,128]{2,1,0:T(8,128)S(1)}, f32[21,8,128]{2,1,0:T(8,128)S(1)}, u32[]{:S(2)}, u32[]{:S(2)}) %collective-permute-start.4) | collective-permute-done | bytes 86048 | tf_op jit(solution)/shard_map/ppermute | solution.py:1087
  18.7 0.1 fusion.7
  18.8 0.9 %collective-permute-start.7 = (f32[17,8,128]{2,1,0:T(8,128)S(1)}, f32[17,8,128]{2,1,0:T(8,128)S(1)}, u32[]{:S(2)}, u32[]{:S(2)}) collective-permute-start(f32[17,8,128]{2,1,0:T(8,128)S(1)} %get-tuple-element.154), channel_id=1, source_target_pairs={{0,28},{1,29},{2,30},{3,31},{4,8},{5,9},{6,10},{7,11},{8,4},{9,5},... | collective-permute-start | bytes 208904 | tf_op jit(solution)/shard_map/ppermute | solution.py:1088
  19.7 0.7 %collective-permute-start.6 = (f32[17,8,128]{2,1,0:T(8,128)S(1)}, f32[17,8,128]{2,1,0:T(8,128)S(1)}, u32[]{:S(2)}, u32[]{:S(2)}) collective-permute-start(f32[17,8,128]{2,1,0:T(8,128)S(1)} %get-tuple-element.155), channel_id=1, source_target_pairs={{0,4},{1,5},{2,6},{3,7},{4,0},{5,1},{6,2},{7,3},{8,12},{9,13},{10,... | collective-permute-start | bytes 208904 | tf_op jit(solution)/shard_map/ppermute | solution.py:1087
  20.4 3.8 %collective-permute-done.7 = f32[17,8,128]{2,1,0:T(8,128)S(1)} collective-permute-done((f32[17,8,128]{2,1,0:T(8,128)S(1)}, f32[17,8,128]{2,1,0:T(8,128)S(1)}, u32[]{:S(2)}, u32[]{:S(2)}) %collective-permute-start.7) | collective-permute-done | bytes 69664 | tf_op jit(solution)/shard_map/ppermute | solution.py:1088
  24.2 0.4 first_apply.1
  24.6 2.1 %collective-permute-start.8 = (f32[17,8,128]{2,1,0:T(8,128)S(1)}, f32[17,8,128]{2,1,0:T(8,128)S(1)}, u32[]{:S(2)}, u32[]{:S(2)}) collective-permute-start(f32[17,8,128]{2,1,0:T(8,128)S(1)} %get-tuple-element.71), channel_id=1, source_target_pairs={{0,1},{1,0},{2,3},{3,2},{4,5},{5,4},{6,7},{7,6},{8,9},{9,8},{10,11... | collective-permute-start | bytes 208904 | tf_op jit(solution)/shard_map/ppermute | solution.py:1087
  26.7 0.1 pad.19.clone
  26.8 0.4 rest_of_apply.1
  27.2 1.8 %collective-permute-done.8 = f32[17,8,128]{2,1,0:T(8,128)S(1)} collective-permute-done((f32[17,8,128]{2,1,0:T(8,128)S(1)}, f32[17,8,128]{2,1,0:T(8,128)S(1)}, u32[]{:S(2)}, u32[]{:S(2)}) %collective-permute-start.8) | collective-permute-done | bytes 69664 | tf_op jit(solution)/shard_map/ppermute | solution.py:1087
  29.0 1.2 %collective-permute-start.12 = (f32[8,128]{1,0:T(8,128)S(1)}, f32[8,128]{1,0:T(8,128)S(1)}, u32[]{:S(2)}, u32[]{:S(2)}) collective-permute-start(f32[8,128]{1,0:T(8,128)S(1)} %fusion.14), channel_id=1, source_target_pairs={{0,16},{1,17},{2,18},{3,19},{4,20},{5,21},{6,22},{7,23},{8,24},{9,... | collective-permute-start | bytes 12296 | tf_op jit(solution)/shard_map/ppermute | solution.py:1098
  30.3 0.1 fusion.3
  30.4 2.1 %collective-permute-start.11 = (f32[2,10,8,128]{3,2,1,0:T(8,128)S(1)}, f32[2,10,8,128]{3,2,1,0:T(8,128)S(1)}, u32[]{:S(2)}, u32[]{:S(2)}) collective-permute-start(f32[2,10,8,128]{3,2,1,0:T(8,128)S(1)} %get-tuple-element.141), channel_id=1, source_target_pairs={{0,1},{1,0},{2,3},{3,2},{4,8},{5,9},{6,10},{7,11},{8,4},{9,5},{10,... | collective-permute-start | bytes 245768 | tf_op jit(solution)/shard_map/ppermute | solution.py:1088
  32.5 0.1 porosity.1.refs_6_.refs_10_
  32.6 0.1 collective-permute-done.12
  32.6 2.3 %collective-permute-done.11.refs_5_ = f32[2,10,8,128]{3,2,1,0:T(8,128)S(1)} collective-permute-done((f32[2,10,8,128]{3,2,1,0:T(8,128)S(1)}, f32[2,10,8,128]{3,2,1,0:T(8,128)S(1)}, u32[]{:S(2)}, u32[]{:S(2)}) %collective-permute-start.11) | collective-permute-done | bytes 81952 | tf_op jit(solution)/shard_map/ppermute | solution.py:1088
  34.9 1.3 %second_solve.1 = (f32[8,8,8,128]{3,2,1,0:T(8,128)S(1)}, f32[104,1280]{1,0:T(8,128)S(1)}, f32[10,16,128]{2,1,0:T(8,128)S(1)}, f32[20,8,128]{2,1,0:T(8,128)S(1)},...) custom-call(f32[8,4,8,128]{3,2,1,0:T(8,128)S(1)} %get-tuple-element.68.refs_1_.refs_0_, ...), custom_call_target="tpu_custom_call" | custom-call | flops 900000000 | bytes 2700000 | tf_op jit(solution)/shard_map/second_solve/pallas_call | solution.py:1056
  36.2 2.1 %collective-permute-start.13 = (f32[20,8,128]{2,1,0:T(8,128)S(1)}, f32[20,8,128]{2,1,0:T(8,128)S(1)}, u32[]{:S(2)}, u32[]{:S(2)}) collective-permute-start(f32[20,8,128]{2,1,0:T(8,128)S(1)} %get-tuple-element.82), channel_id=1, source_target_pairs={{0,1},{1,0},{2,3},{3,2},{4,5},{5,4},{6,7},{7,6},{8,9},{9,8},{10,11... | collective-permute-start | bytes 245768 | tf_op jit(solution)/shard_map/ppermute | solution.py:1087
  38.3 0.2 first_sums.1.refs_10_
  38.5 0.5 rest_of_solve.3
  39.0 1.8 %collective-permute-done.13 = f32[20,8,128]{2,1,0:T(8,128)S(1)} collective-permute-done((f32[20,8,128]{2,1,0:T(8,128)S(1)}, f32[20,8,128]{2,1,0:T(8,128)S(1)}, u32[]{:S(2)}, u32[]{:S(2)}) %collective-permute-start.13) | collective-permute-done | bytes 81952 | tf_op jit(solution)/shard_map/ppermute | solution.py:1087
  40.8 0.1 fusion.11
  40.9 2.2 %collective-permute-start.16 = (f32[2,8,8,128]{3,2,1,0:T(8,128)S(1)}, f32[2,8,8,128]{3,2,1,0:T(8,128)S(1)}, u32[]{:S(2)}, u32[]{:S(2)}) collective-permute-start(f32[2,8,8,128]{3,2,1,0:T(8,128)S(1)} %get-tuple-element.139), channel_id=1, source_target_pairs={{0,1},{1,0},{2,3},{3,2},{4,8},{5,9},{6,10},{7,11},{8,4},{9,5},{10,... | collective-permute-start | bytes 196616 | tf_op jit(solution)/shard_map/ppermute | solution.py:1088
  43.0 2.2 %collective-permute-done.16.refs_4_ = f32[2,8,8,128]{3,2,1,0:T(8,128)S(1)} collective-permute-done((f32[2,8,8,128]{3,2,1,0:T(8,128)S(1)}, f32[2,8,8,128]{3,2,1,0:T(8,128)S(1)}, u32[]{:S(2)}, u32[]{:S(2)}) %collective-permute-start.16) | collective-permute-done | bytes 65568 | tf_op jit(solution)/shard_map/ppermute | solution.py:1088
  45.3 1.5 %late_apply.1 = (f32[8,8,8,128]{3,2,1,0:T(8,128)S(1)}, f32[8,8,8,128]{3,2,1,0:T(8,128)S(1)}, f32[10,8,128]{2,1,0:T(8,128)S(1)}, f32[10,8,128]{2,1,0:T(8,128)S(1)...) custom-call(f32[10,64,128]{2,1,0:T(8,128)S(1)} %get-tuple-element.81.refs_0_, ...), custom_call_target="tpu_custom_call" | custom-call | flops 800000000 | bytes 2400000 | tf_op jit(solution)/shard_map/late_apply/pallas_call | solution.py:1056
  46.8 4.3 %all-to-all-start = ((f32[32,4,128]{2,1,0:T(4,128)}), f32[32,4,128]{2,1,0:T(4,128)S(1)}, u32[]{:S(2)}, u32[]{:S(2)}) async-start(f32[32,4,128]{2,1,0:T(4,128)} %get-tuple-element.109), calls=%async_computation | async-start | bytes 131072 | tf_op jit(solution)/shard_map/all_to_all | solution.py:1124
  51.1 1.8 %collective-permute-start.17 = (f32[10,8,128]{2,1,0:T(8,128)S(1)}, f32[10,8,128]{2,1,0:T(8,128)S(1)}, u32[]{:S(2)}, u32[]{:S(2)}) collective-permute-start(f32[10,8,128]{2,1,0:T(8,128)S(1)} %get-tuple-element.91), channel_id=1, source_target_pairs={{0,1},{1,0},{2,3},{3,2},{4,5},{5,4},{6,7},{7,6},{8,9},{9,8},{10,11... | collective-permute-start | bytes 122888 | tf_op jit(solution)/shard_map/ppermute | solution.py:1087
  52.9 0.5 collective-permute-start.19
  53.4 2.5 %collective-permute-start.20 = (f32[10,8,128]{2,1,0:T(8,128)S(1)}, f32[10,8,128]{2,1,0:T(8,128)S(1)}, u32[]{:S(2)}, u32[]{:S(2)}) collective-permute-start(f32[10,8,128]{2,1,0:T(8,128)S(1)} %get-tuple-element.94), channel_id=1, source_target_pairs={{0,1},{1,0},{2,3},{3,2},{4,8},{5,9},{6,10},{7,11},{8,4},{9,5},{10,... | collective-permute-start | bytes 122888 | tf_op jit(solution)/shard_map/ppermute | solution.py:1088
  55.9 0.1 prepare.1
  56.0 1.9 %collective-permute-done.20.refs_9_ = f32[10,8,128]{2,1,0:T(8,128)S(1)} collective-permute-done((f32[10,8,128]{2,1,0:T(8,128)S(1)}, f32[10,8,128]{2,1,0:T(8,128)S(1)}, u32[]{:S(2)}, u32[]{:S(2)}) %collective-permute-start.20) | collective-permute-done | bytes 40992 | tf_op jit(solution)/shard_map/ppermute | solution.py:1088
  57.9 1.0 %all-to-all-done.refs_12_ = f32[32,4,128]{2,1,0:T(4,128)S(1)} async-done(((f32[32,4,128]{2,1,0:T(4,128)}), f32[32,4,128]{2,1,0:T(4,128)S(1)}, u32[]{:S(2)}, u32[]{:S(2)}) %all-to-all-start) | async-done | bytes 65568 | tf_op jit(solution)/shard_map/all_to_all | solution.py:1124
  58.9 1.3 %late_final.1 = (f32[8,8,8,128]{3,2,1,0:T(8,128)}, f32[8,8,8,128]{3,2,1,0:T(8,128)}, f32[8,8,8,128]{3,2,1,0:T(8,128)}, f32[2]{0:T(128)}) custom-call(f32[8,8,8,128]{3,2,1,0:T(8,128)S(1)} %get-tuple-element.100.refs_0_, f32[8,8,8,128]{3,2,1,0:T(8,128)S(1)} %get-tuple-element.101.refs_1_, f32[8,8,8,128]{3,2,1,0:T(8,128)S(1)} %get-tuple-element.84.refs_1_.refs_9_.refs_2_, ...), custom_call_target="tpu_custom_call" | custom-call | flops 800000000 | bytes 2400000 | tf_op jit(solution)/shard_map/late_final/pallas_call | solution.py:1056
  (66 shorter events, 0.3 us)
Async XLA Ops:
  0.6 1.0 %copy-start = (f32[1,1,8,8,8,128]{5,4,3,2,1,0:T(8,128)S(1)}, f32[1,1,8,8,8,128]{5,4,3,2,1,0:T(8,128)}, u32[]{:S(2)}) copy-start(f32[1,1,8,8,8,128]{5,4,3,2,1,0:T(8,128)} %param.9) | copy-start | bytes 786436
  1.6 11.4 %copy-start.3 = (f32[10,104,128]{2,1,0:T(8,128)S(1)}, f32[10,104,128]{2,1,0:T(8,128)}, u32[]{:S(2)}) copy-start(f32[10,104,128]{2,1,0:T(8,128)} %constant.47.clone.refs_9_.refs_11_) | copy-start | bytes 1597444
  1.7 4.6 %collective-permute-start.1 = (f32[8,8,128]{2,1,0:T(8,128)S(1)}, f32[8,8,128]{2,1,0:T(8,128)S(1)}, u32[]{:S(2)}, u32[]{:S(2)}) collective-permute-start(f32[8,8,128]{2,1,0:T(8,128)S(1)} %get-tuple-element.60), channel_id=1, source_target_pairs={{0,4},{1,2},{2,1},{3,7},{4,0},{5,6},{6,5},{7,3},{8,12},{9,10},{10,... | collective-permute-start | bytes 98312 | tf_op jit(solution)/shard_map/ppermute | solution.py:1088
  2.2 6.1 %collective-permute-start = (f32[9,8,128]{2,1,0:T(8,128)S(1)}, f32[9,8,128]{2,1,0:T(8,128)S(1)}, u32[]{:S(2)}, u32[]{:S(2)}) collective-permute-start(f32[9,8,128]{2,1,0:T(8,128)S(1)} %get-tuple-element.59), channel_id=1, source_target_pairs={{0,1},{1,0},{2,3},{3,2},{4,5},{5,4},{6,7},{7,6},{8,9},{9,8},{10,11... | collective-permute-start | bytes 110600 | tf_op jit(solution)/shard_map/ppermute | solution.py:1087
  6.3 6.7 %copy-start.1 = (f32[1,1,8,8,8,128]{5,4,3,2,1,0:T(8,128)S(1)}, f32[1,1,8,8,8,128]{5,4,3,2,1,0:T(8,128)}, u32[]{:S(2)}) copy-start(f32[1,1,8,8,8,128]{5,4,3,2,1,0:T(8,128)} %param.9) | copy-start | bytes 786436
  8.3 0.7 %copy-start.8 = (s32[1,1,128]{2,1,0:T(1,128)S(1)}, s32[1,1,128]{2,1,0:T(1,128)}, u32[]{:S(2)}) copy-start(s32[1,1,128]{2,1,0:T(1,128)} %param.10) | copy-start | bytes 1540
  8.3 4.6 %copy-start.5 = (f32[104,112]{1,0:T(8,128)S(1)}, f32[104,112]{1,0:T(8,128)}, u32[]{:S(2)}) copy-start(f32[104,112]{1,0:T(8,128)} %constant.45.clone.refs_7_.refs_9_) | copy-start | bytes 139780
  8.4 2.7 %collective-permute-start.2 = (f32[11,8,128]{2,1,0:T(8,128)S(1)}, f32[11,8,128]{2,1,0:T(8,128)S(1)}, u32[]{:S(2)}, u32[]{:S(2)}) collective-permute-start(f32[11,8,128]{2,1,0:T(8,128)S(1)} %pad_maximum_fusion.8), channel_id=1, source_target_pairs={{0,4},{1,5},{2,6},{3,7},{4,0},{5,1},{6,2},{7,3},{8,12},{9,13},{10,... | collective-permute-start | bytes 135176 | tf_op jit(solution)/shard_map/ppermute | solution.py:1087
  9.0 4.0 %collective-permute-start.3 = (f32[10,8,128]{2,1,0:T(8,128)S(1)}, f32[10,8,128]{2,1,0:T(8,128)S(1)}, u32[]{:S(2)}, u32[]{:S(2)}) collective-permute-start(f32[10,8,128]{2,1,0:T(8,128)S(1)} %get-tuple-element.134), channel_id=1, source_target_pairs={{0,1},{1,0},{2,3},{3,2},{4,8},{5,9},{6,10},{7,11},{8,4},{9,5},{10,... | collective-permute-start | bytes 122888 | tf_op jit(solution)/shard_map/ppermute | solution.py:1088
  11.0 2.0 %copy-start.7 = (f32[48,104]{1,0:T(8,128)S(1)}, f32[48,104]{1,0:T(8,128)}, u32[]{:S(2)}) copy-start(f32[48,104]{1,0:T(8,128)} %constant.46.clone.refs_8_.refs_10_) | copy-start | bytes 59908
  13.0 3.1 %copy-start.6 = (f32[64,104]{1,0:T(8,128)S(1)}, f32[64,104]{1,0:T(8,128)}, u32[]{:S(2)}) copy-start(f32[64,104]{1,0:T(8,128)} %constant.48.clone.refs_2_) | copy-start | bytes 79876
  14.0 4.6 %collective-permute-start.4 = (f32[21,8,128]{2,1,0:T(8,128)S(1)}, f32[21,8,128]{2,1,0:T(8,128)S(1)}, u32[]{:S(2)}, u32[]{:S(2)}) collective-permute-start(f32[21,8,128]{2,1,0:T(8,128)S(1)} %get-tuple-element.64), channel_id=1, source_target_pairs={{0,1},{1,0},{2,3},{3,2},{4,5},{5,4},{6,7},{7,6},{8,9},{9,8},{10,11... | collective-permute-start | bytes 258056 | tf_op jit(solution)/shard_map/ppermute | solution.py:1087
  16.1 2.5 %collective-permute-start.5 = (f32[21,8,128]{2,1,0:T(8,128)S(1)}, f32[21,8,128]{2,1,0:T(8,128)S(1)}, u32[]{:S(2)}, u32[]{:S(2)}) collective-permute-start(f32[21,8,128]{2,1,0:T(8,128)S(1)} %get-tuple-element.65), channel_id=1, source_target_pairs={{0,4},{1,2},{2,1},{3,7},{4,0},{5,6},{6,5},{7,3},{8,12},{9,10},{10,... | collective-permute-start | bytes 258056 | tf_op jit(solution)/shard_map/ppermute | solution.py:1088
  18.8 5.3 %collective-permute-start.7 = (f32[17,8,128]{2,1,0:T(8,128)S(1)}, f32[17,8,128]{2,1,0:T(8,128)S(1)}, u32[]{:S(2)}, u32[]{:S(2)}) collective-permute-start(f32[17,8,128]{2,1,0:T(8,128)S(1)} %get-tuple-element.154), channel_id=1, source_target_pairs={{0,28},{1,29},{2,30},{3,31},{4,8},{5,9},{6,10},{7,11},{8,4},{9,5},... | collective-permute-start | bytes 208904 | tf_op jit(solution)/shard_map/ppermute | solution.py:1088
  19.7 4.5 %collective-permute-start.6 = (f32[17,8,128]{2,1,0:T(8,128)S(1)}, f32[17,8,128]{2,1,0:T(8,128)S(1)}, u32[]{:S(2)}, u32[]{:S(2)}) collective-permute-start(f32[17,8,128]{2,1,0:T(8,128)S(1)} %get-tuple-element.155), channel_id=1, source_target_pairs={{0,4},{1,5},{2,6},{3,7},{4,0},{5,1},{6,2},{7,3},{8,12},{9,13},{10,... | collective-permute-start | bytes 208904 | tf_op jit(solution)/shard_map/ppermute | solution.py:1087
  24.6 4.4 %collective-permute-start.8 = (f32[17,8,128]{2,1,0:T(8,128)S(1)}, f32[17,8,128]{2,1,0:T(8,128)S(1)}, u32[]{:S(2)}, u32[]{:S(2)}) collective-permute-start(f32[17,8,128]{2,1,0:T(8,128)S(1)} %get-tuple-element.71), channel_id=1, source_target_pairs={{0,1},{1,0},{2,3},{3,2},{4,5},{5,4},{6,7},{7,6},{8,9},{9,8},{10,11... | collective-permute-start | bytes 208904 | tf_op jit(solution)/shard_map/ppermute | solution.py:1087
  26.8 3.4 %collective-permute-start.9 = (f32[16,8,128]{2,1,0:T(8,128)S(1)}, f32[16,8,128]{2,1,0:T(8,128)S(1)}, u32[]{:S(2)}, u32[]{:S(2)}) collective-permute-start(f32[16,8,128]{2,1,0:T(8,128)S(1)} %get-tuple-element.72), channel_id=1, source_target_pairs={{0,4},{1,2},{2,1},{3,7},{4,0},{5,6},{6,5},{7,3},{8,12},{9,10},{10,... | collective-permute-start | bytes 196616 | tf_op jit(solution)/shard_map/ppermute | solution.py:1088
  29.0 3.6 %collective-permute-start.12 = (f32[8,128]{1,0:T(8,128)S(1)}, f32[8,128]{1,0:T(8,128)S(1)}, u32[]{:S(2)}, u32[]{:S(2)}) collective-permute-start(f32[8,128]{1,0:T(8,128)S(1)} %fusion.14), channel_id=1, source_target_pairs={{0,16},{1,17},{2,18},{3,19},{4,20},{5,21},{6,22},{7,23},{8,24},{9,... | collective-permute-start | bytes 12296 | tf_op jit(solution)/shard_map/ppermute | solution.py:1098
  30.4 4.5 %collective-permute-start.11 = (f32[2,10,8,128]{3,2,1,0:T(8,128)S(1)}, f32[2,10,8,128]{3,2,1,0:T(8,128)S(1)}, u32[]{:S(2)}, u32[]{:S(2)}) collective-permute-start(f32[2,10,8,128]{3,2,1,0:T(8,128)S(1)} %get-tuple-element.141), channel_id=1, source_target_pairs={{0,1},{1,0},{2,3},{3,2},{4,8},{5,9},{6,10},{7,11},{8,4},{9,5},{10,... | collective-permute-start | bytes 245768 | tf_op jit(solution)/shard_map/ppermute | solution.py:1088
  32.5 2.4 %collective-permute-start.10 = (f32[2,10,8,128]{3,2,1,0:T(8,128)S(1)}, f32[2,10,8,128]{3,2,1,0:T(8,128)S(1)}, u32[]{:S(2)}, u32[]{:S(2)}) collective-permute-start(f32[2,10,8,128]{3,2,1,0:T(8,128)S(1)} %get-tuple-element.142), channel_id=1, source_target_pairs={{0,4},{1,5},{2,6},{3,7},{4,0},{5,1},{6,2},{7,3},{8,12},{9,13},{10,... | collective-permute-start | bytes 245768 | tf_op jit(solution)/shard_map/ppermute | solution.py:1087
  32.5 2.4 %copy-start.4 = (f32[288,128]{1,0:T(8,128)S(1)}, f32[288,128]{1,0:T(8,128)}, u32[]{:S(2)}) copy-start(f32[288,128]{1,0:T(8,128)} %constant.44.clone.refs_7_.refs_11_) | copy-start | bytes 442372
  36.2 4.5 %collective-permute-start.13 = (f32[20,8,128]{2,1,0:T(8,128)S(1)}, f32[20,8,128]{2,1,0:T(8,128)S(1)}, u32[]{:S(2)}, u32[]{:S(2)}) collective-permute-start(f32[20,8,128]{2,1,0:T(8,128)S(1)} %get-tuple-element.82), channel_id=1, source_target_pairs={{0,1},{1,0},{2,3},{3,2},{4,5},{5,4},{6,7},{7,6},{8,9},{9,8},{10,11... | collective-permute-start | bytes 245768 | tf_op jit(solution)/shard_map/ppermute | solution.py:1087
  38.3 2.4 %collective-permute-start.14 = (f32[20,8,128]{2,1,0:T(8,128)S(1)}, f32[20,8,128]{2,1,0:T(8,128)S(1)}, u32[]{:S(2)}, u32[]{:S(2)}) collective-permute-start(f32[20,8,128]{2,1,0:T(8,128)S(1)} %get-tuple-element.83), channel_id=1, source_target_pairs={{0,4},{1,2},{2,1},{3,7},{4,0},{5,6},{6,5},{7,3},{8,12},{9,10},{10,... | collective-permute-start | bytes 245768 | tf_op jit(solution)/shard_map/ppermute | solution.py:1088
  40.9 4.4 %collective-permute-start.16 = (f32[2,8,8,128]{3,2,1,0:T(8,128)S(1)}, f32[2,8,8,128]{3,2,1,0:T(8,128)S(1)}, u32[]{:S(2)}, u32[]{:S(2)}) collective-permute-start(f32[2,8,8,128]{3,2,1,0:T(8,128)S(1)} %get-tuple-element.139), channel_id=1, source_target_pairs={{0,1},{1,0},{2,3},{3,2},{4,8},{5,9},{6,10},{7,11},{8,4},{9,5},{10,... | collective-permute-start | bytes 196616 | tf_op jit(solution)/shard_map/ppermute | solution.py:1088
  43.0 2.2 %collective-permute-start.15 = (f32[2,8,8,128]{3,2,1,0:T(8,128)S(1)}, f32[2,8,8,128]{3,2,1,0:T(8,128)S(1)}, u32[]{:S(2)}, u32[]{:S(2)}) collective-permute-start(f32[2,8,8,128]{3,2,1,0:T(8,128)S(1)} %get-tuple-element.140), channel_id=1, source_target_pairs={{0,4},{1,5},{2,6},{3,7},{4,0},{5,1},{6,2},{7,3},{8,12},{9,13},{10,... | collective-permute-start | bytes 196616 | tf_op jit(solution)/shard_map/ppermute | solution.py:1087
  45.3 10.6 %copy-start.2 = (f32[1,1,8,8,8,128]{5,4,3,2,1,0:T(8,128)S(1)}, f32[1,1,8,8,8,128]{5,4,3,2,1,0:T(8,128)}, u32[]{:S(2)}) copy-start(f32[1,1,8,8,8,128]{5,4,3,2,1,0:T(8,128)} %param.8) | copy-start | bytes 786436
  46.8 12.1 %all-to-all-start = ((f32[32,4,128]{2,1,0:T(4,128)}), f32[32,4,128]{2,1,0:T(4,128)S(1)}, u32[]{:S(2)}, u32[]{:S(2)}) async-start(f32[32,4,128]{2,1,0:T(4,128)} %get-tuple-element.109), calls=%async_computation | async-start | bytes 131072 | tf_op jit(solution)/shard_map/all_to_all | solution.py:1124
  51.1 4.9 %collective-permute-start.17 = (f32[10,8,128]{2,1,0:T(8,128)S(1)}, f32[10,8,128]{2,1,0:T(8,128)S(1)}, u32[]{:S(2)}, u32[]{:S(2)}) collective-permute-start(f32[10,8,128]{2,1,0:T(8,128)S(1)} %get-tuple-element.91), channel_id=1, source_target_pairs={{0,1},{1,0},{2,3},{3,2},{4,5},{5,4},{6,7},{7,6},{8,9},{9,8},{10,11... | collective-permute-start | bytes 122888 | tf_op jit(solution)/shard_map/ppermute | solution.py:1087
  52.9 3.1 %collective-permute-start.18 = (f32[10,8,128]{2,1,0:T(8,128)S(1)}, f32[10,8,128]{2,1,0:T(8,128)S(1)}, u32[]{:S(2)}, u32[]{:S(2)}) collective-permute-start(f32[10,8,128]{2,1,0:T(8,128)S(1)} %get-tuple-element.92), channel_id=1, source_target_pairs={{0,4},{1,2},{2,1},{3,7},{4,0},{5,6},{6,5},{7,3},{8,12},{9,10},{10,... | collective-permute-start | bytes 122888 | tf_op jit(solution)/shard_map/ppermute | solution.py:1088
  52.9 3.1 %collective-permute-start.19 = (f32[10,8,128]{2,1,0:T(8,128)S(1)}, f32[10,8,128]{2,1,0:T(8,128)S(1)}, u32[]{:S(2)}, u32[]{:S(2)}) collective-permute-start(f32[10,8,128]{2,1,0:T(8,128)S(1)} %get-tuple-element.93), channel_id=1, source_target_pairs={{0,4},{1,5},{2,6},{3,7},{4,0},{5,1},{6,2},{7,3},{8,12},{9,13},{10,... | collective-permute-start | bytes 122888 | tf_op jit(solution)/shard_map/ppermute | solution.py:1087
  53.4 4.4 %collective-permute-start.20 = (f32[10,8,128]{2,1,0:T(8,128)S(1)}, f32[10,8,128]{2,1,0:T(8,128)S(1)}, u32[]{:S(2)}, u32[]{:S(2)}) collective-permute-start(f32[10,8,128]{2,1,0:T(8,128)S(1)} %get-tuple-element.94), channel_id=1, source_target_pairs={{0,1},{1,0},{2,3},{3,2},{4,8},{5,9},{6,10},{7,11},{8,4},{9,5},{10,... | collective-permute-start | bytes 122888 | tf_op jit(solution)/shard_map/ppermute | solution.py:1088
